TPU v7x, 128 devices: a whole 4x4x4 slice. The times are simulated.
128 devices in a mesh: grp: 4 (over y), seq: 32 (over z, x, core).
Axes of the slice: x: 4, y: 4, z: 4, core: 2. Of those that a mesh axis runs over, the one named last changes fastest.
Arguments:
- query_input: bfloat16 [4, 1536, 4096], P('grp', 'seq'), may hold values from -240 to 240, as said below
- key_input: bfloat16 [4, 1536, 4096], P('grp', 'seq'), may hold values from -240 to 240, as said below
- value_input: bfloat16 [4, 1536, 4096], P('grp', 'seq'), may hold values from -6 to 6
- resid: bfloat16 [4, 1536, 4096], P('grp', 'seq'), may hold values from -6 to 6
- gate: float32 [4, 4096], P('grp'), may hold values from 0.5 to 2
- query_norm_gain: float32 [4096], replicated, may hold values from 0.7 to 2
- key_norm_gain: float32 [4096], replicated, may hold values from 0.7 to 2
- output_weight: bfloat16 [4096, 4096], P('seq'), may hold values from -0.09375 to 0.09375
- latents: bfloat16 [16, 64, 128, 16], P('grp', 'seq'), may hold values from -6 to 6
- w_in: bfloat16 [3, 144, 384], replicated, may hold values from -0.3125 to 0.3125
- b_in: float32 [384], replicated, may hold values from -3 to 3
- norm_gain: float32 [384], replicated, may hold values from 0.5 to 2
- w_mid: bfloat16 [3, 3456, 384], replicated, may hold values from -0.0625 to 0.0625
- b_mid: float32 [384], replicated, may hold values from -3 to 3
Outputs:
- attn_out: bfloat16 [4, 1536, 4096], P('grp', 'seq')
- decoded: bfloat16 [4, 16, 64, 128, 384], P('grp', None, 'seq')
Inputs may be any that keep to these rules, and one draw needn't show every extreme that they name: `query_input`: projected query features; a few tokens of a request may have one head's features scaled by up to 40. `key_input`: projected key features; a few tokens of a request may have one head's features scaled by up to 40.
All inputs are finite; a program needn't handle non-finite values.
Results may differ from a plain program's by a relative error of at most 0.011.
Values may be sent and summed in bfloat16 or wider, within the bound.
No kernel may reach another device: no remote copies, remote signals or barrier semaphores. Data moves between devices by JAX's collectives and lax.ppermute only.
A program may use at most 384 MiB of HBM per device.

v0:
```python
import jax
import jax.numpy as jnp
from jax import lax
from jax.sharding import PartitionSpec as P


def for_sending(x):
    return jax.tree.map(lambda a: a.astype(jnp.bfloat16) if a.dtype == jnp.float32 else a, x)


def padded_2(cells, sides, width):
    for axis, dim in sides:
        count = lax.axis_size(axis)
        ends = count - 1
        head = lax.slice_in_dim(cells, 0, width, axis=dim)
        tail = lax.slice_in_dim(cells, cells.shape[dim] - width, cells.shape[dim], axis=dim)
        cells = jnp.concatenate(
            [
                lax.ppermute(tail, axis, [(i, (i + 1) % count) for i in range(ends)]),
                cells,
                lax.ppermute(head, axis, [((i + 1) % count, i) for i in range(ends)]),
            ],
            axis=dim,
        )
    return cells


def rms_scaled(token_rows, gain_vec):
    values = token_rows.astype(jnp.float32)
    factor = lax.rsqrt(jnp.mean(values * values, axis=-1, keepdims=True) + 1e-06)
    return values * factor * gain_vec


def attend_head(query_matrix, keys_here, values_here):
    row_count = query_matrix.shape[0]
    head_width = query_matrix.shape[1]
    block_rows = 512
    blocks = query_matrix.reshape(row_count // block_rows, block_rows, head_width)

    def one_block(query_rows):
        scores = jnp.einsum(
            "qd,kd->qk", query_rows, keys_here, preferred_element_type=jnp.float32
        ) * head_width ** (-0.5)
        row_peak = jnp.max(scores, axis=-1, keepdims=True)
        exponent = jnp.exp(scores - row_peak)
        weights = (exponent / jnp.sum(exponent, axis=-1, keepdims=True)).astype(jnp.bfloat16)
        return jnp.dot(weights, values_here, preferred_element_type=jnp.float32).astype(
            jnp.bfloat16
        )

    return lax.map(one_block, blocks).reshape(row_count, head_width)


def conv_rows(frames, kernel):
    frame_count = frames.shape[0] - 2
    height = frames.shape[1] - 2
    width_cells = frames.shape[2]
    padded = jnp.pad(frames, ((0, 0), (0, 0), (1, 1), (0, 0)))
    columns = jnp.concatenate(
        [
            padded[:, row_tap : row_tap + height, col_tap : col_tap + width_cells, :]
            for row_tap in range(3)
            for col_tap in range(3)
        ],
        axis=-1,
    )
    flattened = columns.reshape(frames.shape[0], height * width_cells, columns.shape[-1])
    summed = jnp.zeros((frame_count * height * width_cells, kernel.shape[2]), jnp.float32)
    for time_tap in range(3):
        taken = flattened[time_tap : time_tap + frame_count].reshape(
            frame_count * height * width_cells, columns.shape[-1]
        )
        summed = summed + jnp.dot(taken, kernel[time_tap], preferred_element_type=jnp.float32)
    return summed.reshape(frame_count, height, width_cells, kernel.shape[2])


def lead_frames(frames):
    lead = jnp.zeros((2,) + frames.shape[1:], frames.dtype)
    return jnp.concatenate([lead, frames], axis=0)


def activate(hidden_rows, gain_vec):
    return jax.nn.silu(rms_scaled(hidden_rows, gain_vec)).astype(jnp.bfloat16)


def on_device(
    query_input,
    key_input,
    value_input,
    resid,
    gate,
    query_norm_gain,
    key_norm_gain,
    output_weight,
    latents,
    w_in,
    b_in,
    norm_gain,
    w_mid,
    b_mid,
):
    cohort_index = lax.axis_index("grp")
    decoder_here = cohort_index == lax.axis_size("grp") - 1
    clip_frames = lax.all_gather(latents, "grp", axis=0, tiled=True)
    channels = w_in.shape[2]
    tok_rows = query_input.shape[1]
    query_matrix = rms_scaled(query_input[0], query_norm_gain).astype(jnp.bfloat16)
    keys_normed = rms_scaled(key_input[0], key_norm_gain).astype(jnp.bfloat16)
    head_query, head_key, head_value = (
        lax.all_to_all(query_matrix, "seq", split_axis=1, concat_axis=0, tiled=True),
        lax.all_to_all(keys_normed, "seq", split_axis=1, concat_axis=0, tiled=True),
        lax.all_to_all(value_input[0], "seq", split_axis=1, concat_axis=0, tiled=True),
    )

    def attention_core():
        outputs = [attend_head(head_query, head_key, head_value)]
        return jnp.concatenate(outputs, axis=1)

    def attention_blank():
        return jnp.zeros(head_query.shape, jnp.bfloat16)

    heads_out = lax.cond(decoder_here, attention_blank, attention_core)
    token_out = lax.all_to_all(
        for_sending(heads_out), "seq", split_axis=0, concat_axis=1, tiled=True
    ).astype(heads_out.dtype)
    start_sum = jnp.zeros((tok_rows, output_weight.shape[1]), jnp.float32)
    weight_piece = lax.all_gather(output_weight, "seq", axis=0, tiled=True)
    part_cols = lax.slice_in_dim(token_out, 0, weight_piece.shape[0], axis=1)
    projected = start_sum + jnp.dot(part_cols, weight_piece, preferred_element_type=jnp.float32)
    combined = (resid[0].astype(jnp.float32) + gate[0][None, :] * projected).astype(jnp.bfloat16)
    attn_out = jnp.where(decoder_here, jnp.zeros_like(combined), combined)[None]
    video_shape = clip_frames.shape[:3] + (channels,)
    extended = padded_2(clip_frames, (("seq", 1),), 1)

    def first_segment():
        first_conv = (conv_rows(lead_frames(extended), w_in) + b_in).astype(jnp.bfloat16)
        return (first_conv, activate(first_conv, norm_gain))

    def first_blank():
        return (jnp.zeros(video_shape, jnp.bfloat16), jnp.zeros(video_shape, jnp.bfloat16))

    first_conv, activated = lax.cond(decoder_here, first_segment, first_blank)
    active_ext = padded_2(activated, (("seq", 1),), 1)

    def second_segment():
        second_conv = conv_rows(lead_frames(active_ext), w_mid) + b_mid
        return (first_conv.astype(jnp.float32) + second_conv).astype(jnp.bfloat16)

    def second_blank():
        return jnp.zeros(video_shape, jnp.bfloat16)

    clip_out = lax.cond(decoder_here, second_segment, second_blank)
    return (attn_out, clip_out[None])


def solution(mesh):
    placed = (
        P("grp", "seq", None),
        P("grp", "seq", None),
        P("grp", "seq", None),
        P("grp", "seq", None),
        P("grp", None),
        P(),
        P(),
        P("seq", None),
        P("grp", "seq", None, None),
        P(),
        P(),
        P(),
        P(),
        P(),
    )
    return jax.shard_map(
        on_device,
        mesh=mesh,
        in_specs=placed,
        out_specs=(P("grp", "seq", None), P("grp", None, "seq", None, None)),
        check_vma=False,
    )
```

profile of v0, /device:TPU:27, one launch (start us, length us, event | category | flops | bytes accessed | tf_op | source)
XLA Modules:
  0.0 350.6 jit_solution(7619738966985377446)
XLA Ops:
  8.7 7.6 %all_gather.7 = bf16[16,2,128,16]{2,1,0,3:T(2,128)(2,1)S(1)} all-gather(bf16[4,2,128,16]{2,1,0,3:T(2,128)(2,1)S(1)} %copy.30), channel_id=1, replica_groups=mesh['grp'=4,'seq'=32] {'grp'}, dimensions={0}, use_global_device_ids=true | all-gather | bytes 163840 | tf_op jit(solution)/shard_map/all_gather | solution.py:104
  16.4 6.6 %collective-permute-start = (bf16[16,1,128,16]{2,1,0,3:T(2,128)(2,1)S(1)}, bf16[16,1,128,16]{2,1,0,3:T(2,128)(2,1)S(1)}, u32[]{:S(2)}, u32[]{:S(2)}) collective-permute-start(bf16[16,1,128,16]{2,1,0,3:T(2,128)(2,1)S(1)} %get-tuple-element.113), channel_id=1, source_target_pairs={{0,1},{1,2},{2,3},{3,4},{4,5},{5,6},{6,7},{7,8},{8,9},{9,10},{10,1... | collective-permute-start | bytes 196616 | tf_op jit(solution)/shard_map/ppermute | solution.py:19
  29.3 8.8 %all-to-all-start = ((bf16[48,32,128]{2,0,1:T(8,128)(2,1)}), bf16[48,32,128]{2,0,1:T(8,128)(2,1)}, u32[]{:S(2)}, u32[]{:S(2)}) async-start(bf16[48,32,128]{2,0,1:T(8,128)(2,1)} %copy.26), calls=%async_computation | async-start | bytes 786432 | tf_op jit(solution)/shard_map/all_to_all | solution.py:110
  38.6 31.9 %conditional.4 = (bf16[16,2,128,384]{3,2,1,0:T(8,128)(2,1)}, bf16[16,2,128,384]{3,2,1,0:T(8,128)(2,1)S(1)}) conditional(s32[]{:T(128)} %convert_element_type.75, () %tuple.37, (bf16[16,4,128,16]{2,1,0,3:T(4,128)(2,1)S(1)}, bf16[3,144,384]{2,1,0:T(8,128)(2,1)}, f32[384]{0:T(512)S(1)}, f32[384]{0:T(512)S(1)}) %tuple.75), branch_computations={%region_8.9_spmd, %region_9.11_spmd} | conditional | flops 1385697280 | bytes 66576912 | solution.py:142
  48.1 4.8 %fusion.15 = f32[4096,384]{1,0:T(8,128)} fusion(bf16[4096,144]{0,1:T(8,128)(2,1)S(1)} %reshape.127, bf16[3,144,384]{2,1,0:T(8,128)(2,1)} %get-tuple-element.79), kind=kOutput, calls=%fused_computation.32 | convolution fusion | flops 452984832 | bytes 7581696 | tf_op jit(solution)/shard_map/cond/branch_1_fun/dot_general | solution.py:73
  53.7 4.8 %fusion.17 = f32[4096,384]{1,0:T(8,128)} fusion(bf16[4096,144]{0,1:T(8,128)(2,1)S(1)} %reshape.126, bf16[3,144,384]{2,1,0:T(8,128)(2,1)} %get-tuple-element.79), kind=kOutput, calls=%fused_computation.34 | convolution fusion | flops 452984832 | bytes 7581696 | tf_op jit(solution)/shard_map/cond/branch_1_fun/dot_general | solution.py:73
  59.5 7.8 %multiply_reduce_fusion = (f32[4096]{0:T(1024)S(1)}, f32[4096,384]{1,0:T(8,128)S(1)}) fusion(f32[384]{0:T(512)S(1)} %get-tuple-element.80, bf16[4096,144]{0,1:T(8,128)(2,1)S(1)} %reshape.128, bf16[3,144,384]{2,1,0:T(8,128)(2,1)} %get-tuple-element.79, f32[4096,384]{1,0:T(8,128)} %fusion.17, f32[4096,384]{1,0:T(8,128)} %fusion.15), kind=kOutput, calls=%fused_computation.12 | convolution fusion | flops 463990784 | bytes 20182528 | tf_op jit(solution)/shard_map/cond/branch_1_fun/dot_general | solution.py:73
  79.4 7.7 %all-to-all-start.1 = ((bf16[48,32,128]{2,0,1:T(8,128)(2,1)}), bf16[48,32,128]{2,0,1:T(8,128)(2,1)S(1)}, u32[]{:S(2)}, u32[]{:S(2)}) async-start(bf16[48,32,128]{2,0,1:T(8,128)(2,1)} %copy.27), calls=%async_computation.1 | async-start | bytes 786432 | tf_op jit(solution)/shard_map/all_to_all | solution.py:111
  89.1 53.4 %all-to-all-done.1 = bf16[48,32,128]{2,0,1:T(8,128)(2,1)S(1)} async-done(((bf16[48,32,128]{2,0,1:T(8,128)(2,1)}), bf16[48,32,128]{2,0,1:T(8,128)(2,1)S(1)}, u32[]{:S(2)}, u32[]{:S(2)}) %all-to-all-start.1) | async-done | bytes 393248 | tf_op jit(solution)/shard_map/all_to_all | solution.py:111
  142.5 4.9 %all-to-all-start.2 = ((bf16[48,32,128]{2,0,1:T(8,128)(2,1)}), bf16[48,32,128]{2,0,1:T(8,128)(2,1)}, u32[]{:S(2)}, u32[]{:S(2)}) async-start(bf16[48,32,128]{2,0,1:T(8,128)(2,1)} %copy.28), calls=%async_computation.2 | async-start | bytes 786432 | tf_op jit(solution)/shard_map/all_to_all | solution.py:112
  147.4 9.4 %all-to-all-done.2 = bf16[48,32,128]{2,0,1:T(8,128)(2,1)} async-done(((bf16[48,32,128]{2,0,1:T(8,128)(2,1)}), bf16[48,32,128]{2,0,1:T(8,128)(2,1)}, u32[]{:S(2)}, u32[]{:S(2)}) %all-to-all-start.2) | async-done | bytes 393248 | tf_op jit(solution)/shard_map/all_to_all | solution.py:112
  157.6 5.4 %all-to-all-start.3 = ((bf16[32,48,128]{2,1,0:T(8,128)(2,1)}), bf16[32,48,128]{2,1,0:T(8,128)(2,1)}, u32[]{:S(2)}, u32[]{:S(2)}) async-start(bf16[32,48,128]{2,1,0:T(8,128)(2,1)} %bitcast.26), calls=%async_computation.3 | async-start | bytes 786432 | tf_op jit(solution)/shard_map/all_to_all | solution.py:123
  163.0 5.1 %pad_maximum_fusion = bf16[16,4,128,384]{3,2,1,0:T(8,128)(2,1)} fusion(bf16[16,1,128,384]{3,2,1,0:T(8,128)(2,1)} %collective-permute-done.3, bf16[16,2,128,384]{3,2,1,0:T(8,128)(2,1)S(1)} %get-tuple-element.75, bf16[16,1,128,384]{3,2,1,0:T(8,128)(2,1)} %collective-permute-done.2), kind=kLoop, calls=%fused_computation.66 | loop fusion | flops 6291456 | bytes 12582912 | tf_op jit(solution)/shard_map/concatenate | solution.py:17
  168.1 156.6 %conditional.5 = (bf16[1,16,2,128,384]{4,3,2,1,0:T(8,128)(2,1)S(1)}) conditional(s32[]{:T(128)} %convert_element_type.75, () %tuple.36, (bf16[16,2,128,384]{3,2,1,0:T(8,128)(2,1)}, bf16[16,4,128,384]{3,2,1,0:T(8,128)(2,1)}, bf16[3,3456,384]{2,1,0:T(8,128)(2,1)}, f32[384]{0:T(512)}) %tuple.39), branch_computations={%region_11.12_spmd, %region_12.13_spmd} | conditional | flops 32624345088 | bytes 438541888 | solution.py:152
  168.3 3.8 %concatenate.14 = bf16[18,4,128,384]{3,2,1,0:T(8,128)(2,1)S(1)} pad(bf16[16,4,128,384]{3,2,1,0:T(8,128)(2,1)} %get-tuple-element.67, bf16[]{:T(256)} %constant.44.clone), padding=2_0x0_0x0_0x0_0 | pad | bytes 13369346 | tf_op jit(solution)/shard_map/cond/branch_1_fun/concatenate | solution.py:79
  178.5 3.9 %fusion.23 = bf16[18,2,128,3456]{3,2,1,0:T(8,128)(2,1)} fusion(bf16[18,2,128,3456]{3,2,1,0:T(8,128)(2,1)} %slice_dynamic-update-slice_fusion.5, bf16[18,4,128,384]{3,2,1,0:T(8,128)(2,1)S(1)} %concatenate.14), kind=kLoop, calls=%fused_computation.49 | loop fusion | bytes 10616832 | tf_op jit(solution)/shard_map/cond
  188.6 4.0 %fusion.25 = bf16[18,2,128,3456]{3,2,1,0:T(8,128)(2,1)} fusion(bf16[18,2,128,3456]{3,2,1,0:T(8,128)(2,1)} %slice_dynamic-update-slice_fusion.4, bf16[18,4,128,384]{3,2,1,0:T(8,128)(2,1)S(1)} %concatenate.14), kind=kLoop, calls=%fused_computation.51 | loop fusion | bytes 10616832 | tf_op jit(solution)/shard_map/cond
  192.5 3.8 %fusion.26 = bf16[18,2,128,3456]{3,2,1,0:T(8,128)(2,1)} fusion(bf16[18,2,128,3456]{3,2,1,0:T(8,128)(2,1)} %fusion.25, bf16[18,4,128,384]{3,2,1,0:T(8,128)(2,1)S(1)} %concatenate.14), kind=kLoop, calls=%fused_computation.52 | loop fusion | bytes 10616832 | tf_op jit(solution)/shard_map/cond
  198.7 4.1 %fusion.27 = bf16[18,2,128,3456]{3,2,1,0:T(8,128)(2,1)} fusion(bf16[18,2,128,3456]{3,2,1,0:T(8,128)(2,1)} %slice_dynamic-update-slice_fusion.3, bf16[18,4,128,384]{3,2,1,0:T(8,128)(2,1)S(1)} %concatenate.14), kind=kLoop, calls=%fused_computation.53 | loop fusion | bytes 10616832 | tf_op jit(solution)/shard_map/cond/branch_1_fun/concatenate | solution.py:59
  202.9 55.8 %fusion.50 = (bf16[16,2,128,3456]{3,2,1,0:T(8,128)(2,1)}, bf16[16,2,128,3456]{3,2,1,0:T(8,128)(2,1)}, bf16[16,2,128,3456]{3,2,1,0:T(8,128)(2,1)}) fusion(bf16[18,2,128,3456]{3,2,1,0:T(8,128)(2,1)} %fusion.27), kind=kLoop, calls=%fused_computation.90 | loop fusion | bytes 169869312 | tf_op jit(solution)/shard_map/cond/branch_1_fun/slice | solution.py:70
  258.7 19.3 %fusion.30 = f32[4096,384]{1,0:T(8,128)S(1)} fusion(bf16[4096,3456]{1,0:T(8,128)(2,1)} %bitcast.107, bf16[3,3456,384]{2,1,0:T(8,128)(2,1)} %get-tuple-element.84), kind=kOutput, calls=%fused_computation.59 | convolution fusion | flops 10871635968 | bytes 37257216 | tf_op jit(solution)/shard_map/cond/branch_1_fun/dot_general | solution.py:73
  278.0 21.7 %fusion.32 = f32[4096,384]{1,0:T(8,128)} fusion(bf16[4096,3456]{1,0:T(8,128)(2,1)} %bitcast.106, bf16[3,3456,384]{2,1,0:T(8,128)(2,1)} %get-tuple-element.84), kind=kOutput, calls=%fused_computation.61 | convolution fusion | flops 10871635968 | bytes 37257216 | tf_op jit(solution)/shard_map/cond/branch_1_fun/dot_general | solution.py:73
  299.7 21.7 %add_add_fusion.1 = f32[4096,384]{1,0:T(8,128)S(1)} fusion(f32[4096,384]{1,0:T(8,128)} %fusion.32, f32[4096,384]{1,0:T(8,128)S(1)} %fusion.30, bf16[4096,3456]{1,0:T(8,128)(2,1)} %bitcast.105, bf16[3,3456,384]{2,1,0:T(8,128)(2,1)} %get-tuple-element.84), kind=kOutput, calls=%fused_computation.41 | convolution fusion | flops 10874781696 | bytes 49840128 | tf_op jit(solution)/shard_map/cond/branch_1_fun/dot_general | solution.py:73
  324.8 18.5 %fusion.40 = bf16[1,48,4096]{2,1,0:T(8,128)(2,1)} fusion(bf16[4096,4096]{1,0:T(8,128)(2,1)} %all-gather.2.cloned.1.call-done, bf16[1,48,4096]{2,1,0:T(8,128)(2,1)S(1)} %copy-done.3, f32[4096]{0:T(1024)S(1)} %bitcast.117, pred[]{:T(512)S(6)} %eq.3, bf16[32,48,128]{2,1,0:T(8,128)(2,1)} %all-to-all-done.3), kind=kOutput, calls=%fused_computation.71 | convolution fusion | flops 1611595776 | bytes 34750464 | tf_op jit(solution)/shard_map/dot_general | solution.py:129
  (72 shorter events, 52.9 us)
Async XLA Ops:
  7.2 31.4 %copy-start.6 = (f32[384]{0:T(512)S(1)}, f32[384]{0:T(512)}, u32[]{:S(2)}) copy-start(f32[384]{0:T(512)} %param.32) | copy-start | bytes 4612
  7.2 31.4 %copy-start.7 = (f32[384]{0:T(512)S(1)}, f32[384]{0:T(512)}, u32[]{:S(2)}) copy-start(f32[384]{0:T(512)} %param.33) | copy-start | bytes 4612
  7.2 317.6 %all-gather.2.cloned.1.call-start = ((), (), s32[]{:S(2)}) async-start(), calls=%async_computation.4 | async-start | bytes 34603008 | tf_op jit(solution)/shard_map/all_gather | solution.py:127
  16.4 21.6 %collective-permute-start = (bf16[16,1,128,16]{2,1,0,3:T(2,128)(2,1)S(1)}, bf16[16,1,128,16]{2,1,0,3:T(2,128)(2,1)S(1)}, u32[]{:S(2)}, u32[]{:S(2)}) collective-permute-start(bf16[16,1,128,16]{2,1,0,3:T(2,128)(2,1)S(1)} %get-tuple-element.113), channel_id=1, source_target_pairs={{0,1},{1,2},{2,3},{3,4},{4,5},{5,6},{6,7},{7,8},{8,9},{9,10},{10,1... | collective-permute-start | bytes 196616 | tf_op jit(solution)/shard_map/ppermute | solution.py:19
  23.1 15.0 %collective-permute-start.1 = (bf16[16,1,128,16]{2,1,0,3:T(2,128)(2,1)S(1)}, bf16[16,1,128,16]{2,1,0,3:T(2,128)(2,1)S(1)}, u32[]{:S(2)}, u32[]{:S(2)}) collective-permute-start(bf16[16,1,128,16]{2,1,0,3:T(2,128)(2,1)S(1)} %get-tuple-element.114), channel_id=1, source_target_pairs={{1,0},{2,1},{3,2},{4,3},{5,4},{6,5},{7,6},{8,7},{9,8},{10,9},{11,1... | collective-permute-start | bytes 196616 | tf_op jit(solution)/shard_map/ppermute | solution.py:21
  29.3 50.2 %all-to-all-start = ((bf16[48,32,128]{2,0,1:T(8,128)(2,1)}), bf16[48,32,128]{2,0,1:T(8,128)(2,1)}, u32[]{:S(2)}, u32[]{:S(2)}) async-start(bf16[48,32,128]{2,0,1:T(8,128)(2,1)} %copy.26), calls=%async_computation | async-start | bytes 786432 | tf_op jit(solution)/shard_map/all_to_all | solution.py:110
  70.5 7.5 %copy-start.2 = (bf16[1,48,4096]{2,1,0:T(8,128)(2,1)S(1)}, bf16[1,48,4096]{2,1,0:T(8,128)(2,1)}, u32[]{:S(2)}) copy-start(bf16[1,48,4096]{2,1,0:T(8,128)(2,1)} %param.23) | copy-start | bytes 1179652
  70.5 7.9 %copy-start.4 = (f32[4096]{0:T(1024)S(1)}, f32[4096]{0:T(1024)}, u32[]{:S(2)}) copy-start(f32[4096]{0:T(1024)} %param.28) | copy-start | bytes 49156
  72.5 90.5 %collective-permute-start.2 = (bf16[16,1,128,384]{3,2,1,0:T(8,128)(2,1)}, bf16[16,1,128,384]{3,2,1,0:T(8,128)(2,1)}, u32[]{:S(2)}, u32[]{:S(2)}) collective-permute-start(bf16[16,1,128,384]{3,2,1,0:T(8,128)(2,1)} %get-tuple-element.111), channel_id=1, source_target_pairs={{0,1},{1,2},{2,3},{3,4},{4,5},{5,6},{6,7},{7,8},{8,9},{9,10},{10,1... | collective-permute-start | bytes 4718600 | tf_op jit(solution)/shard_map/ppermute | solution.py:19
  75.8 87.2 %collective-permute-start.3 = (bf16[16,1,128,384]{3,2,1,0:T(8,128)(2,1)}, bf16[16,1,128,384]{3,2,1,0:T(8,128)(2,1)}, u32[]{:S(2)}, u32[]{:S(2)}) collective-permute-start(bf16[16,1,128,384]{3,2,1,0:T(8,128)(2,1)} %get-tuple-element.112), channel_id=1, source_target_pairs={{1,0},{2,1},{3,2},{4,3},{5,4},{6,5},{7,6},{8,7},{9,8},{10,9},{11,1... | collective-permute-start | bytes 4718600 | tf_op jit(solution)/shard_map/ppermute | solution.py:21
  79.4 63.1 %all-to-all-start.1 = ((bf16[48,32,128]{2,0,1:T(8,128)(2,1)}), bf16[48,32,128]{2,0,1:T(8,128)(2,1)S(1)}, u32[]{:S(2)}, u32[]{:S(2)}) async-start(bf16[48,32,128]{2,0,1:T(8,128)(2,1)} %copy.27), calls=%async_computation.1 | async-start | bytes 786432 | tf_op jit(solution)/shard_map/all_to_all | solution.py:111
  142.5 14.3 %all-to-all-start.2 = ((bf16[48,32,128]{2,0,1:T(8,128)(2,1)}), bf16[48,32,128]{2,0,1:T(8,128)(2,1)}, u32[]{:S(2)}, u32[]{:S(2)}) async-start(bf16[48,32,128]{2,0,1:T(8,128)(2,1)} %copy.28), calls=%async_computation.2 | async-start | bytes 786432 | tf_op jit(solution)/shard_map/all_to_all | solution.py:112
  157.6 167.2 %all-to-all-start.3 = ((bf16[32,48,128]{2,1,0:T(8,128)(2,1)}), bf16[32,48,128]{2,1,0:T(8,128)(2,1)}, u32[]{:S(2)}, u32[]{:S(2)}) async-start(bf16[32,48,128]{2,1,0:T(8,128)(2,1)} %bitcast.26), calls=%async_computation.3 | async-start | bytes 786432 | tf_op jit(solution)/shard_map/all_to_all | solution.py:123
  168.1 156.7 %copy-start.3 = (bf16[1,48,4096]{2,1,0:T(8,128)(2,1)S(1)}, bf16[1,48,4096]{2,1,0:T(8,128)(2,1)}, u32[]{:S(2)}) copy-start(bf16[1,48,4096]{2,1,0:T(8,128)(2,1)} %param.25) | copy-start | bytes 1179652
  168.1 156.7 %copy-start.5 = (f32[1,4096]{1,0:T(1,128)S(1)}, f32[1,4096]{1,0:T(1,128)}, u32[]{:S(2)}) copy-start(f32[1,4096]{1,0:T(1,128)} %param.26) | copy-start | bytes 49156
  172.1 4.1 %copy-start = (bf16[16,4,128,384]{3,2,1,0:T(8,128)(2,1)S(1)}, bf16[16,4,128,384]{3,2,1,0:T(8,128)(2,1)}, u32[]{:S(2)}) copy-start(bf16[16,4,128,384]{3,2,1,0:T(8,128)(2,1)} %get-tuple-element.67) | copy-start | bytes 18874372 | tf_op jit(solution)/shard_map/cond
  299.7 21.7 %copy-start.8 = (f32[384]{0:T(512)S(1)}, f32[384]{0:T(512)}, u32[]{:S(2)}) copy-start(f32[384]{0:T(512)} %get-tuple-element.85) | copy-start | bytes 4612 | tf_op jit(solution)/shard_map/cond
  324.7 18.5 %copy-start.1 = (bf16[1,16,2,128,384]{4,3,2,1,0:T(8,128)(2,1)}, bf16[1,16,2,128,384]{4,3,2,1,0:T(8,128)(2,1)S(1)}, u32[]{:S(2)}) copy-start(bf16[1,16,2,128,384]{4,3,2,1,0:T(8,128)(2,1)S(1)} %get-tuple-element.173) | copy-start | bytes 9437188
Sparse Core Ops, SparseCore 0:
  10.3 140.1 all-gather.1
where the time goes:
time: 354 us; the launch traced here: 351 us
  local copies, waits for them, and re-layouts  109 us (31%)
  matrix products  98.5 us (28%)
  waiting for transfers between devices  63.5 us (18%)
  starting transfers between devices  40.7 us (11%)
  other arithmetic  15.5 us (4%)
  between operations  14.8 us (4%)
  blocking collectives  7.55 us (2%)
    dot_general x6, matrix products, conv_rows(): jnp.dot(taken, kernel[time_tap], preferred_element_type=jnp.float32)  80 us
    slice x2, local copies, waits for them, and re-layouts, conv_rows(): flattened[time_tap:time_tap + frame_count]  59.1 us
    all_to_all x1, waiting for transfers between devices, on_device(): lax.all_to_all(keys_normed, 'seq', split_axis=1, concat_axis=0, tiled=True)  53.4 us
    cond x20, local copies, waits for them, and re-layouts  28.7 us
    dot_general x1, matrix products, on_device(): jnp.dot(part_cols, weight_piece, preferred_element_type=jnp.float32)  18.5 us
    ppermute x2, starting transfers between devices, padded_2(): lax.ppermute(tail, axis, [(i, (i + 1) % count) for i in range(ends)])  9.93 us
    all_to_all x1, waiting for transfers between devices, on_device(): lax.all_to_all(value_input[0], 'seq', split_axis=1, concat_axis=0, tiled=...  9.4 us
    all_to_all x1, starting transfers between devices, on_device(): lax.all_to_all(query_matrix, 'seq', split_axis=1, concat_axis=0, tiled=True)  8.79 us
  transfers between devices with their start and end apart: 9, of which 2 were waited for; matrix products, arithmetic and copies ran while one was open for 58% of the time, Pallas kernels for 0%

commit v1 on v0

v1 whole, which is shorter than its diff:
```python
import math
import jax
import jax.numpy as jnp
from jax import lax
from jax.experimental import pallas as pl
from jax.experimental.pallas import tpu as pltpu
from jax.sharding import Mesh, PartitionSpec as P

CHIPS = ("z", "x")
SEQ = ("z", "x", "core")
EPS = 1e-06
MIB = 1024 * 1024


def vmem_spec():
    return pl.BlockSpec(memory_space=pltpu.VMEM)


def smem_spec():
    return pl.BlockSpec(memory_space=pltpu.SMEM)


def norm_pack(q, k, v, gain_q, gain_k):
    rows, width = q.shape
    chips = width // 256
    block = 16

    def body(q_ref, k_ref, v_ref, gq_ref, gk_ref, out_ref):
        def normed(ref, gain):
            x = ref[...].astype(jnp.float32)
            factor = lax.rsqrt(jnp.mean(x * x, axis=-1, keepdims=True) + EPS)
            return (x * factor * gain).astype(jnp.bfloat16)

        scale = 128**-0.5 * math.log2(math.e)
        qn = normed(q_ref, gq_ref[...] * scale)
        kn = normed(k_ref, gk_ref[...])
        for c in range(chips):
            cols = slice(256 * c, 256 * c + 256)
            out_ref[c, 0] = qn[:, cols]
            out_ref[c, 1] = kn[:, cols]
            out_ref[c, 2] = v_ref[:, cols]

    tokens = pl.BlockSpec((block, width), lambda i: (i, 0))
    gains = pl.BlockSpec((1, width), lambda i: (0, 0))
    return pl.pallas_call(
        body,
        grid=(rows // block,),
        out_shape=jax.ShapeDtypeStruct((chips, 3, rows, 256), jnp.bfloat16),
        in_specs=[tokens, tokens, tokens, gains, gains],
        out_specs=pl.BlockSpec((chips, 3, block, 256), lambda i: (0, 0, i, 0)),
        compiler_params=pltpu.CompilerParams(vmem_limit_bytes=32 * MIB),
        name="norm_pack",
    )(q, k, v, gain_q, gain_k)


def weight_blocks(place, w_here, w_there):
    rows, width = w_here.shape
    part = width // 4

    def body(place_ref, here_ref, there_ref, own_ref, up_ref, down_ref):
        core, ring = place_ref[1], place_ref[4]

        def halves(k):
            at = pl.ds(pl.multiple_of(lax.rem(ring + k, 4) * part, part), part)
            here, there = here_ref[:, at], there_ref[:, at]
            return jnp.where(core == 0, here, there), jnp.where(core == 0, there, here)

        @pl.when(place_ref[0] == 0)
        def _():
            own_ref[:rows], own_ref[rows:] = halves(0)
            up_ref[:rows], up_ref[rows : 2 * rows] = halves(1)
            down_ref[:rows], down_ref[rows : 2 * rows] = halves(3)
            up_ref[2 * rows :], down_ref[2 * rows :] = halves(2)

    return pl.pallas_call(
        body,
        out_shape=(
            jax.ShapeDtypeStruct((2 * rows, part), jnp.bfloat16),
            jax.ShapeDtypeStruct((3 * rows, part), jnp.bfloat16),
            jax.ShapeDtypeStruct((3 * rows, part), jnp.bfloat16),
        ),
        in_specs=[smem_spec(), vmem_spec(), vmem_spec()],
        out_specs=(vmem_spec(),) * 3,
        compiler_params=pltpu.CompilerParams(vmem_limit_bytes=24 * MIB),
        name="weight_blocks",
    )(place, w_here, w_there)


def attend(place, here, there):
    chips, _, tok, _ = here.shape
    half = chips * tok
    keys = 2 * half

    def body(place_ref, here_ref, there_ref, out_ref, k_buf, v_buf):
        step = pl.program_id(0)

        @pl.when((step == 0) & (place_ref[0] == 0))
        def _():
            for h in range(2):
                cols = slice(128 * h, 128 * h + 128)
                for n, ref in enumerate((here_ref, there_ref)):
                    span = slice(n * half, n * half + half)
                    k_buf[h, span] = ref[:, 1, :, cols].reshape(half, 128)
                    v_buf[h, span, :128] = ref[:, 2, :, cols].reshape(half, 128)
                v_buf[h, :, 128:] = jnp.ones((keys, 128), jnp.bfloat16)

        @pl.when(place_ref[0] == 0)
        def _():
            queries = here_ref[pl.ds(4 * step, 4), 0].reshape(4 * tok, 256)
            heads = []
            for h in range(2):
                s = lax.dot_general(
                    queries[:, 128 * h : 128 * h + 128],
                    k_buf[h],
                    (((1,), (1,)), ((), ())),
                    preferred_element_type=jnp.float32,
                )
                p = jnp.exp2(s - jnp.max(s, axis=-1, keepdims=True)).astype(jnp.bfloat16)
                o = jnp.dot(p, v_buf[h], preferred_element_type=jnp.float32)
                heads.append(o[:, :128] / o[:, 128:])
            joined = jnp.concatenate(heads, axis=1).astype(jnp.bfloat16)
            for n in range(4):
                at = jnp.where(place_ref[1] == 0, 4 * n + step, 4 * step + n)
                out_ref[at] = joined[tok * n : tok * n + tok]

    return pl.pallas_call(
        body,
        grid=(chips // 4,),
        out_shape=jax.ShapeDtypeStruct((chips, tok, 256), jnp.bfloat16),
        in_specs=[smem_spec(), vmem_spec(), vmem_spec()],
        out_specs=vmem_spec(),
        scratch_shapes=[
            pltpu.VMEM((2, keys, 128), jnp.bfloat16),
            pltpu.VMEM((2, keys, 256), jnp.bfloat16),
        ],
        compiler_params=pltpu.CompilerParams(vmem_limit_bytes=40 * MIB),
        cost_estimate=pl.CostEstimate(
            flops=8 * half * keys * 128,
            bytes_accessed=4 * half * 512,
            transcendentals=2 * half * keys,
        ),
        name="attend",
    )(place, here, there)


def project(place, heads, weights):
    rows = heads[0].shape[0] * heads[0].shape[1]
    part = weights[0].shape[1]
    lot = rows // 4

    def body(place_ref, oo, od, ou, of1, of2, wo, wd, wu, wf1, wf2, fa, fb, up, down, own):
        second = place_ref[5]

        @pl.when(place_ref[0] == 0)
        def _():
            weight = jnp.concatenate(
                [wo[...], wd[:256], wu[:256], wf1[...], wf2[...]], axis=0
            )

            def block(k, cols):
                b = lax.rem(second + k, 4)
                near = [ref[pl.ds(4 * b, 4)].reshape(lot, 256) for ref in (oo, od, ou)]
                low = of1[pl.ds(4 * lax.rem(b, 2), 4)].reshape(lot, 256)
                high = of2[pl.ds(4 * lax.rem(b, 2), 4)].reshape(lot, 256)
                feats = jnp.concatenate(near + [jnp.where(b < 2, low, high)], axis=1)
                return jnp.dot(feats, weight[:, cols], preferred_element_type=jnp.float32)

            whole, cut = slice(0, part), part // 2
            far = block(2, whole).astype(jnp.bfloat16)
            fa[...] = far[:, :cut]
            fb[...] = far[:, cut:]
            up[...] = block(1, whole).astype(jnp.bfloat16)
            down[...] = block(3, whole).astype(jnp.bfloat16)
            own[...] = block(0, whole)

    shape = jax.ShapeDtypeStruct
    return pl.pallas_call(
        body,
        out_shape=(
            shape((lot, part // 2), jnp.bfloat16),
            shape((lot, part // 2), jnp.bfloat16),
            shape((lot, part), jnp.bfloat16),
            shape((lot, part), jnp.bfloat16),
            shape((lot, part), jnp.float32),
        ),
        in_specs=[smem_spec()] + [vmem_spec()] * 10,
        out_specs=(vmem_spec(),) * 5,
        compiler_params=pltpu.CompilerParams(vmem_limit_bytes=40 * MIB),
        cost_estimate=pl.CostEstimate(
            flops=2 * rows * 1024 * part, bytes_accessed=8 * MIB, transcendentals=0
        ),
        name="project",
    )(place, *heads, *weights)


def add_passed(up, down, low, high):
    cut = low.shape[1]

    def body(up_ref, down_ref, low_ref, high_ref, up_out, down_out):
        def total(one, two):
            return (one.astype(jnp.float32) + two.astype(jnp.float32)).astype(jnp.bfloat16)

        up_out[:, :cut] = total(up_ref[:, :cut], low_ref[...])
        up_out[:, cut:] = up_ref[:, cut:]
        down_out[:, :cut] = down_ref[:, :cut]
        down_out[:, cut:] = total(down_ref[:, cut:], high_ref[...])

    return pl.pallas_call(
        body,
        out_shape=(jax.ShapeDtypeStruct(up.shape, up.dtype),) * 2,
        in_specs=[vmem_spec()] * 4,
        out_specs=(vmem_spec(),) * 2,
        name="add_passed",
    )(up, down, low, high)


def add_blocks(place, own, below, above):
    lot, part = own.shape
    tok = lot // 4

    def body(place_ref, own_ref, below_ref, above_ref, *outs):
        for k in range(4):
            at = pl.ds(pl.multiple_of(lax.rem(place_ref[4] + k, 4) * tok, tok), tok)
            total = own_ref[at] + below_ref[at].astype(jnp.float32)
            outs[k][...] = (total + above_ref[at].astype(jnp.float32)).astype(jnp.bfloat16)

    return pl.pallas_call(
        body,
        out_shape=(jax.ShapeDtypeStruct((tok, part), jnp.bfloat16),) * 4,
        in_specs=[smem_spec()] + [vmem_spec()] * 3,
        out_specs=(vmem_spec(),) * 4,
        name="add_blocks",
    )(place, own, below, above)


def finish(place, resid, gate, blocks):
    tok, width = resid.shape
    part = width // 4

    def body(place_ref, resid_ref, gate_ref, *refs):
        out_ref = refs[4]

        @pl.when(place_ref[0] == 0)
        def _():
            for k in range(4):
                at = pl.ds(pl.multiple_of(lax.rem(place_ref[4] + k, 4) * part, part), part)
                total = resid_ref[:, at].astype(jnp.float32)
                total += gate_ref[:, at] * refs[k][...].astype(jnp.float32)
                out_ref[:, at] = total.astype(jnp.bfloat16)

        @pl.when(place_ref[0] == 1)
        def _():
            out_ref[...] = jnp.zeros(out_ref.shape, out_ref.dtype)

    return pl.pallas_call(
        body,
        out_shape=jax.ShapeDtypeStruct(resid.shape, jnp.bfloat16),
        in_specs=[smem_spec()] + [vmem_spec()] * 6,
        out_specs=vmem_spec(),
        name="finish",
    )(place, resid, gate, *blocks)


def filter_weights(place, w_mid):
    steps, deep, vc = w_mid.shape
    taps = w_mid.reshape(steps, 3, 3, vc, vc)

    def body(place_ref, w_ref, out_ref):
        @pl.when(place_ref[0] == 1)
        def _():
            up, mid, down = (w_ref[0, n, 0].astype(jnp.float32) for n in range(3))
            ends = 0.5 * (up + down)
            mid = 0.5 * mid
            for n, g in enumerate((up, ends + mid, ends - mid, down)):
                out_ref[n] = jnp.transpose(g).astype(jnp.bfloat16)

    return pl.pallas_call(
        body,
        grid_spec=pltpu.PrefetchScalarGridSpec(
            num_scalar_prefetch=1,
            grid=(3 * steps,),
            in_specs=[
                pl.BlockSpec(
                    (1, 3, 1, vc, vc),
                    lambda i, where: (where[0] * (i // 3), 0, where[0] * (i % 3), 0, 0),
                )
            ],
            out_specs=pl.BlockSpec((4, vc, vc), lambda i, where: (0, 0, where[0] * i)),
        ),
        out_shape=jax.ShapeDtypeStruct((4, vc, deep), jnp.bfloat16),
        compiler_params=pltpu.CompilerParams(vmem_limit_bytes=24 * MIB),
        name="filter_weights",
    )(place, taps)


def decode(place, clip, w_first, filters, vectors):
    frames, _, lc, lw = clip.shape
    vc = w_first.shape[0]
    deep = 3 * vc
    lot = 4

    def body(place_ref, clip_ref, w1_ref, f_ref, vec_ref, out_ref, lat, act, firsts, w2, both, sems):
        step = pl.program_id(0)
        here = place_ref[0] == 1
        loads = [pltpu.make_async_copy(f_ref.at[n], w2.at[n], sems.at[n]) for n in range(4)]

        def moved(x):
            lane = lax.broadcasted_iota(jnp.int32, x.shape, x.ndim - 1)
            left = jnp.where(lane == 0, 0.0, pltpu.roll(x, 1, x.ndim - 1))
            right = jnp.where(lane == lw - 1, 0.0, pltpu.roll(x, lw - 1, x.ndim - 1))
            return left, x, right

        def first(f):
            sides = []
            for row in range(4):
                taps = [lat[f + dt, row : row + 3].reshape(9 * lc, lw) for dt in range(3)]
                taps.append(jnp.zeros((w1_ref.shape[1] - 27 * lc, lw), jnp.bfloat16))
                sides.append(jnp.concatenate(taps, axis=0))
            y = jnp.dot(
                w1_ref[...], jnp.concatenate(sides, axis=1), preferred_element_type=jnp.float32
            )
            acts = []
            for row in range(4):
                hidden = y[:, row * lw : row * lw + lw] + vec_ref[0]
                hidden = hidden.astype(jnp.bfloat16).astype(jnp.float32)
                if row in (1, 2):
                    firsts[lax.rem(f, 2 * lot), row - 1] = hidden
                factor = lax.rsqrt(jnp.mean(hidden * hidden, axis=0, keepdims=True) + EPS)
                if row == 0:
                    factor = jnp.where(place_ref[2] == 0, 0.0, factor)
                if row == 3:
                    factor = jnp.where(place_ref[2] == place_ref[3], 0.0, factor)
                half = hidden * (0.5 * factor) * vec_ref[1]
                acts.append(half * (1.0 + jnp.tanh(half)))
            a0, a1, a2, a3 = acts
            for n, u in enumerate((a0 - a2, a1 + a2, a2 - a1, a1 - a3)):
                for dx, piece in enumerate(moved(u)):
                    act[n, f + 2, dx * vc : dx * vc + vc] = piece.astype(jnp.bfloat16)

        @pl.when(here & (step == 0))
        def _():
            for load in loads:
                load.start()
            lat[:2] = jnp.zeros((2, 6, 3 * lc, lw), jnp.bfloat16)
            act[:, :2] = jnp.zeros((4, 2, deep, lw), jnp.bfloat16)
            cells = clip_ref[...].astype(jnp.float32)
            for dx, piece in enumerate(moved(cells)):
                lat[2:, :, dx * lc : dx * lc + lc] = piece.astype(jnp.bfloat16)

            @pl.loop(0, lot)
            def _(f):
                first(f)

            for load in loads:
                load.wait()

        def second(and_next):
            base = lot * step
            for n in range(4):
                taps = jnp.concatenate(
                    [act[n, pl.ds(base + j, 3)].reshape(3 * deep, lw) for j in range(lot)], axis=1
                )
                m = jnp.dot(w2[n], taps, preferred_element_type=jnp.float32)
                if n == 0:
                    both[0] = m
                if n == 1:
                    both[0] += m
                    both[1] = m
                if n == 2:
                    both[0] += m
                    both[1] -= m
                if n == 3:
                    both[1] -= m
                if and_next:
                    first(base + lot + n)
            for j in range(lot):
                for r in range(2):
                    whole = both[r, :, j * lw : j * lw + lw]
                    whole += vec_ref[2] + firsts[lax.rem(base + j, 2 * lot), r]
                    out_ref[j, r] = jnp.transpose(whole).astype(jnp.bfloat16)

        @pl.when(here & (step < frames // lot - 1))
        def _():
            second(True)

        @pl.when(here & (step == frames // lot - 1))
        def _():
            second(False)

        @pl.when(jnp.logical_not(here))
        def _():
            out_ref[...] = jnp.zeros(out_ref.shape, out_ref.dtype)

    return pl.pallas_call(
        body,
        grid=(frames // lot,),
        out_shape=jax.ShapeDtypeStruct((frames, 2, lw, vc), jnp.bfloat16),
        in_specs=[
            smem_spec(),
            vmem_spec(),
            vmem_spec(),
            pl.BlockSpec(memory_space=pl.ANY),
            vmem_spec(),
        ],
        out_specs=pl.BlockSpec((lot, 2, lw, vc), lambda i: (i, 0, 0, 0)),
        scratch_shapes=[
            pltpu.VMEM((frames + 2, 6, 3 * lc, lw), jnp.bfloat16),
            pltpu.VMEM((4, frames + 2, deep, lw), jnp.bfloat16),
            pltpu.VMEM((2 * lot, 2, vc, lw), jnp.float32),
            pltpu.VMEM((4, vc, 3 * deep), jnp.bfloat16),
            pltpu.VMEM((2, vc, lot * lw), jnp.float32),
            pltpu.SemaphoreType.DMA((4,)),
        ],
        compiler_params=pltpu.CompilerParams(vmem_limit_bytes=56 * MIB),
        cost_estimate=pl.CostEstimate(
            flops=8 * frames * lw * 3 * deep * vc,
            bytes_accessed=frames * 2 * lw * vc * 2 + 12 * deep * vc * 2,
            transcendentals=frames * 4 * lw * vc,
        ),
        name="decode",
    )(place, clip, w_first, filters, vectors)


def on_device(
    query_input,
    key_input,
    value_input,
    resid,
    gate,
    query_norm_gain,
    key_norm_gain,
    output_weight,
    latents,
    w_in,
    b_in,
    norm_gain,
    w_mid,
    b_mid,
):
    last = lax.axis_size("grp") - 1
    decoder_here = lax.axis_index("grp") == last
    count = lax.axis_size(SEQ)
    side = lax.axis_size("z")
    core, at_z, at_x = lax.axis_index("core"), lax.axis_index("z"), lax.axis_index("x")
    place = jnp.stack(
        [
            decoder_here.astype(jnp.int32),
            core,
            lax.axis_index(SEQ),
            jnp.int32(count - 1),
            jnp.where(core == 0, at_z, at_x),
            jnp.where(core == 0, at_x, at_z),
        ]
    )
    channels = w_in.shape[2]

    def along(first_ring, shift):
        pairs = []
        for g in range(last):
            for z in range(side):
                for x in range(side):
                    for c in range(2):
                        on_z = (c == 0) == first_ring
                        to_z = (z + shift) % side if on_z else z
                        to_x = x if on_z else (x + shift) % side
                        at = g * count
                        pairs.append((at + (z * side + x) * 2 + c, at + (to_z * side + to_x) * 2 + c))
        return pairs

    def send(x, first_ring, shift):
        return lax.ppermute(x, ("grp",) + SEQ, along(first_ring, shift))

    swap = [(2 * i, 2 * i + 1) for i in range(last * count // 2)]
    swap += [(b, a) for a, b in swap]

    own = jnp.swapaxes(latents, 2, 3)
    clip = jnp.concatenate(
        [lax.ppermute(own, "grp", [(g, last)]) for g in range(last)] + [own], axis=0
    )
    packed = norm_pack(
        query_input[0], key_input[0], value_input[0], query_norm_gain[None], key_norm_gain[None]
    )
    filters = filter_weights(place, w_mid)
    packed, clip = lax.optimization_barrier((packed, clip))
    here = lax.all_to_all(packed, CHIPS, split_axis=0, concat_axis=0, tiled=True)

    links = [(last * count + i, last * count + i + 1) for i in range(count - 1)]
    cells = jnp.concatenate(
        [
            lax.ppermute(clip, ("grp",) + SEQ, links),
            clip,
            lax.ppermute(clip, ("grp",) + SEQ, [(b, a) for a, b in links]),
        ],
        axis=1,
    )
    w_first = jnp.pad(w_in.reshape(-1, channels).T, ((0, 0), (0, 512 - 27 * latents.shape[3])))
    vectors = jnp.broadcast_to(
        jnp.stack([b_in, norm_gain, b_mid])[:, :, None], (3, channels, latents.shape[2])
    )
    decoded = decode(place, cells, w_first, filters, vectors)

    weight_there = lax.ppermute(output_weight, ("grp",) + SEQ, swap)
    w_own, w_up, w_down = weight_blocks(place, output_weight, weight_there)
    w_below, w_above = send(w_up, True, 1), send(w_down, True, -1)
    w_far = send(w_below[256:], True, 1), send(w_above[256:], True, -1)

    here, decoded = lax.optimization_barrier((here, decoded))
    there = lax.ppermute(here, ("grp",) + SEQ, swap)
    heads = attend(place, here, there)
    below, above = send(heads, True, 1), send(heads, True, -1)
    middle = heads.shape[0] // 2
    far = send(below[:middle], True, 1), send(above[middle:], True, -1)
    far_low, far_high, up, down, mine = project(
        place, (heads, below, above) + far, (w_own, w_below, w_above) + w_far
    )
    up, down = add_passed(up, down, send(far_low, False, 1), send(far_high, False, -1))
    sums = add_blocks(place, mine, send(up, False, 1), send(down, False, -1))
    blocks = (sums[0], send(sums[3], True, -1), send(sums[2], True, 2), send(sums[1], True, 1))
    attn_out = finish(place, resid[0], gate, blocks)
    return attn_out[None], decoded[None]


def solution(mesh):
    fine = Mesh(mesh.devices.reshape(4, 4, 4, 2), ("grp",) + SEQ)
    placed = (
        P("grp", SEQ, None),
        P("grp", SEQ, None),
        P("grp", SEQ, None),
        P("grp", SEQ, None),
        P("grp", None),
        P(),
        P(),
        P(SEQ, None),
        P("grp", SEQ, None, None),
        P(),
        P(),
        P(),
        P(),
        P(),
    )
    return jax.shard_map(
        on_device,
        mesh=fine,
        in_specs=placed,
        out_specs=(P("grp", SEQ, None), P("grp", None, SEQ, None, None)),
        check_vma=False,
    )
```

time: 354 us -> 153 us (0.43)
  the two profiles are of different devices: /device:TPU:27 before, /device:TPU:0 now
where the time goes in v1:
time: 153 us; the launch traced here: 151 us
  starting transfers between devices  74 us (48%)
  waiting for transfers between devices  32.2 us (21%)
  Pallas kernels  22.2 us (15%)
  local copies, waits for them, and re-layouts  19.5 us (13%)
  other arithmetic  1.58 us (1%)
    ppermute x15, starting transfers between devices, send(): return lax.ppermute(x, ('grp',) + SEQ, along(first_ring, shift))  53.2 us
    ppermute x15, waiting for transfers between devices, send(): return lax.ppermute(x, ('grp',) + SEQ, along(first_ring, shift))  17 us
    unnamed x46, local copies, waits for them, and re-layouts  16.3 us
    all_to_all x1, waiting for transfers between devices, on_device(): lax.all_to_all(packed, CHIPS, split_axis=0, concat_axis=0, tiled=True)  15.2 us
    all_to_all x1, starting transfers between devices, on_device(): lax.all_to_all(packed, CHIPS, split_axis=0, concat_axis=0, tiled=True)  7.89 us
    ppermute x3, starting transfers between devices, on_device(): lax.ppermute(own, 'grp', [(g, last)])  7.72 us
    pallas_call x1, Pallas kernels, attend(): pl.pallas_call(body, grid=(chips // 4,), out_shape=jax.ShapeDtypeStruct((...  5.95 us
    pallas_call x1, Pallas kernels, decode(): pl.pallas_call(body, grid=(frames // lot,), out_shape=jax.ShapeDtypeStruc...  3.63 us
  transfers between devices with their start and end apart: 23, of which 9 were waited for; matrix products, arithmetic and copies ran while one was open for 3% of the time, Pallas kernels for 9%

profile of v1, /device:TPU:0, one launch (start us, length us, event | category | flops | bytes accessed | tf_op | source)
XLA Modules:
  0.0 150.6 jit_solution(14869968675573137314)
XLA Ops:
  2.1 6.3 %collective-permute-start = (bf16[4,2,16,128]{3,2,1,0:T(8,128)(2,1)}, bf16[4,2,16,128]{3,2,1,0:T(8,128)(2,1)S(1)}, u32[]{:S(2)}, u32[]{:S(2)}) collective-permute-start(bf16[4,2,16,128]{3,2,1,0:T(8,128)(2,1)} %bitcast.29), channel_id=1, source_target_pairs={{0,96},{1,97},{2,98},{3,99},{4,100},{5,101},{6,102},{7,103},{8,104... | collective-permute-start | bytes 98312 | tf_op jit(solution)/shard_map/ppermute | solution.py:478
  12.8 1.9 %norm_pack.1 = bf16[16,3,48,256]{3,2,1,0:T(8,128)(2,1)} custom-call(bf16[48,4096]{1,0:T(8,128)(2,1)S(1)} %bitcast.18, bf16[48,4096]{1,0:T(8,128)(2,1)S(1)} %bitcast.19, bf16[48,4096]{1,0:T(8,128)(2,1)S(1)} %bitcast.20, f32[1,4096]{1,0:T(1,128)S(1)} %bitcast.21, f32[1,4096]{1,0:T(1,128)S(1)} %bitcast.22), custom_call_target="tpu_custom_call" | custom-call | tf_op jit(solution)/shard_map/norm_pack/pallas_call | solution.py:45
  16.9 1.9 %collective-permute-start.10 = (bf16[128,4096]{1,0:T(8,128)(2,1)}, bf16[128,4096]{1,0:T(8,128)(2,1)S(1)}, u32[]{:S(2)}, u32[]{:S(2)}) collective-permute-start(bf16[128,4096]{1,0:T(8,128)(2,1)} %here_ref.1), channel_id=1, source_target_pairs={{0,1},{2,3},{4,5},{6,7},{8,9},{10,11},{12,13},{14,15},{16,17},{18,... | collective-permute-start | bytes 3145736 | tf_op jit(solution)/shard_map/ppermute | solution.py:502
  21.0 3.3 %copy-done.1 = bf16[3,3456,384]{2,1,0:T(8,128)(2,1)S(1)} copy-done((bf16[3,3456,384]{2,1,0:T(8,128)(2,1)S(1)}, bf16[3,3456,384]{2,1,0:T(8,128)(2,1)}, u32[]{:S(2)}) %copy-start.1) | copy-done | bytes 7962648
  25.5 4.1 %copy-done = bf16[4,384,3456]{2,1,0:T(8,128)(2,1)} copy-done((bf16[4,384,3456]{2,1,0:T(8,128)(2,1)}, bf16[4,384,3456]{2,1,0:T(8,128)(2,1)S(1)}, u32[]{:S(2)}) %copy-start) | copy-done | bytes 10616856
  29.6 7.9 %all-to-all-start = ((bf16[16,3,48,256]{3,2,1,0:T(8,128)(2,1)}), bf16[16,3,48,256]{3,2,1,0:T(8,128)(2,1)S(1)}, u32[]{:S(2)}, u32[]{:S(2)}) async-start(bf16[16,3,48,256]{3,2,1,0:T(8,128)(2,1)} %norm_pack.1), calls=%async_computation | async-start | bytes 2359296 | tf_op jit(solution)/shard_map/all_to_all | solution.py:485
  39.3 3.6 %decode.1 = bf16[16,2,128,384]{3,2,1,0:T(8,128)(2,1)} custom-call(s32[6]{0:T(128)} %copy-done.11, bf16[16,6,16,128]{3,2,1,0:T(8,128)(2,1)} %pad_maximum_fusion.clip_ref, bf16[384,512]{1,0:T(8,128)(2,1)} %pad.4.w1_ref, bf16[4,384,3456]{2,1,0:T(8,128)(2,1)} %copy-done, f32[3,384,128]{2,1,0:T(8,128)} %broadcast_in_dim.20.vec_ref), custom_call_target="tpu_custom_call" | custom-call | flops 21743271936 | bytes 13762560 | tf_op jit(solution)/shard_map/decode/pallas_call | solution.py:394
  43.0 15.2 %all-to-all-done.here_ref = bf16[16,3,48,256]{3,2,1,0:T(8,128)(2,1)S(1)} async-done(((bf16[16,3,48,256]{3,2,1,0:T(8,128)(2,1)}), bf16[16,3,48,256]{3,2,1,0:T(8,128)(2,1)S(1)}, u32[]{:S(2)}, u32[]{:S(2)}) %all-to-all-start) | async-done | bytes 1179680 | tf_op jit(solution)/shard_map/all_to_all | solution.py:485
  60.8 2.3 %collective-permute-start.11 = (bf16[384,1024]{1,0:T(8,128)(2,1)S(1)}, bf16[384,1024]{1,0:T(8,128)(2,1)S(1)}, u32[]{:S(2)}, u32[]{:S(2)}) collective-permute-start(bf16[384,1024]{1,0:T(8,128)(2,1)S(1)} %get-tuple-element.24), channel_id=1, source_target_pairs={{0,8},{1,3},{2,10},{3,5},{4,12},{5,7},{6,14},{7,1},{8,16},{9,11},{... | collective-permute-start | bytes 2359304 | tf_op jit(solution)/shard_map/ppermute | solution.py:471
  63.1 5.0 %collective-permute-start.12 = (bf16[384,1024]{1,0:T(8,128)(2,1)S(1)}, bf16[384,1024]{1,0:T(8,128)(2,1)S(1)}, u32[]{:S(2)}, u32[]{:S(2)}) collective-permute-start(bf16[384,1024]{1,0:T(8,128)(2,1)S(1)} %get-tuple-element.25), channel_id=1, source_target_pairs={{0,24},{1,7},{2,26},{3,1},{4,28},{5,3},{6,30},{7,5},{8,0},{9,15},{... | collective-permute-start | bytes 2359304 | tf_op jit(solution)/shard_map/ppermute | solution.py:471
  68.1 6.0 %attend.1.oo = bf16[16,48,256]{2,1,0:T(8,128)(2,1)S(1)} custom-call(s32[6]{0:T(128)S(1)} %copy-done.12, bf16[16,3,48,256]{3,2,1,0:T(8,128)(2,1)S(1)} %all-to-all-done.here_ref, bf16[16,3,48,256]{3,2,1,0:T(8,128)(2,1)S(1)} %collective-permute-done.5.there_ref), custom_call_target="tpu_custom_call" | custom-call | flops 1207959552 | bytes 1572864 | tf_op jit(solution)/shard_map/attend/pallas_call | solution.py:126
  75.9 5.1 %collective-permute-start.7 = (bf16[16,48,256]{2,1,0:T(8,128)(2,1)S(1)}, bf16[16,48,256]{2,1,0:T(8,128)(2,1)S(1)}, u32[]{:S(2)}, u32[]{:S(2)}) collective-permute-start(bf16[16,48,256]{2,1,0:T(8,128)(2,1)S(1)} %attend.1.oo), channel_id=1, source_target_pairs={{0,24},{1,7},{2,26},{3,1},{4,28},{5,3},{6,30},{7,5},{8,0},{9,15},{... | collective-permute-start | bytes 1179656 | tf_op jit(solution)/shard_map/ppermute | solution.py:471
  83.1 5.1 %collective-permute-start.14 = (bf16[128,1024]{1,0:T(8,128)(2,1)S(1)}, bf16[128,1024]{1,0:T(8,128)(2,1)S(1)}, u32[]{:S(2)}, u32[]{:S(2)}) collective-permute-start(bf16[128,1024]{1,0:T(8,128)(2,1)S(1)} %slice.19), channel_id=1, source_target_pairs={{0,24},{1,7},{2,26},{3,1},{4,28},{5,3},{6,30},{7,5},{8,0},{9,15},{... | collective-permute-start | bytes 786440 | tf_op jit(solution)/shard_map/ppermute | solution.py:471
  90.2 5.1 %collective-permute-start.9 = (bf16[8,48,256]{2,1,0:T(8,128)(2,1)S(1)}, bf16[8,48,256]{2,1,0:T(8,128)(2,1)S(1)}, u32[]{:S(2)}, u32[]{:S(2)}) collective-permute-start(bf16[8,48,256]{2,1,0:T(8,128)(2,1)S(1)} %slice.17), channel_id=1, source_target_pairs={{0,24},{1,7},{2,26},{3,1},{4,28},{5,3},{6,30},{7,5},{8,0},{9,15},{... | collective-permute-start | bytes 589832 | tf_op jit(solution)/shard_map/ppermute | solution.py:471
  98.5 2.4 %project.1 = (bf16[192,512]{1,0:T(8,128)(2,1)S(1)}, bf16[192,512]{1,0:T(8,128)(2,1)S(1)}, bf16[192,1024]{1,0:T(8,128)(2,1)S(1)}, bf16[192,1024]{1,0:T(8,128)(2,1)S(1)}, f32[192,1024]{1,0:T(8,128)S(1)}) custom-call(s32[6]{0:T(128)S(1)} %copy-done.12, bf16[16,48,256]{2,1,0:T(8,128)(2,1)S(1)} %attend.1.oo, bf16[16,48,256]{2,1,0:T(8,128)(2,1)S(1)} %collective-permute-done.6.od, ...), custom_call_target="tpu_custom_call" | custom-call | flops 1610612736 | bytes 8388608 | tf_op jit(solution)/shard_map/project/pallas_call | solution.py:177
  105.2 5.1 %collective-permute-start.16 = (bf16[192,512]{1,0:T(8,128)(2,1)S(1)}, bf16[192,512]{1,0:T(8,128)(2,1)S(1)}, u32[]{:S(2)}, u32[]{:S(2)}) collective-permute-start(bf16[192,512]{1,0:T(8,128)(2,1)S(1)} %get-tuple-element.30), channel_id=1, source_target_pairs={{0,6},{1,25},{2,0},{3,27},{4,2},{5,29},{6,4},{7,31},{8,14},{9,1},{... | collective-permute-start | bytes 589832 | tf_op jit(solution)/shard_map/ppermute | solution.py:471
  114.2 2.2 %add_passed.1 = (bf16[192,1024]{1,0:T(8,128)(2,1)}, bf16[192,1024]{1,0:T(8,128)(2,1)}) custom-call(bf16[192,1024]{1,0:T(8,128)(2,1)} %copy-done.7, bf16[192,1024]{1,0:T(8,128)(2,1)} %copy-done.8, bf16[192,512]{1,0:T(8,128)(2,1)} %copy-done.15, bf16[192,512]{1,0:T(8,128)(2,1)} %copy-done.16), custom_call_target="tpu_custom_call" | custom-call | tf_op jit(solution)/shard_map/add_passed/pallas_call | solution.py:208
  118.3 5.6 %collective-permute-start.18 = (bf16[192,1024]{1,0:T(8,128)(2,1)}, bf16[192,1024]{1,0:T(8,128)(2,1)S(1)}, u32[]{:S(2)}, u32[]{:S(2)}) collective-permute-start(bf16[192,1024]{1,0:T(8,128)(2,1)} %get-tuple-element.32), channel_id=1, source_target_pairs={{0,6},{1,25},{2,0},{3,27},{4,2},{5,29},{6,4},{7,31},{8,14},{9,1},{... | collective-permute-start | bytes 1179656 | tf_op jit(solution)/shard_map/ppermute | solution.py:471
  123.9 4.0 %collective-permute-done.17.below_ref = bf16[192,1024]{1,0:T(8,128)(2,1)S(1)} collective-permute-done((bf16[192,1024]{1,0:T(8,128)(2,1)}, bf16[192,1024]{1,0:T(8,128)(2,1)S(1)}, u32[]{:S(2)}, u32[]{:S(2)}) %collective-permute-start.17) | collective-permute-done | bytes 393248 | tf_op jit(solution)/shard_map/ppermute | solution.py:471
  130.3 2.2 %add_blocks.1 = (bf16[48,1024]{1,0:T(8,128)(2,1)}, bf16[48,1024]{1,0:T(8,128)(2,1)}, bf16[48,1024]{1,0:T(8,128)(2,1)}, bf16[48,1024]{1,0:T(8,128)(2,1)}) custom-call(s32[6]{0:T(128)} %copy-done.11, f32[192,1024]{1,0:T(8,128)} %copy-done.3, bf16[192,1024]{1,0:T(8,128)(2,1)} %copy-done.13, bf16[192,1024]{1,0:T(8,128)(2,1)} %copy-done.14), custom_call_target="tpu_custom_call" | custom-call | tf_op jit(solution)/shard_map/add_blocks/pallas_call | solution.py:227
  132.5 5.6 %collective-permute-start.19 = (bf16[48,1024]{1,0:T(8,128)(2,1)}, bf16[48,1024]{1,0:T(8,128)(2,1)S(1)}, u32[]{:S(2)}, u32[]{:S(2)}) collective-permute-start(bf16[48,1024]{1,0:T(8,128)(2,1)} %get-tuple-element.34), channel_id=1, source_target_pairs={{0,24},{1,7},{2,26},{3,1},{4,28},{5,3},{6,30},{7,5},{8,0},{9,15},{... | collective-permute-start | bytes 294920 | tf_op jit(solution)/shard_map/ppermute | solution.py:471
  140.0 2.8 %collective-permute-start.21 = (bf16[48,1024]{1,0:T(8,128)(2,1)}, bf16[48,1024]{1,0:T(8,128)(2,1)S(1)}, u32[]{:S(2)}, u32[]{:S(2)}) collective-permute-start(bf16[48,1024]{1,0:T(8,128)(2,1)} %get-tuple-element.36), channel_id=1, source_target_pairs={{0,8},{1,3},{2,10},{3,5},{4,12},{5,7},{6,14},{7,1},{8,16},{9,11},{... | collective-permute-start | bytes 294920 | tf_op jit(solution)/shard_map/ppermute | solution.py:471
  142.8 3.5 %collective-permute-done.20.refs_2_ = bf16[48,1024]{1,0:T(8,128)(2,1)S(1)} collective-permute-done((bf16[48,1024]{1,0:T(8,128)(2,1)}, bf16[48,1024]{1,0:T(8,128)(2,1)S(1)}, u32[]{:S(2)}, u32[]{:S(2)}) %collective-permute-start.20) | collective-permute-done | bytes 98336 | tf_op jit(solution)/shard_map/ppermute | solution.py:471
  148.6 2.0 %finish.1 = bf16[48,4096]{1,0:T(8,128)(2,1)} custom-call(s32[6]{0:T(128)} %copy-done.11, bf16[48,4096]{1,0:T(8,128)(2,1)} %bitcast.24, f32[1,4096]{1,0:T(1,128)} %gate_ref.1, bf16[48,1024]{1,0:T(8,128)(2,1)} %get-tuple-element.33.refs_0_, bf16[48,1024]{1,0:T(8,128)(2,1)} %copy-done.17, bf16[48,1024]{1,0:T(8,128)(2,1)} %copy-done.18, bf16[48,1024]{1,0:T(8,128)(2,1)} %copy-done.19), custom_call_target="tpu_custom_call" | custom-call | tf_op jit(solution)/shard_map/finish/pallas_call | solution.py:255
  (91 shorter events, 41.3 us)
Async XLA Ops:
  0.7 14.1 %collective-permute-start.2 = (bf16[4,2,16,128]{3,2,1,0:T(8,128)(2,1)}, bf16[4,2,16,128]{3,2,1,0:T(8,128)(2,1)S(1)}, u32[]{:S(2)}, u32[]{:S(2)}) collective-permute-start(bf16[4,2,16,128]{3,2,1,0:T(8,128)(2,1)} %bitcast.27), channel_id=1, source_target_pairs={{64,96},{65,97},{66,98},{67,99},{68,100},{69,101},{70,102},{71,103... | collective-permute-start | bytes 98312 | tf_op jit(solution)/shard_map/ppermute | solution.py:478
  1.5 13.3 %collective-permute-start.1 = (bf16[4,2,16,128]{3,2,1,0:T(8,128)(2,1)}, bf16[4,2,16,128]{3,2,1,0:T(8,128)(2,1)S(1)}, u32[]{:S(2)}, u32[]{:S(2)}) collective-permute-start(bf16[4,2,16,128]{3,2,1,0:T(8,128)(2,1)} %bitcast.28), channel_id=1, source_target_pairs={{32,96},{33,97},{34,98},{35,99},{36,100},{37,101},{38,102},{39,103... | collective-permute-start | bytes 98312 | tf_op jit(solution)/shard_map/ppermute | solution.py:478
  2.1 12.6 %collective-permute-start = (bf16[4,2,16,128]{3,2,1,0:T(8,128)(2,1)}, bf16[4,2,16,128]{3,2,1,0:T(8,128)(2,1)S(1)}, u32[]{:S(2)}, u32[]{:S(2)}) collective-permute-start(bf16[4,2,16,128]{3,2,1,0:T(8,128)(2,1)} %bitcast.29), channel_id=1, source_target_pairs={{0,96},{1,97},{2,98},{3,99},{4,100},{5,101},{6,102},{7,103},{8,104... | collective-permute-start | bytes 98312 | tf_op jit(solution)/shard_map/ppermute | solution.py:478
  15.6 21.9 %collective-permute-start.4 = (bf16[16,2,16,128]{3,2,1,0:T(8,128)(2,1)S(1)}, bf16[16,2,16,128]{3,2,1,0:T(8,128)(2,1)S(1)}, u32[]{:S(2)}, u32[]{:S(2)}) collective-permute-start(bf16[16,2,16,128]{3,2,1,0:T(8,128)(2,1)S(1)} %pad_maximum_fusion.1), channel_id=1, source_target_pairs={{97,96},{98,97},{99,98},{100,99},{101,100},{102,101},{103,102},{10... | collective-permute-start | bytes 393224 | tf_op jit(solution)/shard_map/ppermute | solution.py:492
  16.2 21.2 %collective-permute-start.3 = (bf16[16,2,16,128]{3,2,1,0:T(8,128)(2,1)S(1)}, bf16[16,2,16,128]{3,2,1,0:T(8,128)(2,1)S(1)}, u32[]{:S(2)}, u32[]{:S(2)}) collective-permute-start(bf16[16,2,16,128]{3,2,1,0:T(8,128)(2,1)S(1)} %pad_maximum_fusion.1), channel_id=1, source_target_pairs={{96,97},{97,98},{98,99},{99,100},{100,101},{101,102},{102,103},{10... | collective-permute-start | bytes 393224 | tf_op jit(solution)/shard_map/ppermute | solution.py:490
  16.9 43.2 %collective-permute-start.10 = (bf16[128,4096]{1,0:T(8,128)(2,1)}, bf16[128,4096]{1,0:T(8,128)(2,1)S(1)}, u32[]{:S(2)}, u32[]{:S(2)}) collective-permute-start(bf16[128,4096]{1,0:T(8,128)(2,1)} %here_ref.1), channel_id=1, source_target_pairs={{0,1},{2,3},{4,5},{6,7},{8,9},{10,11},{12,13},{14,15},{16,17},{18,... | collective-permute-start | bytes 3145736 | tf_op jit(solution)/shard_map/ppermute | solution.py:502
  29.6 28.6 %all-to-all-start = ((bf16[16,3,48,256]{3,2,1,0:T(8,128)(2,1)}), bf16[16,3,48,256]{3,2,1,0:T(8,128)(2,1)S(1)}, u32[]{:S(2)}, u32[]{:S(2)}) async-start(bf16[16,3,48,256]{3,2,1,0:T(8,128)(2,1)} %norm_pack.1), calls=%async_computation | async-start | bytes 2359296 | tf_op jit(solution)/shard_map/all_to_all | solution.py:485
  39.3 20.8 %copy-start.12 = (s32[6]{0:T(128)S(1)}, s32[6]{0:T(128)}, u32[]{:S(2)}) copy-start(s32[6]{0:T(128)} %copy-done.11) | copy-start | bytes 76
  58.1 9.9 %collective-permute-start.5 = (bf16[16,3,48,256]{3,2,1,0:T(8,128)(2,1)S(1)}, bf16[16,3,48,256]{3,2,1,0:T(8,128)(2,1)S(1)}, u32[]{:S(2)}, u32[]{:S(2)}) collective-permute-start(bf16[16,3,48,256]{3,2,1,0:T(8,128)(2,1)S(1)} %all-to-all-done.here_ref), channel_id=1, source_target_pairs={{0,1},{2,3},{4,5},{6,7},{8,9},{10,11},{12,13},{14,15},{16,17},{18,... | collective-permute-start | bytes 3538952 | tf_op jit(solution)/shard_map/ppermute | solution.py:508
  60.8 20.3 %collective-permute-start.11 = (bf16[384,1024]{1,0:T(8,128)(2,1)S(1)}, bf16[384,1024]{1,0:T(8,128)(2,1)S(1)}, u32[]{:S(2)}, u32[]{:S(2)}) collective-permute-start(bf16[384,1024]{1,0:T(8,128)(2,1)S(1)} %get-tuple-element.24), channel_id=1, source_target_pairs={{0,8},{1,3},{2,10},{3,5},{4,12},{5,7},{6,14},{7,1},{8,16},{9,11},{... | collective-permute-start | bytes 2359304 | tf_op jit(solution)/shard_map/ppermute | solution.py:471
  63.1 20.0 %collective-permute-start.12 = (bf16[384,1024]{1,0:T(8,128)(2,1)S(1)}, bf16[384,1024]{1,0:T(8,128)(2,1)S(1)}, u32[]{:S(2)}, u32[]{:S(2)}) collective-permute-start(bf16[384,1024]{1,0:T(8,128)(2,1)S(1)} %get-tuple-element.25), channel_id=1, source_target_pairs={{0,24},{1,7},{2,26},{3,1},{4,28},{5,3},{6,30},{7,5},{8,0},{9,15},{... | collective-permute-start | bytes 2359304 | tf_op jit(solution)/shard_map/ppermute | solution.py:471
  74.0 14.2 %collective-permute-start.6 = (bf16[16,48,256]{2,1,0:T(8,128)(2,1)S(1)}, bf16[16,48,256]{2,1,0:T(8,128)(2,1)S(1)}, u32[]{:S(2)}, u32[]{:S(2)}) collective-permute-start(bf16[16,48,256]{2,1,0:T(8,128)(2,1)S(1)} %attend.1.oo), channel_id=1, source_target_pairs={{0,8},{1,3},{2,10},{3,5},{4,12},{5,7},{6,14},{7,1},{8,16},{9,11},{... | collective-permute-start | bytes 1179656 | tf_op jit(solution)/shard_map/ppermute | solution.py:471
  75.9 14.2 %collective-permute-start.7 = (bf16[16,48,256]{2,1,0:T(8,128)(2,1)S(1)}, bf16[16,48,256]{2,1,0:T(8,128)(2,1)S(1)}, u32[]{:S(2)}, u32[]{:S(2)}) collective-permute-start(bf16[16,48,256]{2,1,0:T(8,128)(2,1)S(1)} %attend.1.oo), channel_id=1, source_target_pairs={{0,24},{1,7},{2,26},{3,1},{4,28},{5,3},{6,30},{7,5},{8,0},{9,15},{... | collective-permute-start | bytes 1179656 | tf_op jit(solution)/shard_map/ppermute | solution.py:471
  81.1 14.2 %collective-permute-start.13 = (bf16[128,1024]{1,0:T(8,128)(2,1)S(1)}, bf16[128,1024]{1,0:T(8,128)(2,1)S(1)}, u32[]{:S(2)}, u32[]{:S(2)}) collective-permute-start(bf16[128,1024]{1,0:T(8,128)(2,1)S(1)} %slice.18), channel_id=1, source_target_pairs={{0,8},{1,3},{2,10},{3,5},{4,12},{5,7},{6,14},{7,1},{8,16},{9,11},{... | collective-permute-start | bytes 786440 | tf_op jit(solution)/shard_map/ppermute | solution.py:471
  83.1 12.3 %collective-permute-start.14 = (bf16[128,1024]{1,0:T(8,128)(2,1)S(1)}, bf16[128,1024]{1,0:T(8,128)(2,1)S(1)}, u32[]{:S(2)}, u32[]{:S(2)}) collective-permute-start(bf16[128,1024]{1,0:T(8,128)(2,1)S(1)} %slice.19), channel_id=1, source_target_pairs={{0,24},{1,7},{2,26},{3,1},{4,28},{5,3},{6,30},{7,5},{8,0},{9,15},{... | collective-permute-start | bytes 786440 | tf_op jit(solution)/shard_map/ppermute | solution.py:471
  88.3 8.8 %collective-permute-start.8 = (bf16[8,48,256]{2,1,0:T(8,128)(2,1)S(1)}, bf16[8,48,256]{2,1,0:T(8,128)(2,1)S(1)}, u32[]{:S(2)}, u32[]{:S(2)}) collective-permute-start(bf16[8,48,256]{2,1,0:T(8,128)(2,1)S(1)} %slice.16), channel_id=1, source_target_pairs={{0,8},{1,3},{2,10},{3,5},{4,12},{5,7},{6,14},{7,1},{8,16},{9,11},{... | collective-permute-start | bytes 589832 | tf_op jit(solution)/shard_map/ppermute | solution.py:471
  90.2 8.3 %collective-permute-start.9 = (bf16[8,48,256]{2,1,0:T(8,128)(2,1)S(1)}, bf16[8,48,256]{2,1,0:T(8,128)(2,1)S(1)}, u32[]{:S(2)}, u32[]{:S(2)}) collective-permute-start(bf16[8,48,256]{2,1,0:T(8,128)(2,1)S(1)} %slice.17), channel_id=1, source_target_pairs={{0,24},{1,7},{2,26},{3,1},{4,28},{5,3},{6,30},{7,5},{8,0},{9,15},{... | collective-permute-start | bytes 589832 | tf_op jit(solution)/shard_map/ppermute | solution.py:471
  103.3 8.8 %collective-permute-start.15 = (bf16[192,512]{1,0:T(8,128)(2,1)S(1)}, bf16[192,512]{1,0:T(8,128)(2,1)S(1)}, u32[]{:S(2)}, u32[]{:S(2)}) collective-permute-start(bf16[192,512]{1,0:T(8,128)(2,1)S(1)} %get-tuple-element.29), channel_id=1, source_target_pairs={{0,2},{1,9},{2,4},{3,11},{4,6},{5,13},{6,0},{7,15},{8,10},{9,17},{... | collective-permute-start | bytes 589832 | tf_op jit(solution)/shard_map/ppermute | solution.py:471
  105.2 8.3 %collective-permute-start.16 = (bf16[192,512]{1,0:T(8,128)(2,1)S(1)}, bf16[192,512]{1,0:T(8,128)(2,1)S(1)}, u32[]{:S(2)}, u32[]{:S(2)}) collective-permute-start(bf16[192,512]{1,0:T(8,128)(2,1)S(1)} %get-tuple-element.30), channel_id=1, source_target_pairs={{0,6},{1,25},{2,0},{3,27},{4,2},{5,29},{6,4},{7,31},{8,14},{9,1},{... | collective-permute-start | bytes 589832 | tf_op jit(solution)/shard_map/ppermute | solution.py:471
  116.4 11.5 %collective-permute-start.17 = (bf16[192,1024]{1,0:T(8,128)(2,1)}, bf16[192,1024]{1,0:T(8,128)(2,1)S(1)}, u32[]{:S(2)}, u32[]{:S(2)}) collective-permute-start(bf16[192,1024]{1,0:T(8,128)(2,1)} %get-tuple-element.31), channel_id=1, source_target_pairs={{0,2},{1,9},{2,4},{3,11},{4,6},{5,13},{6,0},{7,15},{8,10},{9,17},{... | collective-permute-start | bytes 1179656 | tf_op jit(solution)/shard_map/ppermute | solution.py:471
  118.3 11.2 %collective-permute-start.18 = (bf16[192,1024]{1,0:T(8,128)(2,1)}, bf16[192,1024]{1,0:T(8,128)(2,1)S(1)}, u32[]{:S(2)}, u32[]{:S(2)}) collective-permute-start(bf16[192,1024]{1,0:T(8,128)(2,1)} %get-tuple-element.32), channel_id=1, source_target_pairs={{0,6},{1,25},{2,0},{3,27},{4,2},{5,29},{6,4},{7,31},{8,14},{9,1},{... | collective-permute-start | bytes 1179656 | tf_op jit(solution)/shard_map/ppermute | solution.py:471
  132.5 10.3 %collective-permute-start.19 = (bf16[48,1024]{1,0:T(8,128)(2,1)}, bf16[48,1024]{1,0:T(8,128)(2,1)S(1)}, u32[]{:S(2)}, u32[]{:S(2)}) collective-permute-start(bf16[48,1024]{1,0:T(8,128)(2,1)} %get-tuple-element.34), channel_id=1, source_target_pairs={{0,24},{1,7},{2,26},{3,1},{4,28},{5,3},{6,30},{7,5},{8,0},{9,15},{... | collective-permute-start | bytes 294920 | tf_op jit(solution)/shard_map/ppermute | solution.py:471
  138.1 8.2 %collective-permute-start.20 = (bf16[48,1024]{1,0:T(8,128)(2,1)}, bf16[48,1024]{1,0:T(8,128)(2,1)S(1)}, u32[]{:S(2)}, u32[]{:S(2)}) collective-permute-start(bf16[48,1024]{1,0:T(8,128)(2,1)} %get-tuple-element.35), channel_id=1, source_target_pairs={{0,16},{1,5},{2,18},{3,7},{4,20},{5,1},{6,22},{7,3},{8,24},{9,13},... | collective-permute-start | bytes 294920 | tf_op jit(solution)/shard_map/ppermute | solution.py:471
  140.0 7.9 %collective-permute-start.21 = (bf16[48,1024]{1,0:T(8,128)(2,1)}, bf16[48,1024]{1,0:T(8,128)(2,1)S(1)}, u32[]{:S(2)}, u32[]{:S(2)}) collective-permute-start(bf16[48,1024]{1,0:T(8,128)(2,1)} %get-tuple-element.36), channel_id=1, source_target_pairs={{0,8},{1,3},{2,10},{3,5},{4,12},{5,7},{6,14},{7,1},{8,16},{9,11},{... | collective-permute-start | bytes 294920 | tf_op jit(solution)/shard_map/ppermute | solution.py:471
  (22 other events, 109.5 us)

commit v2 on v1

v2 whole, which is shorter than its diff:
```python
import math
import jax
import jax.numpy as jnp
from jax import lax
from jax.experimental import pallas as pl
from jax.experimental.pallas import tpu as pltpu
from jax.sharding import Mesh, PartitionSpec as P

CHIPS = ("z", "x")
SEQ = ("z", "x", "core")
EPS = 1e-06
MIB = 1024 * 1024


def vmem_spec():
    return pl.BlockSpec(memory_space=pltpu.VMEM)


def smem_spec():
    return pl.BlockSpec(memory_space=pltpu.SMEM)


def norm_pack(q, k, v, gain_q, gain_k):
    rows, width = q.shape
    chips = width // 256
    block = 16

    def body(q_ref, k_ref, v_ref, gq_ref, gk_ref, out_ref):
        def normed(ref, gain):
            x = ref[...].astype(jnp.float32)
            factor = lax.rsqrt(jnp.mean(x * x, axis=-1, keepdims=True) + EPS)
            return (x * factor * gain).astype(jnp.bfloat16)

        scale = 128**-0.5 * math.log2(math.e)
        qn = normed(q_ref, gq_ref[...] * scale)
        kn = normed(k_ref, gk_ref[...])
        for c in range(chips):
            cols = slice(256 * c, 256 * c + 256)
            out_ref[c, 0] = qn[:, cols]
            out_ref[c, 1] = kn[:, cols]
            out_ref[c, 2] = v_ref[:, cols]

    tokens = pl.BlockSpec((block, width), lambda i: (i, 0))
    gains = pl.BlockSpec((1, width), lambda i: (0, 0))
    return pl.pallas_call(
        body,
        grid=(rows // block,),
        out_shape=jax.ShapeDtypeStruct((chips, 3, rows, 256), jnp.bfloat16),
        in_specs=[tokens, tokens, tokens, gains, gains],
        out_specs=pl.BlockSpec((chips, 3, block, 256), lambda i: (0, 0, i, 0)),
        compiler_params=pltpu.CompilerParams(vmem_limit_bytes=60 * MIB),
        name="norm_pack",
    )(q, k, v, gain_q, gain_k)


def weight_halves(place, w_here, w_there):
    rows, width = w_here.shape
    part = width // 2

    def body(place_ref, here_ref, there_ref, keep_ref, give_ref):
        here_at = pl.ds(pl.multiple_of(place_ref[1] * rows, rows), rows)
        there_at = pl.ds(pl.multiple_of((1 - place_ref[1]) * rows, rows), rows)

        @pl.when(place_ref[0] == 0)
        def _():
            for k, out in enumerate((keep_ref, give_ref)):
                half = jnp.bitwise_xor(place_ref[4] // 2, k)
                at = pl.ds(pl.multiple_of(half * part, part), part)
                out[here_at] = here_ref[:, at]
                out[there_at] = there_ref[:, at]

    return pl.pallas_call(
        body,
        out_shape=(jax.ShapeDtypeStruct((2 * rows, part), jnp.bfloat16),) * 2,
        in_specs=[smem_spec(), vmem_spec(), vmem_spec()],
        out_specs=(vmem_spec(),) * 2,
        compiler_params=pltpu.CompilerParams(vmem_limit_bytes=16 * MIB),
        name="weight_halves",
    )(place, w_here, w_there)


def inner(position):
    return ((position + 1) // 2) % 2


def attend(place, here, there):
    chips, _, tok, _ = here.shape
    half = chips * tok
    keys = 2 * half

    def body(place_ref, here_ref, there_ref, near_ref, other_ref, k_buf, v_buf):
        step = pl.program_id(0)

        @pl.when((step == 0) & (place_ref[0] == 0))
        def _():
            for h in range(2):
                cols = slice(128 * h, 128 * h + 128)
                for n, ref in enumerate((here_ref, there_ref)):
                    span = slice(n * half, n * half + half)
                    k_buf[h, span] = ref[:, 1, :, cols].reshape(half, 128)
                    v_buf[h, span, :128] = ref[:, 2, :, cols].reshape(half, 128)
                v_buf[h, :, 128:] = jnp.ones((keys, 128), jnp.bfloat16)

        @pl.when(place_ref[0] == 0)
        def _():
            queries = here_ref[pl.ds(4 * step, 4), 0].reshape(4 * tok, 256)
            heads = []
            for h in range(2):
                s = lax.dot_general(
                    queries[:, 128 * h : 128 * h + 128],
                    k_buf[h],
                    (((1,), (1,)), ((), ())),
                    preferred_element_type=jnp.float32,
                )
                p = jnp.exp2(s - jnp.max(s, axis=-1, keepdims=True)).astype(jnp.bfloat16)
                o = jnp.dot(p, v_buf[h], preferred_element_type=jnp.float32)
                heads.append(o[:, :128] / o[:, 128:])
            joined = jnp.concatenate(heads, axis=1).astype(jnp.bfloat16)
            for n in range(4):
                first = jnp.where(place_ref[1] == 0, step, n)
                second = jnp.where(place_ref[1] == 0, n, step)
                high = first // 2
                slot = jnp.where(second == 0, 0, jnp.where(second == 3, 1, second + 1))
                near = inner(first) == inner(place_ref[4])
                piece = joined[tok * n : tok * n + tok]

                @pl.when(near)
                def _():
                    near_ref[slot, high] = piece

                @pl.when(jnp.logical_not(near))
                def _():
                    other_ref[slot, high] = piece

    return pl.pallas_call(
        body,
        grid=(chips // 4,),
        out_shape=(jax.ShapeDtypeStruct((4, 2, tok, 256), jnp.bfloat16),) * 2,
        in_specs=[smem_spec(), vmem_spec(), vmem_spec()],
        out_specs=(vmem_spec(),) * 2,
        scratch_shapes=[
            pltpu.VMEM((2, keys, 128), jnp.bfloat16),
            pltpu.VMEM((2, keys, 256), jnp.bfloat16),
        ],
        compiler_params=pltpu.CompilerParams(vmem_limit_bytes=40 * MIB),
        cost_estimate=pl.CostEstimate(flops=0, bytes_accessed=0, transcendentals=0),
        name="attend",
    )(place, here, there)


def project(place, heads, weights):
    _, two, tok, _ = heads[0].shape
    part = weights[0].shape[1]
    lot = two * tok

    def body(place_ref, h0, h1, h2, h3, w0, w1, w2, w3, own_ref, one_ref, zero_ref, far_ref):
        second = place_ref[5]
        slot = jnp.where(second == 0, 0, jnp.where(second == 3, 1, second + 1))

        @pl.when(place_ref[0] == 0)
        def _():
            weight = jnp.concatenate([w0[...], w1[...], w2[...], w3[...]], axis=0)
            feats = jnp.concatenate(
                [
                    jnp.concatenate(
                        [h[jnp.bitwise_xor(slot, k)].reshape(lot, 256) for h in (h0, h1, h2, h3)],
                        axis=1,
                    )
                    for k in range(4)
                ],
                axis=0,
            )
            out = jnp.dot(feats, weight, preferred_element_type=jnp.float32)
            for k, ref in enumerate((own_ref, one_ref, zero_ref, far_ref)):
                ref[...] = out[lot * k : lot * k + lot].reshape(two, tok, part).astype(ref.dtype)

    shape = (two, tok, part)
    return pl.pallas_call(
        body,
        out_shape=(jax.ShapeDtypeStruct(shape, jnp.float32),)
        + (jax.ShapeDtypeStruct(shape, jnp.bfloat16),) * 3,
        in_specs=[smem_spec()] + [vmem_spec()] * 8,
        out_specs=(vmem_spec(),) * 4,
        compiler_params=pltpu.CompilerParams(vmem_limit_bytes=40 * MIB),
        cost_estimate=pl.CostEstimate(
            flops=8 * lot * 1024 * part, bytes_accessed=8 * MIB, transcendentals=0
        ),
        name="project",
    )(place, *heads, *weights)


def add_up(place, own, others):
    def body(place_ref, own_ref, a_ref, b_ref, c_ref, keep_ref, give_ref):
        mine = place_ref[4] // 2

        @pl.when(place_ref[0] == 0)
        def _():
            for at, out in ((mine, keep_ref), (1 - mine, give_ref)):
                total = own_ref[at]
                for ref in (a_ref, b_ref, c_ref):
                    total += ref[at].astype(jnp.float32)
                out[...] = total.astype(out.dtype)

    return pl.pallas_call(
        body,
        out_shape=(
            jax.ShapeDtypeStruct(own.shape[1:], jnp.float32),
            jax.ShapeDtypeStruct(own.shape[1:], jnp.bfloat16),
        ),
        in_specs=[smem_spec()] + [vmem_spec()] * 4,
        out_specs=(vmem_spec(),) * 2,
        compiler_params=pltpu.CompilerParams(vmem_limit_bytes=24 * MIB),
        name="add_up",
    )(place, own, *others)


def finish(place, resid, gate, kept, got):
    part = kept.shape[1]

    def body(place_ref, resid_ref, gate_ref, kept_ref, got_ref, out_ref):
        @pl.when(place_ref[0] == 0)
        def _():
            for k, ref in enumerate((kept_ref, got_ref)):
                half = jnp.bitwise_xor(place_ref[4] // 2, k)
                at = pl.ds(pl.multiple_of(half * part, part), part)
                total = resid_ref[:, at].astype(jnp.float32)
                total += gate_ref[:, at] * ref[...].astype(jnp.float32)
                out_ref[:, at] = total.astype(jnp.bfloat16)

        @pl.when(place_ref[0] == 1)
        def _():
            out_ref[...] = jnp.zeros(out_ref.shape, out_ref.dtype)

    return pl.pallas_call(
        body,
        out_shape=jax.ShapeDtypeStruct(resid.shape, jnp.bfloat16),
        in_specs=[smem_spec()] + [vmem_spec()] * 4,
        out_specs=vmem_spec(),
        compiler_params=pltpu.CompilerParams(vmem_limit_bytes=16 * MIB),
        name="finish",
    )(place, resid, gate, kept, got)


def filter_weights(place, w_mid):
    steps, deep, vc = w_mid.shape
    taps = w_mid.reshape(steps, 3, 3, vc, vc)

    def block(w_ref, out_ref):
        up, mid, down = (w_ref[0, n, 0] for n in range(3))
        ends = 0.5 * (up.astype(jnp.float32) + down.astype(jnp.float32))
        half = 0.5 * mid.astype(jnp.float32)
        for n, g in enumerate((up, ends + half, ends - half, down)):
            out_ref[n] = jnp.transpose(g.astype(jnp.bfloat16))

    def body(place_ref, w_ref, out_ref):
        @pl.when(place_ref[0] == 1)
        def _():
            pltpu.emit_pipeline(
                block,
                grid=(3 * steps,),
                in_specs=[pl.BlockSpec((1, 3, 1, vc, vc), lambda i: (i // 3, 0, i % 3, 0, 0))],
                out_specs=[pl.BlockSpec((4, vc, vc), lambda i: (0, 0, i))],
            )(w_ref, out_ref)

    return pl.pallas_call(
        body,
        out_shape=jax.ShapeDtypeStruct((4, vc, deep), jnp.bfloat16),
        in_specs=[smem_spec(), pl.BlockSpec(memory_space=pl.ANY)],
        out_specs=pl.BlockSpec(memory_space=pl.ANY),
        compiler_params=pltpu.CompilerParams(vmem_limit_bytes=60 * MIB),
        name="filter_weights",
    )(place, taps)


def decode(place, clip, w_first, filters, vectors):
    frames, _, lc, lw = clip.shape
    vc = w_first.shape[0]
    deep = 3 * vc
    lot = 4

    def body(place_ref, clip_ref, w1_ref, f_ref, vec_ref, out_ref, lat, act, firsts, w2, both, sems):
        step = pl.program_id(0)
        here = place_ref[0] == 1
        loads = [pltpu.make_async_copy(f_ref.at[n], w2.at[n], sems.at[n]) for n in range(4)]

        def moved(x):
            lane = lax.broadcasted_iota(jnp.int32, x.shape, x.ndim - 1)
            left = jnp.where(lane == 0, 0.0, pltpu.roll(x, 1, x.ndim - 1))
            right = jnp.where(lane == lw - 1, 0.0, pltpu.roll(x, lw - 1, x.ndim - 1))
            return left, x, right

        def first(f):
            sides = []
            for row in range(4):
                taps = [lat[f + dt, row : row + 3].reshape(9 * lc, lw) for dt in range(3)]
                taps.append(jnp.zeros((w1_ref.shape[1] - 27 * lc, lw), jnp.bfloat16))
                sides.append(jnp.concatenate(taps, axis=0))
            y = jnp.dot(
                w1_ref[...], jnp.concatenate(sides, axis=1), preferred_element_type=jnp.float32
            )
            acts = []
            for row in range(4):
                hidden = y[:, row * lw : row * lw + lw] + vec_ref[0]
                hidden = hidden.astype(jnp.bfloat16).astype(jnp.float32)
                if row in (1, 2):
                    firsts[lax.rem(f, 2 * lot), row - 1] = hidden
                factor = lax.rsqrt(jnp.mean(hidden * hidden, axis=0, keepdims=True) + EPS)
                if row == 0:
                    factor = jnp.where(place_ref[2] == 0, 0.0, factor)
                if row == 3:
                    factor = jnp.where(place_ref[2] == place_ref[3], 0.0, factor)
                half = hidden * (0.5 * factor) * vec_ref[1]
                acts.append(half * (1.0 + jnp.tanh(half)))
            a0, a1, a2, a3 = acts
            for n, u in enumerate((a0 - a2, a1 + a2, a2 - a1, a1 - a3)):
                for dx, piece in enumerate(moved(u)):
                    act[n, f + 2, dx * vc : dx * vc + vc] = piece.astype(jnp.bfloat16)

        @pl.when(here & (step == 0))
        def _():
            for load in loads:
                load.start()
            lat[:2] = jnp.zeros((2, 6, 3 * lc, lw), jnp.bfloat16)
            act[:, :2] = jnp.zeros((4, 2, deep, lw), jnp.bfloat16)
            cells = clip_ref[...].astype(jnp.float32)
            for dx, piece in enumerate(moved(cells)):
                lat[2:, :, dx * lc : dx * lc + lc] = piece.astype(jnp.bfloat16)

            @pl.loop(0, lot)
            def _(f):
                first(f)

            for load in loads:
                load.wait()

        def second(and_next):
            base = lot * step
            for n in range(4):
                taps = jnp.concatenate(
                    [act[n, pl.ds(base + j, 3)].reshape(3 * deep, lw) for j in range(lot)], axis=1
                )
                m = jnp.dot(w2[n], taps, preferred_element_type=jnp.float32)
                if n == 0:
                    both[0] = m
                if n == 1:
                    both[0] += m
                    both[1] = m
                if n == 2:
                    both[0] += m
                    both[1] -= m
                if n == 3:
                    both[1] -= m
                if and_next:
                    first(base + lot + n)
            for j in range(lot):
                for r in range(2):
                    whole = both[r, :, j * lw : j * lw + lw]
                    whole += vec_ref[2] + firsts[lax.rem(base + j, 2 * lot), r]
                    out_ref[j, r] = jnp.transpose(whole).astype(jnp.bfloat16)

        @pl.when(here & (step < frames // lot - 1))
        def _():
            second(True)

        @pl.when(here & (step == frames // lot - 1))
        def _():
            second(False)

        @pl.when(jnp.logical_not(here))
        def _():
            out_ref[...] = jnp.zeros(out_ref.shape, out_ref.dtype)

    return pl.pallas_call(
        body,
        grid=(frames // lot,),
        out_shape=jax.ShapeDtypeStruct((frames, 2, lw, vc), jnp.bfloat16),
        in_specs=[
            smem_spec(),
            vmem_spec(),
            vmem_spec(),
            pl.BlockSpec(memory_space=pl.ANY),
            vmem_spec(),
        ],
        out_specs=pl.BlockSpec((lot, 2, lw, vc), lambda i: (i, 0, 0, 0)),
        scratch_shapes=[
            pltpu.VMEM((frames + 2, 6, 3 * lc, lw), jnp.bfloat16),
            pltpu.VMEM((4, frames + 2, deep, lw), jnp.bfloat16),
            pltpu.VMEM((2 * lot, 2, vc, lw), jnp.float32),
            pltpu.VMEM((4, vc, 3 * deep), jnp.bfloat16),
            pltpu.VMEM((2, vc, lot * lw), jnp.float32),
            pltpu.SemaphoreType.DMA((4,)),
        ],
        compiler_params=pltpu.CompilerParams(vmem_limit_bytes=48 * MIB),
        cost_estimate=pl.CostEstimate(flops=0, bytes_accessed=0, transcendentals=0),
        name="decode",
    )(place, clip, w_first, filters, vectors)


def on_device(
    query_input,
    key_input,
    value_input,
    resid,
    gate,
    query_norm_gain,
    key_norm_gain,
    output_weight,
    latents,
    w_in,
    b_in,
    norm_gain,
    w_mid,
    b_mid,
):
    last = lax.axis_size("grp") - 1
    decoder_here = lax.axis_index("grp") == last
    count = lax.axis_size(SEQ)
    side = lax.axis_size("z")
    core, at_z, at_x = lax.axis_index("core"), lax.axis_index("z"), lax.axis_index("x")
    place = jnp.stack(
        [
            decoder_here.astype(jnp.int32),
            core,
            lax.axis_index(SEQ),
            jnp.int32(count - 1),
            jnp.where(core == 0, at_z, at_x),
            jnp.where(core == 0, at_x, at_z),
        ]
    )
    channels = w_in.shape[2]

    def swap(x, ring, step):
        def partner(place):
            return (place ^ 1, side - 1 - place, place ^ 2)[step]

        pairs = []
        for at in range(last * count):
            g, z, x_, c = at // count, at // (2 * side) % side, at // 2 % side, at % 2
            if ring == 2:
                c = 1 - c
            elif (ring == 0) == (c == 0):
                z = partner(z)
            else:
                x_ = partner(x_)
            pairs.append((at, ((g * side + z) * side + x_) * 2 + c))
        return lax.ppermute(x, ("grp",) + SEQ, pairs)

    w_there = swap(output_weight, 2, 0)
    packed = norm_pack(
        query_input[0], key_input[0], value_input[0], query_norm_gain[None], key_norm_gain[None]
    )
    packed, w_there = lax.optimization_barrier((packed, w_there))
    here = lax.all_to_all(packed, CHIPS, split_axis=0, concat_axis=0, tiled=True)
    w_own, w_give = weight_halves(place, output_weight, w_there)
    w_own, w_give, latents, w_mid = lax.optimization_barrier((w_own, w_give, latents, w_mid))
    w_next, w_back, w_far = swap(w_own, 0, 0), swap(w_give, 0, 1), swap(w_give, 0, 2)

    own = jnp.swapaxes(latents, 2, 3)
    pieces = [lax.ppermute(own, "grp", [(g, last)]) for g in range(last)]
    filters = filter_weights(place, w_mid)
    pieces, filters = lax.optimization_barrier((pieces, filters))
    clip = jnp.concatenate(pieces + [own], axis=0)
    here, w_next, w_back, clip = lax.optimization_barrier((here, w_next, w_back, clip))
    links = [(last * count + i, last * count + i + 1) for i in range(count - 1)]
    cells = jnp.concatenate(
        [
            lax.ppermute(clip, ("grp",) + SEQ, links),
            clip,
            lax.ppermute(clip, ("grp",) + SEQ, [(b, a) for a, b in links]),
        ],
        axis=1,
    )
    w_first = jnp.pad(w_in.reshape(-1, channels).T, ((0, 0), (0, 512 - 27 * latents.shape[3])))
    vectors = jnp.broadcast_to(
        jnp.stack([b_in, norm_gain, b_mid])[:, :, None], (3, channels, latents.shape[2])
    )
    there = swap(here, 2, 0)
    near, other = attend(place, here, there)
    heads = near, swap(other, 0, 0), swap(near, 0, 1), swap(other, 0, 2)
    mine, one, zero, far = project(place, heads, (w_own, w_next, w_back, w_far))
    mine, one, zero, far, cells = lax.optimization_barrier((mine, one, zero, far, cells))
    decoded = decode(place, cells, w_first, filters, vectors)
    kept, give = add_up(place, mine, (swap(one, 1, 1), swap(zero, 1, 0), swap(far, 1, 2)))
    attn_out = finish(place, resid[0], gate, kept, swap(give, 0, 1))
    return attn_out[None], decoded[None]


def solution(mesh):
    fine = Mesh(mesh.devices.reshape(4, 4, 4, 2), ("grp",) + SEQ)
    placed = (
        P("grp", SEQ, None),
        P("grp", SEQ, None),
        P("grp", SEQ, None),
        P("grp", SEQ, None),
        P("grp", None),
        P(),
        P(),
        P(SEQ, None),
        P("grp", SEQ, None, None),
        P(),
        P(),
        P(),
        P(),
        P(),
    )
    return jax.shard_map(
        on_device,
        mesh=fine,
        in_specs=placed,
        out_specs=(P("grp", SEQ, None), P("grp", None, SEQ, None, None)),
        check_vma=False,
    )
```

time: 153 us -> 105 us (0.69); the launches traced: 151 us -> 105 us
  starting transfers between devices: 74 us -> 52.7 us
  local copies, waits for them, and re-layouts: 19.5 us -> 2.19 us
  waiting for transfers between devices: 32.2 us -> 28 us
  Pallas kernels: 22.2 us -> 20.6 us
    ppermute x20 -> x15, starting transfers between devices: 64.8 us -> 43.4 us  [the longest x12 40.8 us: swap(): return lax.ppermute(x, ('grp',) + SEQ, pairs)]
    unnamed x46 -> x20, local copies, waits for them, and re-layouts: 16.3 us -> 0.7 us
    all_to_all x1, waiting for transfers between devices: 15.2 us -> 0.01 us  [on_device(): lax.all_to_all(packed, CHIPS, split_axis=0, concat_axis=0, tiled=True)]
    ppermute x20 -> x15, waiting for transfers between devices: 17.1 us -> 28 us  [the longest x12 28 us: swap(): return lax.ppermute(x, ('grp',) + SEQ, pairs)]
    pallas_call x6 -> x5, Pallas kernels: 14.6 us -> 12.9 us  [the longest x1 6.41 us: attend(): pl.pallas_call(body, grid=(chips // 4,), out_shape=(jax.ShapeDtypeStruct(...]
    pallas_call x1, Pallas kernels: 1.92 us -> 3.48 us  [norm_pack(): pl.pallas_call(body, grid=(rows // block,), out_shape=jax.ShapeDtypeStruc...]
  transfers between devices with their start and end apart: 23 -> 18, of which waited for: 9 -> 7; matrix products, arithmetic and copies ran while one was open for 3% -> 1% of each run, Pallas kernels for 9% -> 15%
where the time goes in v2:
time: 105 us
  starting transfers between devices  52.7 us (50%)
  waiting for transfers between devices  28 us (27%)
  Pallas kernels  20.6 us (20%)
  local copies, waits for them, and re-layouts  2.19 us (2%)
  between operations  1.11 us (1%)
    ppermute x12, starting transfers between devices, swap(): return lax.ppermute(x, ('grp',) + SEQ, pairs)  40.8 us
    ppermute x12, waiting for transfers between devices, swap(): return lax.ppermute(x, ('grp',) + SEQ, pairs)  28 us
    all_to_all x1, starting transfers between devices, on_device(): lax.all_to_all(packed, CHIPS, split_axis=0, concat_axis=0, tiled=True)  7.96 us
    pallas_call x1, Pallas kernels, attend(): pl.pallas_call(body, grid=(chips // 4,), out_shape=(jax.ShapeDtypeStruct(...  6.41 us
    pallas_call x1, Pallas kernels, norm_pack(): pl.pallas_call(body, grid=(rows // block,), out_shape=jax.ShapeDtypeStruc...  3.48 us
    pallas_call x1, Pallas kernels, project(): pl.pallas_call(body, out_shape=(jax.ShapeDtypeStruct(shape, jnp.float32),...  3.04 us
    pallas_call x1, Pallas kernels, decode(): pl.pallas_call(body, grid=(frames // lot,), out_shape=jax.ShapeDtypeStruc...  2.8 us
    ppermute x3, starting transfers between devices, on_device(): pieces = [lax.ppermute(own, 'grp', [(g, last)]) for g in range(last)]  2.62 us
  transfers between devices with their start and end apart: 18, of which 7 were waited for; matrix products, arithmetic and copies ran while one was open for 1% of the time, Pallas kernels for 15%

profile of v2, /device:TPU:0, one launch (start us, length us, event | category | flops | bytes accessed | tf_op | source)
XLA Modules:
  0.0 104.7 jit_solution(8913100200662583650)
XLA Ops:
  0.6 2.1 %collective-permute-start = (bf16[128,4096]{1,0:T(8,128)(2,1)}, bf16[128,4096]{1,0:T(8,128)(2,1)S(1)}, u32[]{:S(2)}, u32[]{:S(2)}) collective-permute-start(bf16[128,4096]{1,0:T(8,128)(2,1)} %here_ref.1), channel_id=1, source_target_pairs={{0,1},{1,0},{2,3},{3,2},{4,5},{5,4},{6,7},{7,6},{8,9},{9,8},{10,11... | collective-permute-start | bytes 3145736 | tf_op jit(solution)/shard_map/ppermute | solution.py:446
  2.7 3.5 %norm_pack.1 = bf16[16,3,48,256]{3,2,1,0:T(8,128)(2,1)} custom-call(bf16[48,4096]{1,0:T(8,128)(2,1)} %bitcast.21, bf16[48,4096]{1,0:T(8,128)(2,1)} %bitcast.22, bf16[48,4096]{1,0:T(8,128)(2,1)} %bitcast.23, f32[1,4096]{1,0:T(1,128)} %bitcast.30, f32[1,4096]{1,0:T(1,128)} %bitcast.31), custom_call_target="tpu_custom_call" | custom-call | tf_op jit(solution)/shard_map/norm_pack/pallas_call | solution.py:45
  6.2 8.0 %all-to-all-start = ((bf16[16,3,48,256]{3,2,1,0:T(8,128)(2,1)}), bf16[16,3,48,256]{3,2,1,0:T(8,128)(2,1)S(1)}, u32[]{:S(2)}, u32[]{:S(2)}) async-start(bf16[16,3,48,256]{3,2,1,0:T(8,128)(2,1)} %norm_pack.1), calls=%async_computation | async-start | bytes 2359296 | tf_op jit(solution)/shard_map/all_to_all | solution.py:453
  14.3 2.1 %weight_halves.1 = (bf16[256,2048]{1,0:T(8,128)(2,1)}, bf16[256,2048]{1,0:T(8,128)(2,1)}) custom-call(s32[6]{0:T(128)S(1)} %stack.39.place_ref, bf16[128,4096]{1,0:T(8,128)(2,1)S(1)} %copy-done, bf16[128,4096]{1,0:T(8,128)(2,1)S(1)} %collective-permute-done.there_ref), custom_call_target="tpu_custom_call" | custom-call | tf_op jit(solution)/shard_map/weight_halves/pallas_call | solution.py:72
  16.4 3.8 %collective-permute-start.1 = (bf16[256,2048]{1,0:T(8,128)(2,1)}, bf16[256,2048]{1,0:T(8,128)(2,1)S(1)}, u32[]{:S(2)}, u32[]{:S(2)}) collective-permute-start(bf16[256,2048]{1,0:T(8,128)(2,1)} %get-tuple-element.35.w0), channel_id=1, source_target_pairs={{0,8},{1,3},{2,10},{3,1},{4,12},{5,7},{6,14},{7,5},{8,0},{9,11},{1... | collective-permute-start | bytes 3145736 | tf_op jit(solution)/shard_map/ppermute | solution.py:446
  20.2 4.0 %collective-permute-start.2 = (bf16[256,2048]{1,0:T(8,128)(2,1)}, bf16[256,2048]{1,0:T(8,128)(2,1)S(1)}, u32[]{:S(2)}, u32[]{:S(2)}) collective-permute-start(bf16[256,2048]{1,0:T(8,128)(2,1)} %get-tuple-element.36), channel_id=1, source_target_pairs={{0,24},{1,7},{2,26},{3,5},{4,28},{5,3},{6,30},{7,1},{8,16},{9,15},... | collective-permute-start | bytes 3145736 | tf_op jit(solution)/shard_map/ppermute | solution.py:446
  27.6 13.4 %collective-permute-done.1.w1 = bf16[256,2048]{1,0:T(8,128)(2,1)S(1)} collective-permute-done((bf16[256,2048]{1,0:T(8,128)(2,1)}, bf16[256,2048]{1,0:T(8,128)(2,1)S(1)}, u32[]{:S(2)}, u32[]{:S(2)}) %collective-permute-start.1) | collective-permute-done | bytes 1048608 | tf_op jit(solution)/shard_map/ppermute | solution.py:446
  41.0 1.8 %collective-permute-done.2.w2 = bf16[256,2048]{1,0:T(8,128)(2,1)S(1)} collective-permute-done((bf16[256,2048]{1,0:T(8,128)(2,1)}, bf16[256,2048]{1,0:T(8,128)(2,1)S(1)}, u32[]{:S(2)}, u32[]{:S(2)}) %collective-permute-start.2) | collective-permute-done | bytes 1048608 | tf_op jit(solution)/shard_map/ppermute | solution.py:446
  42.8 1.9 %collective-permute-start.6 = (bf16[16,3,48,256]{3,2,1,0:T(8,128)(2,1)S(1)}, bf16[16,3,48,256]{3,2,1,0:T(8,128)(2,1)S(1)}, u32[]{:S(2)}, u32[]{:S(2)}) collective-permute-start(bf16[16,3,48,256]{3,2,1,0:T(8,128)(2,1)S(1)} %all-to-all-done.here_ref), channel_id=1, source_target_pairs={{0,1},{1,0},{2,3},{3,2},{4,5},{5,4},{6,7},{7,6},{8,9},{9,8},{10,11... | collective-permute-start | bytes 3538952 | tf_op jit(solution)/shard_map/ppermute | solution.py:446
  44.7 4.2 %collective-permute-start.10 = (bf16[256,2048]{1,0:T(8,128)(2,1)}, bf16[256,2048]{1,0:T(8,128)(2,1)S(1)}, u32[]{:S(2)}, u32[]{:S(2)}) collective-permute-start(bf16[256,2048]{1,0:T(8,128)(2,1)} %get-tuple-element.36), channel_id=1, source_target_pairs={{0,16},{1,5},{2,18},{3,7},{4,20},{5,1},{6,22},{7,3},{8,24},{9,13},... | collective-permute-start | bytes 3145736 | tf_op jit(solution)/shard_map/ppermute | solution.py:446
  50.9 6.4 %attend.1 = (bf16[4,2,48,256]{3,2,1,0:T(8,128)(2,1)S(1)}, bf16[4,2,48,256]{3,2,1,0:T(8,128)(2,1)S(1)}) custom-call(s32[6]{0:T(128)S(1)} %copy-done.3, bf16[16,3,48,256]{3,2,1,0:T(8,128)(2,1)S(1)} %all-to-all-done.here_ref, bf16[16,3,48,256]{3,2,1,0:T(8,128)(2,1)S(1)} %collective-permute-done.6.there_ref), custom_call_target="tpu_custom_call" | custom-call | tf_op jit(solution)/shard_map/attend/pallas_call | solution.py:135
  57.3 3.0 %collective-permute-start.7 = (bf16[4,2,48,256]{3,2,1,0:T(8,128)(2,1)S(1)}, bf16[4,2,48,256]{3,2,1,0:T(8,128)(2,1)S(1)}, u32[]{:S(2)}, u32[]{:S(2)}) collective-permute-start(bf16[4,2,48,256]{3,2,1,0:T(8,128)(2,1)S(1)} %get-tuple-element.44), channel_id=1, source_target_pairs={{0,8},{1,3},{2,10},{3,1},{4,12},{5,7},{6,14},{7,5},{8,0},{9,11},{1... | collective-permute-start | bytes 589832 | tf_op jit(solution)/shard_map/ppermute | solution.py:446
  60.3 2.6 %collective-permute-start.8 = (bf16[4,2,48,256]{3,2,1,0:T(8,128)(2,1)S(1)}, bf16[4,2,48,256]{3,2,1,0:T(8,128)(2,1)S(1)}, u32[]{:S(2)}, u32[]{:S(2)}) collective-permute-start(bf16[4,2,48,256]{3,2,1,0:T(8,128)(2,1)S(1)} %get-tuple-element.43.h0), channel_id=1, source_target_pairs={{0,24},{1,7},{2,26},{3,5},{4,28},{5,3},{6,30},{7,1},{8,16},{9,15},... | collective-permute-start | bytes 589832 | tf_op jit(solution)/shard_map/ppermute | solution.py:446
  63.0 4.2 %collective-permute-start.9 = (bf16[4,2,48,256]{3,2,1,0:T(8,128)(2,1)S(1)}, bf16[4,2,48,256]{3,2,1,0:T(8,128)(2,1)S(1)}, u32[]{:S(2)}, u32[]{:S(2)}) collective-permute-start(bf16[4,2,48,256]{3,2,1,0:T(8,128)(2,1)S(1)} %get-tuple-element.44), channel_id=1, source_target_pairs={{0,16},{1,5},{2,18},{3,7},{4,20},{5,1},{6,22},{7,3},{8,24},{9,13},... | collective-permute-start | bytes 589832 | tf_op jit(solution)/shard_map/ppermute | solution.py:446
  67.3 1.8 %collective-permute-done.8.h2 = bf16[4,2,48,256]{3,2,1,0:T(8,128)(2,1)S(1)} collective-permute-done((bf16[4,2,48,256]{3,2,1,0:T(8,128)(2,1)S(1)}, bf16[4,2,48,256]{3,2,1,0:T(8,128)(2,1)S(1)}, u32[]{:S(2)}, u32[]{:S(2)}) %collective-permute-start.8) | collective-permute-done | bytes 196640 | tf_op jit(solution)/shard_map/ppermute | solution.py:446
  69.1 2.9 %collective-permute-done.9.h3 = bf16[4,2,48,256]{3,2,1,0:T(8,128)(2,1)S(1)} collective-permute-done((bf16[4,2,48,256]{3,2,1,0:T(8,128)(2,1)S(1)}, bf16[4,2,48,256]{3,2,1,0:T(8,128)(2,1)S(1)}, u32[]{:S(2)}, u32[]{:S(2)}) %collective-permute-start.9) | collective-permute-done | bytes 196640 | tf_op jit(solution)/shard_map/ppermute | solution.py:446
  72.0 3.0 %project.1 = (f32[2,48,2048]{2,1,0:T(8,128)S(1)}, bf16[2,48,2048]{2,1,0:T(8,128)(2,1)S(1)}, bf16[2,48,2048]{2,1,0:T(8,128)(2,1)S(1)}, bf16[2,48,2048]{2,1,0:T(8,128)(2,1)S(1)}) custom-call(s32[6]{0:T(128)S(1)} %copy-done.3, bf16[4,2,48,256]{3,2,1,0:T(8,128)(2,1)S(1)} %get-tuple-element.43.h0, bf16[4,2,48,256]{3,2,1,0:T(8,128)(2,1)S(1)} %collective-permute-done.7.h1, ...), custom_call_target="tpu_custom_call" | custom-call | flops 1610612736 | bytes 8388608 | tf_op jit(solution)/shard_map/project/pallas_call | solution.py:178
  75.1 4.5 %collective-permute-start.13 = (bf16[2,48,2048]{2,1,0:T(8,128)(2,1)S(1)}, bf16[2,48,2048]{2,1,0:T(8,128)(2,1)S(1)}, u32[]{:S(2)}, u32[]{:S(2)}) collective-permute-start(bf16[2,48,2048]{2,1,0:T(8,128)(2,1)S(1)} %get-tuple-element.53), channel_id=1, source_target_pairs={{0,6},{1,25},{2,4},{3,27},{4,2},{5,29},{6,0},{7,31},{8,14},{9,17},... | collective-permute-start | bytes 1179656 | tf_op jit(solution)/shard_map/ppermute | solution.py:446
  79.6 1.9 %collective-permute-start.14 = (bf16[2,48,2048]{2,1,0:T(8,128)(2,1)S(1)}, bf16[2,48,2048]{2,1,0:T(8,128)(2,1)S(1)}, u32[]{:S(2)}, u32[]{:S(2)}) collective-permute-start(bf16[2,48,2048]{2,1,0:T(8,128)(2,1)S(1)} %get-tuple-element.54), channel_id=1, source_target_pairs={{0,2},{1,9},{2,0},{3,11},{4,6},{5,13},{6,4},{7,15},{8,10},{9,1},{1... | collective-permute-start | bytes 1179656 | tf_op jit(solution)/shard_map/ppermute | solution.py:446
  81.5 4.0 %collective-permute-start.15 = (bf16[2,48,2048]{2,1,0:T(8,128)(2,1)S(1)}, bf16[2,48,2048]{2,1,0:T(8,128)(2,1)S(1)}, u32[]{:S(2)}, u32[]{:S(2)}) collective-permute-start(bf16[2,48,2048]{2,1,0:T(8,128)(2,1)S(1)} %get-tuple-element.55), channel_id=1, source_target_pairs={{0,4},{1,17},{2,6},{3,19},{4,0},{5,21},{6,2},{7,23},{8,12},{9,25},... | collective-permute-start | bytes 1179656 | tf_op jit(solution)/shard_map/ppermute | solution.py:446
  86.0 3.3 %collective-permute-done.14.b_ref = bf16[2,48,2048]{2,1,0:T(8,128)(2,1)S(1)} collective-permute-done((bf16[2,48,2048]{2,1,0:T(8,128)(2,1)S(1)}, bf16[2,48,2048]{2,1,0:T(8,128)(2,1)S(1)}, u32[]{:S(2)}, u32[]{:S(2)}) %collective-permute-start.14) | collective-permute-done | bytes 393248 | tf_op jit(solution)/shard_map/ppermute | solution.py:446
  89.3 4.3 %collective-permute-done.15.c_ref = bf16[2,48,2048]{2,1,0:T(8,128)(2,1)S(1)} collective-permute-done((bf16[2,48,2048]{2,1,0:T(8,128)(2,1)S(1)}, bf16[2,48,2048]{2,1,0:T(8,128)(2,1)S(1)}, u32[]{:S(2)}, u32[]{:S(2)}) %collective-permute-start.15) | collective-permute-done | bytes 393248 | tf_op jit(solution)/shard_map/ppermute | solution.py:446
  94.3 4.6 %collective-permute-start.16 = (bf16[48,2048]{1,0:T(8,128)(2,1)S(1)}, bf16[48,2048]{1,0:T(8,128)(2,1)S(1)}, u32[]{:S(2)}, u32[]{:S(2)}) collective-permute-start(bf16[48,2048]{1,0:T(8,128)(2,1)S(1)} %get-tuple-element.57), channel_id=1, source_target_pairs={{0,24},{1,7},{2,26},{3,5},{4,28},{5,3},{6,30},{7,1},{8,16},{9,15},... | collective-permute-start | bytes 589832 | tf_op jit(solution)/shard_map/ppermute | solution.py:446
  100.4 2.8 %decode.1 = bf16[16,2,128,384]{3,2,1,0:T(8,128)(2,1)} custom-call(s32[6]{0:T(128)S(1)} %copy-done.4, bf16[16,6,16,128]{3,2,1,0:T(8,128)(2,1)S(1)} %pad_maximum_fusion.clip_ref, bf16[384,512]{1,0:T(8,128)(2,1)S(1)} %pad.4.w1_ref, bf16[4,384,3456]{2,1,0:T(8,128)(2,1)} %filter_weights.1.f_ref, f32[3,384,128]{2,1,0:T(8,128)S(1)} %broadcast_in_dim.21.vec_ref), custom_call_target="tpu_custom_call" | custom-call | tf_op jit(solution)/shard_map/decode/pallas_call | solution.py:373
  (50 shorter events, 9.5 us)
Async XLA Ops:
  0.6 13.6 %copy-start = (bf16[128,4096]{1,0:T(8,128)(2,1)S(1)}, bf16[128,4096]{1,0:T(8,128)(2,1)}, u32[]{:S(2)}) copy-start(bf16[128,4096]{1,0:T(8,128)(2,1)} %here_ref.1) | copy-start | bytes 3145732
  0.6 5.6 %collective-permute-start = (bf16[128,4096]{1,0:T(8,128)(2,1)}, bf16[128,4096]{1,0:T(8,128)(2,1)S(1)}, u32[]{:S(2)}, u32[]{:S(2)}) collective-permute-start(bf16[128,4096]{1,0:T(8,128)(2,1)} %here_ref.1), channel_id=1, source_target_pairs={{0,1},{1,0},{2,3},{3,2},{4,5},{5,4},{6,7},{7,6},{8,9},{9,8},{10,11... | collective-permute-start | bytes 3145736 | tf_op jit(solution)/shard_map/ppermute | solution.py:446
  2.7 21.4 %copy-start.6 = (bf16[4,2,128,16]{2,3,1,0:T(8,128)(2,1)S(1)}, bf16[4,2,128,16]{2,3,1,0:T(8,128)(2,1)}, u32[]{:S(2)}) copy-start(bf16[4,2,128,16]{2,3,1,0:T(8,128)(2,1)} %param.22) | copy-start | bytes 98308
  6.2 36.6 %all-to-all-start = ((bf16[16,3,48,256]{3,2,1,0:T(8,128)(2,1)}), bf16[16,3,48,256]{3,2,1,0:T(8,128)(2,1)S(1)}, u32[]{:S(2)}, u32[]{:S(2)}) async-start(bf16[16,3,48,256]{3,2,1,0:T(8,128)(2,1)} %norm_pack.1), calls=%async_computation | async-start | bytes 2359296 | tf_op jit(solution)/shard_map/all_to_all | solution.py:453
  16.4 24.6 %collective-permute-start.1 = (bf16[256,2048]{1,0:T(8,128)(2,1)}, bf16[256,2048]{1,0:T(8,128)(2,1)S(1)}, u32[]{:S(2)}, u32[]{:S(2)}) collective-permute-start(bf16[256,2048]{1,0:T(8,128)(2,1)} %get-tuple-element.35.w0), channel_id=1, source_target_pairs={{0,8},{1,3},{2,10},{3,1},{4,12},{5,7},{6,14},{7,5},{8,0},{9,11},{1... | collective-permute-start | bytes 3145736 | tf_op jit(solution)/shard_map/ppermute | solution.py:446
  20.2 22.6 %collective-permute-start.2 = (bf16[256,2048]{1,0:T(8,128)(2,1)}, bf16[256,2048]{1,0:T(8,128)(2,1)S(1)}, u32[]{:S(2)}, u32[]{:S(2)}) collective-permute-start(bf16[256,2048]{1,0:T(8,128)(2,1)} %get-tuple-element.36), channel_id=1, source_target_pairs={{0,24},{1,7},{2,26},{3,5},{4,28},{5,3},{6,30},{7,1},{8,16},{9,15},... | collective-permute-start | bytes 3145736 | tf_op jit(solution)/shard_map/ppermute | solution.py:446
  24.2 3.3 %collective-permute-start.3 = (bf16[4,2,16,128]{3,2,1,0:T(8,128)(2,1)S(1)}, bf16[4,2,16,128]{3,2,1,0:T(8,128)(2,1)S(1)}, u32[]{:S(2)}, u32[]{:S(2)}) collective-permute-start(bf16[4,2,16,128]{3,2,1,0:T(8,128)(2,1)S(1)} %bitcast.26), channel_id=1, source_target_pairs={{0,96},{1,97},{2,98},{3,99},{4,100},{5,101},{6,102},{7,103},{8,104... | collective-permute-start | bytes 98312 | tf_op jit(solution)/shard_map/ppermute | solution.py:459
  25.5 2.0 %collective-permute-start.4 = (bf16[4,2,16,128]{3,2,1,0:T(8,128)(2,1)S(1)}, bf16[4,2,16,128]{3,2,1,0:T(8,128)(2,1)S(1)}, u32[]{:S(2)}, u32[]{:S(2)}) collective-permute-start(bf16[4,2,16,128]{3,2,1,0:T(8,128)(2,1)S(1)} %bitcast.27), channel_id=1, source_target_pairs={{32,96},{33,97},{34,98},{35,99},{36,100},{37,101},{38,102},{39,103... | collective-permute-start | bytes 98312 | tf_op jit(solution)/shard_map/ppermute | solution.py:459
  26.1 1.4 %collective-permute-start.5 = (bf16[4,2,16,128]{3,2,1,0:T(8,128)(2,1)S(1)}, bf16[4,2,16,128]{3,2,1,0:T(8,128)(2,1)S(1)}, u32[]{:S(2)}, u32[]{:S(2)}) collective-permute-start(bf16[4,2,16,128]{3,2,1,0:T(8,128)(2,1)S(1)} %bitcast.28), channel_id=1, source_target_pairs={{64,96},{65,97},{66,98},{67,99},{68,100},{69,101},{70,102},{71,103... | collective-permute-start | bytes 98312 | tf_op jit(solution)/shard_map/ppermute | solution.py:459
  42.8 7.5 %collective-permute-start.6 = (bf16[16,3,48,256]{3,2,1,0:T(8,128)(2,1)S(1)}, bf16[16,3,48,256]{3,2,1,0:T(8,128)(2,1)S(1)}, u32[]{:S(2)}, u32[]{:S(2)}) collective-permute-start(bf16[16,3,48,256]{3,2,1,0:T(8,128)(2,1)S(1)} %all-to-all-done.here_ref), channel_id=1, source_target_pairs={{0,1},{1,0},{2,3},{3,2},{4,5},{5,4},{6,7},{7,6},{8,9},{9,8},{10,11... | collective-permute-start | bytes 3538952 | tf_op jit(solution)/shard_map/ppermute | solution.py:446
  44.7 22.6 %collective-permute-start.10 = (bf16[256,2048]{1,0:T(8,128)(2,1)}, bf16[256,2048]{1,0:T(8,128)(2,1)S(1)}, u32[]{:S(2)}, u32[]{:S(2)}) collective-permute-start(bf16[256,2048]{1,0:T(8,128)(2,1)} %get-tuple-element.36), channel_id=1, source_target_pairs={{0,16},{1,5},{2,18},{3,7},{4,20},{5,1},{6,22},{7,3},{8,24},{9,13},... | collective-permute-start | bytes 3145736 | tf_op jit(solution)/shard_map/ppermute | solution.py:446
  48.9 14.1 %collective-permute-start.12 = (bf16[16,2,16,128]{3,2,1,0:T(8,128)(2,1)S(1)}, bf16[16,2,16,128]{3,2,1,0:T(8,128)(2,1)S(1)}, u32[]{:S(2)}, u32[]{:S(2)}) collective-permute-start(bf16[16,2,16,128]{3,2,1,0:T(8,128)(2,1)S(1)} %pad_maximum_fusion.1), channel_id=1, source_target_pairs={{97,96},{98,97},{99,98},{100,99},{101,100},{102,101},{103,102},{10... | collective-permute-start | bytes 393224 | tf_op jit(solution)/shard_map/ppermute | solution.py:469
  49.6 17.6 %collective-permute-start.11 = (bf16[16,2,16,128]{3,2,1,0:T(8,128)(2,1)S(1)}, bf16[16,2,16,128]{3,2,1,0:T(8,128)(2,1)S(1)}, u32[]{:S(2)}, u32[]{:S(2)}) collective-permute-start(bf16[16,2,16,128]{3,2,1,0:T(8,128)(2,1)S(1)} %pad_maximum_fusion.1), channel_id=1, source_target_pairs={{96,97},{97,98},{98,99},{99,100},{100,101},{101,102},{102,103},{10... | collective-permute-start | bytes 393224 | tf_op jit(solution)/shard_map/ppermute | solution.py:467
  57.3 10.0 %collective-permute-start.7 = (bf16[4,2,48,256]{3,2,1,0:T(8,128)(2,1)S(1)}, bf16[4,2,48,256]{3,2,1,0:T(8,128)(2,1)S(1)}, u32[]{:S(2)}, u32[]{:S(2)}) collective-permute-start(bf16[4,2,48,256]{3,2,1,0:T(8,128)(2,1)S(1)} %get-tuple-element.44), channel_id=1, source_target_pairs={{0,8},{1,3},{2,10},{3,1},{4,12},{5,7},{6,14},{7,5},{8,0},{9,11},{1... | collective-permute-start | bytes 589832 | tf_op jit(solution)/shard_map/ppermute | solution.py:446
  60.3 8.8 %collective-permute-start.8 = (bf16[4,2,48,256]{3,2,1,0:T(8,128)(2,1)S(1)}, bf16[4,2,48,256]{3,2,1,0:T(8,128)(2,1)S(1)}, u32[]{:S(2)}, u32[]{:S(2)}) collective-permute-start(bf16[4,2,48,256]{3,2,1,0:T(8,128)(2,1)S(1)} %get-tuple-element.43.h0), channel_id=1, source_target_pairs={{0,24},{1,7},{2,26},{3,5},{4,28},{5,3},{6,30},{7,1},{8,16},{9,15},... | collective-permute-start | bytes 589832 | tf_op jit(solution)/shard_map/ppermute | solution.py:446
  63.0 9.1 %collective-permute-start.9 = (bf16[4,2,48,256]{3,2,1,0:T(8,128)(2,1)S(1)}, bf16[4,2,48,256]{3,2,1,0:T(8,128)(2,1)S(1)}, u32[]{:S(2)}, u32[]{:S(2)}) collective-permute-start(bf16[4,2,48,256]{3,2,1,0:T(8,128)(2,1)S(1)} %get-tuple-element.44), channel_id=1, source_target_pairs={{0,16},{1,5},{2,18},{3,7},{4,20},{5,1},{6,22},{7,3},{8,24},{9,13},... | collective-permute-start | bytes 589832 | tf_op jit(solution)/shard_map/ppermute | solution.py:446
  67.2 32.8 %copy-start.7 = (f32[384]{0:T(512)S(1)}, f32[384]{0:T(512)}, u32[]{:S(2)}) copy-start(f32[384]{0:T(512)} %param.27) | copy-start | bytes 4612
  67.3 32.8 %copy-start.8 = (f32[384]{0:T(512)S(1)}, f32[384]{0:T(512)}, u32[]{:S(2)}) copy-start(f32[384]{0:T(512)} %param.25) | copy-start | bytes 4612
  67.3 32.8 %copy-start.9 = (f32[384]{0:T(512)S(1)}, f32[384]{0:T(512)}, u32[]{:S(2)}) copy-start(f32[384]{0:T(512)} %param.24) | copy-start | bytes 4612
  75.1 25.3 %copy-start.4 = (s32[6]{0:T(128)S(1)}, s32[6]{0:T(128)}, u32[]{:S(2)}) copy-start(s32[6]{0:T(128)} %copy-done.2) | copy-start | bytes 76
  75.1 10.9 %collective-permute-start.13 = (bf16[2,48,2048]{2,1,0:T(8,128)(2,1)S(1)}, bf16[2,48,2048]{2,1,0:T(8,128)(2,1)S(1)}, u32[]{:S(2)}, u32[]{:S(2)}) collective-permute-start(bf16[2,48,2048]{2,1,0:T(8,128)(2,1)S(1)} %get-tuple-element.53), channel_id=1, source_target_pairs={{0,6},{1,25},{2,4},{3,27},{4,2},{5,29},{6,0},{7,31},{8,14},{9,17},... | collective-permute-start | bytes 1179656 | tf_op jit(solution)/shard_map/ppermute | solution.py:446
  79.6 9.7 %collective-permute-start.14 = (bf16[2,48,2048]{2,1,0:T(8,128)(2,1)S(1)}, bf16[2,48,2048]{2,1,0:T(8,128)(2,1)S(1)}, u32[]{:S(2)}, u32[]{:S(2)}) collective-permute-start(bf16[2,48,2048]{2,1,0:T(8,128)(2,1)S(1)} %get-tuple-element.54), channel_id=1, source_target_pairs={{0,2},{1,9},{2,0},{3,11},{4,6},{5,13},{6,4},{7,15},{8,10},{9,1},{1... | collective-permute-start | bytes 1179656 | tf_op jit(solution)/shard_map/ppermute | solution.py:446
  81.5 12.0 %collective-permute-start.15 = (bf16[2,48,2048]{2,1,0:T(8,128)(2,1)S(1)}, bf16[2,48,2048]{2,1,0:T(8,128)(2,1)S(1)}, u32[]{:S(2)}, u32[]{:S(2)}) collective-permute-start(bf16[2,48,2048]{2,1,0:T(8,128)(2,1)S(1)} %get-tuple-element.55), channel_id=1, source_target_pairs={{0,4},{1,17},{2,6},{3,19},{4,0},{5,21},{6,2},{7,23},{8,12},{9,25},... | collective-permute-start | bytes 1179656 | tf_op jit(solution)/shard_map/ppermute | solution.py:446
  94.3 9.0 %collective-permute-start.16 = (bf16[48,2048]{1,0:T(8,128)(2,1)S(1)}, bf16[48,2048]{1,0:T(8,128)(2,1)S(1)}, u32[]{:S(2)}, u32[]{:S(2)}) collective-permute-start(bf16[48,2048]{1,0:T(8,128)(2,1)S(1)} %get-tuple-element.57), channel_id=1, source_target_pairs={{0,24},{1,7},{2,26},{3,5},{4,28},{5,3},{6,30},{7,1},{8,16},{9,15},... | collective-permute-start | bytes 589832 | tf_op jit(solution)/shard_map/ppermute | solution.py:446
  (4 other events, 18.9 us)

commit v3 on v2

--- a/solution.py
+++ b/solution.py
@@ -86,34 +86,33 @@
 def attend(place, here, there):
     chips, _, tok, _ = here.shape
     half = chips * tok
-    keys = 2 * half
-
-    def body(place_ref, here_ref, there_ref, near_ref, other_ref, k_buf, v_buf):
+
+    def body(place_ref, here_ref, there_ref, near_ref, other_ref):
         step = pl.program_id(0)
 
-        @pl.when((step == 0) & (place_ref[0] == 0))
-        def _():
+        @pl.when(place_ref[0] == 0)
+        def _():
+            queries = here_ref[pl.ds(4 * step, 4), 0].reshape(4 * tok, 256)
+            ones = jnp.ones((half, 128), jnp.bfloat16)
+            heads = []
             for h in range(2):
                 cols = slice(128 * h, 128 * h + 128)
-                for n, ref in enumerate((here_ref, there_ref)):
-                    span = slice(n * half, n * half + half)
-                    k_buf[h, span] = ref[:, 1, :, cols].reshape(half, 128)
-                    v_buf[h, span, :128] = ref[:, 2, :, cols].reshape(half, 128)
-                v_buf[h, :, 128:] = jnp.ones((keys, 128), jnp.bfloat16)
-
-        @pl.when(place_ref[0] == 0)
-        def _():
-            queries = here_ref[pl.ds(4 * step, 4), 0].reshape(4 * tok, 256)
-            heads = []
-            for h in range(2):
-                s = lax.dot_general(
-                    queries[:, 128 * h : 128 * h + 128],
-                    k_buf[h],
-                    (((1,), (1,)), ((), ())),
-                    preferred_element_type=jnp.float32,
-                )
-                p = jnp.exp2(s - jnp.max(s, axis=-1, keepdims=True)).astype(jnp.bfloat16)
-                o = jnp.dot(p, v_buf[h], preferred_element_type=jnp.float32)
+                scores = [
+                    lax.dot_general(
+                        queries[:, cols],
+                        ref[:, 1, :, cols].reshape(half, 128),
+                        (((1,), (1,)), ((), ())),
+                        preferred_element_type=jnp.float32,
+                    )
+                    for ref in (here_ref, there_ref)
+                ]
+                peak = jnp.maximum(*(jnp.max(s, axis=-1, keepdims=True) for s in scores))
+                o = None
+                for s, ref in zip(scores, (here_ref, there_ref)):
+                    values = jnp.concatenate([ref[:, 2, :, cols].reshape(half, 128), ones], axis=1)
+                    p = jnp.exp2(s - peak).astype(jnp.bfloat16)
+                    part = jnp.dot(p, values, preferred_element_type=jnp.float32)
+                    o = part if o is None else o + part
                 heads.append(o[:, :128] / o[:, 128:])
             joined = jnp.concatenate(heads, axis=1).astype(jnp.bfloat16)
             for n in range(4):
@@ -138,10 +137,6 @@
         out_shape=(jax.ShapeDtypeStruct((4, 2, tok, 256), jnp.bfloat16),) * 2,
         in_specs=[smem_spec(), vmem_spec(), vmem_spec()],
         out_specs=(vmem_spec(),) * 2,
-        scratch_shapes=[
-            pltpu.VMEM((2, keys, 128), jnp.bfloat16),
-            pltpu.VMEM((2, keys, 256), jnp.bfloat16),
-        ],
         compiler_params=pltpu.CompilerParams(vmem_limit_bytes=40 * MIB),
         cost_estimate=pl.CostEstimate(flops=0, bytes_accessed=0, transcendentals=0),
         name="attend",
@@ -449,18 +444,16 @@
     packed = norm_pack(
         query_input[0], key_input[0], value_input[0], query_norm_gain[None], key_norm_gain[None]
     )
-    packed, w_there = lax.optimization_barrier((packed, w_there))
+    packed, latents, w_mid = lax.optimization_barrier((packed, latents, w_mid))
     here = lax.all_to_all(packed, CHIPS, split_axis=0, concat_axis=0, tiled=True)
-    w_own, w_give = weight_halves(place, output_weight, w_there)
-    w_own, w_give, latents, w_mid = lax.optimization_barrier((w_own, w_give, latents, w_mid))
-    w_next, w_back, w_far = swap(w_own, 0, 0), swap(w_give, 0, 1), swap(w_give, 0, 2)
 
     own = jnp.swapaxes(latents, 2, 3)
     pieces = [lax.ppermute(own, "grp", [(g, last)]) for g in range(last)]
     filters = filter_weights(place, w_mid)
-    pieces, filters = lax.optimization_barrier((pieces, filters))
+    pieces, filters, w_there = lax.optimization_barrier((pieces, filters, w_there))
+    w_own, w_give = weight_halves(place, output_weight, w_there)
+    w_next, w_back = swap(w_own, 0, 0), swap(w_give, 0, 1)
     clip = jnp.concatenate(pieces + [own], axis=0)
-    here, w_next, w_back, clip = lax.optimization_barrier((here, w_next, w_back, clip))
     links = [(last * count + i, last * count + i + 1) for i in range(count - 1)]
     cells = jnp.concatenate(
         [
@@ -474,13 +467,18 @@
     vectors = jnp.broadcast_to(
         jnp.stack([b_in, norm_gain, b_mid])[:, :, None], (3, channels, latents.shape[2])
     )
+    here, cells, w_back = lax.optimization_barrier((here, cells, w_back))
     there = swap(here, 2, 0)
+    w_far = swap(w_back, 0, 0)
     near, other = attend(place, here, there)
-    heads = near, swap(other, 0, 0), swap(near, 0, 1), swap(other, 0, 2)
+    from_far = swap(other, 0, 2)
+    heads = near, swap(other, 0, 0), swap(near, 0, 1), from_far
     mine, one, zero, far = project(place, heads, (w_own, w_next, w_back, w_far))
     mine, one, zero, far, cells = lax.optimization_barrier((mine, one, zero, far, cells))
+    sums = swap(far, 1, 2), swap(one, 1, 1), swap(zero, 1, 0)
     decoded = decode(place, cells, w_first, filters, vectors)
-    kept, give = add_up(place, mine, (swap(one, 1, 1), swap(zero, 1, 0), swap(far, 1, 2)))
+    mine, decoded = lax.optimization_barrier((mine, decoded))
+    kept, give = add_up(place, mine, sums)
     attn_out = finish(place, resid[0], gate, kept, swap(give, 0, 1))
     return attn_out[None], decoded[None]
 

time: 105 us -> 111 us (1.057)
  waiting for transfers between devices: 28 us -> 32.9 us
    all_to_all x1, waiting for transfers between devices: 0.01 us -> 4.6 us  [on_device(): lax.all_to_all(packed, CHIPS, split_axis=0, concat_axis=0, tiled=True)]
    ppermute x3, starting transfers between devices: 2.62 us -> 5.05 us  [on_device(): pieces = [lax.ppermute(own, 'grp', [(g, last)]) for g in range(last)]]
    ppermute x12, starting transfers between devices: 40.8 us -> 38.4 us  [swap(): return lax.ppermute(x, ('grp',) + SEQ, pairs)]
  transfers between devices with their start and end apart: 18 -> 18, of which waited for: 7 -> 8; matrix products, arithmetic and copies ran while one was open for 1% -> 1% of each run, Pallas kernels for 15% -> 14%
where the time goes in v3:
time: 111 us; the launch traced here: 110 us
  starting transfers between devices  52.8 us (48%)
  waiting for transfers between devices  32.9 us (30%)
  Pallas kernels  21 us (19%)
  local copies, waits for them, and re-layouts  2.43 us (2%)
    ppermute x12, starting transfers between devices, swap(): return lax.ppermute(x, ('grp',) + SEQ, pairs)  38.4 us
    ppermute x12, waiting for transfers between devices, swap(): return lax.ppermute(x, ('grp',) + SEQ, pairs)  28.3 us
    all_to_all x1, starting transfers between devices, on_device(): lax.all_to_all(packed, CHIPS, split_axis=0, concat_axis=0, tiled=True)  7.96 us
    pallas_call x1, Pallas kernels, attend(): pl.pallas_call(body, grid=(chips // 4,), out_shape=(jax.ShapeDtypeStruct(...  6.15 us
    ppermute x3, starting transfers between devices, on_device(): pieces = [lax.ppermute(own, 'grp', [(g, last)]) for g in range(last)]  5.05 us
    all_to_all x1, waiting for transfers between devices, on_device(): lax.all_to_all(packed, CHIPS, split_axis=0, concat_axis=0, tiled=True)  4.6 us
    pallas_call x1, Pallas kernels, project(): pl.pallas_call(body, out_shape=(jax.ShapeDtypeStruct(shape, jnp.float32),...  3.92 us
    pallas_call x1, Pallas kernels, norm_pack(): pl.pallas_call(body, grid=(rows // block,), out_shape=jax.ShapeDtypeStruc...  3.48 us
  transfers between devices with their start and end apart: 18, of which 8 were waited for; matrix products, arithmetic and copies ran while one was open for 1% of the time, Pallas kernels for 14%

profile of v3, /device:TPU:0, one launch (start us, length us, event | category | flops | bytes accessed | tf_op | source)
XLA Modules:
  0.0 110.3 jit_solution(17642692693211099889)
XLA Ops:
  0.6 1.9 %collective-permute-start.3 = (bf16[128,4096]{1,0:T(8,128)(2,1)}, bf16[128,4096]{1,0:T(8,128)(2,1)S(1)}, u32[]{:S(2)}, u32[]{:S(2)}) collective-permute-start(bf16[128,4096]{1,0:T(8,128)(2,1)} %here_ref.1), channel_id=1, source_target_pairs={{0,1},{1,0},{2,3},{3,2},{4,5},{5,4},{6,7},{7,6},{8,9},{9,8},{10,11... | collective-permute-start | bytes 3145736 | tf_op jit(solution)/shard_map/ppermute | solution.py:441
  2.6 3.5 %norm_pack.1 = bf16[16,3,48,256]{3,2,1,0:T(8,128)(2,1)} custom-call(bf16[48,4096]{1,0:T(8,128)(2,1)} %bitcast.21, bf16[48,4096]{1,0:T(8,128)(2,1)} %bitcast.22, bf16[48,4096]{1,0:T(8,128)(2,1)} %bitcast.23, f32[1,4096]{1,0:T(1,128)} %bitcast.31, f32[1,4096]{1,0:T(1,128)} %bitcast.32), custom_call_target="tpu_custom_call" | custom-call | tf_op jit(solution)/shard_map/norm_pack/pallas_call | solution.py:45
  6.1 8.0 %all-to-all-start = ((bf16[16,3,48,256]{3,2,1,0:T(8,128)(2,1)}), bf16[16,3,48,256]{3,2,1,0:T(8,128)(2,1)S(1)}, u32[]{:S(2)}, u32[]{:S(2)}) async-start(bf16[16,3,48,256]{3,2,1,0:T(8,128)(2,1)} %norm_pack.1), calls=%async_computation | async-start | bytes 2359296 | tf_op jit(solution)/shard_map/all_to_all | solution.py:448
  14.0 3.7 %collective-permute-start = (bf16[4,2,16,128]{3,2,1,0:T(8,128)(2,1)S(1)}, bf16[4,2,16,128]{3,2,1,0:T(8,128)(2,1)S(1)}, u32[]{:S(2)}, u32[]{:S(2)}) collective-permute-start(bf16[4,2,16,128]{3,2,1,0:T(8,128)(2,1)S(1)} %bitcast.26), channel_id=1, source_target_pairs={{0,96},{1,97},{2,98},{3,99},{4,100},{5,101},{6,102},{7,103},{8,104... | collective-permute-start | bytes 98312 | tf_op jit(solution)/shard_map/ppermute | solution.py:451
  23.6 5.2 %collective-permute-start.6 = (bf16[256,2048]{1,0:T(8,128)(2,1)}, bf16[256,2048]{1,0:T(8,128)(2,1)}, u32[]{:S(2)}, u32[]{:S(2)}) collective-permute-start(bf16[256,2048]{1,0:T(8,128)(2,1)} %get-tuple-element.37), channel_id=1, source_target_pairs={{0,24},{1,7},{2,26},{3,5},{4,28},{5,3},{6,30},{7,1},{8,16},{9,15},... | collective-permute-start | bytes 3145736 | tf_op jit(solution)/shard_map/ppermute | solution.py:441
  30.3 4.6 %all-to-all-done.here_ref = bf16[16,3,48,256]{3,2,1,0:T(8,128)(2,1)S(1)} async-done(((bf16[16,3,48,256]{3,2,1,0:T(8,128)(2,1)}), bf16[16,3,48,256]{3,2,1,0:T(8,128)(2,1)S(1)}, u32[]{:S(2)}, u32[]{:S(2)}) %all-to-all-start) | async-done | bytes 1179680 | tf_op jit(solution)/shard_map/all_to_all | solution.py:448
  34.9 8.7 %collective-permute-done.6.w2 = bf16[256,2048]{1,0:T(8,128)(2,1)} collective-permute-done((bf16[256,2048]{1,0:T(8,128)(2,1)}, bf16[256,2048]{1,0:T(8,128)(2,1)}, u32[]{:S(2)}, u32[]{:S(2)}) %collective-permute-start.6) | collective-permute-done | bytes 1048608 | tf_op jit(solution)/shard_map/ppermute | solution.py:441
  45.5 2.3 %collective-permute-start.11 = (bf16[256,2048]{1,0:T(8,128)(2,1)}, bf16[256,2048]{1,0:T(8,128)(2,1)S(1)}, u32[]{:S(2)}, u32[]{:S(2)}) collective-permute-start(bf16[256,2048]{1,0:T(8,128)(2,1)} %copy-done.4), channel_id=1, source_target_pairs={{0,8},{1,3},{2,10},{3,1},{4,12},{5,7},{6,14},{7,5},{8,0},{9,11},{1... | collective-permute-start | bytes 3145736 | tf_op jit(solution)/shard_map/ppermute | solution.py:441
  47.8 3.5 %collective-permute-start.12 = (bf16[256,2048]{1,0:T(8,128)(2,1)}, bf16[256,2048]{1,0:T(8,128)(2,1)S(1)}, u32[]{:S(2)}, u32[]{:S(2)}) collective-permute-start(bf16[256,2048]{1,0:T(8,128)(2,1)} %collective-permute-done.6.w2), channel_id=1, source_target_pairs={{0,8},{1,3},{2,10},{3,1},{4,12},{5,7},{6,14},{7,5},{8,0},{9,11},{1... | collective-permute-start | bytes 3145736 | tf_op jit(solution)/shard_map/ppermute | solution.py:441
  51.3 6.1 %attend.1 = (bf16[4,2,48,256]{3,2,1,0:T(8,128)(2,1)S(1)}, bf16[4,2,48,256]{3,2,1,0:T(8,128)(2,1)S(1)}) custom-call(s32[6]{0:T(128)S(1)} %copy-done.2, bf16[16,3,48,256]{3,2,1,0:T(8,128)(2,1)S(1)} %all-to-all-done.here_ref, bf16[16,3,48,256]{3,2,1,0:T(8,128)(2,1)S(1)} %collective-permute-done.7.there_ref), custom_call_target="tpu_custom_call" | custom-call | tf_op jit(solution)/shard_map/attend/pallas_call | solution.py:134
  57.5 4.2 %collective-permute-start.10 = (bf16[4,2,48,256]{3,2,1,0:T(8,128)(2,1)S(1)}, bf16[4,2,48,256]{3,2,1,0:T(8,128)(2,1)S(1)}, u32[]{:S(2)}, u32[]{:S(2)}) collective-permute-start(bf16[4,2,48,256]{3,2,1,0:T(8,128)(2,1)S(1)} %get-tuple-element.40), channel_id=1, source_target_pairs={{0,16},{1,5},{2,18},{3,7},{4,20},{5,1},{6,22},{7,3},{8,24},{9,13},... | collective-permute-start | bytes 589832 | tf_op jit(solution)/shard_map/ppermute | solution.py:441
  61.7 2.3 %collective-permute-start.8 = (bf16[4,2,48,256]{3,2,1,0:T(8,128)(2,1)S(1)}, bf16[4,2,48,256]{3,2,1,0:T(8,128)(2,1)S(1)}, u32[]{:S(2)}, u32[]{:S(2)}) collective-permute-start(bf16[4,2,48,256]{3,2,1,0:T(8,128)(2,1)S(1)} %get-tuple-element.40), channel_id=1, source_target_pairs={{0,8},{1,3},{2,10},{3,1},{4,12},{5,7},{6,14},{7,5},{8,0},{9,11},{1... | collective-permute-start | bytes 589832 | tf_op jit(solution)/shard_map/ppermute | solution.py:441
  64.0 3.6 %collective-permute-start.9 = (bf16[4,2,48,256]{3,2,1,0:T(8,128)(2,1)S(1)}, bf16[4,2,48,256]{3,2,1,0:T(8,128)(2,1)S(1)}, u32[]{:S(2)}, u32[]{:S(2)}) collective-permute-start(bf16[4,2,48,256]{3,2,1,0:T(8,128)(2,1)S(1)} %get-tuple-element.39.h0), channel_id=1, source_target_pairs={{0,24},{1,7},{2,26},{3,5},{4,28},{5,3},{6,30},{7,1},{8,16},{9,15},... | collective-permute-start | bytes 589832 | tf_op jit(solution)/shard_map/ppermute | solution.py:441
  67.7 5.9 %collective-permute-done.12.w3 = bf16[256,2048]{1,0:T(8,128)(2,1)S(1)} collective-permute-done((bf16[256,2048]{1,0:T(8,128)(2,1)}, bf16[256,2048]{1,0:T(8,128)(2,1)S(1)}, u32[]{:S(2)}, u32[]{:S(2)}) %collective-permute-start.12) | collective-permute-done | bytes 1048608 | tf_op jit(solution)/shard_map/ppermute | solution.py:441
  73.6 3.2 %collective-permute-done.10.h3 = bf16[4,2,48,256]{3,2,1,0:T(8,128)(2,1)S(1)} collective-permute-done((bf16[4,2,48,256]{3,2,1,0:T(8,128)(2,1)S(1)}, bf16[4,2,48,256]{3,2,1,0:T(8,128)(2,1)S(1)}, u32[]{:S(2)}, u32[]{:S(2)}) %collective-permute-start.10) | collective-permute-done | bytes 196640 | tf_op jit(solution)/shard_map/ppermute | solution.py:441
  77.8 3.9 %project.1 = (f32[2,48,2048]{2,1,0:T(8,128)S(1)}, bf16[2,48,2048]{2,1,0:T(8,128)(2,1)}, bf16[2,48,2048]{2,1,0:T(8,128)(2,1)S(1)}, bf16[2,48,2048]{2,1,0:T(8,128)(2,1)}) custom-call(s32[6]{0:T(128)S(1)} %copy-done.2, bf16[4,2,48,256]{3,2,1,0:T(8,128)(2,1)S(1)} %get-tuple-element.39.h0, bf16[4,2,48,256]{3,2,1,0:T(8,128)(2,1)S(1)} %collective-permute-done.8.h1, ...), custom_call_target="tpu_custom_call" | custom-call | flops 1610612736 | bytes 8388608 | tf_op jit(solution)/shard_map/project/pallas_call | solution.py:173
  81.7 3.8 %collective-permute-start.13 = (bf16[2,48,2048]{2,1,0:T(8,128)(2,1)}, bf16[2,48,2048]{2,1,0:T(8,128)(2,1)S(1)}, u32[]{:S(2)}, u32[]{:S(2)}) collective-permute-start(bf16[2,48,2048]{2,1,0:T(8,128)(2,1)} %get-tuple-element.52), channel_id=1, source_target_pairs={{0,4},{1,17},{2,6},{3,19},{4,0},{5,21},{6,2},{7,23},{8,12},{9,25},... | collective-permute-start | bytes 1179656 | tf_op jit(solution)/shard_map/ppermute | solution.py:441
  85.6 4.0 %collective-permute-start.14 = (bf16[2,48,2048]{2,1,0:T(8,128)(2,1)}, bf16[2,48,2048]{2,1,0:T(8,128)(2,1)S(1)}, u32[]{:S(2)}, u32[]{:S(2)}) collective-permute-start(bf16[2,48,2048]{2,1,0:T(8,128)(2,1)} %get-tuple-element.53), channel_id=1, source_target_pairs={{0,6},{1,25},{2,4},{3,27},{4,2},{5,29},{6,0},{7,31},{8,14},{9,17},... | collective-permute-start | bytes 1179656 | tf_op jit(solution)/shard_map/ppermute | solution.py:441
  89.6 2.1 %collective-permute-start.15 = (bf16[2,48,2048]{2,1,0:T(8,128)(2,1)S(1)}, bf16[2,48,2048]{2,1,0:T(8,128)(2,1)S(1)}, u32[]{:S(2)}, u32[]{:S(2)}) collective-permute-start(bf16[2,48,2048]{2,1,0:T(8,128)(2,1)S(1)} %get-tuple-element.54), channel_id=1, source_target_pairs={{0,2},{1,9},{2,0},{3,11},{4,6},{5,13},{6,4},{7,15},{8,10},{9,1},{1... | collective-permute-start | bytes 1179656 | tf_op jit(solution)/shard_map/ppermute | solution.py:441
  92.3 2.8 %decode.1 = bf16[16,2,128,384]{3,2,1,0:T(8,128)(2,1)} custom-call(s32[6]{0:T(128)S(1)} %copy-done.2, bf16[16,6,16,128]{3,2,1,0:T(8,128)(2,1)S(1)} %pad_maximum_fusion.clip_ref, bf16[384,512]{1,0:T(8,128)(2,1)S(1)} %pad.4.w1_ref, bf16[4,384,3456]{2,1,0:T(8,128)(2,1)} %filter_weights.1.f_ref, f32[3,384,128]{2,1,0:T(8,128)S(1)} %broadcast_in_dim.20.vec_ref), custom_call_target="tpu_custom_call" | custom-call | tf_op jit(solution)/shard_map/decode/pallas_call | solution.py:368
  95.1 2.2 %collective-permute-done.14.b_ref = bf16[2,48,2048]{2,1,0:T(8,128)(2,1)S(1)} collective-permute-done((bf16[2,48,2048]{2,1,0:T(8,128)(2,1)}, bf16[2,48,2048]{2,1,0:T(8,128)(2,1)S(1)}, u32[]{:S(2)}, u32[]{:S(2)}) %collective-permute-start.14) | collective-permute-done | bytes 393248 | tf_op jit(solution)/shard_map/ppermute | solution.py:441
  97.3 2.0 %collective-permute-done.15.c_ref = bf16[2,48,2048]{2,1,0:T(8,128)(2,1)S(1)} collective-permute-done((bf16[2,48,2048]{2,1,0:T(8,128)(2,1)S(1)}, bf16[2,48,2048]{2,1,0:T(8,128)(2,1)S(1)}, u32[]{:S(2)}, u32[]{:S(2)}) %collective-permute-start.15) | collective-permute-done | bytes 393248 | tf_op jit(solution)/shard_map/ppermute | solution.py:441
  100.0 3.5 %collective-permute-start.16 = (bf16[48,2048]{1,0:T(8,128)(2,1)S(1)}, bf16[48,2048]{1,0:T(8,128)(2,1)S(1)}, u32[]{:S(2)}, u32[]{:S(2)}) collective-permute-start(bf16[48,2048]{1,0:T(8,128)(2,1)S(1)} %get-tuple-element.56), channel_id=1, source_target_pairs={{0,24},{1,7},{2,26},{3,5},{4,28},{5,3},{6,30},{7,1},{8,16},{9,15},... | collective-permute-start | bytes 589832 | tf_op jit(solution)/shard_map/ppermute | solution.py:441
  103.6 5.2 %collective-permute-done.16.got_ref = bf16[48,2048]{1,0:T(8,128)(2,1)S(1)} collective-permute-done((bf16[48,2048]{1,0:T(8,128)(2,1)S(1)}, bf16[48,2048]{1,0:T(8,128)(2,1)S(1)}, u32[]{:S(2)}, u32[]{:S(2)}) %collective-permute-start.16) | collective-permute-done | bytes 196640 | tf_op jit(solution)/shard_map/ppermute | solution.py:441
  (52 shorter events, 12.8 us)
Async XLA Ops:
  0.6 19.9 %collective-permute-start.3 = (bf16[128,4096]{1,0:T(8,128)(2,1)}, bf16[128,4096]{1,0:T(8,128)(2,1)S(1)}, u32[]{:S(2)}, u32[]{:S(2)}) collective-permute-start(bf16[128,4096]{1,0:T(8,128)(2,1)} %here_ref.1), channel_id=1, source_target_pairs={{0,1},{1,0},{2,3},{3,2},{4,5},{5,4},{6,7},{7,6},{8,9},{9,8},{10,11... | collective-permute-start | bytes 3145736 | tf_op jit(solution)/shard_map/ppermute | solution.py:441
  6.1 28.8 %all-to-all-start = ((bf16[16,3,48,256]{3,2,1,0:T(8,128)(2,1)}), bf16[16,3,48,256]{3,2,1,0:T(8,128)(2,1)S(1)}, u32[]{:S(2)}, u32[]{:S(2)}) async-start(bf16[16,3,48,256]{3,2,1,0:T(8,128)(2,1)} %norm_pack.1), calls=%async_computation | async-start | bytes 2359296 | tf_op jit(solution)/shard_map/all_to_all | solution.py:448
  14.0 6.5 %collective-permute-start = (bf16[4,2,16,128]{3,2,1,0:T(8,128)(2,1)S(1)}, bf16[4,2,16,128]{3,2,1,0:T(8,128)(2,1)S(1)}, u32[]{:S(2)}, u32[]{:S(2)}) collective-permute-start(bf16[4,2,16,128]{3,2,1,0:T(8,128)(2,1)S(1)} %bitcast.26), channel_id=1, source_target_pairs={{0,96},{1,97},{2,98},{3,99},{4,100},{5,101},{6,102},{7,103},{8,104... | collective-permute-start | bytes 98312 | tf_op jit(solution)/shard_map/ppermute | solution.py:451
  17.8 2.8 %collective-permute-start.1 = (bf16[4,2,16,128]{3,2,1,0:T(8,128)(2,1)S(1)}, bf16[4,2,16,128]{3,2,1,0:T(8,128)(2,1)S(1)}, u32[]{:S(2)}, u32[]{:S(2)}) collective-permute-start(bf16[4,2,16,128]{3,2,1,0:T(8,128)(2,1)S(1)} %bitcast.27), channel_id=1, source_target_pairs={{32,96},{33,97},{34,98},{35,99},{36,100},{37,101},{38,102},{39,103... | collective-permute-start | bytes 98312 | tf_op jit(solution)/shard_map/ppermute | solution.py:451
  18.4 2.1 %collective-permute-start.2 = (bf16[4,2,16,128]{3,2,1,0:T(8,128)(2,1)S(1)}, bf16[4,2,16,128]{3,2,1,0:T(8,128)(2,1)S(1)}, u32[]{:S(2)}, u32[]{:S(2)}) collective-permute-start(bf16[4,2,16,128]{3,2,1,0:T(8,128)(2,1)S(1)} %bitcast.28), channel_id=1, source_target_pairs={{64,96},{65,97},{66,98},{67,99},{68,100},{69,101},{70,102},{71,103... | collective-permute-start | bytes 98312 | tf_op jit(solution)/shard_map/ppermute | solution.py:451
  23.6 54.2 %copy-start.5 = (bf16[256,2048]{1,0:T(8,128)(2,1)S(1)}, bf16[256,2048]{1,0:T(8,128)(2,1)}, u32[]{:S(2)}) copy-start(bf16[256,2048]{1,0:T(8,128)(2,1)} %copy-done.4) | copy-start | bytes 3145732
  23.6 19.9 %collective-permute-start.6 = (bf16[256,2048]{1,0:T(8,128)(2,1)}, bf16[256,2048]{1,0:T(8,128)(2,1)}, u32[]{:S(2)}, u32[]{:S(2)}) collective-permute-start(bf16[256,2048]{1,0:T(8,128)(2,1)} %get-tuple-element.37), channel_id=1, source_target_pairs={{0,24},{1,7},{2,26},{3,5},{4,28},{5,3},{6,30},{7,1},{8,16},{9,15},... | collective-permute-start | bytes 3145736 | tf_op jit(solution)/shard_map/ppermute | solution.py:441
  28.8 1.4 %collective-permute-start.4 = (bf16[16,2,16,128]{3,2,1,0:T(8,128)(2,1)S(1)}, bf16[16,2,16,128]{3,2,1,0:T(8,128)(2,1)S(1)}, u32[]{:S(2)}, u32[]{:S(2)}) collective-permute-start(bf16[16,2,16,128]{3,2,1,0:T(8,128)(2,1)S(1)} %pad_maximum_fusion.1), channel_id=1, source_target_pairs={{96,97},{97,98},{98,99},{99,100},{100,101},{101,102},{102,103},{10... | collective-permute-start | bytes 393224 | tf_op jit(solution)/shard_map/ppermute | solution.py:460
  29.5 0.7 collective-permute-start.5
  43.6 7.8 %collective-permute-start.7 = (bf16[16,3,48,256]{3,2,1,0:T(8,128)(2,1)S(1)}, bf16[16,3,48,256]{3,2,1,0:T(8,128)(2,1)S(1)}, u32[]{:S(2)}, u32[]{:S(2)}) collective-permute-start(bf16[16,3,48,256]{3,2,1,0:T(8,128)(2,1)S(1)} %all-to-all-done.here_ref), channel_id=1, source_target_pairs={{0,1},{1,0},{2,3},{3,2},{4,5},{5,4},{6,7},{7,6},{8,9},{9,8},{10,11... | collective-permute-start | bytes 3538952 | tf_op jit(solution)/shard_map/ppermute | solution.py:441
  45.5 22.2 %collective-permute-start.11 = (bf16[256,2048]{1,0:T(8,128)(2,1)}, bf16[256,2048]{1,0:T(8,128)(2,1)S(1)}, u32[]{:S(2)}, u32[]{:S(2)}) collective-permute-start(bf16[256,2048]{1,0:T(8,128)(2,1)} %copy-done.4), channel_id=1, source_target_pairs={{0,8},{1,3},{2,10},{3,1},{4,12},{5,7},{6,14},{7,5},{8,0},{9,11},{1... | collective-permute-start | bytes 3145736 | tf_op jit(solution)/shard_map/ppermute | solution.py:441
  47.8 25.8 %collective-permute-start.12 = (bf16[256,2048]{1,0:T(8,128)(2,1)}, bf16[256,2048]{1,0:T(8,128)(2,1)S(1)}, u32[]{:S(2)}, u32[]{:S(2)}) collective-permute-start(bf16[256,2048]{1,0:T(8,128)(2,1)} %collective-permute-done.6.w2), channel_id=1, source_target_pairs={{0,8},{1,3},{2,10},{3,1},{4,12},{5,7},{6,14},{7,5},{8,0},{9,11},{1... | collective-permute-start | bytes 3145736 | tf_op jit(solution)/shard_map/ppermute | solution.py:441
  57.5 34.3 %copy-start.6 = (bf16[3,144,384]{2,1,0:T(8,128)(2,1)S(1)}, bf16[3,144,384]{2,1,0:T(8,128)(2,1)}, u32[]{:S(2)}) copy-start(bf16[3,144,384]{2,1,0:T(8,128)(2,1)} %param.23) | copy-start | bytes 995332
  57.5 19.3 %collective-permute-start.10 = (bf16[4,2,48,256]{3,2,1,0:T(8,128)(2,1)S(1)}, bf16[4,2,48,256]{3,2,1,0:T(8,128)(2,1)S(1)}, u32[]{:S(2)}, u32[]{:S(2)}) collective-permute-start(bf16[4,2,48,256]{3,2,1,0:T(8,128)(2,1)S(1)} %get-tuple-element.40), channel_id=1, source_target_pairs={{0,16},{1,5},{2,18},{3,7},{4,20},{5,1},{6,22},{7,3},{8,24},{9,13},... | collective-permute-start | bytes 589832 | tf_op jit(solution)/shard_map/ppermute | solution.py:441
  61.7 16.1 %collective-permute-start.8 = (bf16[4,2,48,256]{3,2,1,0:T(8,128)(2,1)S(1)}, bf16[4,2,48,256]{3,2,1,0:T(8,128)(2,1)S(1)}, u32[]{:S(2)}, u32[]{:S(2)}) collective-permute-start(bf16[4,2,48,256]{3,2,1,0:T(8,128)(2,1)S(1)} %get-tuple-element.40), channel_id=1, source_target_pairs={{0,8},{1,3},{2,10},{3,1},{4,12},{5,7},{6,14},{7,5},{8,0},{9,11},{1... | collective-permute-start | bytes 589832 | tf_op jit(solution)/shard_map/ppermute | solution.py:441
  64.0 28.0 %copy-start.8 = (f32[384]{0:T(512)S(1)}, f32[384]{0:T(512)}, u32[]{:S(2)}) copy-start(f32[384]{0:T(512)} %param.24) | copy-start | bytes 4612
  64.0 28.0 %copy-start.9 = (f32[384]{0:T(512)S(1)}, f32[384]{0:T(512)}, u32[]{:S(2)}) copy-start(f32[384]{0:T(512)} %param.25) | copy-start | bytes 4612
  64.0 28.0 %copy-start.10 = (f32[384]{0:T(512)S(1)}, f32[384]{0:T(512)}, u32[]{:S(2)}) copy-start(f32[384]{0:T(512)} %param.27) | copy-start | bytes 4612
  64.0 13.8 %collective-permute-start.9 = (bf16[4,2,48,256]{3,2,1,0:T(8,128)(2,1)S(1)}, bf16[4,2,48,256]{3,2,1,0:T(8,128)(2,1)S(1)}, u32[]{:S(2)}, u32[]{:S(2)}) collective-permute-start(bf16[4,2,48,256]{3,2,1,0:T(8,128)(2,1)S(1)} %get-tuple-element.39.h0), channel_id=1, source_target_pairs={{0,24},{1,7},{2,26},{3,5},{4,28},{5,3},{6,30},{7,1},{8,16},{9,15},... | collective-permute-start | bytes 589832 | tf_op jit(solution)/shard_map/ppermute | solution.py:441
  81.7 13.4 %collective-permute-start.13 = (bf16[2,48,2048]{2,1,0:T(8,128)(2,1)}, bf16[2,48,2048]{2,1,0:T(8,128)(2,1)S(1)}, u32[]{:S(2)}, u32[]{:S(2)}) collective-permute-start(bf16[2,48,2048]{2,1,0:T(8,128)(2,1)} %get-tuple-element.52), channel_id=1, source_target_pairs={{0,4},{1,17},{2,6},{3,19},{4,0},{5,21},{6,2},{7,23},{8,12},{9,25},... | collective-permute-start | bytes 1179656 | tf_op jit(solution)/shard_map/ppermute | solution.py:441
  85.6 11.7 %collective-permute-start.14 = (bf16[2,48,2048]{2,1,0:T(8,128)(2,1)}, bf16[2,48,2048]{2,1,0:T(8,128)(2,1)S(1)}, u32[]{:S(2)}, u32[]{:S(2)}) collective-permute-start(bf16[2,48,2048]{2,1,0:T(8,128)(2,1)} %get-tuple-element.53), channel_id=1, source_target_pairs={{0,6},{1,25},{2,4},{3,27},{4,2},{5,29},{6,0},{7,31},{8,14},{9,17},... | collective-permute-start | bytes 1179656 | tf_op jit(solution)/shard_map/ppermute | solution.py:441
  89.6 9.7 %collective-permute-start.15 = (bf16[2,48,2048]{2,1,0:T(8,128)(2,1)S(1)}, bf16[2,48,2048]{2,1,0:T(8,128)(2,1)S(1)}, u32[]{:S(2)}, u32[]{:S(2)}) collective-permute-start(bf16[2,48,2048]{2,1,0:T(8,128)(2,1)S(1)} %get-tuple-element.54), channel_id=1, source_target_pairs={{0,2},{1,9},{2,0},{3,11},{4,6},{5,13},{6,4},{7,15},{8,10},{9,1},{1... | collective-permute-start | bytes 1179656 | tf_op jit(solution)/shard_map/ppermute | solution.py:441
  92.3 16.5 %copy-start.1 = (bf16[1,48,4096]{2,1,0:T(8,128)(2,1)S(1)}, bf16[1,48,4096]{2,1,0:T(8,128)(2,1)}, u32[]{:S(2)}) copy-start(bf16[1,48,4096]{2,1,0:T(8,128)(2,1)} %param.17) | copy-start | bytes 1179652
  100.0 8.8 %collective-permute-start.16 = (bf16[48,2048]{1,0:T(8,128)(2,1)S(1)}, bf16[48,2048]{1,0:T(8,128)(2,1)S(1)}, u32[]{:S(2)}, u32[]{:S(2)}) collective-permute-start(bf16[48,2048]{1,0:T(8,128)(2,1)S(1)} %get-tuple-element.56), channel_id=1, source_target_pairs={{0,24},{1,7},{2,26},{3,5},{4,28},{5,3},{6,30},{7,1},{8,16},{9,15},... | collective-permute-start | bytes 589832 | tf_op jit(solution)/shard_map/ppermute | solution.py:441
  (5 other events, 33.3 us)

commit v4 on v3

--- a/solution.py
+++ b/solution.py
@@ -262,7 +262,7 @@
         out_shape=jax.ShapeDtypeStruct((4, vc, deep), jnp.bfloat16),
         in_specs=[smem_spec(), pl.BlockSpec(memory_space=pl.ANY)],
         out_specs=pl.BlockSpec(memory_space=pl.ANY),
-        compiler_params=pltpu.CompilerParams(vmem_limit_bytes=60 * MIB),
+        compiler_params=pltpu.CompilerParams(vmem_limit_bytes=56 * MIB),
         name="filter_weights",
     )(place, taps)
 
@@ -440,34 +440,32 @@
             pairs.append((at, ((g * side + z) * side + x_) * 2 + c))
         return lax.ppermute(x, ("grp",) + SEQ, pairs)
 
-    w_there = swap(output_weight, 2, 0)
     packed = norm_pack(
         query_input[0], key_input[0], value_input[0], query_norm_gain[None], key_norm_gain[None]
     )
-    packed, latents, w_mid = lax.optimization_barrier((packed, latents, w_mid))
+    packed, w_here = lax.optimization_barrier((packed, output_weight))
     here = lax.all_to_all(packed, CHIPS, split_axis=0, concat_axis=0, tiled=True)
 
+    w_own, w_give = weight_halves(place, w_here, swap(w_here, 2, 0))
+    w_own, w_give, latents, w_mid = lax.optimization_barrier((w_own, w_give, latents, w_mid))
+    w_next, w_back = swap(w_own, 0, 0), swap(w_give, 0, 1)
+
     own = jnp.swapaxes(latents, 2, 3)
-    pieces = [lax.ppermute(own, "grp", [(g, last)]) for g in range(last)]
+    clip = jnp.concatenate(
+        [lax.ppermute(own, "grp", [(g, last)]) for g in range(last)] + [own], axis=0
+    )
+    links = [(last * count + i, last * count + i + 1) for i in range(count - 1)]
+    above = lax.ppermute(clip, ("grp",) + SEQ, links)
+    below = lax.ppermute(clip, ("grp",) + SEQ, [(b, a) for a, b in links])
     filters = filter_weights(place, w_mid)
-    pieces, filters, w_there = lax.optimization_barrier((pieces, filters, w_there))
-    w_own, w_give = weight_halves(place, output_weight, w_there)
-    w_next, w_back = swap(w_own, 0, 0), swap(w_give, 0, 1)
-    clip = jnp.concatenate(pieces + [own], axis=0)
-    links = [(last * count + i, last * count + i + 1) for i in range(count - 1)]
-    cells = jnp.concatenate(
-        [
-            lax.ppermute(clip, ("grp",) + SEQ, links),
-            clip,
-            lax.ppermute(clip, ("grp",) + SEQ, [(b, a) for a, b in links]),
-        ],
-        axis=1,
-    )
+    above, below, filters = lax.optimization_barrier((above, below, filters))
+    cells = jnp.concatenate([above, clip, below], axis=1)
     w_first = jnp.pad(w_in.reshape(-1, channels).T, ((0, 0), (0, 512 - 27 * latents.shape[3])))
     vectors = jnp.broadcast_to(
         jnp.stack([b_in, norm_gain, b_mid])[:, :, None], (3, channels, latents.shape[2])
     )
-    here, cells, w_back = lax.optimization_barrier((here, cells, w_back))
+
+    here, cells, w_next, w_back = lax.optimization_barrier((here, cells, w_next, w_back))
     there = swap(here, 2, 0)
     w_far = swap(w_back, 0, 0)
     near, other = attend(place, here, there)

time: 111 us -> 103 us (0.928)
  waiting for transfers between devices: 32.9 us -> 24.7 us
  local copies, waits for them, and re-layouts: 2.43 us -> 5.18 us
  starting transfers between devices: 52.8 us -> 50.2 us
    ppermute x12, waiting for transfers between devices: 28.3 us -> 18.2 us  [swap(): return lax.ppermute(x, ('grp',) + SEQ, pairs)]
    ppermute x5, starting transfers between devices: 6.39 us -> 3.96 us  [the longest x3 2.62 us: on_device(): lax.ppermute(own, 'grp', [(g, last)])]
    reshape x1, local copies, waits for them, and re-layouts: 0.19 us -> 1.9 us  [on_device(): w_in.reshape(-1, channels)]
    all_to_all x1, waiting for transfers between devices: 4.6 us -> 6.21 us  [on_device(): lax.all_to_all(packed, CHIPS, split_axis=0, concat_axis=0, tiled=True)]
  transfers between devices with their start and end apart: 18 -> 18, of which waited for: 8 -> 8; matrix products, arithmetic and copies ran while one was open for 1% -> 3% of each run, Pallas kernels for 14% -> 11%
where the time goes in v4:
time: 103 us; the launch traced here: 102 us
  starting transfers between devices  50.2 us (49%)
  waiting for transfers between devices  24.7 us (24%)
  Pallas kernels  20.8 us (20%)
  local copies, waits for them, and re-layouts  5.18 us (5%)
  between operations  1.05 us (1%)
    ppermute x12, starting transfers between devices, swap(): return lax.ppermute(x, ('grp',) + SEQ, pairs)  38.3 us
    ppermute x12, waiting for transfers between devices, swap(): return lax.ppermute(x, ('grp',) + SEQ, pairs)  18.2 us
    all_to_all x1, starting transfers between devices, on_device(): lax.all_to_all(packed, CHIPS, split_axis=0, concat_axis=0, tiled=True)  7.97 us
    all_to_all x1, waiting for transfers between devices, on_device(): lax.all_to_all(packed, CHIPS, split_axis=0, concat_axis=0, tiled=True)  6.21 us
    pallas_call x1, Pallas kernels, attend(): pl.pallas_call(body, grid=(chips // 4,), out_shape=(jax.ShapeDtypeStruct(...  6.12 us
    pallas_call x1, Pallas kernels, norm_pack(): pl.pallas_call(body, grid=(rows // block,), out_shape=jax.ShapeDtypeStruc...  3.56 us
    pallas_call x1, Pallas kernels, project(): pl.pallas_call(body, out_shape=(jax.ShapeDtypeStruct(shape, jnp.float32),...  3.36 us
    pallas_call x1, Pallas kernels, decode(): pl.pallas_call(body, grid=(frames // lot,), out_shape=jax.ShapeDtypeStruc...  2.8 us
  transfers between devices with their start and end apart: 18, of which 8 were waited for; matrix products, arithmetic and copies ran while one was open for 3% of the time, Pallas kernels for 11%

profile of v4, /device:TPU:0, one launch (start us, length us, event | category | flops | bytes accessed | tf_op | source)
XLA Modules:
  0.0 102.0 jit_solution(17368646805115025359)
XLA Ops:
  0.7 3.6 %norm_pack.1 = bf16[16,3,48,256]{3,2,1,0:T(8,128)(2,1)} custom-call(bf16[48,4096]{1,0:T(8,128)(2,1)} %bitcast.21, bf16[48,4096]{1,0:T(8,128)(2,1)} %bitcast.22, bf16[48,4096]{1,0:T(8,128)(2,1)} %bitcast.23, f32[1,4096]{1,0:T(1,128)} %bitcast.31, f32[1,4096]{1,0:T(1,128)} %bitcast.32), custom_call_target="tpu_custom_call" | custom-call | tf_op jit(solution)/shard_map/norm_pack/pallas_call | solution.py:45
  4.2 1.9 %collective-permute-start = (bf16[128,4096]{1,0:T(8,128)(2,1)}, bf16[128,4096]{1,0:T(8,128)(2,1)S(1)}, u32[]{:S(2)}, u32[]{:S(2)}) collective-permute-start(bf16[128,4096]{1,0:T(8,128)(2,1)} %here_ref), channel_id=1, source_target_pairs={{0,1},{1,0},{2,3},{3,2},{4,5},{5,4},{6,7},{7,6},{8,9},{9,8},{10,11... | collective-permute-start | bytes 3145736 | tf_op jit(solution)/shard_map/ppermute | solution.py:441
  6.1 8.0 %all-to-all-start = ((bf16[16,3,48,256]{3,2,1,0:T(8,128)(2,1)}), bf16[16,3,48,256]{3,2,1,0:T(8,128)(2,1)S(1)}, u32[]{:S(2)}, u32[]{:S(2)}) async-start(bf16[16,3,48,256]{3,2,1,0:T(8,128)(2,1)} %norm_pack.1), calls=%async_computation | async-start | bytes 2359296 | tf_op jit(solution)/shard_map/all_to_all | solution.py:447
  14.2 2.1 %weight_halves.1 = (bf16[256,2048]{1,0:T(8,128)(2,1)}, bf16[256,2048]{1,0:T(8,128)(2,1)}) custom-call(s32[6]{0:T(128)S(1)} %stack.39.place_ref, bf16[128,4096]{1,0:T(8,128)(2,1)S(1)} %copy-done, bf16[128,4096]{1,0:T(8,128)(2,1)S(1)} %collective-permute-done.there_ref), custom_call_target="tpu_custom_call" | custom-call | tf_op jit(solution)/shard_map/weight_halves/pallas_call | solution.py:72
  16.3 3.8 %collective-permute-start.6 = (bf16[256,2048]{1,0:T(8,128)(2,1)}, bf16[256,2048]{1,0:T(8,128)(2,1)S(1)}, u32[]{:S(2)}, u32[]{:S(2)}) collective-permute-start(bf16[256,2048]{1,0:T(8,128)(2,1)} %get-tuple-element.40.w0), channel_id=1, source_target_pairs={{0,8},{1,3},{2,10},{3,1},{4,12},{5,7},{6,14},{7,5},{8,0},{9,11},{1... | collective-permute-start | bytes 3145736 | tf_op jit(solution)/shard_map/ppermute | solution.py:441
  20.1 4.0 %collective-permute-start.7 = (bf16[256,2048]{1,0:T(8,128)(2,1)}, bf16[256,2048]{1,0:T(8,128)(2,1)}, u32[]{:S(2)}, u32[]{:S(2)}) collective-permute-start(bf16[256,2048]{1,0:T(8,128)(2,1)} %get-tuple-element.41), channel_id=1, source_target_pairs={{0,24},{1,7},{2,26},{3,5},{4,28},{5,3},{6,30},{7,1},{8,16},{9,15},... | collective-permute-start | bytes 3145736 | tf_op jit(solution)/shard_map/ppermute | solution.py:441
  29.2 6.2 %all-to-all-done.here_ref = bf16[16,3,48,256]{3,2,1,0:T(8,128)(2,1)S(1)} async-done(((bf16[16,3,48,256]{3,2,1,0:T(8,128)(2,1)}), bf16[16,3,48,256]{3,2,1,0:T(8,128)(2,1)S(1)}, u32[]{:S(2)}, u32[]{:S(2)}) %all-to-all-start) | async-done | bytes 1179680 | tf_op jit(solution)/shard_map/all_to_all | solution.py:447
  35.4 5.5 %collective-permute-done.6.w1 = bf16[256,2048]{1,0:T(8,128)(2,1)S(1)} collective-permute-done((bf16[256,2048]{1,0:T(8,128)(2,1)}, bf16[256,2048]{1,0:T(8,128)(2,1)S(1)}, u32[]{:S(2)}, u32[]{:S(2)}) %collective-permute-start.6) | collective-permute-done | bytes 1048608 | tf_op jit(solution)/shard_map/ppermute | solution.py:441
  40.9 1.9 %collective-permute-done.7.w2 = bf16[256,2048]{1,0:T(8,128)(2,1)} collective-permute-done((bf16[256,2048]{1,0:T(8,128)(2,1)}, bf16[256,2048]{1,0:T(8,128)(2,1)}, u32[]{:S(2)}, u32[]{:S(2)}) %collective-permute-start.7) | collective-permute-done | bytes 1048608 | tf_op jit(solution)/shard_map/ppermute | solution.py:441
  42.8 1.9 %collective-permute-start.8 = (bf16[16,3,48,256]{3,2,1,0:T(8,128)(2,1)S(1)}, bf16[16,3,48,256]{3,2,1,0:T(8,128)(2,1)S(1)}, u32[]{:S(2)}, u32[]{:S(2)}) collective-permute-start(bf16[16,3,48,256]{3,2,1,0:T(8,128)(2,1)S(1)} %all-to-all-done.here_ref), channel_id=1, source_target_pairs={{0,1},{1,0},{2,3},{3,2},{4,5},{5,4},{6,7},{7,6},{8,9},{9,8},{10,11... | collective-permute-start | bytes 3538952 | tf_op jit(solution)/shard_map/ppermute | solution.py:441
  44.7 3.2 %collective-permute-start.12 = (bf16[256,2048]{1,0:T(8,128)(2,1)}, bf16[256,2048]{1,0:T(8,128)(2,1)S(1)}, u32[]{:S(2)}, u32[]{:S(2)}) collective-permute-start(bf16[256,2048]{1,0:T(8,128)(2,1)} %collective-permute-done.7.w2), channel_id=1, source_target_pairs={{0,8},{1,3},{2,10},{3,1},{4,12},{5,7},{6,14},{7,5},{8,0},{9,11},{1... | collective-permute-start | bytes 3145736 | tf_op jit(solution)/shard_map/ppermute | solution.py:441
  48.6 6.1 %attend.1 = (bf16[4,2,48,256]{3,2,1,0:T(8,128)(2,1)S(1)}, bf16[4,2,48,256]{3,2,1,0:T(8,128)(2,1)S(1)}) custom-call(s32[6]{0:T(128)S(1)} %copy-done.3, bf16[16,3,48,256]{3,2,1,0:T(8,128)(2,1)S(1)} %all-to-all-done.here_ref, bf16[16,3,48,256]{3,2,1,0:T(8,128)(2,1)S(1)} %collective-permute-done.8.there_ref), custom_call_target="tpu_custom_call" | custom-call | tf_op jit(solution)/shard_map/attend/pallas_call | solution.py:134
  54.8 3.6 %collective-permute-start.10 = (bf16[4,2,48,256]{3,2,1,0:T(8,128)(2,1)S(1)}, bf16[4,2,48,256]{3,2,1,0:T(8,128)(2,1)S(1)}, u32[]{:S(2)}, u32[]{:S(2)}) collective-permute-start(bf16[4,2,48,256]{3,2,1,0:T(8,128)(2,1)S(1)} %get-tuple-element.43.h0), channel_id=1, source_target_pairs={{0,24},{1,7},{2,26},{3,5},{4,28},{5,3},{6,30},{7,1},{8,16},{9,15},... | collective-permute-start | bytes 589832 | tf_op jit(solution)/shard_map/ppermute | solution.py:441
  58.5 3.0 %collective-permute-start.11 = (bf16[4,2,48,256]{3,2,1,0:T(8,128)(2,1)S(1)}, bf16[4,2,48,256]{3,2,1,0:T(8,128)(2,1)S(1)}, u32[]{:S(2)}, u32[]{:S(2)}) collective-permute-start(bf16[4,2,48,256]{3,2,1,0:T(8,128)(2,1)S(1)} %get-tuple-element.44), channel_id=1, source_target_pairs={{0,16},{1,5},{2,18},{3,7},{4,20},{5,1},{6,22},{7,3},{8,24},{9,13},... | collective-permute-start | bytes 589832 | tf_op jit(solution)/shard_map/ppermute | solution.py:441
  61.4 3.2 %collective-permute-start.9 = (bf16[4,2,48,256]{3,2,1,0:T(8,128)(2,1)S(1)}, bf16[4,2,48,256]{3,2,1,0:T(8,128)(2,1)S(1)}, u32[]{:S(2)}, u32[]{:S(2)}) collective-permute-start(bf16[4,2,48,256]{3,2,1,0:T(8,128)(2,1)S(1)} %get-tuple-element.44), channel_id=1, source_target_pairs={{0,8},{1,3},{2,10},{3,1},{4,12},{5,7},{6,14},{7,5},{8,0},{9,11},{1... | collective-permute-start | bytes 589832 | tf_op jit(solution)/shard_map/ppermute | solution.py:441
  64.7 2.9 %collective-permute-done.11.h3 = bf16[4,2,48,256]{3,2,1,0:T(8,128)(2,1)S(1)} collective-permute-done((bf16[4,2,48,256]{3,2,1,0:T(8,128)(2,1)S(1)}, bf16[4,2,48,256]{3,2,1,0:T(8,128)(2,1)S(1)}, u32[]{:S(2)}, u32[]{:S(2)}) %collective-permute-start.11) | collective-permute-done | bytes 196640 | tf_op jit(solution)/shard_map/ppermute | solution.py:441
  70.2 3.4 %project.1 = (f32[2,48,2048]{2,1,0:T(8,128)S(1)}, bf16[2,48,2048]{2,1,0:T(8,128)(2,1)S(1)}, bf16[2,48,2048]{2,1,0:T(8,128)(2,1)S(1)}, bf16[2,48,2048]{2,1,0:T(8,128)(2,1)S(1)}) custom-call(s32[6]{0:T(128)S(1)} %copy-done.3, bf16[4,2,48,256]{3,2,1,0:T(8,128)(2,1)S(1)} %get-tuple-element.43.h0, bf16[4,2,48,256]{3,2,1,0:T(8,128)(2,1)S(1)} %collective-permute-done.9.h1, ...), custom_call_target="tpu_custom_call" | custom-call | flops 1610612736 | bytes 8388608 | tf_op jit(solution)/shard_map/project/pallas_call | solution.py:173
  73.6 4.5 %collective-permute-start.13 = (bf16[2,48,2048]{2,1,0:T(8,128)(2,1)S(1)}, bf16[2,48,2048]{2,1,0:T(8,128)(2,1)S(1)}, u32[]{:S(2)}, u32[]{:S(2)}) collective-permute-start(bf16[2,48,2048]{2,1,0:T(8,128)(2,1)S(1)} %get-tuple-element.56), channel_id=1, source_target_pairs={{0,4},{1,17},{2,6},{3,19},{4,0},{5,21},{6,2},{7,23},{8,12},{9,25},... | collective-permute-start | bytes 1179656 | tf_op jit(solution)/shard_map/ppermute | solution.py:441
  78.1 3.2 %collective-permute-start.14 = (bf16[2,48,2048]{2,1,0:T(8,128)(2,1)S(1)}, bf16[2,48,2048]{2,1,0:T(8,128)(2,1)S(1)}, u32[]{:S(2)}, u32[]{:S(2)}) collective-permute-start(bf16[2,48,2048]{2,1,0:T(8,128)(2,1)S(1)} %get-tuple-element.57), channel_id=1, source_target_pairs={{0,6},{1,25},{2,4},{3,27},{4,2},{5,29},{6,0},{7,31},{8,14},{9,17},... | collective-permute-start | bytes 1179656 | tf_op jit(solution)/shard_map/ppermute | solution.py:441
  81.3 2.1 %collective-permute-start.15 = (bf16[2,48,2048]{2,1,0:T(8,128)(2,1)S(1)}, bf16[2,48,2048]{2,1,0:T(8,128)(2,1)S(1)}, u32[]{:S(2)}, u32[]{:S(2)}) collective-permute-start(bf16[2,48,2048]{2,1,0:T(8,128)(2,1)S(1)} %get-tuple-element.58), channel_id=1, source_target_pairs={{0,2},{1,9},{2,0},{3,11},{4,6},{5,13},{6,4},{7,15},{8,10},{9,1},{1... | collective-permute-start | bytes 1179656 | tf_op jit(solution)/shard_map/ppermute | solution.py:441
  83.5 1.9 %copy.17 = bf16[432,384]{0,1:T(8,128)(2,1)} copy(bf16[432,384]{1,0:T(8,128)(2,1)} %bitcast.25) | data formatting | bytes 663552 | tf_op jit(solution)/shard_map/reshape | solution.py:463
  86.7 2.8 %decode.1 = bf16[16,2,128,384]{3,2,1,0:T(8,128)(2,1)} custom-call(s32[6]{0:T(128)S(1)} %copy-done.4, bf16[16,6,16,128]{3,2,1,0:T(8,128)(2,1)S(1)} %pad_maximum_fusion.clip_ref, bf16[384,512]{1,0:T(8,128)(2,1)S(1)} %pad.4.w1_ref, bf16[4,384,3456]{2,1,0:T(8,128)(2,1)} %filter_weights.1.f_ref, f32[3,384,128]{2,1,0:T(8,128)S(1)} %broadcast_in_dim.20.vec_ref), custom_call_target="tpu_custom_call" | custom-call | tf_op jit(solution)/shard_map/decode/pallas_call | solution.py:368
  91.7 3.8 %collective-permute-start.16 = (bf16[48,2048]{1,0:T(8,128)(2,1)S(1)}, bf16[48,2048]{1,0:T(8,128)(2,1)S(1)}, u32[]{:S(2)}, u32[]{:S(2)}) collective-permute-start(bf16[48,2048]{1,0:T(8,128)(2,1)S(1)} %get-tuple-element.60), channel_id=1, source_target_pairs={{0,24},{1,7},{2,26},{3,5},{4,28},{5,3},{6,30},{7,1},{8,16},{9,15},... | collective-permute-start | bytes 589832 | tf_op jit(solution)/shard_map/ppermute | solution.py:441
  95.5 5.0 %collective-permute-done.16.got_ref = bf16[48,2048]{1,0:T(8,128)(2,1)S(1)} collective-permute-done((bf16[48,2048]{1,0:T(8,128)(2,1)S(1)}, bf16[48,2048]{1,0:T(8,128)(2,1)S(1)}, u32[]{:S(2)}, u32[]{:S(2)}) %collective-permute-start.16) | collective-permute-done | bytes 196640 | tf_op jit(solution)/shard_map/ppermute | solution.py:441
  (54 shorter events, 13.4 us)
Async XLA Ops:
  0.6 23.5 %copy-start.8 = (bf16[4,2,128,16]{2,3,1,0:T(8,128)(2,1)S(1)}, bf16[4,2,128,16]{2,3,1,0:T(8,128)(2,1)}, u32[]{:S(2)}) copy-start(bf16[4,2,128,16]{2,3,1,0:T(8,128)(2,1)} %param.22) | copy-start | bytes 98308
  4.2 10.0 %collective-permute-start = (bf16[128,4096]{1,0:T(8,128)(2,1)}, bf16[128,4096]{1,0:T(8,128)(2,1)S(1)}, u32[]{:S(2)}, u32[]{:S(2)}) collective-permute-start(bf16[128,4096]{1,0:T(8,128)(2,1)} %here_ref), channel_id=1, source_target_pairs={{0,1},{1,0},{2,3},{3,2},{4,5},{5,4},{6,7},{7,6},{8,9},{9,8},{10,11... | collective-permute-start | bytes 3145736 | tf_op jit(solution)/shard_map/ppermute | solution.py:441
  6.1 29.2 %all-to-all-start = ((bf16[16,3,48,256]{3,2,1,0:T(8,128)(2,1)}), bf16[16,3,48,256]{3,2,1,0:T(8,128)(2,1)S(1)}, u32[]{:S(2)}, u32[]{:S(2)}) async-start(bf16[16,3,48,256]{3,2,1,0:T(8,128)(2,1)} %norm_pack.1), calls=%async_computation | async-start | bytes 2359296 | tf_op jit(solution)/shard_map/all_to_all | solution.py:447
  16.3 24.6 %collective-permute-start.6 = (bf16[256,2048]{1,0:T(8,128)(2,1)}, bf16[256,2048]{1,0:T(8,128)(2,1)S(1)}, u32[]{:S(2)}, u32[]{:S(2)}) collective-permute-start(bf16[256,2048]{1,0:T(8,128)(2,1)} %get-tuple-element.40.w0), channel_id=1, source_target_pairs={{0,8},{1,3},{2,10},{3,1},{4,12},{5,7},{6,14},{7,5},{8,0},{9,11},{1... | collective-permute-start | bytes 3145736 | tf_op jit(solution)/shard_map/ppermute | solution.py:441
  20.1 22.7 %collective-permute-start.7 = (bf16[256,2048]{1,0:T(8,128)(2,1)}, bf16[256,2048]{1,0:T(8,128)(2,1)}, u32[]{:S(2)}, u32[]{:S(2)}) collective-permute-start(bf16[256,2048]{1,0:T(8,128)(2,1)} %get-tuple-element.41), channel_id=1, source_target_pairs={{0,24},{1,7},{2,26},{3,5},{4,28},{5,3},{6,30},{7,1},{8,16},{9,15},... | collective-permute-start | bytes 3145736 | tf_op jit(solution)/shard_map/ppermute | solution.py:441
  24.1 2.9 %collective-permute-start.1 = (bf16[4,2,16,128]{3,2,1,0:T(8,128)(2,1)S(1)}, bf16[4,2,16,128]{3,2,1,0:T(8,128)(2,1)S(1)}, u32[]{:S(2)}, u32[]{:S(2)}) collective-permute-start(bf16[4,2,16,128]{3,2,1,0:T(8,128)(2,1)S(1)} %bitcast.26), channel_id=1, source_target_pairs={{0,96},{1,97},{2,98},{3,99},{4,100},{5,101},{6,102},{7,103},{8,104... | collective-permute-start | bytes 98312 | tf_op jit(solution)/shard_map/ppermute | solution.py:455
  25.4 1.6 %collective-permute-start.2 = (bf16[4,2,16,128]{3,2,1,0:T(8,128)(2,1)S(1)}, bf16[4,2,16,128]{3,2,1,0:T(8,128)(2,1)S(1)}, u32[]{:S(2)}, u32[]{:S(2)}) collective-permute-start(bf16[4,2,16,128]{3,2,1,0:T(8,128)(2,1)S(1)} %bitcast.27), channel_id=1, source_target_pairs={{32,96},{33,97},{34,98},{35,99},{36,100},{37,101},{38,102},{39,103... | collective-permute-start | bytes 98312 | tf_op jit(solution)/shard_map/ppermute | solution.py:455
  26.1 0.9 collective-permute-start.3
  27.0 2.0 %collective-permute-start.4 = (bf16[16,2,16,128]{3,2,1,0:T(8,128)(2,1)S(1)}, bf16[16,2,16,128]{3,2,1,0:T(8,128)(2,1)S(1)}, u32[]{:S(2)}, u32[]{:S(2)}) collective-permute-start(bf16[16,2,16,128]{3,2,1,0:T(8,128)(2,1)S(1)} %pad_maximum_fusion.1), channel_id=1, source_target_pairs={{96,97},{97,98},{98,99},{99,100},{100,101},{101,102},{102,103},{10... | collective-permute-start | bytes 393224 | tf_op jit(solution)/shard_map/ppermute | solution.py:458
  27.7 1.4 %collective-permute-start.5 = (bf16[16,2,16,128]{3,2,1,0:T(8,128)(2,1)S(1)}, bf16[16,2,16,128]{3,2,1,0:T(8,128)(2,1)S(1)}, u32[]{:S(2)}, u32[]{:S(2)}) collective-permute-start(bf16[16,2,16,128]{3,2,1,0:T(8,128)(2,1)S(1)} %pad_maximum_fusion.1), channel_id=1, source_target_pairs={{97,96},{98,97},{99,98},{100,99},{101,100},{102,101},{103,102},{10... | collective-permute-start | bytes 393224 | tf_op jit(solution)/shard_map/ppermute | solution.py:459
  40.9 17.5 %copy-start.6 = (bf16[256,2048]{1,0:T(8,128)(2,1)}, bf16[256,2048]{1,0:T(8,128)(2,1)S(1)}, u32[]{:S(2)}) copy-start(bf16[256,2048]{1,0:T(8,128)(2,1)S(1)} %collective-permute-done.6.w1) | copy-start | bytes 3145732
  42.8 5.1 %collective-permute-start.8 = (bf16[16,3,48,256]{3,2,1,0:T(8,128)(2,1)S(1)}, bf16[16,3,48,256]{3,2,1,0:T(8,128)(2,1)S(1)}, u32[]{:S(2)}, u32[]{:S(2)}) collective-permute-start(bf16[16,3,48,256]{3,2,1,0:T(8,128)(2,1)S(1)} %all-to-all-done.here_ref), channel_id=1, source_target_pairs={{0,1},{1,0},{2,3},{3,2},{4,5},{5,4},{6,7},{7,6},{8,9},{9,8},{10,11... | collective-permute-start | bytes 3538952 | tf_op jit(solution)/shard_map/ppermute | solution.py:441
  44.7 19.9 %collective-permute-start.12 = (bf16[256,2048]{1,0:T(8,128)(2,1)}, bf16[256,2048]{1,0:T(8,128)(2,1)S(1)}, u32[]{:S(2)}, u32[]{:S(2)}) collective-permute-start(bf16[256,2048]{1,0:T(8,128)(2,1)} %collective-permute-done.7.w2), channel_id=1, source_target_pairs={{0,8},{1,3},{2,10},{3,1},{4,12},{5,7},{6,14},{7,5},{8,0},{9,11},{1... | collective-permute-start | bytes 3145736 | tf_op jit(solution)/shard_map/ppermute | solution.py:441
  48.6 36.7 %copy-start.10 = (f32[384]{0:T(512)S(1)}, f32[384]{0:T(512)}, u32[]{:S(2)}) copy-start(f32[384]{0:T(512)} %param.25) | copy-start | bytes 4612
  48.6 36.7 %copy-start.11 = (f32[384]{0:T(512)S(1)}, f32[384]{0:T(512)}, u32[]{:S(2)}) copy-start(f32[384]{0:T(512)} %param.27) | copy-start | bytes 4612
  54.8 30.6 %copy-start.9 = (f32[384]{0:T(512)S(1)}, f32[384]{0:T(512)}, u32[]{:S(2)}) copy-start(f32[384]{0:T(512)} %param.24) | copy-start | bytes 4612
  54.8 9.9 %collective-permute-start.10 = (bf16[4,2,48,256]{3,2,1,0:T(8,128)(2,1)S(1)}, bf16[4,2,48,256]{3,2,1,0:T(8,128)(2,1)S(1)}, u32[]{:S(2)}, u32[]{:S(2)}) collective-permute-start(bf16[4,2,48,256]{3,2,1,0:T(8,128)(2,1)S(1)} %get-tuple-element.43.h0), channel_id=1, source_target_pairs={{0,24},{1,7},{2,26},{3,5},{4,28},{5,3},{6,30},{7,1},{8,16},{9,15},... | collective-permute-start | bytes 589832 | tf_op jit(solution)/shard_map/ppermute | solution.py:441
  58.4 28.2 %copy-start.4 = (s32[6]{0:T(128)S(1)}, s32[6]{0:T(128)}, u32[]{:S(2)}) copy-start(s32[6]{0:T(128)} %copy-done.2) | copy-start | bytes 76
  58.5 9.1 %collective-permute-start.11 = (bf16[4,2,48,256]{3,2,1,0:T(8,128)(2,1)S(1)}, bf16[4,2,48,256]{3,2,1,0:T(8,128)(2,1)S(1)}, u32[]{:S(2)}, u32[]{:S(2)}) collective-permute-start(bf16[4,2,48,256]{3,2,1,0:T(8,128)(2,1)S(1)} %get-tuple-element.44), channel_id=1, source_target_pairs={{0,16},{1,5},{2,18},{3,7},{4,20},{5,1},{6,22},{7,3},{8,24},{9,13},... | collective-permute-start | bytes 589832 | tf_op jit(solution)/shard_map/ppermute | solution.py:441
  61.4 7.6 %collective-permute-start.9 = (bf16[4,2,48,256]{3,2,1,0:T(8,128)(2,1)S(1)}, bf16[4,2,48,256]{3,2,1,0:T(8,128)(2,1)S(1)}, u32[]{:S(2)}, u32[]{:S(2)}) collective-permute-start(bf16[4,2,48,256]{3,2,1,0:T(8,128)(2,1)S(1)} %get-tuple-element.44), channel_id=1, source_target_pairs={{0,8},{1,3},{2,10},{3,1},{4,12},{5,7},{6,14},{7,5},{8,0},{9,11},{1... | collective-permute-start | bytes 589832 | tf_op jit(solution)/shard_map/ppermute | solution.py:441
  73.6 15.9 %collective-permute-start.13 = (bf16[2,48,2048]{2,1,0:T(8,128)(2,1)S(1)}, bf16[2,48,2048]{2,1,0:T(8,128)(2,1)S(1)}, u32[]{:S(2)}, u32[]{:S(2)}) collective-permute-start(bf16[2,48,2048]{2,1,0:T(8,128)(2,1)S(1)} %get-tuple-element.56), channel_id=1, source_target_pairs={{0,4},{1,17},{2,6},{3,19},{4,0},{5,21},{6,2},{7,23},{8,12},{9,25},... | collective-permute-start | bytes 1179656 | tf_op jit(solution)/shard_map/ppermute | solution.py:441
  78.1 11.4 %collective-permute-start.14 = (bf16[2,48,2048]{2,1,0:T(8,128)(2,1)S(1)}, bf16[2,48,2048]{2,1,0:T(8,128)(2,1)S(1)}, u32[]{:S(2)}, u32[]{:S(2)}) collective-permute-start(bf16[2,48,2048]{2,1,0:T(8,128)(2,1)S(1)} %get-tuple-element.57), channel_id=1, source_target_pairs={{0,6},{1,25},{2,4},{3,27},{4,2},{5,29},{6,0},{7,31},{8,14},{9,17},... | collective-permute-start | bytes 1179656 | tf_op jit(solution)/shard_map/ppermute | solution.py:441
  81.3 9.7 %collective-permute-start.15 = (bf16[2,48,2048]{2,1,0:T(8,128)(2,1)S(1)}, bf16[2,48,2048]{2,1,0:T(8,128)(2,1)S(1)}, u32[]{:S(2)}, u32[]{:S(2)}) collective-permute-start(bf16[2,48,2048]{2,1,0:T(8,128)(2,1)S(1)} %get-tuple-element.58), channel_id=1, source_target_pairs={{0,2},{1,9},{2,0},{3,11},{4,6},{5,13},{6,4},{7,15},{8,10},{9,1},{1... | collective-permute-start | bytes 1179656 | tf_op jit(solution)/shard_map/ppermute | solution.py:441
  91.7 8.8 %collective-permute-start.16 = (bf16[48,2048]{1,0:T(8,128)(2,1)S(1)}, bf16[48,2048]{1,0:T(8,128)(2,1)S(1)}, u32[]{:S(2)}, u32[]{:S(2)}) collective-permute-start(bf16[48,2048]{1,0:T(8,128)(2,1)S(1)} %get-tuple-element.60), channel_id=1, source_target_pairs={{0,24},{1,7},{2,26},{3,5},{4,28},{5,3},{6,30},{7,1},{8,16},{9,15},... | collective-permute-start | bytes 589832 | tf_op jit(solution)/shard_map/ppermute | solution.py:441
  (6 other events, 57.3 us)

commit v5 on v4

--- a/solution.py
+++ b/solution.py
@@ -53,41 +53,40 @@
     )(q, k, v, gain_q, gain_k)
 
 
-def weight_halves(place, w_here, w_there):
+def partners(position):
+    return position, jnp.bitwise_xor(position, 1), 3 - position, jnp.bitwise_xor(position, 2)
+
+
+def weight_blocks(place, w_here, w_there):
     rows, width = w_here.shape
-    part = width // 2
-
-    def body(place_ref, here_ref, there_ref, keep_ref, give_ref):
+    part = width // 4
+
+    def body(place_ref, here_ref, there_ref, *outs):
         here_at = pl.ds(pl.multiple_of(place_ref[1] * rows, rows), rows)
         there_at = pl.ds(pl.multiple_of((1 - place_ref[1]) * rows, rows), rows)
 
         @pl.when(place_ref[0] == 0)
         def _():
-            for k, out in enumerate((keep_ref, give_ref)):
-                half = jnp.bitwise_xor(place_ref[4] // 2, k)
-                at = pl.ds(pl.multiple_of(half * part, part), part)
+            for chip, out in zip(partners(place_ref[4]), outs):
+                at = pl.ds(pl.multiple_of(chip * part, part), part)
                 out[here_at] = here_ref[:, at]
                 out[there_at] = there_ref[:, at]
 
     return pl.pallas_call(
         body,
-        out_shape=(jax.ShapeDtypeStruct((2 * rows, part), jnp.bfloat16),) * 2,
+        out_shape=(jax.ShapeDtypeStruct((2 * rows, part), jnp.bfloat16),) * 4,
         in_specs=[smem_spec(), vmem_spec(), vmem_spec()],
-        out_specs=(vmem_spec(),) * 2,
+        out_specs=(vmem_spec(),) * 4,
         compiler_params=pltpu.CompilerParams(vmem_limit_bytes=16 * MIB),
-        name="weight_halves",
+        name="weight_blocks",
     )(place, w_here, w_there)
-
-
-def inner(position):
-    return ((position + 1) // 2) % 2
 
 
 def attend(place, here, there):
     chips, _, tok, _ = here.shape
     half = chips * tok
 
-    def body(place_ref, here_ref, there_ref, near_ref, other_ref):
+    def body(place_ref, here_ref, there_ref, out_ref):
         step = pl.program_id(0)
 
         @pl.when(place_ref[0] == 0)
@@ -116,27 +115,15 @@
                 heads.append(o[:, :128] / o[:, 128:])
             joined = jnp.concatenate(heads, axis=1).astype(jnp.bfloat16)
             for n in range(4):
-                first = jnp.where(place_ref[1] == 0, step, n)
-                second = jnp.where(place_ref[1] == 0, n, step)
-                high = first // 2
-                slot = jnp.where(second == 0, 0, jnp.where(second == 3, 1, second + 1))
-                near = inner(first) == inner(place_ref[4])
-                piece = joined[tok * n : tok * n + tok]
-
-                @pl.when(near)
-                def _():
-                    near_ref[slot, high] = piece
-
-                @pl.when(jnp.logical_not(near))
-                def _():
-                    other_ref[slot, high] = piece
+                at = jnp.where(place_ref[1] == 0, 4 * n + step, 4 * step + n)
+                out_ref[at] = joined[tok * n : tok * n + tok]
 
     return pl.pallas_call(
         body,
         grid=(chips // 4,),
-        out_shape=(jax.ShapeDtypeStruct((4, 2, tok, 256), jnp.bfloat16),) * 2,
+        out_shape=jax.ShapeDtypeStruct((chips, tok, 256), jnp.bfloat16),
         in_specs=[smem_spec(), vmem_spec(), vmem_spec()],
-        out_specs=(vmem_spec(),) * 2,
+        out_specs=vmem_spec(),
         compiler_params=pltpu.CompilerParams(vmem_limit_bytes=40 * MIB),
         cost_estimate=pl.CostEstimate(flops=0, bytes_accessed=0, transcendentals=0),
         name="attend",
@@ -144,32 +131,28 @@
 
 
 def project(place, heads, weights):
-    _, two, tok, _ = heads[0].shape
+    chips, tok, _ = heads[0].shape
     part = weights[0].shape[1]
-    lot = two * tok
-
-    def body(place_ref, h0, h1, h2, h3, w0, w1, w2, w3, own_ref, one_ref, zero_ref, far_ref):
-        second = place_ref[5]
-        slot = jnp.where(second == 0, 0, jnp.where(second == 3, 1, second + 1))
-
+    lot = chips // 4 * tok
+
+    def body(place_ref, h0, h1, h2, h3, w0, w1, w2, w3, *outs):
         @pl.when(place_ref[0] == 0)
         def _():
             weight = jnp.concatenate([w0[...], w1[...], w2[...], w3[...]], axis=0)
             feats = jnp.concatenate(
                 [
                     jnp.concatenate(
-                        [h[jnp.bitwise_xor(slot, k)].reshape(lot, 256) for h in (h0, h1, h2, h3)],
-                        axis=1,
+                        [h[pl.ds(4 * chip, 4)].reshape(lot, 256) for h in (h0, h1, h2, h3)], axis=1
                     )
-                    for k in range(4)
+                    for chip in partners(place_ref[5])
                 ],
                 axis=0,
             )
             out = jnp.dot(feats, weight, preferred_element_type=jnp.float32)
-            for k, ref in enumerate((own_ref, one_ref, zero_ref, far_ref)):
-                ref[...] = out[lot * k : lot * k + lot].reshape(two, tok, part).astype(ref.dtype)
-
-    shape = (two, tok, part)
+            for k, ref in enumerate(outs):
+                ref[...] = out[lot * k : lot * k + lot].reshape(4, tok, part).astype(ref.dtype)
+
+    shape = (4, tok, part)
     return pl.pallas_call(
         body,
         out_shape=(jax.ShapeDtypeStruct(shape, jnp.float32),)
@@ -185,39 +168,34 @@
 
 
 def add_up(place, own, others):
-    def body(place_ref, own_ref, a_ref, b_ref, c_ref, keep_ref, give_ref):
-        mine = place_ref[4] // 2
-
+    def body(place_ref, own_ref, a_ref, b_ref, c_ref, *outs):
         @pl.when(place_ref[0] == 0)
         def _():
-            for at, out in ((mine, keep_ref), (1 - mine, give_ref)):
-                total = own_ref[at]
+            for chip, out in zip(partners(place_ref[4]), outs):
+                total = own_ref[chip]
                 for ref in (a_ref, b_ref, c_ref):
-                    total += ref[at].astype(jnp.float32)
+                    total += ref[chip].astype(jnp.float32)
                 out[...] = total.astype(out.dtype)
 
     return pl.pallas_call(
         body,
-        out_shape=(
-            jax.ShapeDtypeStruct(own.shape[1:], jnp.float32),
-            jax.ShapeDtypeStruct(own.shape[1:], jnp.bfloat16),
-        ),
+        out_shape=(jax.ShapeDtypeStruct(own.shape[1:], jnp.float32),)
+        + (jax.ShapeDtypeStruct(own.shape[1:], jnp.bfloat16),) * 3,
         in_specs=[smem_spec()] + [vmem_spec()] * 4,
-        out_specs=(vmem_spec(),) * 2,
+        out_specs=(vmem_spec(),) * 4,
         compiler_params=pltpu.CompilerParams(vmem_limit_bytes=24 * MIB),
         name="add_up",
     )(place, own, *others)
 
 
-def finish(place, resid, gate, kept, got):
-    part = kept.shape[1]
-
-    def body(place_ref, resid_ref, gate_ref, kept_ref, got_ref, out_ref):
+def finish(place, resid, gate, blocks):
+    part = blocks[0].shape[1]
+
+    def body(place_ref, resid_ref, gate_ref, b0, b1, b2, b3, out_ref):
         @pl.when(place_ref[0] == 0)
         def _():
-            for k, ref in enumerate((kept_ref, got_ref)):
-                half = jnp.bitwise_xor(place_ref[4] // 2, k)
-                at = pl.ds(pl.multiple_of(half * part, part), part)
+            for chip, ref in zip(partners(place_ref[4]), (b0, b1, b2, b3)):
+                at = pl.ds(pl.multiple_of(chip * part, part), part)
                 total = resid_ref[:, at].astype(jnp.float32)
                 total += gate_ref[:, at] * ref[...].astype(jnp.float32)
                 out_ref[:, at] = total.astype(jnp.bfloat16)
@@ -229,54 +207,66 @@
     return pl.pallas_call(
         body,
         out_shape=jax.ShapeDtypeStruct(resid.shape, jnp.bfloat16),
-        in_specs=[smem_spec()] + [vmem_spec()] * 4,
+        in_specs=[smem_spec()] + [vmem_spec()] * 6,
         out_specs=vmem_spec(),
         compiler_params=pltpu.CompilerParams(vmem_limit_bytes=16 * MIB),
         name="finish",
-    )(place, resid, gate, kept, got)
-
-
-def filter_weights(place, w_mid):
+    )(place, resid, gate, *blocks)
+
+
+def filter_weights(place, w_mid, start, count):
     steps, deep, vc = w_mid.shape
     taps = w_mid.reshape(steps, 3, 3, vc, vc)
 
     def block(w_ref, out_ref):
-        up, mid, down = (w_ref[0, n, 0] for n in range(3))
+        up, mid, down = (jnp.transpose(w_ref[0, n, 0]) for n in range(3))
         ends = 0.5 * (up.astype(jnp.float32) + down.astype(jnp.float32))
         half = 0.5 * mid.astype(jnp.float32)
         for n, g in enumerate((up, ends + half, ends - half, down)):
-            out_ref[n] = jnp.transpose(g.astype(jnp.bfloat16))
+            out_ref[n] = g.astype(jnp.bfloat16)
 
     def body(place_ref, w_ref, out_ref):
         @pl.when(place_ref[0] == 1)
         def _():
             pltpu.emit_pipeline(
                 block,
-                grid=(3 * steps,),
-                in_specs=[pl.BlockSpec((1, 3, 1, vc, vc), lambda i: (i // 3, 0, i % 3, 0, 0))],
+                grid=(count,),
+                in_specs=[
+                    pl.BlockSpec(
+                        (1, 3, 1, vc, vc), lambda i: ((i + start) // 3, 0, (i + start) % 3, 0, 0)
+                    )
+                ],
                 out_specs=[pl.BlockSpec((4, vc, vc), lambda i: (0, 0, i))],
             )(w_ref, out_ref)
 
     return pl.pallas_call(
         body,
-        out_shape=jax.ShapeDtypeStruct((4, vc, deep), jnp.bfloat16),
+        out_shape=jax.ShapeDtypeStruct((4, vc, count * vc), jnp.bfloat16),
         in_specs=[smem_spec(), pl.BlockSpec(memory_space=pl.ANY)],
         out_specs=pl.BlockSpec(memory_space=pl.ANY),
         compiler_params=pltpu.CompilerParams(vmem_limit_bytes=56 * MIB),
-        name="filter_weights",
+        name="filter_weights_%d" % start,
     )(place, taps)
 
 
-def decode(place, clip, w_first, filters, vectors):
+def decode(place, clip, w_in, filters, vectors):
     frames, _, lc, lw = clip.shape
-    vc = w_first.shape[0]
+    fan, vc = w_in.shape
     deep = 3 * vc
     lot = 4
-
-    def body(place_ref, clip_ref, w1_ref, f_ref, vec_ref, out_ref, lat, act, firsts, w2, both, sems):
+    wide = 512
+    cut = filters[0].shape[2]
+
+    def body(
+        place_ref, clip_ref, win_ref, fa_ref, fb_ref, rows_ref, out_ref,
+        lat, act, firsts, w1_ref, vec_ref, w2, both, sems,
+    ):
         step = pl.program_id(0)
         here = place_ref[0] == 1
-        loads = [pltpu.make_async_copy(f_ref.at[n], w2.at[n], sems.at[n]) for n in range(4)]
+        loads = [
+            pltpu.make_async_copy(fa_ref, w2.at[:, :, pl.ds(0, cut)], sems.at[0]),
+            pltpu.make_async_copy(fb_ref, w2.at[:, :, pl.ds(cut, 3 * deep - cut)], sems.at[1]),
+        ]
 
         def moved(x):
             lane = lax.broadcasted_iota(jnp.int32, x.shape, x.ndim - 1)
@@ -288,7 +278,7 @@
             sides = []
             for row in range(4):
                 taps = [lat[f + dt, row : row + 3].reshape(9 * lc, lw) for dt in range(3)]
-                taps.append(jnp.zeros((w1_ref.shape[1] - 27 * lc, lw), jnp.bfloat16))
+                taps.append(jnp.zeros((wide - fan, lw), jnp.bfloat16))
                 sides.append(jnp.concatenate(taps, axis=0))
             y = jnp.dot(
                 w1_ref[...], jnp.concatenate(sides, axis=1), preferred_element_type=jnp.float32
@@ -296,7 +286,6 @@
             acts = []
             for row in range(4):
                 hidden = y[:, row * lw : row * lw + lw] + vec_ref[0]
-                hidden = hidden.astype(jnp.bfloat16).astype(jnp.float32)
                 if row in (1, 2):
                     firsts[lax.rem(f, 2 * lot), row - 1] = hidden
                 factor = lax.rsqrt(jnp.mean(hidden * hidden, axis=0, keepdims=True) + EPS)
@@ -315,6 +304,11 @@
         def _():
             for load in loads:
                 load.start()
+            w1_ref[:, :fan] = jnp.transpose(win_ref[...])
+            w1_ref[:, fan:] = jnp.zeros((vc, wide - fan), jnp.bfloat16)
+            for n in range(3):
+                row = jnp.broadcast_to(rows_ref[n : n + 1], (lw, vc))
+                vec_ref[n] = jnp.transpose(row)
             lat[:2] = jnp.zeros((2, 6, 3 * lc, lw), jnp.bfloat16)
             act[:, :2] = jnp.zeros((4, 2, deep, lw), jnp.bfloat16)
             cells = clip_ref[...].astype(jnp.float32)
@@ -374,6 +368,7 @@
             vmem_spec(),
             vmem_spec(),
             pl.BlockSpec(memory_space=pl.ANY),
+            pl.BlockSpec(memory_space=pl.ANY),
             vmem_spec(),
         ],
         out_specs=pl.BlockSpec((lot, 2, lw, vc), lambda i: (i, 0, 0, 0)),
@@ -381,14 +376,16 @@
             pltpu.VMEM((frames + 2, 6, 3 * lc, lw), jnp.bfloat16),
             pltpu.VMEM((4, frames + 2, deep, lw), jnp.bfloat16),
             pltpu.VMEM((2 * lot, 2, vc, lw), jnp.float32),
+            pltpu.VMEM((vc, wide), jnp.bfloat16),
+            pltpu.VMEM((3, vc, lw), jnp.float32),
             pltpu.VMEM((4, vc, 3 * deep), jnp.bfloat16),
             pltpu.VMEM((2, vc, lot * lw), jnp.float32),
-            pltpu.SemaphoreType.DMA((4,)),
+            pltpu.SemaphoreType.DMA((2,)),
         ],
         compiler_params=pltpu.CompilerParams(vmem_limit_bytes=48 * MIB),
         cost_estimate=pl.CostEstimate(flops=0, bytes_accessed=0, transcendentals=0),
         name="decode",
-    )(place, clip, w_first, filters, vectors)
+    )(place, clip, w_in, *filters, vectors)
 
 
 def on_device(
@@ -443,41 +440,40 @@
     packed = norm_pack(
         query_input[0], key_input[0], value_input[0], query_norm_gain[None], key_norm_gain[None]
     )
-    packed, w_here = lax.optimization_barrier((packed, output_weight))
+    packed, w_here, latents, w_mid = lax.optimization_barrier((packed, output_weight, latents, w_mid))
     here = lax.all_to_all(packed, CHIPS, split_axis=0, concat_axis=0, tiled=True)
 
-    w_own, w_give = weight_halves(place, w_here, swap(w_here, 2, 0))
-    w_own, w_give, latents, w_mid = lax.optimization_barrier((w_own, w_give, latents, w_mid))
-    w_next, w_back = swap(w_own, 0, 0), swap(w_give, 0, 1)
-
+    w_there = swap(w_here, 2, 0)
     own = jnp.swapaxes(latents, 2, 3)
-    clip = jnp.concatenate(
-        [lax.ppermute(own, "grp", [(g, last)]) for g in range(last)] + [own], axis=0
-    )
+    pieces = [lax.ppermute(own, "grp", [(g, last)]) for g in range(last)]
+    early = filter_weights(place, w_mid, 0, 5)
+    pieces, early, w_there = lax.optimization_barrier((pieces, early, w_there))
+    weights = weight_blocks(place, w_here, w_there)
+    w_zero, w_one = swap(weights[1], 0, 0), swap(weights[2], 0, 1)
+    clip = jnp.concatenate(pieces + [own], axis=0)
     links = [(last * count + i, last * count + i + 1) for i in range(count - 1)]
     above = lax.ppermute(clip, ("grp",) + SEQ, links)
     below = lax.ppermute(clip, ("grp",) + SEQ, [(b, a) for a, b in links])
-    filters = filter_weights(place, w_mid)
-    above, below, filters = lax.optimization_barrier((above, below, filters))
+    late = filter_weights(place, w_mid, 5, 4)
+    above, below, late = lax.optimization_barrier((above, below, late))
     cells = jnp.concatenate([above, clip, below], axis=1)
-    w_first = jnp.pad(w_in.reshape(-1, channels).T, ((0, 0), (0, 512 - 27 * latents.shape[3])))
-    vectors = jnp.broadcast_to(
-        jnp.stack([b_in, norm_gain, b_mid])[:, :, None], (3, channels, latents.shape[2])
+
+    here, cells, w_zero, w_one = lax.optimization_barrier((here, cells, w_zero, w_one))
+    there = swap(here, 2, 0)
+    w_far = swap(weights[3], 0, 2)
+    heads = attend(place, here, there)
+    from_far = swap(heads, 0, 2)
+    heads = heads, swap(heads, 0, 0), swap(heads, 0, 1), from_far
+    mine, zero, one, far = project(place, heads, (weights[0], w_zero, w_one, w_far))
+    mine, zero, one, far, cells = lax.optimization_barrier((mine, zero, one, far, cells))
+    sums = swap(far, 1, 2), swap(zero, 1, 0), swap(one, 1, 1)
+    decoded = decode(
+        place, cells, w_in.reshape(-1, channels), (early, late), jnp.stack([b_in, norm_gain, b_mid])
     )
-
-    here, cells, w_next, w_back = lax.optimization_barrier((here, cells, w_next, w_back))
-    there = swap(here, 2, 0)
-    w_far = swap(w_back, 0, 0)
-    near, other = attend(place, here, there)
-    from_far = swap(other, 0, 2)
-    heads = near, swap(other, 0, 0), swap(near, 0, 1), from_far
-    mine, one, zero, far = project(place, heads, (w_own, w_next, w_back, w_far))
-    mine, one, zero, far, cells = lax.optimization_barrier((mine, one, zero, far, cells))
-    sums = swap(far, 1, 2), swap(one, 1, 1), swap(zero, 1, 0)
-    decoded = decode(place, cells, w_first, filters, vectors)
     mine, decoded = lax.optimization_barrier((mine, decoded))
-    kept, give = add_up(place, mine, sums)
-    attn_out = finish(place, resid[0], gate, kept, swap(give, 0, 1))
+    blocks = add_up(place, mine, sums)
+    blocks = (blocks[0],) + tuple(swap(blocks[n + 1], 0, n) for n in range(3))
+    attn_out = finish(place, resid[0], gate, blocks)
     return attn_out[None], decoded[None]
 
 

time: 103 us -> 106 us (1.029)
  starting transfers between devices: 50.2 us -> 59.1 us
  local copies, waits for them, and re-layouts: 5.18 us -> 1.05 us
  Pallas kernels: 20.8 us -> 19.6 us
    ppermute x12 -> x14, starting transfers between devices: 38.3 us -> 44.7 us  [swap(): return lax.ppermute(x, ('grp',) + SEQ, pairs)]
    ppermute x12 -> x14, waiting for transfers between devices: 18.2 us -> 21.7 us  [swap(): return lax.ppermute(x, ('grp',) + SEQ, pairs)]
    all_to_all x1, waiting for transfers between devices: 6.21 us -> 2.86 us  [on_device(): lax.all_to_all(packed, CHIPS, split_axis=0, concat_axis=0, tiled=True)]
    ppermute x3, starting transfers between devices: 2.62 us -> 5.05 us  [on_device(): pieces = [lax.ppermute(own, 'grp', [(g, last)]) for g in range(last)]]
    reshape x1 -> x0, local copies, waits for them, and re-layouts: 1.9 us -> none  [on_device(): w_in.reshape(-1, channels)]
    unnamed x24, local copies, waits for them, and re-layouts: 1.95 us -> 0.43 us
    pallas_call x3 -> x4, Pallas kernels: 8.88 us -> 8.82 us  [the longest x1 5.67 us: attend(): pl.pallas_call(body, grid=(chips // 4,), out_shape=jax.ShapeDtypeStruct((...]
  transfers between devices with their start and end apart: 18 -> 20, of which waited for: 8 -> 9; matrix products, arithmetic and copies ran while one was open for 3% -> 1% of each run, Pallas kernels for 11% -> 11%
where the time goes in v5:
time: 106 us; the launch traced here: 105 us
  starting transfers between devices  59.1 us (56%)
  waiting for transfers between devices  24.5 us (23%)
  Pallas kernels  19.6 us (18%)
  between operations  1.12 us (1%)
    ppermute x14, starting transfers between devices, swap(): return lax.ppermute(x, ('grp',) + SEQ, pairs)  44.7 us
    ppermute x14, waiting for transfers between devices, swap(): return lax.ppermute(x, ('grp',) + SEQ, pairs)  21.7 us
    all_to_all x1, starting transfers between devices, on_device(): lax.all_to_all(packed, CHIPS, split_axis=0, concat_axis=0, tiled=True)  7.97 us
    pallas_call x1, Pallas kernels, attend(): pl.pallas_call(body, grid=(chips // 4,), out_shape=jax.ShapeDtypeStruct((...  5.67 us
    ppermute x3, starting transfers between devices, on_device(): pieces = [lax.ppermute(own, 'grp', [(g, last)]) for g in range(last)]  5.05 us
    pallas_call x1, Pallas kernels, norm_pack(): pl.pallas_call(body, grid=(rows // block,), out_shape=jax.ShapeDtypeStruc...  3.48 us
    all_to_all x1, waiting for transfers between devices, on_device(): lax.all_to_all(packed, CHIPS, split_axis=0, concat_axis=0, tiled=True)  2.86 us
    pallas_call x1, Pallas kernels, decode(): pl.pallas_call(body, grid=(frames // lot,), out_shape=jax.ShapeDtypeStruc...  2.78 us
  transfers between devices with their start and end apart: 20, of which 9 were waited for; matrix products, arithmetic and copies ran while one was open for 1% of the time, Pallas kernels for 11%

profile of v5, /device:TPU:0, one launch (start us, length us, event | category | flops | bytes accessed | tf_op | source)
XLA Modules:
  0.0 105.4 jit_solution(8024085584648413367)
XLA Ops:
  0.6 3.5 %norm_pack.1 = bf16[16,3,48,256]{3,2,1,0:T(8,128)(2,1)} custom-call(bf16[48,4096]{1,0:T(8,128)(2,1)} %bitcast.21, bf16[48,4096]{1,0:T(8,128)(2,1)} %bitcast.22, bf16[48,4096]{1,0:T(8,128)(2,1)} %bitcast.23, f32[1,4096]{1,0:T(1,128)} %bitcast.30, f32[1,4096]{1,0:T(1,128)} %bitcast.31), custom_call_target="tpu_custom_call" | custom-call | tf_op jit(solution)/shard_map/norm_pack/pallas_call | solution.py:45
  6.0 8.0 %all-to-all-start = ((bf16[16,3,48,256]{3,2,1,0:T(8,128)(2,1)}), bf16[16,3,48,256]{3,2,1,0:T(8,128)(2,1)S(1)}, u32[]{:S(2)}, u32[]{:S(2)}) async-start(bf16[16,3,48,256]{3,2,1,0:T(8,128)(2,1)} %norm_pack.1), calls=%async_computation | async-start | bytes 2359296 | tf_op jit(solution)/shard_map/all_to_all | solution.py:444
  14.0 3.7 %collective-permute-start = (bf16[4,2,16,128]{3,2,1,0:T(8,128)(2,1)S(1)}, bf16[4,2,16,128]{3,2,1,0:T(8,128)(2,1)S(1)}, u32[]{:S(2)}, u32[]{:S(2)}) collective-permute-start(bf16[4,2,16,128]{3,2,1,0:T(8,128)(2,1)S(1)} %bitcast.25), channel_id=1, source_target_pairs={{0,96},{1,97},{2,98},{3,99},{4,100},{5,101},{6,102},{7,103},{8,104... | collective-permute-start | bytes 98312 | tf_op jit(solution)/shard_map/ppermute | solution.py:448
  22.6 3.8 %collective-permute-start.6 = (bf16[256,1024]{1,0:T(8,128)(2,1)}, bf16[256,1024]{1,0:T(8,128)(2,1)S(1)}, u32[]{:S(2)}, u32[]{:S(2)}) collective-permute-start(bf16[256,1024]{1,0:T(8,128)(2,1)} %get-tuple-element.47), channel_id=1, source_target_pairs={{0,8},{1,3},{2,10},{3,1},{4,12},{5,7},{6,14},{7,5},{8,0},{9,11},{1... | collective-permute-start | bytes 1572872 | tf_op jit(solution)/shard_map/ppermute | solution.py:438
  26.5 4.0 %collective-permute-start.7 = (bf16[256,1024]{1,0:T(8,128)(2,1)}, bf16[256,1024]{1,0:T(8,128)(2,1)S(1)}, u32[]{:S(2)}, u32[]{:S(2)}) collective-permute-start(bf16[256,1024]{1,0:T(8,128)(2,1)} %get-tuple-element.48), channel_id=1, source_target_pairs={{0,24},{1,7},{2,26},{3,5},{4,28},{5,3},{6,30},{7,1},{8,16},{9,15},... | collective-permute-start | bytes 1572872 | tf_op jit(solution)/shard_map/ppermute | solution.py:438
  32.6 2.9 %all-to-all-done.here_ref = bf16[16,3,48,256]{3,2,1,0:T(8,128)(2,1)S(1)} async-done(((bf16[16,3,48,256]{3,2,1,0:T(8,128)(2,1)}), bf16[16,3,48,256]{3,2,1,0:T(8,128)(2,1)S(1)}, u32[]{:S(2)}, u32[]{:S(2)}) %all-to-all-start) | async-done | bytes 1179680 | tf_op jit(solution)/shard_map/all_to_all | solution.py:444
  36.3 3.7 %collective-permute-done.7.w2 = bf16[256,1024]{1,0:T(8,128)(2,1)S(1)} collective-permute-done((bf16[256,1024]{1,0:T(8,128)(2,1)}, bf16[256,1024]{1,0:T(8,128)(2,1)S(1)}, u32[]{:S(2)}, u32[]{:S(2)}) %collective-permute-start.7) | collective-permute-done | bytes 524320 | tf_op jit(solution)/shard_map/ppermute | solution.py:438
  41.9 3.2 %collective-permute-start.12 = (bf16[256,1024]{1,0:T(8,128)(2,1)}, bf16[256,1024]{1,0:T(8,128)(2,1)S(1)}, u32[]{:S(2)}, u32[]{:S(2)}) collective-permute-start(bf16[256,1024]{1,0:T(8,128)(2,1)} %copy-done.7), channel_id=1, source_target_pairs={{0,16},{1,5},{2,18},{3,7},{4,20},{5,1},{6,22},{7,3},{8,24},{9,13},... | collective-permute-start | bytes 1572872 | tf_op jit(solution)/shard_map/ppermute | solution.py:438
  45.1 5.7 %attend.1.h0 = bf16[16,48,256]{2,1,0:T(8,128)(2,1)S(1)} custom-call(s32[6]{0:T(128)S(1)} %copy-done.5, bf16[16,3,48,256]{3,2,1,0:T(8,128)(2,1)S(1)} %all-to-all-done.here_ref, bf16[16,3,48,256]{3,2,1,0:T(8,128)(2,1)S(1)} %collective-permute-done.8.there_ref), custom_call_target="tpu_custom_call" | custom-call | tf_op jit(solution)/shard_map/attend/pallas_call | solution.py:121
  50.9 2.8 %collective-permute-start.10 = (bf16[16,48,256]{2,1,0:T(8,128)(2,1)S(1)}, bf16[16,48,256]{2,1,0:T(8,128)(2,1)S(1)}, u32[]{:S(2)}, u32[]{:S(2)}) collective-permute-start(bf16[16,48,256]{2,1,0:T(8,128)(2,1)S(1)} %attend.1.h0), channel_id=1, source_target_pairs={{0,24},{1,7},{2,26},{3,5},{4,28},{5,3},{6,30},{7,1},{8,16},{9,15},... | collective-permute-start | bytes 1179656 | tf_op jit(solution)/shard_map/ppermute | solution.py:438
  53.7 4.0 %collective-permute-start.11 = (bf16[16,48,256]{2,1,0:T(8,128)(2,1)S(1)}, bf16[16,48,256]{2,1,0:T(8,128)(2,1)S(1)}, u32[]{:S(2)}, u32[]{:S(2)}) collective-permute-start(bf16[16,48,256]{2,1,0:T(8,128)(2,1)S(1)} %attend.1.h0), channel_id=1, source_target_pairs={{0,16},{1,5},{2,18},{3,7},{4,20},{5,1},{6,22},{7,3},{8,24},{9,13},... | collective-permute-start | bytes 1179656 | tf_op jit(solution)/shard_map/ppermute | solution.py:438
  57.6 3.3 %collective-permute-start.9 = (bf16[16,48,256]{2,1,0:T(8,128)(2,1)S(1)}, bf16[16,48,256]{2,1,0:T(8,128)(2,1)S(1)}, u32[]{:S(2)}, u32[]{:S(2)}) collective-permute-start(bf16[16,48,256]{2,1,0:T(8,128)(2,1)S(1)} %attend.1.h0), channel_id=1, source_target_pairs={{0,8},{1,3},{2,10},{3,1},{4,12},{5,7},{6,14},{7,5},{8,0},{9,11},{1... | collective-permute-start | bytes 1179656 | tf_op jit(solution)/shard_map/ppermute | solution.py:438
  61.0 5.2 %collective-permute-done.10.h2 = bf16[16,48,256]{2,1,0:T(8,128)(2,1)S(1)} collective-permute-done((bf16[16,48,256]{2,1,0:T(8,128)(2,1)S(1)}, bf16[16,48,256]{2,1,0:T(8,128)(2,1)S(1)}, u32[]{:S(2)}, u32[]{:S(2)}) %collective-permute-start.10) | collective-permute-done | bytes 393248 | tf_op jit(solution)/shard_map/ppermute | solution.py:438
  66.2 2.8 %collective-permute-done.9.h1 = bf16[16,48,256]{2,1,0:T(8,128)(2,1)S(1)} collective-permute-done((bf16[16,48,256]{2,1,0:T(8,128)(2,1)S(1)}, bf16[16,48,256]{2,1,0:T(8,128)(2,1)S(1)}, u32[]{:S(2)}, u32[]{:S(2)}) %collective-permute-start.9) | collective-permute-done | bytes 393248 | tf_op jit(solution)/shard_map/ppermute | solution.py:438
  69.0 2.3 %project.1 = (f32[4,48,1024]{2,1,0:T(8,128)S(1)}, bf16[4,48,1024]{2,1,0:T(8,128)(2,1)S(1)}, bf16[4,48,1024]{2,1,0:T(8,128)(2,1)S(1)}, bf16[4,48,1024]{2,1,0:T(8,128)(2,1)S(1)}) custom-call(s32[6]{0:T(128)S(1)} %copy-done.5, bf16[16,48,256]{2,1,0:T(8,128)(2,1)S(1)} %attend.1.h0, bf16[16,48,256]{2,1,0:T(8,128)(2,1)S(1)} %collective-permute-done.9.h1, ...), custom_call_target="tpu_custom_call" | custom-call | flops 1610612736 | bytes 8388608 | tf_op jit(solution)/shard_map/project/pallas_call | solution.py:156
  71.4 4.1 %collective-permute-start.13 = (bf16[4,48,1024]{2,1,0:T(8,128)(2,1)S(1)}, bf16[4,48,1024]{2,1,0:T(8,128)(2,1)S(1)}, u32[]{:S(2)}, u32[]{:S(2)}) collective-permute-start(bf16[4,48,1024]{2,1,0:T(8,128)(2,1)S(1)} %get-tuple-element.64), channel_id=1, source_target_pairs={{0,4},{1,17},{2,6},{3,19},{4,0},{5,21},{6,2},{7,23},{8,12},{9,25},... | collective-permute-start | bytes 1179656 | tf_op jit(solution)/shard_map/ppermute | solution.py:438
  75.4 2.5 %collective-permute-start.14 = (bf16[4,48,1024]{2,1,0:T(8,128)(2,1)S(1)}, bf16[4,48,1024]{2,1,0:T(8,128)(2,1)S(1)}, u32[]{:S(2)}, u32[]{:S(2)}) collective-permute-start(bf16[4,48,1024]{2,1,0:T(8,128)(2,1)S(1)} %get-tuple-element.65), channel_id=1, source_target_pairs={{0,2},{1,9},{2,0},{3,11},{4,6},{5,13},{6,4},{7,15},{8,10},{9,1},{1... | collective-permute-start | bytes 1179656 | tf_op jit(solution)/shard_map/ppermute | solution.py:438
  77.9 3.5 %collective-permute-start.15 = (bf16[4,48,1024]{2,1,0:T(8,128)(2,1)S(1)}, bf16[4,48,1024]{2,1,0:T(8,128)(2,1)S(1)}, u32[]{:S(2)}, u32[]{:S(2)}) collective-permute-start(bf16[4,48,1024]{2,1,0:T(8,128)(2,1)S(1)} %get-tuple-element.66), channel_id=1, source_target_pairs={{0,6},{1,25},{2,4},{3,27},{4,2},{5,29},{6,0},{7,31},{8,14},{9,17},... | collective-permute-start | bytes 1179656 | tf_op jit(solution)/shard_map/ppermute | solution.py:438
  81.5 2.8 %decode.1 = bf16[16,2,128,384]{3,2,1,0:T(8,128)(2,1)} custom-call(s32[6]{0:T(128)S(1)} %copy-done.5, bf16[16,6,16,128]{3,2,1,0:T(8,128)(2,1)S(1)} %pad_maximum_fusion.clip_ref, bf16[432,384]{1,0:T(8,128)(2,1)S(1)} %bitcast.17, bf16[4,384,1920]{2,1,0:T(8,128)(2,1)} %filter_weights_0.1.fa_ref, bf16[4,384,1536]{2,1,0:T(8,128)(2,1)S(1)} %copy-done, ...), custom_call_target="tpu_custom_call" | custom-call | tf_op jit(solution)/shard_map/decode/pallas_call | solution.py:362
  85.9 2.9 %collective-permute-done.15.c_ref = bf16[4,48,1024]{2,1,0:T(8,128)(2,1)S(1)} collective-permute-done((bf16[4,48,1024]{2,1,0:T(8,128)(2,1)S(1)}, bf16[4,48,1024]{2,1,0:T(8,128)(2,1)S(1)}, u32[]{:S(2)}, u32[]{:S(2)}) %collective-permute-start.15) | collective-permute-done | bytes 393248 | tf_op jit(solution)/shard_map/ppermute | solution.py:438
  89.5 3.3 %collective-permute-start.16 = (bf16[48,1024]{1,0:T(8,128)(2,1)S(1)}, bf16[48,1024]{1,0:T(8,128)(2,1)S(1)}, u32[]{:S(2)}, u32[]{:S(2)}) collective-permute-start(bf16[48,1024]{1,0:T(8,128)(2,1)S(1)} %get-tuple-element.68), channel_id=1, source_target_pairs={{0,8},{1,3},{2,10},{3,1},{4,12},{5,7},{6,14},{7,5},{8,0},{9,11},{1... | collective-permute-start | bytes 294920 | tf_op jit(solution)/shard_map/ppermute | solution.py:438
  92.8 3.1 %collective-permute-start.17 = (bf16[48,1024]{1,0:T(8,128)(2,1)S(1)}, bf16[48,1024]{1,0:T(8,128)(2,1)S(1)}, u32[]{:S(2)}, u32[]{:S(2)}) collective-permute-start(bf16[48,1024]{1,0:T(8,128)(2,1)S(1)} %get-tuple-element.69), channel_id=1, source_target_pairs={{0,24},{1,7},{2,26},{3,5},{4,28},{5,3},{6,30},{7,1},{8,16},{9,15},... | collective-permute-start | bytes 294920 | tf_op jit(solution)/shard_map/ppermute | solution.py:438
  96.0 3.4 %collective-permute-start.18 = (bf16[48,1024]{1,0:T(8,128)(2,1)S(1)}, bf16[48,1024]{1,0:T(8,128)(2,1)S(1)}, u32[]{:S(2)}, u32[]{:S(2)}) collective-permute-start(bf16[48,1024]{1,0:T(8,128)(2,1)S(1)} %get-tuple-element.70), channel_id=1, source_target_pairs={{0,16},{1,5},{2,18},{3,7},{4,20},{5,1},{6,22},{7,3},{8,24},{9,13},... | collective-permute-start | bytes 294920 | tf_op jit(solution)/shard_map/ppermute | solution.py:438
  100.6 3.4 %collective-permute-done.18.b3 = bf16[48,1024]{1,0:T(8,128)(2,1)S(1)} collective-permute-done((bf16[48,1024]{1,0:T(8,128)(2,1)S(1)}, bf16[48,1024]{1,0:T(8,128)(2,1)S(1)}, u32[]{:S(2)}, u32[]{:S(2)}) %collective-permute-start.18) | collective-permute-done | bytes 98336 | tf_op jit(solution)/shard_map/ppermute | solution.py:438
  (56 shorter events, 16.6 us)
Async XLA Ops:
  4.1 16.5 %collective-permute-start.3 = (bf16[128,4096]{1,0:T(8,128)(2,1)}, bf16[128,4096]{1,0:T(8,128)(2,1)S(1)}, u32[]{:S(2)}, u32[]{:S(2)}) collective-permute-start(bf16[128,4096]{1,0:T(8,128)(2,1)} %here_ref), channel_id=1, source_target_pairs={{0,1},{1,0},{2,3},{3,2},{4,5},{5,4},{6,7},{7,6},{8,9},{9,8},{10,11... | collective-permute-start | bytes 3145736 | tf_op jit(solution)/shard_map/ppermute | solution.py:438
  6.0 29.4 %all-to-all-start = ((bf16[16,3,48,256]{3,2,1,0:T(8,128)(2,1)}), bf16[16,3,48,256]{3,2,1,0:T(8,128)(2,1)S(1)}, u32[]{:S(2)}, u32[]{:S(2)}) async-start(bf16[16,3,48,256]{3,2,1,0:T(8,128)(2,1)} %norm_pack.1), calls=%async_computation | async-start | bytes 2359296 | tf_op jit(solution)/shard_map/all_to_all | solution.py:444
  14.0 6.5 %collective-permute-start = (bf16[4,2,16,128]{3,2,1,0:T(8,128)(2,1)S(1)}, bf16[4,2,16,128]{3,2,1,0:T(8,128)(2,1)S(1)}, u32[]{:S(2)}, u32[]{:S(2)}) collective-permute-start(bf16[4,2,16,128]{3,2,1,0:T(8,128)(2,1)S(1)} %bitcast.25), channel_id=1, source_target_pairs={{0,96},{1,97},{2,98},{3,99},{4,100},{5,101},{6,102},{7,103},{8,104... | collective-permute-start | bytes 98312 | tf_op jit(solution)/shard_map/ppermute | solution.py:448
  17.8 2.8 %collective-permute-start.1 = (bf16[4,2,16,128]{3,2,1,0:T(8,128)(2,1)S(1)}, bf16[4,2,16,128]{3,2,1,0:T(8,128)(2,1)S(1)}, u32[]{:S(2)}, u32[]{:S(2)}) collective-permute-start(bf16[4,2,16,128]{3,2,1,0:T(8,128)(2,1)S(1)} %bitcast.26), channel_id=1, source_target_pairs={{32,96},{33,97},{34,98},{35,99},{36,100},{37,101},{38,102},{39,103... | collective-permute-start | bytes 98312 | tf_op jit(solution)/shard_map/ppermute | solution.py:448
  18.4 2.1 %collective-permute-start.2 = (bf16[4,2,16,128]{3,2,1,0:T(8,128)(2,1)S(1)}, bf16[4,2,16,128]{3,2,1,0:T(8,128)(2,1)S(1)}, u32[]{:S(2)}, u32[]{:S(2)}) collective-permute-start(bf16[4,2,16,128]{3,2,1,0:T(8,128)(2,1)S(1)} %bitcast.27), channel_id=1, source_target_pairs={{64,96},{65,97},{66,98},{67,99},{68,100},{69,101},{70,102},{71,103... | collective-permute-start | bytes 98312 | tf_op jit(solution)/shard_map/ppermute | solution.py:448
  22.6 13.7 %collective-permute-start.6 = (bf16[256,1024]{1,0:T(8,128)(2,1)}, bf16[256,1024]{1,0:T(8,128)(2,1)S(1)}, u32[]{:S(2)}, u32[]{:S(2)}) collective-permute-start(bf16[256,1024]{1,0:T(8,128)(2,1)} %get-tuple-element.47), channel_id=1, source_target_pairs={{0,8},{1,3},{2,10},{3,1},{4,12},{5,7},{6,14},{7,5},{8,0},{9,11},{1... | collective-permute-start | bytes 1572872 | tf_op jit(solution)/shard_map/ppermute | solution.py:438
  26.5 13.5 %collective-permute-start.7 = (bf16[256,1024]{1,0:T(8,128)(2,1)}, bf16[256,1024]{1,0:T(8,128)(2,1)S(1)}, u32[]{:S(2)}, u32[]{:S(2)}) collective-permute-start(bf16[256,1024]{1,0:T(8,128)(2,1)} %get-tuple-element.48), channel_id=1, source_target_pairs={{0,24},{1,7},{2,26},{3,5},{4,28},{5,3},{6,30},{7,1},{8,16},{9,15},... | collective-permute-start | bytes 1572872 | tf_op jit(solution)/shard_map/ppermute | solution.py:438
  30.5 2.0 %collective-permute-start.4 = (bf16[16,2,16,128]{3,2,1,0:T(8,128)(2,1)S(1)}, bf16[16,2,16,128]{3,2,1,0:T(8,128)(2,1)S(1)}, u32[]{:S(2)}, u32[]{:S(2)}) collective-permute-start(bf16[16,2,16,128]{3,2,1,0:T(8,128)(2,1)S(1)} %pad_maximum_fusion.1), channel_id=1, source_target_pairs={{96,97},{97,98},{98,99},{99,100},{100,101},{101,102},{102,103},{10... | collective-permute-start | bytes 393224 | tf_op jit(solution)/shard_map/ppermute | solution.py:455
  31.2 1.4 %collective-permute-start.5 = (bf16[16,2,16,128]{3,2,1,0:T(8,128)(2,1)S(1)}, bf16[16,2,16,128]{3,2,1,0:T(8,128)(2,1)S(1)}, u32[]{:S(2)}, u32[]{:S(2)}) collective-permute-start(bf16[16,2,16,128]{3,2,1,0:T(8,128)(2,1)S(1)} %pad_maximum_fusion.1), channel_id=1, source_target_pairs={{97,96},{98,97},{99,98},{100,99},{101,100},{102,101},{103,102},{10... | collective-permute-start | bytes 393224 | tf_op jit(solution)/shard_map/ppermute | solution.py:456
  40.0 5.1 %collective-permute-start.8 = (bf16[16,3,48,256]{3,2,1,0:T(8,128)(2,1)S(1)}, bf16[16,3,48,256]{3,2,1,0:T(8,128)(2,1)S(1)}, u32[]{:S(2)}, u32[]{:S(2)}) collective-permute-start(bf16[16,3,48,256]{3,2,1,0:T(8,128)(2,1)S(1)} %all-to-all-done.here_ref), channel_id=1, source_target_pairs={{0,1},{1,0},{2,3},{3,2},{4,5},{5,4},{6,7},{7,6},{8,9},{9,8},{10,11... | collective-permute-start | bytes 3538952 | tf_op jit(solution)/shard_map/ppermute | solution.py:438
  41.9 19.0 %collective-permute-start.12 = (bf16[256,1024]{1,0:T(8,128)(2,1)}, bf16[256,1024]{1,0:T(8,128)(2,1)S(1)}, u32[]{:S(2)}, u32[]{:S(2)}) collective-permute-start(bf16[256,1024]{1,0:T(8,128)(2,1)} %copy-done.7), channel_id=1, source_target_pairs={{0,16},{1,5},{2,18},{3,7},{4,20},{5,1},{6,22},{7,3},{8,24},{9,13},... | collective-permute-start | bytes 1572872 | tf_op jit(solution)/shard_map/ppermute | solution.py:438
  50.8 30.6 %copy-start.10 = (f32[384]{0:T(512)S(1)}, f32[384]{0:T(512)}, u32[]{:S(2)}) copy-start(f32[384]{0:T(512)} %param.25) | copy-start | bytes 4612
  50.8 30.6 %copy-start.11 = (f32[384]{0:T(512)S(1)}, f32[384]{0:T(512)}, u32[]{:S(2)}) copy-start(f32[384]{0:T(512)} %param.27) | copy-start | bytes 4612
  50.9 30.6 %copy-start = (bf16[4,384,1536]{2,1,0:T(8,128)(2,1)S(1)}, bf16[4,384,1536]{2,1,0:T(8,128)(2,1)}, u32[]{:S(2)}) copy-start(bf16[4,384,1536]{2,1,0:T(8,128)(2,1)} %filter_weights_5.1.fb_ref) | copy-start | bytes 14155780
  50.9 30.6 %copy-start.3 = (bf16[3,144,384]{2,1,0:T(8,128)(2,1)S(1)}, bf16[3,144,384]{2,1,0:T(8,128)(2,1)}, u32[]{:S(2)}) copy-start(bf16[3,144,384]{2,1,0:T(8,128)(2,1)} %param.23) | copy-start | bytes 995332
  50.9 15.4 %collective-permute-start.10 = (bf16[16,48,256]{2,1,0:T(8,128)(2,1)S(1)}, bf16[16,48,256]{2,1,0:T(8,128)(2,1)S(1)}, u32[]{:S(2)}, u32[]{:S(2)}) collective-permute-start(bf16[16,48,256]{2,1,0:T(8,128)(2,1)S(1)} %attend.1.h0), channel_id=1, source_target_pairs={{0,24},{1,7},{2,26},{3,5},{4,28},{5,3},{6,30},{7,1},{8,16},{9,15},... | collective-permute-start | bytes 1179656 | tf_op jit(solution)/shard_map/ppermute | solution.py:438
  53.7 12.6 %collective-permute-start.11 = (bf16[16,48,256]{2,1,0:T(8,128)(2,1)S(1)}, bf16[16,48,256]{2,1,0:T(8,128)(2,1)S(1)}, u32[]{:S(2)}, u32[]{:S(2)}) collective-permute-start(bf16[16,48,256]{2,1,0:T(8,128)(2,1)S(1)} %attend.1.h0), channel_id=1, source_target_pairs={{0,16},{1,5},{2,18},{3,7},{4,20},{5,1},{6,22},{7,3},{8,24},{9,13},... | collective-permute-start | bytes 1179656 | tf_op jit(solution)/shard_map/ppermute | solution.py:438
  57.6 11.4 %collective-permute-start.9 = (bf16[16,48,256]{2,1,0:T(8,128)(2,1)S(1)}, bf16[16,48,256]{2,1,0:T(8,128)(2,1)S(1)}, u32[]{:S(2)}, u32[]{:S(2)}) collective-permute-start(bf16[16,48,256]{2,1,0:T(8,128)(2,1)S(1)} %attend.1.h0), channel_id=1, source_target_pairs={{0,8},{1,3},{2,10},{3,1},{4,12},{5,7},{6,14},{7,5},{8,0},{9,11},{1... | collective-permute-start | bytes 1179656 | tf_op jit(solution)/shard_map/ppermute | solution.py:438
  71.4 12.9 %collective-permute-start.13 = (bf16[4,48,1024]{2,1,0:T(8,128)(2,1)S(1)}, bf16[4,48,1024]{2,1,0:T(8,128)(2,1)S(1)}, u32[]{:S(2)}, u32[]{:S(2)}) collective-permute-start(bf16[4,48,1024]{2,1,0:T(8,128)(2,1)S(1)} %get-tuple-element.64), channel_id=1, source_target_pairs={{0,4},{1,17},{2,6},{3,19},{4,0},{5,21},{6,2},{7,23},{8,12},{9,25},... | collective-permute-start | bytes 1179656 | tf_op jit(solution)/shard_map/ppermute | solution.py:438
  75.4 10.5 %collective-permute-start.14 = (bf16[4,48,1024]{2,1,0:T(8,128)(2,1)S(1)}, bf16[4,48,1024]{2,1,0:T(8,128)(2,1)S(1)}, u32[]{:S(2)}, u32[]{:S(2)}) collective-permute-start(bf16[4,48,1024]{2,1,0:T(8,128)(2,1)S(1)} %get-tuple-element.65), channel_id=1, source_target_pairs={{0,2},{1,9},{2,0},{3,11},{4,6},{5,13},{6,4},{7,15},{8,10},{9,1},{1... | collective-permute-start | bytes 1179656 | tf_op jit(solution)/shard_map/ppermute | solution.py:438
  77.9 10.9 %collective-permute-start.15 = (bf16[4,48,1024]{2,1,0:T(8,128)(2,1)S(1)}, bf16[4,48,1024]{2,1,0:T(8,128)(2,1)S(1)}, u32[]{:S(2)}, u32[]{:S(2)}) collective-permute-start(bf16[4,48,1024]{2,1,0:T(8,128)(2,1)S(1)} %get-tuple-element.66), channel_id=1, source_target_pairs={{0,6},{1,25},{2,4},{3,27},{4,2},{5,29},{6,0},{7,31},{8,14},{9,17},... | collective-permute-start | bytes 1179656 | tf_op jit(solution)/shard_map/ppermute | solution.py:438
  89.5 9.8 %collective-permute-start.16 = (bf16[48,1024]{1,0:T(8,128)(2,1)S(1)}, bf16[48,1024]{1,0:T(8,128)(2,1)S(1)}, u32[]{:S(2)}, u32[]{:S(2)}) collective-permute-start(bf16[48,1024]{1,0:T(8,128)(2,1)S(1)} %get-tuple-element.68), channel_id=1, source_target_pairs={{0,8},{1,3},{2,10},{3,1},{4,12},{5,7},{6,14},{7,5},{8,0},{9,11},{1... | collective-permute-start | bytes 294920 | tf_op jit(solution)/shard_map/ppermute | solution.py:438
  92.8 7.7 %collective-permute-start.17 = (bf16[48,1024]{1,0:T(8,128)(2,1)S(1)}, bf16[48,1024]{1,0:T(8,128)(2,1)S(1)}, u32[]{:S(2)}, u32[]{:S(2)}) collective-permute-start(bf16[48,1024]{1,0:T(8,128)(2,1)S(1)} %get-tuple-element.69), channel_id=1, source_target_pairs={{0,24},{1,7},{2,26},{3,5},{4,28},{5,3},{6,30},{7,1},{8,16},{9,15},... | collective-permute-start | bytes 294920 | tf_op jit(solution)/shard_map/ppermute | solution.py:438
  96.0 8.0 %collective-permute-start.18 = (bf16[48,1024]{1,0:T(8,128)(2,1)S(1)}, bf16[48,1024]{1,0:T(8,128)(2,1)S(1)}, u32[]{:S(2)}, u32[]{:S(2)}) collective-permute-start(bf16[48,1024]{1,0:T(8,128)(2,1)S(1)} %get-tuple-element.70), channel_id=1, source_target_pairs={{0,16},{1,5},{2,18},{3,7},{4,20},{5,1},{6,22},{7,3},{8,24},{9,13},... | collective-permute-start | bytes 294920 | tf_op jit(solution)/shard_map/ppermute | solution.py:438
  (8 other events, 115.9 us)

commit v6 on v4

--- a/solution.py
+++ b/solution.py
@@ -100,16 +100,16 @@
                 scores = [
                     lax.dot_general(
                         queries[:, cols],
-                        ref[:, 1, :, cols].reshape(half, 128),
+                        ref[:, at, :, cols].reshape(half, 128),
                         (((1,), (1,)), ((), ())),
                         preferred_element_type=jnp.float32,
                     )
-                    for ref in (here_ref, there_ref)
+                    for ref, at in ((here_ref, 1), (there_ref, 0))
                 ]
                 peak = jnp.maximum(*(jnp.max(s, axis=-1, keepdims=True) for s in scores))
                 o = None
-                for s, ref in zip(scores, (here_ref, there_ref)):
-                    values = jnp.concatenate([ref[:, 2, :, cols].reshape(half, 128), ones], axis=1)
+                for s, ref, at in zip(scores, (here_ref, there_ref), (2, 1)):
+                    values = jnp.concatenate([ref[:, at, :, cols].reshape(half, 128), ones], axis=1)
                     p = jnp.exp2(s - peak).astype(jnp.bfloat16)
                     part = jnp.dot(p, values, preferred_element_type=jnp.float32)
                     o = part if o is None else o + part
@@ -236,47 +236,59 @@
     )(place, resid, gate, kept, got)
 
 
-def filter_weights(place, w_mid):
+def filter_weights(place, w_mid, start, count):
     steps, deep, vc = w_mid.shape
     taps = w_mid.reshape(steps, 3, 3, vc, vc)
 
     def block(w_ref, out_ref):
-        up, mid, down = (w_ref[0, n, 0] for n in range(3))
+        up, mid, down = (jnp.transpose(w_ref[0, n, 0]) for n in range(3))
         ends = 0.5 * (up.astype(jnp.float32) + down.astype(jnp.float32))
         half = 0.5 * mid.astype(jnp.float32)
         for n, g in enumerate((up, ends + half, ends - half, down)):
-            out_ref[n] = jnp.transpose(g.astype(jnp.bfloat16))
+            out_ref[n] = g.astype(jnp.bfloat16)
 
     def body(place_ref, w_ref, out_ref):
         @pl.when(place_ref[0] == 1)
         def _():
             pltpu.emit_pipeline(
                 block,
-                grid=(3 * steps,),
-                in_specs=[pl.BlockSpec((1, 3, 1, vc, vc), lambda i: (i // 3, 0, i % 3, 0, 0))],
+                grid=(count,),
+                in_specs=[
+                    pl.BlockSpec(
+                        (1, 3, 1, vc, vc), lambda i: ((i + start) // 3, 0, (i + start) % 3, 0, 0)
+                    )
+                ],
                 out_specs=[pl.BlockSpec((4, vc, vc), lambda i: (0, 0, i))],
             )(w_ref, out_ref)
 
     return pl.pallas_call(
         body,
-        out_shape=jax.ShapeDtypeStruct((4, vc, deep), jnp.bfloat16),
+        out_shape=jax.ShapeDtypeStruct((4, vc, count * vc), jnp.bfloat16),
         in_specs=[smem_spec(), pl.BlockSpec(memory_space=pl.ANY)],
         out_specs=pl.BlockSpec(memory_space=pl.ANY),
         compiler_params=pltpu.CompilerParams(vmem_limit_bytes=56 * MIB),
-        name="filter_weights",
+        name="filter_weights_%d" % start,
     )(place, taps)
 
 
-def decode(place, clip, w_first, filters, vectors):
+def decode(place, clip, w_in, filters, vectors):
     frames, _, lc, lw = clip.shape
-    vc = w_first.shape[0]
+    fan, vc = w_in.shape
     deep = 3 * vc
     lot = 4
-
-    def body(place_ref, clip_ref, w1_ref, f_ref, vec_ref, out_ref, lat, act, firsts, w2, both, sems):
+    wide = 512
+    cut = filters[0].shape[2]
+
+    def body(
+        place_ref, clip_ref, win_ref, fa_ref, fb_ref, rows_ref, out_ref,
+        lat, act, firsts, w1_ref, vec_ref, w2, both, sems,
+    ):
         step = pl.program_id(0)
         here = place_ref[0] == 1
-        loads = [pltpu.make_async_copy(f_ref.at[n], w2.at[n], sems.at[n]) for n in range(4)]
+        loads = [
+            pltpu.make_async_copy(fa_ref, w2.at[:, :, pl.ds(0, cut)], sems.at[0]),
+            pltpu.make_async_copy(fb_ref, w2.at[:, :, pl.ds(cut, 3 * deep - cut)], sems.at[1]),
+        ]
 
         def moved(x):
             lane = lax.broadcasted_iota(jnp.int32, x.shape, x.ndim - 1)
@@ -288,7 +300,7 @@
             sides = []
             for row in range(4):
                 taps = [lat[f + dt, row : row + 3].reshape(9 * lc, lw) for dt in range(3)]
-                taps.append(jnp.zeros((w1_ref.shape[1] - 27 * lc, lw), jnp.bfloat16))
+                taps.append(jnp.zeros((wide - fan, lw), jnp.bfloat16))
                 sides.append(jnp.concatenate(taps, axis=0))
             y = jnp.dot(
                 w1_ref[...], jnp.concatenate(sides, axis=1), preferred_element_type=jnp.float32
@@ -296,7 +308,6 @@
             acts = []
             for row in range(4):
                 hidden = y[:, row * lw : row * lw + lw] + vec_ref[0]
-                hidden = hidden.astype(jnp.bfloat16).astype(jnp.float32)
                 if row in (1, 2):
                     firsts[lax.rem(f, 2 * lot), row - 1] = hidden
                 factor = lax.rsqrt(jnp.mean(hidden * hidden, axis=0, keepdims=True) + EPS)
@@ -315,6 +326,11 @@
         def _():
             for load in loads:
                 load.start()
+            w1_ref[:, :fan] = jnp.transpose(win_ref[...])
+            w1_ref[:, fan:] = jnp.zeros((vc, wide - fan), jnp.bfloat16)
+            for n in range(3):
+                row = jnp.broadcast_to(rows_ref[n : n + 1], (lw, vc))
+                vec_ref[n] = jnp.transpose(row)
             lat[:2] = jnp.zeros((2, 6, 3 * lc, lw), jnp.bfloat16)
             act[:, :2] = jnp.zeros((4, 2, deep, lw), jnp.bfloat16)
             cells = clip_ref[...].astype(jnp.float32)
@@ -374,6 +390,7 @@
             vmem_spec(),
             vmem_spec(),
             pl.BlockSpec(memory_space=pl.ANY),
+            pl.BlockSpec(memory_space=pl.ANY),
             vmem_spec(),
         ],
         out_specs=pl.BlockSpec((lot, 2, lw, vc), lambda i: (i, 0, 0, 0)),
@@ -381,14 +398,16 @@
             pltpu.VMEM((frames + 2, 6, 3 * lc, lw), jnp.bfloat16),
             pltpu.VMEM((4, frames + 2, deep, lw), jnp.bfloat16),
             pltpu.VMEM((2 * lot, 2, vc, lw), jnp.float32),
+            pltpu.VMEM((vc, wide), jnp.bfloat16),
+            pltpu.VMEM((3, vc, lw), jnp.float32),
             pltpu.VMEM((4, vc, 3 * deep), jnp.bfloat16),
             pltpu.VMEM((2, vc, lot * lw), jnp.float32),
-            pltpu.SemaphoreType.DMA((4,)),
+            pltpu.SemaphoreType.DMA((2,)),
         ],
         compiler_params=pltpu.CompilerParams(vmem_limit_bytes=48 * MIB),
         cost_estimate=pl.CostEstimate(flops=0, bytes_accessed=0, transcendentals=0),
         name="decode",
-    )(place, clip, w_first, filters, vectors)
+    )(place, clip, w_in, *filters, vectors)
 
 
 def on_device(
@@ -451,30 +470,31 @@
     w_next, w_back = swap(w_own, 0, 0), swap(w_give, 0, 1)
 
     own = jnp.swapaxes(latents, 2, 3)
-    clip = jnp.concatenate(
-        [lax.ppermute(own, "grp", [(g, last)]) for g in range(last)] + [own], axis=0
-    )
+    pieces = [lax.ppermute(own, "grp", [(g, last)]) for g in range(last)]
+    early = filter_weights(place, w_mid, 0, 5)
+    pieces, early = lax.optimization_barrier((pieces, early))
+    clip = jnp.concatenate(pieces + [own], axis=0)
     links = [(last * count + i, last * count + i + 1) for i in range(count - 1)]
     above = lax.ppermute(clip, ("grp",) + SEQ, links)
     below = lax.ppermute(clip, ("grp",) + SEQ, [(b, a) for a, b in links])
-    filters = filter_weights(place, w_mid)
-    above, below, filters = lax.optimization_barrier((above, below, filters))
+    late = filter_weights(place, w_mid, 5, 4)
+    above, below, late = lax.optimization_barrier((above, below, late))
     cells = jnp.concatenate([above, clip, below], axis=1)
-    w_first = jnp.pad(w_in.reshape(-1, channels).T, ((0, 0), (0, 512 - 27 * latents.shape[3])))
-    vectors = jnp.broadcast_to(
-        jnp.stack([b_in, norm_gain, b_mid])[:, :, None], (3, channels, latents.shape[2])
-    )
-
-    here, cells, w_next, w_back = lax.optimization_barrier((here, cells, w_next, w_back))
-    there = swap(here, 2, 0)
+
+    here, cells = lax.optimization_barrier((here, cells))
+    there = swap(here[:, 1:], 2, 0)
+    there, w_next, w_back = lax.optimization_barrier((there, w_next, w_back))
+    near, other = attend(place, here, there)
+    near, other, w_back = lax.optimization_barrier((near, other, w_back))
     w_far = swap(w_back, 0, 0)
-    near, other = attend(place, here, there)
     from_far = swap(other, 0, 2)
     heads = near, swap(other, 0, 0), swap(near, 0, 1), from_far
     mine, one, zero, far = project(place, heads, (w_own, w_next, w_back, w_far))
     mine, one, zero, far, cells = lax.optimization_barrier((mine, one, zero, far, cells))
     sums = swap(far, 1, 2), swap(one, 1, 1), swap(zero, 1, 0)
-    decoded = decode(place, cells, w_first, filters, vectors)
+    decoded = decode(
+        place, cells, w_in.reshape(-1, channels), (early, late), jnp.stack([b_in, norm_gain, b_mid])
+    )
     mine, decoded = lax.optimization_barrier((mine, decoded))
     kept, give = add_up(place, mine, sums)
     attn_out = finish(place, resid[0], gate, kept, swap(give, 0, 1))

time: 103 us -> 104 us (level)
  waiting for transfers between devices: 24.7 us -> 29.7 us
  local copies, waits for them, and re-layouts: 5.18 us -> 0.23 us
    ppermute x12, waiting for transfers between devices: 18.2 us -> 26 us  [swap(): return lax.ppermute(x, ('grp',) + SEQ, pairs)]
    all_to_all x1, waiting for transfers between devices: 6.21 us -> 3.66 us  [on_device(): lax.all_to_all(packed, CHIPS, split_axis=0, concat_axis=0, tiled=True)]
    ppermute x3, starting transfers between devices: 2.62 us -> 4.9 us  [on_device(): pieces = [lax.ppermute(own, 'grp', [(g, last)]) for g in range(last)]]
    reshape x1 -> x0, local copies, waits for them, and re-layouts: 1.9 us -> none  [on_device(): w_in.reshape(-1, channels)]
    unnamed x24 -> x22, local copies, waits for them, and re-layouts: 1.95 us -> 0.06 us
    ppermute x12, starting transfers between devices: 38.3 us -> 36.7 us  [swap(): return lax.ppermute(x, ('grp',) + SEQ, pairs)]
  transfers between devices with their start and end apart: 18 -> 18, of which waited for: 8 -> 9; matrix products, arithmetic and copies ran while one was open for 3% -> 0% of each run, Pallas kernels for 11% -> 6%
where the time goes in v6:
time: 104 us; the launch traced here: 103 us
  starting transfers between devices  50.9 us (49%)
  waiting for transfers between devices  29.7 us (29%)
  Pallas kernels  21.3 us (20%)
  between operations  1.08 us (1%)
    ppermute x12, starting transfers between devices, swap(): return lax.ppermute(x, ('grp',) + SEQ, pairs)  36.7 us
    ppermute x12, waiting for transfers between devices, swap(): return lax.ppermute(x, ('grp',) + SEQ, pairs)  26 us
    all_to_all x1, starting transfers between devices, on_device(): lax.all_to_all(packed, CHIPS, split_axis=0, concat_axis=0, tiled=True)  7.97 us
    pallas_call x1, Pallas kernels, attend(): pl.pallas_call(body, grid=(chips // 4,), out_shape=(jax.ShapeDtypeStruct(...  6.05 us
    ppermute x3, starting transfers between devices, on_device(): pieces = [lax.ppermute(own, 'grp', [(g, last)]) for g in range(last)]  4.9 us
    all_to_all x1, waiting for transfers between devices, on_device(): lax.all_to_all(packed, CHIPS, split_axis=0, concat_axis=0, tiled=True)  3.66 us
    pallas_call x1, Pallas kernels, norm_pack(): pl.pallas_call(body, grid=(rows // block,), out_shape=jax.ShapeDtypeStruc...  3.56 us
    pallas_call x1, Pallas kernels, project(): pl.pallas_call(body, out_shape=(jax.ShapeDtypeStruct(shape, jnp.float32),...  3.35 us
  transfers between devices with their start and end apart: 18, of which 9 were waited for; matrix products, arithmetic and copies ran while one was open for 0% of the time, Pallas kernels for 6%

profile of v6, /device:TPU:0, one launch (start us, length us, event | category | flops | bytes accessed | tf_op | source)
XLA Modules:
  0.0 103.3 jit_solution(6440620431486770109)
XLA Ops:
  0.7 3.6 %norm_pack.1 = bf16[16,3,48,256]{3,2,1,0:T(8,128)(2,1)} custom-call(bf16[48,4096]{1,0:T(8,128)(2,1)} %bitcast.21, bf16[48,4096]{1,0:T(8,128)(2,1)} %bitcast.22, bf16[48,4096]{1,0:T(8,128)(2,1)} %bitcast.23, f32[1,4096]{1,0:T(1,128)} %bitcast.30, f32[1,4096]{1,0:T(1,128)} %bitcast.31), custom_call_target="tpu_custom_call" | custom-call | tf_op jit(solution)/shard_map/norm_pack/pallas_call | solution.py:45
  6.1 8.0 %all-to-all-start = ((bf16[16,3,48,256]{3,2,1,0:T(8,128)(2,1)}), bf16[16,3,48,256]{3,2,1,0:T(8,128)(2,1)S(1)}, u32[]{:S(2)}, u32[]{:S(2)}) async-start(bf16[16,3,48,256]{3,2,1,0:T(8,128)(2,1)} %norm_pack.1), calls=%async_computation | async-start | bytes 2359296 | tf_op jit(solution)/shard_map/all_to_all | solution.py:466
  14.2 2.1 %weight_halves.1 = (bf16[256,2048]{1,0:T(8,128)(2,1)}, bf16[256,2048]{1,0:T(8,128)(2,1)}) custom-call(s32[6]{0:T(128)S(1)} %stack.39.place_ref, bf16[128,4096]{1,0:T(8,128)(2,1)S(1)} %copy-done.1, bf16[128,4096]{1,0:T(8,128)(2,1)S(1)} %collective-permute-done.there_ref), custom_call_target="tpu_custom_call" | custom-call | tf_op jit(solution)/shard_map/weight_halves/pallas_call | solution.py:72
  16.3 3.6 %collective-permute-start.1 = (bf16[4,2,16,128]{3,2,1,0:T(8,128)(2,1)S(1)}, bf16[4,2,16,128]{3,2,1,0:T(8,128)(2,1)S(1)}, u32[]{:S(2)}, u32[]{:S(2)}) collective-permute-start(bf16[4,2,16,128]{3,2,1,0:T(8,128)(2,1)S(1)} %bitcast.25), channel_id=1, source_target_pairs={{0,96},{1,97},{2,98},{3,99},{4,100},{5,101},{6,102},{7,103},{8,104... | collective-permute-start | bytes 98312 | tf_op jit(solution)/shard_map/ppermute | solution.py:473
  21.9 3.8 %collective-permute-start.7 = (bf16[256,2048]{1,0:T(8,128)(2,1)}, bf16[256,2048]{1,0:T(8,128)(2,1)S(1)}, u32[]{:S(2)}, u32[]{:S(2)}) collective-permute-start(bf16[256,2048]{1,0:T(8,128)(2,1)} %get-tuple-element.52.w0), channel_id=1, source_target_pairs={{0,8},{1,3},{2,10},{3,1},{4,12},{5,7},{6,14},{7,5},{8,0},{9,11},{1... | collective-permute-start | bytes 3145736 | tf_op jit(solution)/shard_map/ppermute | solution.py:460
  25.7 4.0 %collective-permute-start.8 = (bf16[256,2048]{1,0:T(8,128)(2,1)}, bf16[256,2048]{1,0:T(8,128)(2,1)}, u32[]{:S(2)}, u32[]{:S(2)}) collective-permute-start(bf16[256,2048]{1,0:T(8,128)(2,1)} %get-tuple-element.53), channel_id=1, source_target_pairs={{0,24},{1,7},{2,26},{3,5},{4,28},{5,3},{6,30},{7,1},{8,16},{9,15},... | collective-permute-start | bytes 3145736 | tf_op jit(solution)/shard_map/ppermute | solution.py:460
  32.0 3.7 %all-to-all-done.here_ref = bf16[16,3,48,256]{3,2,1,0:T(8,128)(2,1)S(1)} async-done(((bf16[16,3,48,256]{3,2,1,0:T(8,128)(2,1)}), bf16[16,3,48,256]{3,2,1,0:T(8,128)(2,1)S(1)}, u32[]{:S(2)}, u32[]{:S(2)}) %all-to-all-start) | async-done | bytes 1179680 | tf_op jit(solution)/shard_map/all_to_all | solution.py:466
  35.7 2.2 %collective-permute-start.6 = (bf16[16,2,48,256]{3,2,1,0:T(8,128)(2,1)S(1)}, bf16[16,2,48,256]{3,2,1,0:T(8,128)(2,1)S(1)}, u32[]{:S(2)}, u32[]{:S(2)}) collective-permute-start(bf16[16,2,48,256]{3,2,1,0:T(8,128)(2,1)S(1)} %slice.3), channel_id=1, source_target_pairs={{0,1},{1,0},{2,3},{3,2},{4,5},{5,4},{6,7},{7,6},{8,9},{9,8},{10,11... | collective-permute-start | bytes 2359304 | tf_op jit(solution)/shard_map/ppermute | solution.py:460
  37.9 2.3 %collective-permute-done.6.there_ref = bf16[16,2,48,256]{3,2,1,0:T(8,128)(2,1)S(1)} collective-permute-done((bf16[16,2,48,256]{3,2,1,0:T(8,128)(2,1)S(1)}, bf16[16,2,48,256]{3,2,1,0:T(8,128)(2,1)S(1)}, u32[]{:S(2)}, u32[]{:S(2)}) %collective-permute-start.6) | collective-permute-done | bytes 786464 | tf_op jit(solution)/shard_map/ppermute | solution.py:460
  41.9 3.4 %collective-permute-done.8.w2 = bf16[256,2048]{1,0:T(8,128)(2,1)} collective-permute-done((bf16[256,2048]{1,0:T(8,128)(2,1)}, bf16[256,2048]{1,0:T(8,128)(2,1)}, u32[]{:S(2)}, u32[]{:S(2)}) %collective-permute-start.8) | collective-permute-done | bytes 1048608 | tf_op jit(solution)/shard_map/ppermute | solution.py:460
  45.3 6.0 %attend.1 = (bf16[4,2,48,256]{3,2,1,0:T(8,128)(2,1)S(1)}, bf16[4,2,48,256]{3,2,1,0:T(8,128)(2,1)S(1)}) custom-call(s32[6]{0:T(128)S(1)} %copy-done.5, bf16[16,3,48,256]{3,2,1,0:T(8,128)(2,1)S(1)} %all-to-all-done.here_ref, bf16[16,2,48,256]{3,2,1,0:T(8,128)(2,1)S(1)} %collective-permute-done.6.there_ref), custom_call_target="tpu_custom_call" | custom-call | tf_op jit(solution)/shard_map/attend/pallas_call | solution.py:134
  53.3 3.8 %collective-permute-start.10 = (bf16[4,2,48,256]{3,2,1,0:T(8,128)(2,1)S(1)}, bf16[4,2,48,256]{3,2,1,0:T(8,128)(2,1)S(1)}, u32[]{:S(2)}, u32[]{:S(2)}) collective-permute-start(bf16[4,2,48,256]{3,2,1,0:T(8,128)(2,1)S(1)} %get-tuple-element.58.h0), channel_id=1, source_target_pairs={{0,24},{1,7},{2,26},{3,5},{4,28},{5,3},{6,30},{7,1},{8,16},{9,15},... | collective-permute-start | bytes 589832 | tf_op jit(solution)/shard_map/ppermute | solution.py:460
  57.0 4.1 %collective-permute-start.11 = (bf16[4,2,48,256]{3,2,1,0:T(8,128)(2,1)S(1)}, bf16[4,2,48,256]{3,2,1,0:T(8,128)(2,1)S(1)}, u32[]{:S(2)}, u32[]{:S(2)}) collective-permute-start(bf16[4,2,48,256]{3,2,1,0:T(8,128)(2,1)S(1)} %get-tuple-element.59), channel_id=1, source_target_pairs={{0,16},{1,5},{2,18},{3,7},{4,20},{5,1},{6,22},{7,3},{8,24},{9,13},... | collective-permute-start | bytes 589832 | tf_op jit(solution)/shard_map/ppermute | solution.py:460
  61.2 1.9 %collective-permute-start.9 = (bf16[4,2,48,256]{3,2,1,0:T(8,128)(2,1)S(1)}, bf16[4,2,48,256]{3,2,1,0:T(8,128)(2,1)S(1)}, u32[]{:S(2)}, u32[]{:S(2)}) collective-permute-start(bf16[4,2,48,256]{3,2,1,0:T(8,128)(2,1)S(1)} %get-tuple-element.59), channel_id=1, source_target_pairs={{0,8},{1,3},{2,10},{3,1},{4,12},{5,7},{6,14},{7,5},{8,0},{9,11},{1... | collective-permute-start | bytes 589832 | tf_op jit(solution)/shard_map/ppermute | solution.py:460
  63.1 7.4 %collective-permute-done.11.h3 = bf16[4,2,48,256]{3,2,1,0:T(8,128)(2,1)S(1)} collective-permute-done((bf16[4,2,48,256]{3,2,1,0:T(8,128)(2,1)S(1)}, bf16[4,2,48,256]{3,2,1,0:T(8,128)(2,1)S(1)}, u32[]{:S(2)}, u32[]{:S(2)}) %collective-permute-start.11) | collective-permute-done | bytes 196640 | tf_op jit(solution)/shard_map/ppermute | solution.py:460
  70.5 1.9 %collective-permute-done.9.h1 = bf16[4,2,48,256]{3,2,1,0:T(8,128)(2,1)S(1)} collective-permute-done((bf16[4,2,48,256]{3,2,1,0:T(8,128)(2,1)S(1)}, bf16[4,2,48,256]{3,2,1,0:T(8,128)(2,1)S(1)}, u32[]{:S(2)}, u32[]{:S(2)}) %collective-permute-start.9) | collective-permute-done | bytes 196640 | tf_op jit(solution)/shard_map/ppermute | solution.py:460
  72.5 3.3 %project.1 = (f32[2,48,2048]{2,1,0:T(8,128)S(1)}, bf16[2,48,2048]{2,1,0:T(8,128)(2,1)S(1)}, bf16[2,48,2048]{2,1,0:T(8,128)(2,1)S(1)}, bf16[2,48,2048]{2,1,0:T(8,128)(2,1)S(1)}) custom-call(s32[6]{0:T(128)S(1)} %copy-done.5, bf16[4,2,48,256]{3,2,1,0:T(8,128)(2,1)S(1)} %get-tuple-element.58.h0, bf16[4,2,48,256]{3,2,1,0:T(8,128)(2,1)S(1)} %collective-permute-done.9.h1, ...), custom_call_target="tpu_custom_call" | custom-call | flops 1610612736 | bytes 8388608 | tf_op jit(solution)/shard_map/project/pallas_call | solution.py:173
  75.8 3.5 %collective-permute-start.13 = (bf16[2,48,2048]{2,1,0:T(8,128)(2,1)S(1)}, bf16[2,48,2048]{2,1,0:T(8,128)(2,1)S(1)}, u32[]{:S(2)}, u32[]{:S(2)}) collective-permute-start(bf16[2,48,2048]{2,1,0:T(8,128)(2,1)S(1)} %get-tuple-element.72), channel_id=1, source_target_pairs={{0,4},{1,17},{2,6},{3,19},{4,0},{5,21},{6,2},{7,23},{8,12},{9,25},... | collective-permute-start | bytes 1179656 | tf_op jit(solution)/shard_map/ppermute | solution.py:460
  79.4 3.3 %collective-permute-start.14 = (bf16[2,48,2048]{2,1,0:T(8,128)(2,1)S(1)}, bf16[2,48,2048]{2,1,0:T(8,128)(2,1)S(1)}, u32[]{:S(2)}, u32[]{:S(2)}) collective-permute-start(bf16[2,48,2048]{2,1,0:T(8,128)(2,1)S(1)} %get-tuple-element.73), channel_id=1, source_target_pairs={{0,6},{1,25},{2,4},{3,27},{4,2},{5,29},{6,0},{7,31},{8,14},{9,17},... | collective-permute-start | bytes 1179656 | tf_op jit(solution)/shard_map/ppermute | solution.py:460
  82.7 2.5 %collective-permute-start.15 = (bf16[2,48,2048]{2,1,0:T(8,128)(2,1)S(1)}, bf16[2,48,2048]{2,1,0:T(8,128)(2,1)S(1)}, u32[]{:S(2)}, u32[]{:S(2)}) collective-permute-start(bf16[2,48,2048]{2,1,0:T(8,128)(2,1)S(1)} %get-tuple-element.74), channel_id=1, source_target_pairs={{0,2},{1,9},{2,0},{3,11},{4,6},{5,13},{6,4},{7,15},{8,10},{9,1},{1... | collective-permute-start | bytes 1179656 | tf_op jit(solution)/shard_map/ppermute | solution.py:460
  85.4 2.8 %decode.1 = bf16[16,2,128,384]{3,2,1,0:T(8,128)(2,1)} custom-call(s32[6]{0:T(128)S(1)} %copy-done.5, bf16[16,6,16,128]{3,2,1,0:T(8,128)(2,1)S(1)} %pad_maximum_fusion.clip_ref, bf16[432,384]{1,0:T(8,128)(2,1)S(1)} %bitcast.17, bf16[4,384,1920]{2,1,0:T(8,128)(2,1)} %filter_weights_0.1.fa_ref, bf16[4,384,1536]{2,1,0:T(8,128)(2,1)S(1)} %copy-done, ...), custom_call_target="tpu_custom_call" | custom-call | tf_op jit(solution)/shard_map/decode/pallas_call | solution.py:384
  88.2 3.0 %collective-permute-done.14.b_ref = bf16[2,48,2048]{2,1,0:T(8,128)(2,1)S(1)} collective-permute-done((bf16[2,48,2048]{2,1,0:T(8,128)(2,1)S(1)}, bf16[2,48,2048]{2,1,0:T(8,128)(2,1)S(1)}, u32[]{:S(2)}, u32[]{:S(2)}) %collective-permute-start.14) | collective-permute-done | bytes 393248 | tf_op jit(solution)/shard_map/ppermute | solution.py:460
  93.1 3.7 %collective-permute-start.16 = (bf16[48,2048]{1,0:T(8,128)(2,1)S(1)}, bf16[48,2048]{1,0:T(8,128)(2,1)S(1)}, u32[]{:S(2)}, u32[]{:S(2)}) collective-permute-start(bf16[48,2048]{1,0:T(8,128)(2,1)S(1)} %get-tuple-element.76), channel_id=1, source_target_pairs={{0,24},{1,7},{2,26},{3,5},{4,28},{5,3},{6,30},{7,1},{8,16},{9,15},... | collective-permute-start | bytes 589832 | tf_op jit(solution)/shard_map/ppermute | solution.py:460
  96.8 5.0 %collective-permute-done.16.got_ref = bf16[48,2048]{1,0:T(8,128)(2,1)S(1)} collective-permute-done((bf16[48,2048]{1,0:T(8,128)(2,1)S(1)}, bf16[48,2048]{1,0:T(8,128)(2,1)S(1)}, u32[]{:S(2)}, u32[]{:S(2)}) %collective-permute-start.16) | collective-permute-done | bytes 196640 | tf_op jit(solution)/shard_map/ppermute | solution.py:460
  (51 shorter events, 13.3 us)
Async XLA Ops:
  4.2 10.0 %collective-permute-start = (bf16[128,4096]{1,0:T(8,128)(2,1)}, bf16[128,4096]{1,0:T(8,128)(2,1)S(1)}, u32[]{:S(2)}, u32[]{:S(2)}) collective-permute-start(bf16[128,4096]{1,0:T(8,128)(2,1)} %here_ref), channel_id=1, source_target_pairs={{0,1},{1,0},{2,3},{3,2},{4,5},{5,4},{6,7},{7,6},{8,9},{9,8},{10,11... | collective-permute-start | bytes 3145736 | tf_op jit(solution)/shard_map/ppermute | solution.py:460
  6.1 29.5 %all-to-all-start = ((bf16[16,3,48,256]{3,2,1,0:T(8,128)(2,1)}), bf16[16,3,48,256]{3,2,1,0:T(8,128)(2,1)S(1)}, u32[]{:S(2)}, u32[]{:S(2)}) async-start(bf16[16,3,48,256]{3,2,1,0:T(8,128)(2,1)} %norm_pack.1), calls=%async_computation | async-start | bytes 2359296 | tf_op jit(solution)/shard_map/all_to_all | solution.py:466
  16.3 13.4 %collective-permute-start.1 = (bf16[4,2,16,128]{3,2,1,0:T(8,128)(2,1)S(1)}, bf16[4,2,16,128]{3,2,1,0:T(8,128)(2,1)S(1)}, u32[]{:S(2)}, u32[]{:S(2)}) collective-permute-start(bf16[4,2,16,128]{3,2,1,0:T(8,128)(2,1)S(1)} %bitcast.25), channel_id=1, source_target_pairs={{0,96},{1,97},{2,98},{3,99},{4,100},{5,101},{6,102},{7,103},{8,104... | collective-permute-start | bytes 98312 | tf_op jit(solution)/shard_map/ppermute | solution.py:473
  19.9 9.9 %collective-permute-start.2 = (bf16[4,2,16,128]{3,2,1,0:T(8,128)(2,1)S(1)}, bf16[4,2,16,128]{3,2,1,0:T(8,128)(2,1)S(1)}, u32[]{:S(2)}, u32[]{:S(2)}) collective-permute-start(bf16[4,2,16,128]{3,2,1,0:T(8,128)(2,1)S(1)} %bitcast.26), channel_id=1, source_target_pairs={{32,96},{33,97},{34,98},{35,99},{36,100},{37,101},{38,102},{39,103... | collective-permute-start | bytes 98312 | tf_op jit(solution)/shard_map/ppermute | solution.py:473
  20.6 9.2 %collective-permute-start.3 = (bf16[4,2,16,128]{3,2,1,0:T(8,128)(2,1)S(1)}, bf16[4,2,16,128]{3,2,1,0:T(8,128)(2,1)S(1)}, u32[]{:S(2)}, u32[]{:S(2)}) collective-permute-start(bf16[4,2,16,128]{3,2,1,0:T(8,128)(2,1)S(1)} %bitcast.27), channel_id=1, source_target_pairs={{64,96},{65,97},{66,98},{67,99},{68,100},{69,101},{70,102},{71,103... | collective-permute-start | bytes 98312 | tf_op jit(solution)/shard_map/ppermute | solution.py:473
  21.9 20.0 %collective-permute-start.7 = (bf16[256,2048]{1,0:T(8,128)(2,1)}, bf16[256,2048]{1,0:T(8,128)(2,1)S(1)}, u32[]{:S(2)}, u32[]{:S(2)}) collective-permute-start(bf16[256,2048]{1,0:T(8,128)(2,1)} %get-tuple-element.52.w0), channel_id=1, source_target_pairs={{0,8},{1,3},{2,10},{3,1},{4,12},{5,7},{6,14},{7,5},{8,0},{9,11},{1... | collective-permute-start | bytes 3145736 | tf_op jit(solution)/shard_map/ppermute | solution.py:460
  25.7 19.5 %collective-permute-start.8 = (bf16[256,2048]{1,0:T(8,128)(2,1)}, bf16[256,2048]{1,0:T(8,128)(2,1)}, u32[]{:S(2)}, u32[]{:S(2)}) collective-permute-start(bf16[256,2048]{1,0:T(8,128)(2,1)} %get-tuple-element.53), channel_id=1, source_target_pairs={{0,24},{1,7},{2,26},{3,5},{4,28},{5,3},{6,30},{7,1},{8,16},{9,15},... | collective-permute-start | bytes 3145736 | tf_op jit(solution)/shard_map/ppermute | solution.py:460
  29.8 2.0 %collective-permute-start.4 = (bf16[16,2,16,128]{3,2,1,0:T(8,128)(2,1)S(1)}, bf16[16,2,16,128]{3,2,1,0:T(8,128)(2,1)S(1)}, u32[]{:S(2)}, u32[]{:S(2)}) collective-permute-start(bf16[16,2,16,128]{3,2,1,0:T(8,128)(2,1)S(1)} %pad_maximum_fusion.1), channel_id=1, source_target_pairs={{96,97},{97,98},{98,99},{99,100},{100,101},{101,102},{102,103},{10... | collective-permute-start | bytes 393224 | tf_op jit(solution)/shard_map/ppermute | solution.py:478
  30.5 1.4 %collective-permute-start.5 = (bf16[16,2,16,128]{3,2,1,0:T(8,128)(2,1)S(1)}, bf16[16,2,16,128]{3,2,1,0:T(8,128)(2,1)S(1)}, u32[]{:S(2)}, u32[]{:S(2)}) collective-permute-start(bf16[16,2,16,128]{3,2,1,0:T(8,128)(2,1)S(1)} %pad_maximum_fusion.1), channel_id=1, source_target_pairs={{97,96},{98,97},{99,98},{100,99},{101,100},{102,101},{103,102},{10... | collective-permute-start | bytes 393224 | tf_op jit(solution)/shard_map/ppermute | solution.py:479
  31.9 53.3 %copy-start.8 = (f32[384]{0:T(512)S(1)}, f32[384]{0:T(512)}, u32[]{:S(2)}) copy-start(f32[384]{0:T(512)} %param.24) | copy-start | bytes 4612
  31.9 53.3 %copy-start.9 = (f32[384]{0:T(512)S(1)}, f32[384]{0:T(512)}, u32[]{:S(2)}) copy-start(f32[384]{0:T(512)} %param.25) | copy-start | bytes 4612
  31.9 53.3 %copy-start.10 = (f32[384]{0:T(512)S(1)}, f32[384]{0:T(512)}, u32[]{:S(2)}) copy-start(f32[384]{0:T(512)} %param.27) | copy-start | bytes 4612
  32.0 53.4 %copy-start.3 = (bf16[3,144,384]{2,1,0:T(8,128)(2,1)S(1)}, bf16[3,144,384]{2,1,0:T(8,128)(2,1)}, u32[]{:S(2)}) copy-start(bf16[3,144,384]{2,1,0:T(8,128)(2,1)} %param.23) | copy-start | bytes 995332
  35.6 49.7 %copy-start = (bf16[4,384,1536]{2,1,0:T(8,128)(2,1)S(1)}, bf16[4,384,1536]{2,1,0:T(8,128)(2,1)}, u32[]{:S(2)}) copy-start(bf16[4,384,1536]{2,1,0:T(8,128)(2,1)} %filter_weights_5.1.fb_ref) | copy-start | bytes 14155780
  35.7 4.4 %collective-permute-start.6 = (bf16[16,2,48,256]{3,2,1,0:T(8,128)(2,1)S(1)}, bf16[16,2,48,256]{3,2,1,0:T(8,128)(2,1)S(1)}, u32[]{:S(2)}, u32[]{:S(2)}) collective-permute-start(bf16[16,2,48,256]{3,2,1,0:T(8,128)(2,1)S(1)} %slice.3), channel_id=1, source_target_pairs={{0,1},{1,0},{2,3},{3,2},{4,5},{5,4},{6,7},{7,6},{8,9},{9,8},{10,11... | collective-permute-start | bytes 2359304 | tf_op jit(solution)/shard_map/ppermute | solution.py:460
  51.3 21.1 %collective-permute-start.12 = (bf16[256,2048]{1,0:T(8,128)(2,1)}, bf16[256,2048]{1,0:T(8,128)(2,1)S(1)}, u32[]{:S(2)}, u32[]{:S(2)}) collective-permute-start(bf16[256,2048]{1,0:T(8,128)(2,1)} %collective-permute-done.8.w2), channel_id=1, source_target_pairs={{0,8},{1,3},{2,10},{3,1},{4,12},{5,7},{6,14},{7,5},{8,0},{9,11},{1... | collective-permute-start | bytes 3145736 | tf_op jit(solution)/shard_map/ppermute | solution.py:460
  53.3 9.8 %collective-permute-start.10 = (bf16[4,2,48,256]{3,2,1,0:T(8,128)(2,1)S(1)}, bf16[4,2,48,256]{3,2,1,0:T(8,128)(2,1)S(1)}, u32[]{:S(2)}, u32[]{:S(2)}) collective-permute-start(bf16[4,2,48,256]{3,2,1,0:T(8,128)(2,1)S(1)} %get-tuple-element.58.h0), channel_id=1, source_target_pairs={{0,24},{1,7},{2,26},{3,5},{4,28},{5,3},{6,30},{7,1},{8,16},{9,15},... | collective-permute-start | bytes 589832 | tf_op jit(solution)/shard_map/ppermute | solution.py:460
  57.0 13.5 %collective-permute-start.11 = (bf16[4,2,48,256]{3,2,1,0:T(8,128)(2,1)S(1)}, bf16[4,2,48,256]{3,2,1,0:T(8,128)(2,1)S(1)}, u32[]{:S(2)}, u32[]{:S(2)}) collective-permute-start(bf16[4,2,48,256]{3,2,1,0:T(8,128)(2,1)S(1)} %get-tuple-element.59), channel_id=1, source_target_pairs={{0,16},{1,5},{2,18},{3,7},{4,20},{5,1},{6,22},{7,3},{8,24},{9,13},... | collective-permute-start | bytes 589832 | tf_op jit(solution)/shard_map/ppermute | solution.py:460
  61.2 11.3 %collective-permute-start.9 = (bf16[4,2,48,256]{3,2,1,0:T(8,128)(2,1)S(1)}, bf16[4,2,48,256]{3,2,1,0:T(8,128)(2,1)S(1)}, u32[]{:S(2)}, u32[]{:S(2)}) collective-permute-start(bf16[4,2,48,256]{3,2,1,0:T(8,128)(2,1)S(1)} %get-tuple-element.59), channel_id=1, source_target_pairs={{0,8},{1,3},{2,10},{3,1},{4,12},{5,7},{6,14},{7,5},{8,0},{9,11},{1... | collective-permute-start | bytes 589832 | tf_op jit(solution)/shard_map/ppermute | solution.py:460
  75.8 12.3 %collective-permute-start.13 = (bf16[2,48,2048]{2,1,0:T(8,128)(2,1)S(1)}, bf16[2,48,2048]{2,1,0:T(8,128)(2,1)S(1)}, u32[]{:S(2)}, u32[]{:S(2)}) collective-permute-start(bf16[2,48,2048]{2,1,0:T(8,128)(2,1)S(1)} %get-tuple-element.72), channel_id=1, source_target_pairs={{0,4},{1,17},{2,6},{3,19},{4,0},{5,21},{6,2},{7,23},{8,12},{9,25},... | collective-permute-start | bytes 1179656 | tf_op jit(solution)/shard_map/ppermute | solution.py:460
  79.4 11.8 %collective-permute-start.14 = (bf16[2,48,2048]{2,1,0:T(8,128)(2,1)S(1)}, bf16[2,48,2048]{2,1,0:T(8,128)(2,1)S(1)}, u32[]{:S(2)}, u32[]{:S(2)}) collective-permute-start(bf16[2,48,2048]{2,1,0:T(8,128)(2,1)S(1)} %get-tuple-element.73), channel_id=1, source_target_pairs={{0,6},{1,25},{2,4},{3,27},{4,2},{5,29},{6,0},{7,31},{8,14},{9,17},... | collective-permute-start | bytes 1179656 | tf_op jit(solution)/shard_map/ppermute | solution.py:460
  82.7 9.7 %collective-permute-start.15 = (bf16[2,48,2048]{2,1,0:T(8,128)(2,1)S(1)}, bf16[2,48,2048]{2,1,0:T(8,128)(2,1)S(1)}, u32[]{:S(2)}, u32[]{:S(2)}) collective-permute-start(bf16[2,48,2048]{2,1,0:T(8,128)(2,1)S(1)} %get-tuple-element.74), channel_id=1, source_target_pairs={{0,2},{1,9},{2,0},{3,11},{4,6},{5,13},{6,4},{7,15},{8,10},{9,1},{1... | collective-permute-start | bytes 1179656 | tf_op jit(solution)/shard_map/ppermute | solution.py:460
  85.3 16.6 %copy-start.2 = (bf16[1,48,4096]{2,1,0:T(8,128)(2,1)S(1)}, bf16[1,48,4096]{2,1,0:T(8,128)(2,1)}, u32[]{:S(2)}) copy-start(bf16[1,48,4096]{2,1,0:T(8,128)(2,1)} %param.17) | copy-start | bytes 1179652
  93.1 8.8 %collective-permute-start.16 = (bf16[48,2048]{1,0:T(8,128)(2,1)S(1)}, bf16[48,2048]{1,0:T(8,128)(2,1)S(1)}, u32[]{:S(2)}, u32[]{:S(2)}) collective-permute-start(bf16[48,2048]{1,0:T(8,128)(2,1)S(1)} %get-tuple-element.76), channel_id=1, source_target_pairs={{0,24},{1,7},{2,26},{3,5},{4,28},{5,3},{6,30},{7,1},{8,16},{9,15},... | collective-permute-start | bytes 589832 | tf_op jit(solution)/shard_map/ppermute | solution.py:460
  (5 other events, 68.3 us)

commit v7 on v6

--- a/solution.py
+++ b/solution.py
@@ -81,6 +81,21 @@
 
 def inner(position):
     return ((position + 1) // 2) % 2
+
+
+def passed(*arrays):
+    def body(*refs):
+        pass
+
+    return pl.pallas_call(
+        body,
+        out_shape=tuple(jax.ShapeDtypeStruct(x.shape, x.dtype) for x in arrays),
+        in_specs=[pl.BlockSpec(memory_space=pl.ANY)] * len(arrays),
+        out_specs=(pl.BlockSpec(memory_space=pl.ANY),) * len(arrays),
+        input_output_aliases={n: n for n in range(len(arrays))},
+        cost_estimate=pl.CostEstimate(flops=2000000000, bytes_accessed=0, transcendentals=0),
+        name="passed",
+    )(*arrays)
 
 
 def attend(place, here, there):
@@ -462,11 +477,12 @@
     packed = norm_pack(
         query_input[0], key_input[0], value_input[0], query_norm_gain[None], key_norm_gain[None]
     )
-    packed, w_here = lax.optimization_barrier((packed, output_weight))
+    packed, latents, w_mid, w_there = lax.optimization_barrier(
+        (packed, latents, w_mid, swap(output_weight, 2, 0))
+    )
     here = lax.all_to_all(packed, CHIPS, split_axis=0, concat_axis=0, tiled=True)
 
-    w_own, w_give = weight_halves(place, w_here, swap(w_here, 2, 0))
-    w_own, w_give, latents, w_mid = lax.optimization_barrier((w_own, w_give, latents, w_mid))
+    w_own, w_give = weight_halves(place, output_weight, w_there)
     w_next, w_back = swap(w_own, 0, 0), swap(w_give, 0, 1)
 
     own = jnp.swapaxes(latents, 2, 3)
@@ -481,12 +497,11 @@
     above, below, late = lax.optimization_barrier((above, below, late))
     cells = jnp.concatenate([above, clip, below], axis=1)
 
-    here, cells = lax.optimization_barrier((here, cells))
+    w_next, w_back = passed(w_next, w_back)
+    w_far = swap(w_back, 0, 0)
+    here, cells, w_next, w_back = lax.optimization_barrier((here, cells, w_next, w_back))
     there = swap(here[:, 1:], 2, 0)
-    there, w_next, w_back = lax.optimization_barrier((there, w_next, w_back))
     near, other = attend(place, here, there)
-    near, other, w_back = lax.optimization_barrier((near, other, w_back))
-    w_far = swap(w_back, 0, 0)
     from_far = swap(other, 0, 2)
     heads = near, swap(other, 0, 0), swap(near, 0, 1), from_far
     mine, one, zero, far = project(place, heads, (w_own, w_next, w_back, w_far))

time: 104 us -> 104 us (level)
  starting transfers between devices: 50.9 us -> 49.1 us
  local copies, waits for them, and re-layouts: 0.23 us -> 1.44 us
    ppermute x12, waiting for transfers between devices: 26 us -> 30.6 us  [swap(): return lax.ppermute(x, ('grp',) + SEQ, pairs)]
    all_to_all x1, waiting for transfers between devices: 3.66 us -> 0.01 us  [on_device(): lax.all_to_all(packed, CHIPS, split_axis=0, concat_axis=0, tiled=True)]
    ppermute x12, starting transfers between devices: 36.7 us -> 40 us  [swap(): return lax.ppermute(x, ('grp',) + SEQ, pairs)]
    all_to_all x1, starting transfers between devices: 7.97 us -> 4.93 us  [on_device(): lax.all_to_all(packed, CHIPS, split_axis=0, concat_axis=0, tiled=True)]
    ppermute x3, starting transfers between devices: 4.9 us -> 2.9 us  [on_device(): pieces = [lax.ppermute(own, 'grp', [(g, last)]) for g in range(last)]]
    unnamed x22 -> x24, local copies, waits for them, and re-layouts: 0.06 us -> 1.28 us
  transfers between devices with their start and end apart: 18 -> 18, of which waited for: 9 -> 8; matrix products, arithmetic and copies ran while one was open for 0% -> 0% of each run, Pallas kernels for 6% -> 13%
where the time goes in v7:
time: 104 us
  starting transfers between devices  49.1 us (47%)
  waiting for transfers between devices  30.6 us (29%)
  Pallas kernels  21.2 us (20%)
  local copies, waits for them, and re-layouts  1.44 us (1%)
  between operations  1.12 us (1%)
    ppermute x12, starting transfers between devices, swap(): return lax.ppermute(x, ('grp',) + SEQ, pairs)  40 us
    ppermute x12, waiting for transfers between devices, swap(): return lax.ppermute(x, ('grp',) + SEQ, pairs)  30.6 us
    pallas_call x1, Pallas kernels, attend(): pl.pallas_call(body, grid=(chips // 4,), out_shape=(jax.ShapeDtypeStruct(...  6.11 us
    all_to_all x1, starting transfers between devices, on_device(): lax.all_to_all(packed, CHIPS, split_axis=0, concat_axis=0, tiled=True)  4.93 us
    pallas_call x1, Pallas kernels, project(): pl.pallas_call(body, out_shape=(jax.ShapeDtypeStruct(shape, jnp.float32),...  3.67 us
    pallas_call x1, Pallas kernels, norm_pack(): pl.pallas_call(body, grid=(rows // block,), out_shape=jax.ShapeDtypeStruc...  3.48 us
    ppermute x3, starting transfers between devices, on_device(): pieces = [lax.ppermute(own, 'grp', [(g, last)]) for g in range(last)]  2.9 us
    pallas_call x1, Pallas kernels, decode(): pl.pallas_call(body, grid=(frames // lot,), out_shape=jax.ShapeDtypeStruc...  2.78 us
  transfers between devices with their start and end apart: 18, of which 8 were waited for; matrix products, arithmetic and copies ran while one was open for 0% of the time, Pallas kernels for 13%

profile of v7, /device:TPU:0, one launch (start us, length us, event | category | flops | bytes accessed | tf_op | source)
XLA Modules:
  0.0 103.6 jit_solution(8013433682844176425)
XLA Ops:
  0.6 1.9 %collective-permute-start = (bf16[128,4096]{1,0:T(8,128)(2,1)}, bf16[128,4096]{1,0:T(8,128)(2,1)S(1)}, u32[]{:S(2)}, u32[]{:S(2)}) collective-permute-start(bf16[128,4096]{1,0:T(8,128)(2,1)} %here_ref.1), channel_id=1, source_target_pairs={{0,1},{1,0},{2,3},{3,2},{4,5},{5,4},{6,7},{7,6},{8,9},{9,8},{10,11... | collective-permute-start | bytes 3145736 | tf_op jit(solution)/shard_map/ppermute | solution.py:475
  2.6 3.5 %norm_pack.1 = bf16[16,3,48,256]{3,2,1,0:T(8,128)(2,1)} custom-call(bf16[48,4096]{1,0:T(8,128)(2,1)} %bitcast.23, bf16[48,4096]{1,0:T(8,128)(2,1)} %bitcast.24, bf16[48,4096]{1,0:T(8,128)(2,1)} %bitcast.25, f32[1,4096]{1,0:T(1,128)} %bitcast.32, f32[1,4096]{1,0:T(1,128)} %bitcast.33), custom_call_target="tpu_custom_call" | custom-call | tf_op jit(solution)/shard_map/norm_pack/pallas_call | solution.py:45
  7.4 1.7 %weight_halves.1 = (bf16[256,2048]{1,0:T(8,128)(2,1)S(1)}, bf16[256,2048]{1,0:T(8,128)(2,1)}) custom-call(s32[6]{0:T(128)S(1)} %stack.39.place_ref, bf16[128,4096]{1,0:T(8,128)(2,1)S(1)} %copy-done, bf16[128,4096]{1,0:T(8,128)(2,1)S(1)} %collective-permute-done.there_ref), custom_call_target="tpu_custom_call" | custom-call | tf_op jit(solution)/shard_map/weight_halves/pallas_call | solution.py:72
  9.1 3.9 %collective-permute-start.6 = (bf16[256,2048]{1,0:T(8,128)(2,1)S(1)}, bf16[256,2048]{1,0:T(8,128)(2,1)}, u32[]{:S(2)}, u32[]{:S(2)}) collective-permute-start(bf16[256,2048]{1,0:T(8,128)(2,1)S(1)} %get-tuple-element.45.w0), channel_id=1, source_target_pairs={{0,8},{1,3},{2,10},{3,1},{4,12},{5,7},{6,14},{7,5},{8,0},{9,11},{1... | collective-permute-start | bytes 3145736 | tf_op jit(solution)/shard_map/ppermute | solution.py:475
  13.0 4.4 %collective-permute-start.7 = (bf16[256,2048]{1,0:T(8,128)(2,1)}, bf16[256,2048]{1,0:T(8,128)(2,1)}, u32[]{:S(2)}, u32[]{:S(2)}) collective-permute-start(bf16[256,2048]{1,0:T(8,128)(2,1)} %get-tuple-element.46), channel_id=1, source_target_pairs={{0,24},{1,7},{2,26},{3,5},{4,28},{5,3},{6,30},{7,1},{8,16},{9,15},... | collective-permute-start | bytes 3145736 | tf_op jit(solution)/shard_map/ppermute | solution.py:475
  17.4 4.9 %all-to-all-start = ((bf16[16,3,48,256]{3,2,1,0:T(8,128)(2,1)}), bf16[16,3,48,256]{3,2,1,0:T(8,128)(2,1)S(1)}, u32[]{:S(2)}, u32[]{:S(2)}) async-start(bf16[16,3,48,256]{3,2,1,0:T(8,128)(2,1)} %norm_pack.1), calls=%async_computation | async-start | bytes 2359296 | tf_op jit(solution)/shard_map/all_to_all | solution.py:483
  28.8 13.0 %collective-permute-done.7.refs_1_ = bf16[256,2048]{1,0:T(8,128)(2,1)} collective-permute-done((bf16[256,2048]{1,0:T(8,128)(2,1)}, bf16[256,2048]{1,0:T(8,128)(2,1)}, u32[]{:S(2)}, u32[]{:S(2)}) %collective-permute-start.7) | collective-permute-done | bytes 1048608 | tf_op jit(solution)/shard_map/ppermute | solution.py:475
  41.9 3.1 %collective-permute-start.12 = (bf16[256,2048]{1,0:T(8,128)(2,1)}, bf16[256,2048]{1,0:T(8,128)(2,1)}, u32[]{:S(2)}, u32[]{:S(2)}) collective-permute-start(bf16[256,2048]{1,0:T(8,128)(2,1)} %get-tuple-element.53.w2), channel_id=1, source_target_pairs={{0,8},{1,3},{2,10},{3,1},{4,12},{5,7},{6,14},{7,5},{8,0},{9,11},{1... | collective-permute-start | bytes 3145736 | tf_op jit(solution)/shard_map/ppermute | solution.py:475
  45.2 2.2 %collective-permute-start.8 = (bf16[16,2,48,256]{3,2,1,0:T(8,128)(2,1)S(1)}, bf16[16,2,48,256]{3,2,1,0:T(8,128)(2,1)S(1)}, u32[]{:S(2)}, u32[]{:S(2)}) collective-permute-start(bf16[16,2,48,256]{3,2,1,0:T(8,128)(2,1)S(1)} %slice.3), channel_id=1, source_target_pairs={{0,1},{1,0},{2,3},{3,2},{4,5},{5,4},{6,7},{7,6},{8,9},{9,8},{10,11... | collective-permute-start | bytes 2359304 | tf_op jit(solution)/shard_map/ppermute | solution.py:475
  47.4 2.3 %collective-permute-done.8.there_ref = bf16[16,2,48,256]{3,2,1,0:T(8,128)(2,1)S(1)} collective-permute-done((bf16[16,2,48,256]{3,2,1,0:T(8,128)(2,1)S(1)}, bf16[16,2,48,256]{3,2,1,0:T(8,128)(2,1)S(1)}, u32[]{:S(2)}, u32[]{:S(2)}) %collective-permute-start.8) | collective-permute-done | bytes 786464 | tf_op jit(solution)/shard_map/ppermute | solution.py:475
  49.6 6.1 %attend.1 = (bf16[4,2,48,256]{3,2,1,0:T(8,128)(2,1)S(1)}, bf16[4,2,48,256]{3,2,1,0:T(8,128)(2,1)S(1)}) custom-call(s32[6]{0:T(128)S(1)} %copy-done.4, bf16[16,3,48,256]{3,2,1,0:T(8,128)(2,1)S(1)} %all-to-all-done.here_ref, bf16[16,2,48,256]{3,2,1,0:T(8,128)(2,1)S(1)} %collective-permute-done.8.there_ref), custom_call_target="tpu_custom_call" | custom-call | tf_op jit(solution)/shard_map/attend/pallas_call | solution.py:149
  55.7 5.0 %collective-permute-start.10 = (bf16[4,2,48,256]{3,2,1,0:T(8,128)(2,1)S(1)}, bf16[4,2,48,256]{3,2,1,0:T(8,128)(2,1)S(1)}, u32[]{:S(2)}, u32[]{:S(2)}) collective-permute-start(bf16[4,2,48,256]{3,2,1,0:T(8,128)(2,1)S(1)} %get-tuple-element.50.h0), channel_id=1, source_target_pairs={{0,24},{1,7},{2,26},{3,5},{4,28},{5,3},{6,30},{7,1},{8,16},{9,15},... | collective-permute-start | bytes 589832 | tf_op jit(solution)/shard_map/ppermute | solution.py:475
  60.7 3.0 %collective-permute-start.11 = (bf16[4,2,48,256]{3,2,1,0:T(8,128)(2,1)S(1)}, bf16[4,2,48,256]{3,2,1,0:T(8,128)(2,1)S(1)}, u32[]{:S(2)}, u32[]{:S(2)}) collective-permute-start(bf16[4,2,48,256]{3,2,1,0:T(8,128)(2,1)S(1)} %get-tuple-element.51), channel_id=1, source_target_pairs={{0,16},{1,5},{2,18},{3,7},{4,20},{5,1},{6,22},{7,3},{8,24},{9,13},... | collective-permute-start | bytes 589832 | tf_op jit(solution)/shard_map/ppermute | solution.py:475
  63.7 1.9 %collective-permute-start.9 = (bf16[4,2,48,256]{3,2,1,0:T(8,128)(2,1)S(1)}, bf16[4,2,48,256]{3,2,1,0:T(8,128)(2,1)S(1)}, u32[]{:S(2)}, u32[]{:S(2)}) collective-permute-start(bf16[4,2,48,256]{3,2,1,0:T(8,128)(2,1)S(1)} %get-tuple-element.51), channel_id=1, source_target_pairs={{0,8},{1,3},{2,10},{3,1},{4,12},{5,7},{6,14},{7,5},{8,0},{9,11},{1... | collective-permute-start | bytes 589832 | tf_op jit(solution)/shard_map/ppermute | solution.py:475
  65.6 4.2 %collective-permute-done.11.h3 = bf16[4,2,48,256]{3,2,1,0:T(8,128)(2,1)S(1)} collective-permute-done((bf16[4,2,48,256]{3,2,1,0:T(8,128)(2,1)S(1)}, bf16[4,2,48,256]{3,2,1,0:T(8,128)(2,1)S(1)}, u32[]{:S(2)}, u32[]{:S(2)}) %collective-permute-start.11) | collective-permute-done | bytes 196640 | tf_op jit(solution)/shard_map/ppermute | solution.py:475
  71.2 3.7 %project.1 = (f32[2,48,2048]{2,1,0:T(8,128)S(1)}, bf16[2,48,2048]{2,1,0:T(8,128)(2,1)S(1)}, bf16[2,48,2048]{2,1,0:T(8,128)(2,1)S(1)}, bf16[2,48,2048]{2,1,0:T(8,128)(2,1)S(1)}) custom-call(s32[6]{0:T(128)S(1)} %copy-done.4, bf16[4,2,48,256]{3,2,1,0:T(8,128)(2,1)S(1)} %get-tuple-element.50.h0, bf16[4,2,48,256]{3,2,1,0:T(8,128)(2,1)S(1)} %collective-permute-done.9.h1, ...), custom_call_target="tpu_custom_call" | custom-call | flops 1610612736 | bytes 8388608 | tf_op jit(solution)/shard_map/project/pallas_call | solution.py:188
  74.9 4.9 %collective-permute-start.13 = (bf16[2,48,2048]{2,1,0:T(8,128)(2,1)S(1)}, bf16[2,48,2048]{2,1,0:T(8,128)(2,1)S(1)}, u32[]{:S(2)}, u32[]{:S(2)}) collective-permute-start(bf16[2,48,2048]{2,1,0:T(8,128)(2,1)S(1)} %get-tuple-element.64), channel_id=1, source_target_pairs={{0,4},{1,17},{2,6},{3,19},{4,0},{5,21},{6,2},{7,23},{8,12},{9,25},... | collective-permute-start | bytes 1179656 | tf_op jit(solution)/shard_map/ppermute | solution.py:475
  79.9 3.1 %collective-permute-start.14 = (bf16[2,48,2048]{2,1,0:T(8,128)(2,1)S(1)}, bf16[2,48,2048]{2,1,0:T(8,128)(2,1)S(1)}, u32[]{:S(2)}, u32[]{:S(2)}) collective-permute-start(bf16[2,48,2048]{2,1,0:T(8,128)(2,1)S(1)} %get-tuple-element.65), channel_id=1, source_target_pairs={{0,6},{1,25},{2,4},{3,27},{4,2},{5,29},{6,0},{7,31},{8,14},{9,17},... | collective-permute-start | bytes 1179656 | tf_op jit(solution)/shard_map/ppermute | solution.py:475
  83.0 2.1 %collective-permute-start.15 = (bf16[2,48,2048]{2,1,0:T(8,128)(2,1)S(1)}, bf16[2,48,2048]{2,1,0:T(8,128)(2,1)S(1)}, u32[]{:S(2)}, u32[]{:S(2)}) collective-permute-start(bf16[2,48,2048]{2,1,0:T(8,128)(2,1)S(1)} %get-tuple-element.66), channel_id=1, source_target_pairs={{0,2},{1,9},{2,0},{3,11},{4,6},{5,13},{6,4},{7,15},{8,10},{9,1},{1... | collective-permute-start | bytes 1179656 | tf_op jit(solution)/shard_map/ppermute | solution.py:475
  85.3 2.8 %decode.1 = bf16[16,2,128,384]{3,2,1,0:T(8,128)(2,1)} custom-call(s32[6]{0:T(128)S(1)} %copy-done.4, bf16[16,6,16,128]{3,2,1,0:T(8,128)(2,1)S(1)} %pad_maximum_fusion.clip_ref, bf16[432,384]{1,0:T(8,128)(2,1)S(1)} %bitcast.19, bf16[4,384,1920]{2,1,0:T(8,128)(2,1)} %filter_weights_0.1.fa_ref, bf16[4,384,1536]{2,1,0:T(8,128)(2,1)S(1)} %bitcast.17, ...), custom_call_target="tpu_custom_call" | custom-call | tf_op jit(solution)/shard_map/decode/pallas_call | solution.py:399
  88.1 2.7 %collective-permute-done.14.b_ref = bf16[2,48,2048]{2,1,0:T(8,128)(2,1)S(1)} collective-permute-done((bf16[2,48,2048]{2,1,0:T(8,128)(2,1)S(1)}, bf16[2,48,2048]{2,1,0:T(8,128)(2,1)S(1)}, u32[]{:S(2)}, u32[]{:S(2)}) %collective-permute-start.14) | collective-permute-done | bytes 393248 | tf_op jit(solution)/shard_map/ppermute | solution.py:475
  90.8 1.9 %collective-permute-done.15.c_ref = bf16[2,48,2048]{2,1,0:T(8,128)(2,1)S(1)} collective-permute-done((bf16[2,48,2048]{2,1,0:T(8,128)(2,1)S(1)}, bf16[2,48,2048]{2,1,0:T(8,128)(2,1)S(1)}, u32[]{:S(2)}, u32[]{:S(2)}) %collective-permute-start.15) | collective-permute-done | bytes 393248 | tf_op jit(solution)/shard_map/ppermute | solution.py:475
  93.4 4.4 %collective-permute-start.16 = (bf16[48,2048]{1,0:T(8,128)(2,1)S(1)}, bf16[48,2048]{1,0:T(8,128)(2,1)S(1)}, u32[]{:S(2)}, u32[]{:S(2)}) collective-permute-start(bf16[48,2048]{1,0:T(8,128)(2,1)S(1)} %get-tuple-element.68), channel_id=1, source_target_pairs={{0,24},{1,7},{2,26},{3,5},{4,28},{5,3},{6,30},{7,1},{8,16},{9,15},... | collective-permute-start | bytes 589832 | tf_op jit(solution)/shard_map/ppermute | solution.py:475
  97.9 4.3 %collective-permute-done.16.got_ref = bf16[48,2048]{1,0:T(8,128)(2,1)S(1)} collective-permute-done((bf16[48,2048]{1,0:T(8,128)(2,1)S(1)}, bf16[48,2048]{1,0:T(8,128)(2,1)S(1)}, u32[]{:S(2)}, u32[]{:S(2)}) %collective-permute-start.16) | collective-permute-done | bytes 196640 | tf_op jit(solution)/shard_map/ppermute | solution.py:475
  (55 shorter events, 11.5 us)
Async XLA Ops:
  0.6 5.5 %collective-permute-start = (bf16[128,4096]{1,0:T(8,128)(2,1)}, bf16[128,4096]{1,0:T(8,128)(2,1)S(1)}, u32[]{:S(2)}, u32[]{:S(2)}) collective-permute-start(bf16[128,4096]{1,0:T(8,128)(2,1)} %here_ref.1), channel_id=1, source_target_pairs={{0,1},{1,0},{2,3},{3,2},{4,5},{5,4},{6,7},{7,6},{8,9},{9,8},{10,11... | collective-permute-start | bytes 3145736 | tf_op jit(solution)/shard_map/ppermute | solution.py:475
  9.1 19.8 %collective-permute-start.6 = (bf16[256,2048]{1,0:T(8,128)(2,1)S(1)}, bf16[256,2048]{1,0:T(8,128)(2,1)}, u32[]{:S(2)}, u32[]{:S(2)}) collective-permute-start(bf16[256,2048]{1,0:T(8,128)(2,1)S(1)} %get-tuple-element.45.w0), channel_id=1, source_target_pairs={{0,8},{1,3},{2,10},{3,1},{4,12},{5,7},{6,14},{7,5},{8,0},{9,11},{1... | collective-permute-start | bytes 3145736 | tf_op jit(solution)/shard_map/ppermute | solution.py:475
  13.0 28.9 %collective-permute-start.7 = (bf16[256,2048]{1,0:T(8,128)(2,1)}, bf16[256,2048]{1,0:T(8,128)(2,1)}, u32[]{:S(2)}, u32[]{:S(2)}) collective-permute-start(bf16[256,2048]{1,0:T(8,128)(2,1)} %get-tuple-element.46), channel_id=1, source_target_pairs={{0,24},{1,7},{2,26},{3,5},{4,28},{5,3},{6,30},{7,1},{8,16},{9,15},... | collective-permute-start | bytes 3145736 | tf_op jit(solution)/shard_map/ppermute | solution.py:475
  17.4 27.6 %all-to-all-start = ((bf16[16,3,48,256]{3,2,1,0:T(8,128)(2,1)}), bf16[16,3,48,256]{3,2,1,0:T(8,128)(2,1)S(1)}, u32[]{:S(2)}, u32[]{:S(2)}) async-start(bf16[16,3,48,256]{3,2,1,0:T(8,128)(2,1)} %norm_pack.1), calls=%async_computation | async-start | bytes 2359296 | tf_op jit(solution)/shard_map/all_to_all | solution.py:483
  22.4 3.6 %collective-permute-start.1 = (bf16[4,2,16,128]{3,2,1,0:T(8,128)(2,1)S(1)}, bf16[4,2,16,128]{3,2,1,0:T(8,128)(2,1)S(1)}, u32[]{:S(2)}, u32[]{:S(2)}) collective-permute-start(bf16[4,2,16,128]{3,2,1,0:T(8,128)(2,1)S(1)} %bitcast.27), channel_id=1, source_target_pairs={{0,96},{1,97},{2,98},{3,99},{4,100},{5,101},{6,102},{7,103},{8,104... | collective-permute-start | bytes 98312 | tf_op jit(solution)/shard_map/ppermute | solution.py:489
  23.9 2.0 %collective-permute-start.2 = (bf16[4,2,16,128]{3,2,1,0:T(8,128)(2,1)S(1)}, bf16[4,2,16,128]{3,2,1,0:T(8,128)(2,1)S(1)}, u32[]{:S(2)}, u32[]{:S(2)}) collective-permute-start(bf16[4,2,16,128]{3,2,1,0:T(8,128)(2,1)S(1)} %bitcast.28), channel_id=1, source_target_pairs={{32,96},{33,97},{34,98},{35,99},{36,100},{37,101},{38,102},{39,103... | collective-permute-start | bytes 98312 | tf_op jit(solution)/shard_map/ppermute | solution.py:489
  24.6 1.4 %collective-permute-start.3 = (bf16[4,2,16,128]{3,2,1,0:T(8,128)(2,1)S(1)}, bf16[4,2,16,128]{3,2,1,0:T(8,128)(2,1)S(1)}, u32[]{:S(2)}, u32[]{:S(2)}) collective-permute-start(bf16[4,2,16,128]{3,2,1,0:T(8,128)(2,1)S(1)} %bitcast.29), channel_id=1, source_target_pairs={{64,96},{65,97},{66,98},{67,99},{68,100},{69,101},{70,102},{71,103... | collective-permute-start | bytes 98312 | tf_op jit(solution)/shard_map/ppermute | solution.py:489
  26.0 2.0 %collective-permute-start.4 = (bf16[16,2,16,128]{3,2,1,0:T(8,128)(2,1)S(1)}, bf16[16,2,16,128]{3,2,1,0:T(8,128)(2,1)S(1)}, u32[]{:S(2)}, u32[]{:S(2)}) collective-permute-start(bf16[16,2,16,128]{3,2,1,0:T(8,128)(2,1)S(1)} %pad_maximum_fusion.1), channel_id=1, source_target_pairs={{96,97},{97,98},{98,99},{99,100},{100,101},{101,102},{102,103},{10... | collective-permute-start | bytes 393224 | tf_op jit(solution)/shard_map/ppermute | solution.py:494
  26.7 1.4 %collective-permute-start.5 = (bf16[16,2,16,128]{3,2,1,0:T(8,128)(2,1)S(1)}, bf16[16,2,16,128]{3,2,1,0:T(8,128)(2,1)S(1)}, u32[]{:S(2)}, u32[]{:S(2)}) collective-permute-start(bf16[16,2,16,128]{3,2,1,0:T(8,128)(2,1)S(1)} %pad_maximum_fusion.1), channel_id=1, source_target_pairs={{97,96},{98,97},{99,98},{100,99},{101,100},{102,101},{103,102},{10... | collective-permute-start | bytes 393224 | tf_op jit(solution)/shard_map/ppermute | solution.py:495
  41.9 43.3 %slice-start = ((s8[4718592]{0:T(1024)(128)(4,1)}), s8[524288]{0:T(1024)(128)(4,1)S(1)}, s32[]{:S(2)}) async-start(s8[4718592]{0:T(1024)(128)(4,1)} %bitcast.16), calls=%async_computation.1 | async-start | bytes 1048576
  41.9 29.4 %collective-permute-start.12 = (bf16[256,2048]{1,0:T(8,128)(2,1)}, bf16[256,2048]{1,0:T(8,128)(2,1)}, u32[]{:S(2)}, u32[]{:S(2)}) collective-permute-start(bf16[256,2048]{1,0:T(8,128)(2,1)} %get-tuple-element.53.w2), channel_id=1, source_target_pairs={{0,8},{1,3},{2,10},{3,1},{4,12},{5,7},{6,14},{7,5},{8,0},{9,11},{1... | collective-permute-start | bytes 3145736 | tf_op jit(solution)/shard_map/ppermute | solution.py:475
  45.0 40.1 %copy-start.7 = (f32[384]{0:T(512)S(1)}, f32[384]{0:T(512)}, u32[]{:S(2)}) copy-start(f32[384]{0:T(512)} %param.24) | copy-start | bytes 4612
  45.0 40.1 %copy-start.8 = (f32[384]{0:T(512)S(1)}, f32[384]{0:T(512)}, u32[]{:S(2)}) copy-start(f32[384]{0:T(512)} %param.25) | copy-start | bytes 4612
  45.1 40.1 %copy-start.9 = (f32[384]{0:T(512)S(1)}, f32[384]{0:T(512)}, u32[]{:S(2)}) copy-start(f32[384]{0:T(512)} %param.27) | copy-start | bytes 4612
  45.1 40.2 %slice-start.1 = ((s8[4718592]{0:T(1024)(128)(4,1)}), s8[4194304]{0:T(1024)(128)(4,1)S(1)}, s32[]{:S(2)}) async-start(s8[4718592]{0:T(1024)(128)(4,1)} %bitcast.16), calls=%async_computation.2 | async-start | bytes 8388608
  45.1 40.2 %copy-start.2 = (bf16[3,144,384]{2,1,0:T(8,128)(2,1)S(1)}, bf16[3,144,384]{2,1,0:T(8,128)(2,1)}, u32[]{:S(2)}) copy-start(bf16[3,144,384]{2,1,0:T(8,128)(2,1)} %param.23) | copy-start | bytes 995332
  45.2 4.4 %collective-permute-start.8 = (bf16[16,2,48,256]{3,2,1,0:T(8,128)(2,1)S(1)}, bf16[16,2,48,256]{3,2,1,0:T(8,128)(2,1)S(1)}, u32[]{:S(2)}, u32[]{:S(2)}) collective-permute-start(bf16[16,2,48,256]{3,2,1,0:T(8,128)(2,1)S(1)} %slice.3), channel_id=1, source_target_pairs={{0,1},{1,0},{2,3},{3,2},{4,5},{5,4},{6,7},{7,6},{8,9},{9,8},{10,11... | collective-permute-start | bytes 2359304 | tf_op jit(solution)/shard_map/ppermute | solution.py:475
  55.7 9.9 %collective-permute-start.10 = (bf16[4,2,48,256]{3,2,1,0:T(8,128)(2,1)S(1)}, bf16[4,2,48,256]{3,2,1,0:T(8,128)(2,1)S(1)}, u32[]{:S(2)}, u32[]{:S(2)}) collective-permute-start(bf16[4,2,48,256]{3,2,1,0:T(8,128)(2,1)S(1)} %get-tuple-element.50.h0), channel_id=1, source_target_pairs={{0,24},{1,7},{2,26},{3,5},{4,28},{5,3},{6,30},{7,1},{8,16},{9,15},... | collective-permute-start | bytes 589832 | tf_op jit(solution)/shard_map/ppermute | solution.py:475
  60.7 9.1 %collective-permute-start.11 = (bf16[4,2,48,256]{3,2,1,0:T(8,128)(2,1)S(1)}, bf16[4,2,48,256]{3,2,1,0:T(8,128)(2,1)S(1)}, u32[]{:S(2)}, u32[]{:S(2)}) collective-permute-start(bf16[4,2,48,256]{3,2,1,0:T(8,128)(2,1)S(1)} %get-tuple-element.51), channel_id=1, source_target_pairs={{0,16},{1,5},{2,18},{3,7},{4,20},{5,1},{6,22},{7,3},{8,24},{9,13},... | collective-permute-start | bytes 589832 | tf_op jit(solution)/shard_map/ppermute | solution.py:475
  63.7 7.6 %collective-permute-start.9 = (bf16[4,2,48,256]{3,2,1,0:T(8,128)(2,1)S(1)}, bf16[4,2,48,256]{3,2,1,0:T(8,128)(2,1)S(1)}, u32[]{:S(2)}, u32[]{:S(2)}) collective-permute-start(bf16[4,2,48,256]{3,2,1,0:T(8,128)(2,1)S(1)} %get-tuple-element.51), channel_id=1, source_target_pairs={{0,8},{1,3},{2,10},{3,1},{4,12},{5,7},{6,14},{7,5},{8,0},{9,11},{1... | collective-permute-start | bytes 589832 | tf_op jit(solution)/shard_map/ppermute | solution.py:475
  74.9 13.1 %collective-permute-start.13 = (bf16[2,48,2048]{2,1,0:T(8,128)(2,1)S(1)}, bf16[2,48,2048]{2,1,0:T(8,128)(2,1)S(1)}, u32[]{:S(2)}, u32[]{:S(2)}) collective-permute-start(bf16[2,48,2048]{2,1,0:T(8,128)(2,1)S(1)} %get-tuple-element.64), channel_id=1, source_target_pairs={{0,4},{1,17},{2,6},{3,19},{4,0},{5,21},{6,2},{7,23},{8,12},{9,25},... | collective-permute-start | bytes 1179656 | tf_op jit(solution)/shard_map/ppermute | solution.py:475
  79.9 10.9 %collective-permute-start.14 = (bf16[2,48,2048]{2,1,0:T(8,128)(2,1)S(1)}, bf16[2,48,2048]{2,1,0:T(8,128)(2,1)S(1)}, u32[]{:S(2)}, u32[]{:S(2)}) collective-permute-start(bf16[2,48,2048]{2,1,0:T(8,128)(2,1)S(1)} %get-tuple-element.65), channel_id=1, source_target_pairs={{0,6},{1,25},{2,4},{3,27},{4,2},{5,29},{6,0},{7,31},{8,14},{9,17},... | collective-permute-start | bytes 1179656 | tf_op jit(solution)/shard_map/ppermute | solution.py:475
  83.0 9.7 %collective-permute-start.15 = (bf16[2,48,2048]{2,1,0:T(8,128)(2,1)S(1)}, bf16[2,48,2048]{2,1,0:T(8,128)(2,1)S(1)}, u32[]{:S(2)}, u32[]{:S(2)}) collective-permute-start(bf16[2,48,2048]{2,1,0:T(8,128)(2,1)S(1)} %get-tuple-element.66), channel_id=1, source_target_pairs={{0,2},{1,9},{2,0},{3,11},{4,6},{5,13},{6,4},{7,15},{8,10},{9,1},{1... | collective-permute-start | bytes 1179656 | tf_op jit(solution)/shard_map/ppermute | solution.py:475
  93.4 8.8 %collective-permute-start.16 = (bf16[48,2048]{1,0:T(8,128)(2,1)S(1)}, bf16[48,2048]{1,0:T(8,128)(2,1)S(1)}, u32[]{:S(2)}, u32[]{:S(2)}) collective-permute-start(bf16[48,2048]{1,0:T(8,128)(2,1)S(1)} %get-tuple-element.68), channel_id=1, source_target_pairs={{0,24},{1,7},{2,26},{3,5},{4,28},{5,3},{6,30},{7,1},{8,16},{9,15},... | collective-permute-start | bytes 589832 | tf_op jit(solution)/shard_map/ppermute | solution.py:475
  (6 other events, 97.5 us)

commit v8 on v6

--- a/solution.py
+++ b/solution.py
@@ -6,7 +6,6 @@
 from jax.experimental.pallas import tpu as pltpu
 from jax.sharding import Mesh, PartitionSpec as P
 
-CHIPS = ("z", "x")
 SEQ = ("z", "x", "core")
 EPS = 1e-06
 MIB = 1024 * 1024
@@ -22,7 +21,7 @@
 
 def norm_pack(q, k, v, gain_q, gain_k):
     rows, width = q.shape
-    chips = width // 256
+    heads = width // 128
     block = 16
 
     def body(q_ref, k_ref, v_ref, gq_ref, gk_ref, out_ref):
@@ -34,112 +33,115 @@
         scale = 128**-0.5 * math.log2(math.e)
         qn = normed(q_ref, gq_ref[...] * scale)
         kn = normed(k_ref, gk_ref[...])
-        for c in range(chips):
-            cols = slice(256 * c, 256 * c + 256)
-            out_ref[c, 0] = qn[:, cols]
-            out_ref[c, 1] = kn[:, cols]
-            out_ref[c, 2] = v_ref[:, cols]
+        for h in range(heads):
+            cols = slice(128 * h, 128 * h + 128)
+            out_ref[h, 0] = qn[:, cols]
+            out_ref[h, 1] = kn[:, cols]
+            out_ref[h, 2] = v_ref[:, cols]
 
     tokens = pl.BlockSpec((block, width), lambda i: (i, 0))
     gains = pl.BlockSpec((1, width), lambda i: (0, 0))
     return pl.pallas_call(
         body,
         grid=(rows // block,),
-        out_shape=jax.ShapeDtypeStruct((chips, 3, rows, 256), jnp.bfloat16),
+        out_shape=jax.ShapeDtypeStruct((heads, 3, rows, 128), jnp.bfloat16),
         in_specs=[tokens, tokens, tokens, gains, gains],
-        out_specs=pl.BlockSpec((chips, 3, block, 256), lambda i: (0, 0, i, 0)),
+        out_specs=pl.BlockSpec((heads, 3, block, 128), lambda i: (0, 0, i, 0)),
         compiler_params=pltpu.CompilerParams(vmem_limit_bytes=60 * MIB),
         name="norm_pack",
     )(q, k, v, gain_q, gain_k)
 
 
-def weight_halves(place, w_here, w_there):
+def partners(position):
+    return position, jnp.bitwise_xor(position, 1), 3 - position, jnp.bitwise_xor(position, 2)
+
+
+def weight_half(place, w_here, w_there):
     rows, width = w_here.shape
     part = width // 2
 
-    def body(place_ref, here_ref, there_ref, keep_ref, give_ref):
+    def body(place_ref, here_ref, there_ref, out_ref):
         here_at = pl.ds(pl.multiple_of(place_ref[1] * rows, rows), rows)
         there_at = pl.ds(pl.multiple_of((1 - place_ref[1]) * rows, rows), rows)
 
         @pl.when(place_ref[0] == 0)
         def _():
-            for k, out in enumerate((keep_ref, give_ref)):
-                half = jnp.bitwise_xor(place_ref[4] // 2, k)
-                at = pl.ds(pl.multiple_of(half * part, part), part)
-                out[here_at] = here_ref[:, at]
-                out[there_at] = there_ref[:, at]
-
-    return pl.pallas_call(
-        body,
-        out_shape=(jax.ShapeDtypeStruct((2 * rows, part), jnp.bfloat16),) * 2,
+            at = pl.ds(pl.multiple_of(place_ref[1] * part, part), part)
+            out_ref[here_at] = here_ref[:, at]
+            out_ref[there_at] = there_ref[:, at]
+
+    return pl.pallas_call(
+        body,
+        out_shape=jax.ShapeDtypeStruct((2 * rows, part), jnp.bfloat16),
         in_specs=[smem_spec(), vmem_spec(), vmem_spec()],
-        out_specs=(vmem_spec(),) * 2,
+        out_specs=vmem_spec(),
         compiler_params=pltpu.CompilerParams(vmem_limit_bytes=16 * MIB),
-        name="weight_halves",
+        name="weight_half",
     )(place, w_here, w_there)
 
 
-def inner(position):
-    return ((position + 1) // 2) % 2
-
-
-def attend(place, here, there):
-    chips, _, tok, _ = here.shape
-    half = chips * tok
-
-    def body(place_ref, here_ref, there_ref, near_ref, other_ref):
+def attend(place, here):
+    devices, _, tok, width = here.shape
+    keys = devices * tok
+    steps, chains = 4, 2
+    lot = devices // (steps * chains)
+
+    def body(place_ref, here_ref, out_ref):
         step = pl.program_id(0)
 
         @pl.when(place_ref[0] == 0)
         def _():
-            queries = here_ref[pl.ds(4 * step, 4), 0].reshape(4 * tok, 256)
-            ones = jnp.ones((half, 128), jnp.bfloat16)
-            heads = []
-            for h in range(2):
-                cols = slice(128 * h, 128 * h + 128)
-                scores = [
-                    lax.dot_general(
-                        queries[:, cols],
-                        ref[:, at, :, cols].reshape(half, 128),
-                        (((1,), (1,)), ((), ())),
-                        preferred_element_type=jnp.float32,
-                    )
-                    for ref, at in ((here_ref, 1), (there_ref, 0))
-                ]
-                peak = jnp.maximum(*(jnp.max(s, axis=-1, keepdims=True) for s in scores))
-                o = None
-                for s, ref, at in zip(scores, (here_ref, there_ref), (2, 1)):
-                    values = jnp.concatenate([ref[:, at, :, cols].reshape(half, 128), ones], axis=1)
-                    p = jnp.exp2(s - peak).astype(jnp.bfloat16)
-                    part = jnp.dot(p, values, preferred_element_type=jnp.float32)
-                    o = part if o is None else o + part
-                heads.append(o[:, :128] / o[:, 128:])
-            joined = jnp.concatenate(heads, axis=1).astype(jnp.bfloat16)
-            for n in range(4):
-                first = jnp.where(place_ref[1] == 0, step, n)
-                second = jnp.where(place_ref[1] == 0, n, step)
-                high = first // 2
-                slot = jnp.where(second == 0, 0, jnp.where(second == 3, 1, second + 1))
-                near = inner(first) == inner(place_ref[4])
-                piece = joined[tok * n : tok * n + tok]
-
-                @pl.when(near)
-                def _():
-                    near_ref[slot, high] = piece
-
-                @pl.when(jnp.logical_not(near))
-                def _():
-                    other_ref[slot, high] = piece
-
-    return pl.pallas_call(
-        body,
-        grid=(chips // 4,),
-        out_shape=(jax.ShapeDtypeStruct((4, 2, tok, 256), jnp.bfloat16),) * 2,
-        in_specs=[smem_spec(), vmem_spec(), vmem_spec()],
-        out_specs=(vmem_spec(),) * 2,
+            ones = jnp.ones((keys, width), jnp.bfloat16)
+            values = jnp.concatenate([here_ref[:, 2].reshape(keys, width), ones], axis=1)
+            for n in range(chains):
+                at = pl.ds((step * chains + n) * lot, lot)
+                s = lax.dot_general(
+                    here_ref[at, 0].reshape(lot * tok, width),
+                    here_ref[:, 1].reshape(keys, width),
+                    (((1,), (1,)), ((), ())),
+                    preferred_element_type=jnp.float32,
+                )
+                p = jnp.exp2(s - jnp.max(s, axis=-1, keepdims=True)).astype(jnp.bfloat16)
+                o = jnp.dot(p, values, preferred_element_type=jnp.float32)
+                o = (o[:, :width] / o[:, width:]).astype(jnp.bfloat16)
+                out_ref[at] = o.reshape(lot, tok, width)
+
+    return pl.pallas_call(
+        body,
+        grid=(steps,),
+        out_shape=jax.ShapeDtypeStruct((devices, tok, width), jnp.bfloat16),
+        in_specs=[smem_spec(), vmem_spec()],
+        out_specs=vmem_spec(),
         compiler_params=pltpu.CompilerParams(vmem_limit_bytes=40 * MIB),
         cost_estimate=pl.CostEstimate(flops=0, bytes_accessed=0, transcendentals=0),
         name="attend",
+    )(place, here)
+
+
+def pair_heads(place, here, there):
+    devices, tok, width = here.shape
+
+    def body(place_ref, here_ref, there_ref, *outs):
+        core = place_ref[1]
+        here_at = pl.ds(pl.multiple_of(core * width, width), width)
+        there_at = pl.ds(pl.multiple_of((1 - core) * width, width), width)
+
+        @pl.when(place_ref[0] == 0)
+        def _():
+            for first, out in zip(partners(place_ref[4]), outs):
+                for second in range(4):
+                    chip = jnp.where(core == 0, 4 * first + second, 4 * second + first)
+                    at = pl.ds(2 * chip, 2)
+                    out[second, :, :, here_at] = here_ref[at]
+                    out[second, :, :, there_at] = there_ref[at]
+
+    return pl.pallas_call(
+        body,
+        out_shape=(jax.ShapeDtypeStruct((4, 2, tok, 2 * width), jnp.bfloat16),) * 4,
+        in_specs=[smem_spec(), vmem_spec(), vmem_spec()],
+        out_specs=(vmem_spec(),) * 4,
+        compiler_params=pltpu.CompilerParams(vmem_limit_bytes=16 * MIB),
+        name="pair_heads",
     )(place, here, there)
 
 
@@ -148,25 +150,19 @@
     part = weights[0].shape[1]
     lot = two * tok
 
-    def body(place_ref, h0, h1, h2, h3, w0, w1, w2, w3, own_ref, one_ref, zero_ref, far_ref):
-        second = place_ref[5]
-        slot = jnp.where(second == 0, 0, jnp.where(second == 3, 1, second + 1))
-
+    def body(place_ref, h0, h1, h2, h3, w0, w1, w2, w3, *outs):
         @pl.when(place_ref[0] == 0)
         def _():
             weight = jnp.concatenate([w0[...], w1[...], w2[...], w3[...]], axis=0)
             feats = jnp.concatenate(
                 [
-                    jnp.concatenate(
-                        [h[jnp.bitwise_xor(slot, k)].reshape(lot, 256) for h in (h0, h1, h2, h3)],
-                        axis=1,
-                    )
-                    for k in range(4)
+                    jnp.concatenate([h[chip].reshape(lot, 256) for h in (h0, h1, h2, h3)], axis=1)
+                    for chip in partners(place_ref[5])
                 ],
                 axis=0,
             )
             out = jnp.dot(feats, weight, preferred_element_type=jnp.float32)
-            for k, ref in enumerate((own_ref, one_ref, zero_ref, far_ref)):
+            for k, ref in enumerate(outs):
                 ref[...] = out[lot * k : lot * k + lot].reshape(two, tok, part).astype(ref.dtype)
 
     shape = (two, tok, part)
@@ -186,11 +182,11 @@
 
 def add_up(place, own, others):
     def body(place_ref, own_ref, a_ref, b_ref, c_ref, keep_ref, give_ref):
-        mine = place_ref[4] // 2
+        core = place_ref[1]
 
         @pl.when(place_ref[0] == 0)
         def _():
-            for at, out in ((mine, keep_ref), (1 - mine, give_ref)):
+            for at, out in ((core, keep_ref), (1 - core, give_ref)):
                 total = own_ref[at]
                 for ref in (a_ref, b_ref, c_ref):
                     total += ref[at].astype(jnp.float32)
@@ -215,8 +211,7 @@
     def body(place_ref, resid_ref, gate_ref, kept_ref, got_ref, out_ref):
         @pl.when(place_ref[0] == 0)
         def _():
-            for k, ref in enumerate((kept_ref, got_ref)):
-                half = jnp.bitwise_xor(place_ref[4] // 2, k)
+            for half, ref in ((place_ref[1], kept_ref), (1 - place_ref[1], got_ref)):
                 at = pl.ds(pl.multiple_of(half * part, part), part)
                 total = resid_ref[:, at].astype(jnp.float32)
                 total += gate_ref[:, at] * ref[...].astype(jnp.float32)
@@ -463,11 +458,12 @@
         query_input[0], key_input[0], value_input[0], query_norm_gain[None], key_norm_gain[None]
     )
     packed, w_here = lax.optimization_barrier((packed, output_weight))
-    here = lax.all_to_all(packed, CHIPS, split_axis=0, concat_axis=0, tiled=True)
-
-    w_own, w_give = weight_halves(place, w_here, swap(w_here, 2, 0))
-    w_own, w_give, latents, w_mid = lax.optimization_barrier((w_own, w_give, latents, w_mid))
-    w_next, w_back = swap(w_own, 0, 0), swap(w_give, 0, 1)
+    here = lax.all_to_all(packed, SEQ, split_axis=0, concat_axis=0, tiled=True)
+
+    w_own = weight_half(place, w_here, swap(w_here, 2, 0))
+    w_own, latents, w_mid = lax.optimization_barrier((w_own, latents, w_mid))
+    w_back = swap(w_own, 0, 1)
+    w_next = swap(w_own, 0, 0)
 
     own = jnp.swapaxes(latents, 2, 3)
     pieces = [lax.ppermute(own, "grp", [(g, last)]) for g in range(last)]
@@ -482,14 +478,15 @@
     cells = jnp.concatenate([above, clip, below], axis=1)
 
     here, cells = lax.optimization_barrier((here, cells))
-    there = swap(here[:, 1:], 2, 0)
-    there, w_next, w_back = lax.optimization_barrier((there, w_next, w_back))
-    near, other = attend(place, here, there)
-    near, other, w_back = lax.optimization_barrier((near, other, w_back))
+    head = attend(place, here)
+    head, w_back = lax.optimization_barrier((head, w_back))
+    head_there = swap(head, 2, 0)
     w_far = swap(w_back, 0, 0)
-    from_far = swap(other, 0, 2)
-    heads = near, swap(other, 0, 0), swap(near, 0, 1), from_far
-    mine, one, zero, far = project(place, heads, (w_own, w_next, w_back, w_far))
+    head_there, w_next = lax.optimization_barrier((head_there, w_next))
+    heads = pair_heads(place, head, head_there)
+    from_far = swap(heads[3], 0, 2)
+    heads = heads[0], swap(heads[1], 0, 0), swap(heads[2], 0, 1), from_far
+    mine, zero, one, far = project(place, heads, (w_own, w_next, w_back, w_far))
     mine, one, zero, far, cells = lax.optimization_barrier((mine, one, zero, far, cells))
     sums = swap(far, 1, 2), swap(one, 1, 1), swap(zero, 1, 0)
     decoded = decode(
@@ -497,7 +494,7 @@
     )
     mine, decoded = lax.optimization_barrier((mine, decoded))
     kept, give = add_up(place, mine, sums)
-    attn_out = finish(place, resid[0], gate, kept, swap(give, 0, 1))
+    attn_out = finish(place, resid[0], gate, kept, swap(give, 2, 0))
     return attn_out[None], decoded[None]
 
 

time: 104 us -> 93 us (0.89)
  the two profiles are of different devices: /device:TPU:0 before, /device:TPU:56 now
where the time goes in v8:
time: 93 us; the launch traced here: 92.3 us
  Pallas kernels  58.1 us (62%)
  starting transfers between devices  30.1 us (32%)
  local copies, waits for them, and re-layouts  2.86 us (3%)
  between operations  1.12 us (1%)
    pallas_call x1, Pallas kernels, decode(): pl.pallas_call(body, grid=(frames // lot,), out_shape=jax.ShapeDtypeStruc...  35.6 us
    pallas_call x2, Pallas kernels, filter_weights(): pl.pallas_call(body, out_shape=jax.ShapeDtypeStruct((4, vc, count * vc),...  13.7 us
    ppermute x12, starting transfers between devices, swap(): return lax.ppermute(x, ('grp',) + SEQ, pairs)  10.5 us
    all_to_all x1, starting transfers between devices, on_device(): here = lax.all_to_all(packed, SEQ, split_axis=0, concat_axis=0, tiled=True)  8.05 us
    ppermute x1, starting transfers between devices, on_device(): below = lax.ppermute(clip, ('grp',) + SEQ, [(b, a) for a, b in links])  5.61 us
    ppermute x3, starting transfers between devices, on_device(): pieces = [lax.ppermute(own, 'grp', [(g, last)]) for g in range(last)]  3.86 us
    pallas_call x1, Pallas kernels, norm_pack(): pl.pallas_call(body, grid=(rows // block,), out_shape=jax.ShapeDtypeStruc...  3.58 us
    unnamed x26, local copies, waits for them, and re-layouts  2.77 us
  transfers between devices with their start and end apart: 18, of which 0 were waited for; matrix products, arithmetic and copies ran while one was open for 0% of the time, Pallas kernels for 55%

profile of v8, /device:TPU:56, one launch (start us, length us, event | category | flops | bytes accessed | tf_op | source)
XLA Modules:
  0.0 92.3 jit_solution(13409518197508698547)
XLA Ops:
  0.7 3.6 %norm_pack.1 = bf16[32,3,48,128]{3,2,1,0:T(8,128)(2,1)} custom-call(bf16[48,4096]{1,0:T(8,128)(2,1)} %bitcast.21, bf16[48,4096]{1,0:T(8,128)(2,1)} %bitcast.22, bf16[48,4096]{1,0:T(8,128)(2,1)} %bitcast.23, f32[1,4096]{1,0:T(1,128)} %bitcast.30, f32[1,4096]{1,0:T(1,128)} %bitcast.31), custom_call_target="tpu_custom_call" | custom-call | tf_op jit(solution)/shard_map/norm_pack/pallas_call | solution.py:44
  4.2 0.7 collective-permute-start
  5.0 8.1 %all-to-all-start = ((bf16[32,3,48,128]{3,2,1,0:T(8,128)(2,1)}), bf16[32,3,48,128]{3,2,1,0:T(8,128)(2,1)S(1)}, u32[]{:S(2)}, u32[]{:S(2)}) async-start(bf16[32,3,48,128]{3,2,1,0:T(8,128)(2,1)} %norm_pack.1), calls=%async_computation | async-start | bytes 2359296 | tf_op jit(solution)/shard_map/all_to_all | solution.py:461
  13.1 1.0 %copy-done.2 = bf16[128,4096]{1,0:T(8,128)(2,1)} copy-done((bf16[128,4096]{1,0:T(8,128)(2,1)}, bf16[128,4096]{1,0:T(8,128)(2,1)S(1)}, u32[]{:S(2)}) %copy-start.2) | copy-done | bytes 1048600
  14.1 1.2 %copy-done.3 = bf16[128,4096]{1,0:T(8,128)(2,1)S(1)} copy-done((bf16[128,4096]{1,0:T(8,128)(2,1)S(1)}, bf16[128,4096]{1,0:T(8,128)(2,1)}, u32[]{:S(2)}) %copy-start.3) | copy-done | bytes 1048600
  16.4 1.6 %collective-permute-start.6 = (bf16[256,2048]{1,0:T(8,128)(2,1)S(1)}, bf16[256,2048]{1,0:T(8,128)(2,1)}, u32[]{:S(2)}, u32[]{:S(2)}) collective-permute-start(bf16[256,2048]{1,0:T(8,128)(2,1)S(1)} %weight_half.1.w0), channel_id=1, source_target_pairs={{0,24},{1,7},{2,26},{3,5},{4,28},{5,3},{6,30},{7,1},{8,16},{9,15},... | collective-permute-start | bytes 3145736 | tf_op jit(solution)/shard_map/ppermute | solution.py:455
  18.0 1.3 %collective-permute-start.1 = (bf16[4,2,16,128]{3,2,1,0:T(8,128)(2,1)S(1)}, bf16[4,2,16,128]{3,2,1,0:T(8,128)(2,1)S(1)}, u32[]{:S(2)}, u32[]{:S(2)}) collective-permute-start(bf16[4,2,16,128]{3,2,1,0:T(8,128)(2,1)S(1)} %bitcast.25), channel_id=1, source_target_pairs={{0,96},{1,97},{2,98},{3,99},{4,100},{5,101},{6,102},{7,103},{8,104... | collective-permute-start | bytes 98312 | tf_op jit(solution)/shard_map/ppermute | solution.py:469
  19.3 1.3 %collective-permute-start.2 = (bf16[4,2,16,128]{3,2,1,0:T(8,128)(2,1)S(1)}, bf16[4,2,16,128]{3,2,1,0:T(8,128)(2,1)S(1)}, u32[]{:S(2)}, u32[]{:S(2)}) collective-permute-start(bf16[4,2,16,128]{3,2,1,0:T(8,128)(2,1)S(1)} %bitcast.26), channel_id=1, source_target_pairs={{32,96},{33,97},{34,98},{35,99},{36,100},{37,101},{38,102},{39,103... | collective-permute-start | bytes 98312 | tf_op jit(solution)/shard_map/ppermute | solution.py:469
  20.6 1.3 %collective-permute-start.3 = (bf16[4,2,16,128]{3,2,1,0:T(8,128)(2,1)S(1)}, bf16[4,2,16,128]{3,2,1,0:T(8,128)(2,1)S(1)}, u32[]{:S(2)}, u32[]{:S(2)}) collective-permute-start(bf16[4,2,16,128]{3,2,1,0:T(8,128)(2,1)S(1)} %bitcast.27), channel_id=1, source_target_pairs={{64,96},{65,97},{66,98},{67,99},{68,100},{69,101},{70,102},{71,103... | collective-permute-start | bytes 98312 | tf_op jit(solution)/shard_map/ppermute | solution.py:469
  21.9 7.8 %filter_weights_0.1.fa_ref = bf16[4,384,1920]{2,1,0:T(8,128)(2,1)} custom-call(s32[6]{0:T(128)} %copy-done.6, bf16[3,3,3,384,384]{4,3,2,1,0:T(8,128)(2,1)} %bitcast.18), custom_call_target="tpu_custom_call" | custom-call | tf_op jit(solution)/shard_map/filter_weights_0/pallas_call | solution.py:259
  29.7 2.1 %collective-permute-start.4 = (bf16[16,2,16,128]{3,2,1,0:T(8,128)(2,1)S(1)}, bf16[16,2,16,128]{3,2,1,0:T(8,128)(2,1)S(1)}, u32[]{:S(2)}, u32[]{:S(2)}) collective-permute-start(bf16[16,2,16,128]{3,2,1,0:T(8,128)(2,1)S(1)} %pad_maximum_fusion.1), channel_id=1, source_target_pairs={{96,97},{97,98},{98,99},{99,100},{100,101},{101,102},{102,103},{10... | collective-permute-start | bytes 393224 | tf_op jit(solution)/shard_map/ppermute | solution.py:474
  31.8 5.6 %collective-permute-start.5 = (bf16[16,2,16,128]{3,2,1,0:T(8,128)(2,1)S(1)}, bf16[16,2,16,128]{3,2,1,0:T(8,128)(2,1)S(1)}, u32[]{:S(2)}, u32[]{:S(2)}) collective-permute-start(bf16[16,2,16,128]{3,2,1,0:T(8,128)(2,1)S(1)} %pad_maximum_fusion.1), channel_id=1, source_target_pairs={{97,96},{98,97},{99,98},{100,99},{101,100},{102,101},{103,102},{10... | collective-permute-start | bytes 393224 | tf_op jit(solution)/shard_map/ppermute | solution.py:475
  37.4 1.7 %collective-permute-start.8 = (bf16[256,2048]{1,0:T(8,128)(2,1)S(1)}, bf16[256,2048]{1,0:T(8,128)(2,1)}, u32[]{:S(2)}, u32[]{:S(2)}) collective-permute-start(bf16[256,2048]{1,0:T(8,128)(2,1)S(1)} %weight_half.1.w0), channel_id=1, source_target_pairs={{0,8},{1,3},{2,10},{3,1},{4,12},{5,7},{6,14},{7,5},{8,0},{9,11},{1... | collective-permute-start | bytes 3145736 | tf_op jit(solution)/shard_map/ppermute | solution.py:455
  39.1 6.0 %filter_weights_5.1.fb_ref = bf16[4,384,1536]{2,1,0:T(8,128)(2,1)} custom-call(s32[6]{0:T(128)} %copy-done.6, bf16[3,3,3,384,384]{4,3,2,1,0:T(8,128)(2,1)} %bitcast.19), custom_call_target="tpu_custom_call" | custom-call | tf_op jit(solution)/shard_map/filter_weights_5/pallas_call | solution.py:259
  45.9 0.9 collective-permute-start.12
  46.8 0.7 collective-permute-start.7
  48.0 0.7 collective-permute-start.10
  48.7 0.7 collective-permute-start.11
  50.1 1.6 %project.1 = (f32[2,48,2048]{2,1,0:T(8,128)S(1)}, bf16[2,48,2048]{2,1,0:T(8,128)(2,1)S(1)}, bf16[2,48,2048]{2,1,0:T(8,128)(2,1)S(1)}, bf16[2,48,2048]{2,1,0:T(8,128)(2,1)S(1)}) custom-call(s32[6]{0:T(128)S(1)} %copy-done.7, bf16[4,2,48,256]{3,2,1,0:T(8,128)(2,1)S(1)} %get-tuple-element.50.h0, bf16[4,2,48,256]{3,2,1,0:T(8,128)(2,1)S(1)} %collective-permute-done.9.h1, ...), custom_call_target="tpu_custom_call" | custom-call | flops 1610612736 | bytes 8388608 | tf_op jit(solution)/shard_map/project/pallas_call | solution.py:169
  51.7 0.7 collective-permute-start.13
  52.4 0.7 collective-permute-start.14
  53.1 0.9 collective-permute-start.15
  54.1 35.6 %decode.1 = bf16[16,2,128,384]{3,2,1,0:T(8,128)(2,1)} custom-call(s32[6]{0:T(128)S(1)} %copy-done.7, bf16[16,6,16,128]{3,2,1,0:T(8,128)(2,1)S(1)} %pad_maximum_fusion.clip_ref, bf16[432,384]{1,0:T(8,128)(2,1)S(1)} %bitcast.17, bf16[4,384,1920]{2,1,0:T(8,128)(2,1)} %filter_weights_0.1.fa_ref, bf16[4,384,1536]{2,1,0:T(8,128)(2,1)S(1)} %copy-done, ...), custom_call_target="tpu_custom_call" | custom-call | tf_op jit(solution)/shard_map/decode/pallas_call | solution.py:379
  91.0 1.3 %finish.1 = bf16[48,4096]{1,0:T(8,128)(2,1)} custom-call(s32[6]{0:T(128)S(1)} %copy-done.7, bf16[48,4096]{1,0:T(8,128)(2,1)S(1)} %bitcast.16, f32[1,4096]{1,0:T(1,128)S(1)} %copy-done.8, f32[48,2048]{1,0:T(8,128)S(1)} %get-tuple-element.69.kept_ref, bf16[48,2048]{1,0:T(8,128)(2,1)S(1)} %collective-permute-done.16.got_ref), custom_call_target="tpu_custom_call" | custom-call | tf_op jit(solution)/shard_map/finish/pallas_call | solution.py:224
  (55 shorter events, 4.4 us)
Async XLA Ops:
  0.6 13.5 %copy-start.1 = (bf16[128,4096]{1,0:T(8,128)(2,1)S(1)}, bf16[128,4096]{1,0:T(8,128)(2,1)}, u32[]{:S(2)}) copy-start(bf16[128,4096]{1,0:T(8,128)(2,1)} %here_ref) | copy-start | bytes 3145732
  0.6 17.4 %copy-start.9 = (bf16[4,2,128,16]{2,3,1,0:T(8,128)(2,1)S(1)}, bf16[4,2,128,16]{2,3,1,0:T(8,128)(2,1)}, u32[]{:S(2)}) copy-start(bf16[4,2,128,16]{2,3,1,0:T(8,128)(2,1)} %param.22) | copy-start | bytes 98308
  4.2 8.9 %collective-permute-start = (bf16[128,4096]{1,0:T(8,128)(2,1)}, bf16[128,4096]{1,0:T(8,128)(2,1)S(1)}, u32[]{:S(2)}, u32[]{:S(2)}) collective-permute-start(bf16[128,4096]{1,0:T(8,128)(2,1)} %here_ref), channel_id=1, source_target_pairs={{0,1},{1,0},{2,3},{3,2},{4,5},{5,4},{6,7},{7,6},{8,9},{9,8},{10,11... | collective-permute-start | bytes 3145736 | tf_op jit(solution)/shard_map/ppermute | solution.py:455
  5.0 40.2 %all-to-all-start = ((bf16[32,3,48,128]{3,2,1,0:T(8,128)(2,1)}), bf16[32,3,48,128]{3,2,1,0:T(8,128)(2,1)S(1)}, u32[]{:S(2)}, u32[]{:S(2)}) async-start(bf16[32,3,48,128]{3,2,1,0:T(8,128)(2,1)} %norm_pack.1), calls=%async_computation | async-start | bytes 2359296 | tf_op jit(solution)/shard_map/all_to_all | solution.py:461
  16.4 29.5 %collective-permute-start.6 = (bf16[256,2048]{1,0:T(8,128)(2,1)S(1)}, bf16[256,2048]{1,0:T(8,128)(2,1)}, u32[]{:S(2)}, u32[]{:S(2)}) collective-permute-start(bf16[256,2048]{1,0:T(8,128)(2,1)S(1)} %weight_half.1.w0), channel_id=1, source_target_pairs={{0,24},{1,7},{2,26},{3,5},{4,28},{5,3},{6,30},{7,1},{8,16},{9,15},... | collective-permute-start | bytes 3145736 | tf_op jit(solution)/shard_map/ppermute | solution.py:455
  18.0 11.6 %collective-permute-start.1 = (bf16[4,2,16,128]{3,2,1,0:T(8,128)(2,1)S(1)}, bf16[4,2,16,128]{3,2,1,0:T(8,128)(2,1)S(1)}, u32[]{:S(2)}, u32[]{:S(2)}) collective-permute-start(bf16[4,2,16,128]{3,2,1,0:T(8,128)(2,1)S(1)} %bitcast.25), channel_id=1, source_target_pairs={{0,96},{1,97},{2,98},{3,99},{4,100},{5,101},{6,102},{7,103},{8,104... | collective-permute-start | bytes 98312 | tf_op jit(solution)/shard_map/ppermute | solution.py:469
  19.3 10.4 %collective-permute-start.2 = (bf16[4,2,16,128]{3,2,1,0:T(8,128)(2,1)S(1)}, bf16[4,2,16,128]{3,2,1,0:T(8,128)(2,1)S(1)}, u32[]{:S(2)}, u32[]{:S(2)}) collective-permute-start(bf16[4,2,16,128]{3,2,1,0:T(8,128)(2,1)S(1)} %bitcast.26), channel_id=1, source_target_pairs={{32,96},{33,97},{34,98},{35,99},{36,100},{37,101},{38,102},{39,103... | collective-permute-start | bytes 98312 | tf_op jit(solution)/shard_map/ppermute | solution.py:469
  20.6 9.1 %collective-permute-start.3 = (bf16[4,2,16,128]{3,2,1,0:T(8,128)(2,1)S(1)}, bf16[4,2,16,128]{3,2,1,0:T(8,128)(2,1)S(1)}, u32[]{:S(2)}, u32[]{:S(2)}) collective-permute-start(bf16[4,2,16,128]{3,2,1,0:T(8,128)(2,1)S(1)} %bitcast.27), channel_id=1, source_target_pairs={{64,96},{65,97},{66,98},{67,99},{68,100},{69,101},{70,102},{71,103... | collective-permute-start | bytes 98312 | tf_op jit(solution)/shard_map/ppermute | solution.py:469
  29.7 15.5 %copy-start.7 = (s32[6]{0:T(128)S(1)}, s32[6]{0:T(128)}, u32[]{:S(2)}) copy-start(s32[6]{0:T(128)} %copy-done.6) | copy-start | bytes 76
  29.7 15.4 %collective-permute-start.4 = (bf16[16,2,16,128]{3,2,1,0:T(8,128)(2,1)S(1)}, bf16[16,2,16,128]{3,2,1,0:T(8,128)(2,1)S(1)}, u32[]{:S(2)}, u32[]{:S(2)}) collective-permute-start(bf16[16,2,16,128]{3,2,1,0:T(8,128)(2,1)S(1)} %pad_maximum_fusion.1), channel_id=1, source_target_pairs={{96,97},{97,98},{98,99},{99,100},{100,101},{101,102},{102,103},{10... | collective-permute-start | bytes 393224 | tf_op jit(solution)/shard_map/ppermute | solution.py:474
  31.8 13.3 %collective-permute-start.5 = (bf16[16,2,16,128]{3,2,1,0:T(8,128)(2,1)S(1)}, bf16[16,2,16,128]{3,2,1,0:T(8,128)(2,1)S(1)}, u32[]{:S(2)}, u32[]{:S(2)}) collective-permute-start(bf16[16,2,16,128]{3,2,1,0:T(8,128)(2,1)S(1)} %pad_maximum_fusion.1), channel_id=1, source_target_pairs={{97,96},{98,97},{99,98},{100,99},{101,100},{102,101},{103,102},{10... | collective-permute-start | bytes 393224 | tf_op jit(solution)/shard_map/ppermute | solution.py:475
  37.4 10.0 %collective-permute-start.8 = (bf16[256,2048]{1,0:T(8,128)(2,1)S(1)}, bf16[256,2048]{1,0:T(8,128)(2,1)}, u32[]{:S(2)}, u32[]{:S(2)}) collective-permute-start(bf16[256,2048]{1,0:T(8,128)(2,1)S(1)} %weight_half.1.w0), channel_id=1, source_target_pairs={{0,8},{1,3},{2,10},{3,1},{4,12},{5,7},{6,14},{7,5},{8,0},{9,11},{1... | collective-permute-start | bytes 3145736 | tf_op jit(solution)/shard_map/ppermute | solution.py:455
  45.1 8.9 %copy-start.5 = (bf16[3,144,384]{2,1,0:T(8,128)(2,1)S(1)}, bf16[3,144,384]{2,1,0:T(8,128)(2,1)}, u32[]{:S(2)}) copy-start(bf16[3,144,384]{2,1,0:T(8,128)(2,1)} %param.23) | copy-start | bytes 995332
  45.9 4.2 %collective-permute-start.12 = (bf16[256,2048]{1,0:T(8,128)(2,1)}, bf16[256,2048]{1,0:T(8,128)(2,1)S(1)}, u32[]{:S(2)}, u32[]{:S(2)}) collective-permute-start(bf16[256,2048]{1,0:T(8,128)(2,1)} %collective-permute-done.6.w2), channel_id=1, source_target_pairs={{0,8},{1,3},{2,10},{3,1},{4,12},{5,7},{6,14},{7,5},{8,0},{9,11},{1... | collective-permute-start | bytes 3145736 | tf_op jit(solution)/shard_map/ppermute | solution.py:455
  46.8 0.7 collective-permute-start.7
  48.0 2.0 %collective-permute-start.10 = (bf16[4,2,48,256]{3,2,1,0:T(8,128)(2,1)S(1)}, bf16[4,2,48,256]{3,2,1,0:T(8,128)(2,1)S(1)}, u32[]{:S(2)}, u32[]{:S(2)}) collective-permute-start(bf16[4,2,48,256]{3,2,1,0:T(8,128)(2,1)S(1)} %get-tuple-element.52), channel_id=1, source_target_pairs={{0,24},{1,7},{2,26},{3,5},{4,28},{5,3},{6,30},{7,1},{8,16},{9,15},... | collective-permute-start | bytes 589832 | tf_op jit(solution)/shard_map/ppermute | solution.py:455
  48.7 1.4 %collective-permute-start.11 = (bf16[4,2,48,256]{3,2,1,0:T(8,128)(2,1)S(1)}, bf16[4,2,48,256]{3,2,1,0:T(8,128)(2,1)S(1)}, u32[]{:S(2)}, u32[]{:S(2)}) collective-permute-start(bf16[4,2,48,256]{3,2,1,0:T(8,128)(2,1)S(1)} %get-tuple-element.53), channel_id=1, source_target_pairs={{0,16},{1,5},{2,18},{3,7},{4,20},{5,1},{6,22},{7,3},{8,24},{9,13},... | collective-permute-start | bytes 589832 | tf_op jit(solution)/shard_map/ppermute | solution.py:455
  49.4 0.7 collective-permute-start.9
  51.7 38.0 %collective-permute-start.13 = (bf16[2,48,2048]{2,1,0:T(8,128)(2,1)S(1)}, bf16[2,48,2048]{2,1,0:T(8,128)(2,1)S(1)}, u32[]{:S(2)}, u32[]{:S(2)}) collective-permute-start(bf16[2,48,2048]{2,1,0:T(8,128)(2,1)S(1)} %get-tuple-element.66), channel_id=1, source_target_pairs={{0,4},{1,17},{2,6},{3,19},{4,0},{5,21},{6,2},{7,23},{8,12},{9,25},... | collective-permute-start | bytes 1179656 | tf_op jit(solution)/shard_map/ppermute | solution.py:455
  52.4 37.3 %collective-permute-start.14 = (bf16[2,48,2048]{2,1,0:T(8,128)(2,1)S(1)}, bf16[2,48,2048]{2,1,0:T(8,128)(2,1)S(1)}, u32[]{:S(2)}, u32[]{:S(2)}) collective-permute-start(bf16[2,48,2048]{2,1,0:T(8,128)(2,1)S(1)} %get-tuple-element.67), channel_id=1, source_target_pairs={{0,6},{1,25},{2,4},{3,27},{4,2},{5,29},{6,0},{7,31},{8,14},{9,17},... | collective-permute-start | bytes 1179656 | tf_op jit(solution)/shard_map/ppermute | solution.py:455
  53.1 36.6 %collective-permute-start.15 = (bf16[2,48,2048]{2,1,0:T(8,128)(2,1)S(1)}, bf16[2,48,2048]{2,1,0:T(8,128)(2,1)S(1)}, u32[]{:S(2)}, u32[]{:S(2)}) collective-permute-start(bf16[2,48,2048]{2,1,0:T(8,128)(2,1)S(1)} %get-tuple-element.68), channel_id=1, source_target_pairs={{0,2},{1,9},{2,0},{3,11},{4,6},{5,13},{6,4},{7,15},{8,10},{9,1},{1... | collective-permute-start | bytes 1179656 | tf_op jit(solution)/shard_map/ppermute | solution.py:455
  54.1 36.9 %copy-start.4 = (bf16[1,48,4096]{2,1,0:T(8,128)(2,1)S(1)}, bf16[1,48,4096]{2,1,0:T(8,128)(2,1)}, u32[]{:S(2)}) copy-start(bf16[1,48,4096]{2,1,0:T(8,128)(2,1)} %param.17) | copy-start | bytes 1179652
  54.1 36.9 %copy-start.8 = (f32[1,4096]{1,0:T(1,128)S(1)}, f32[1,4096]{1,0:T(1,128)}, u32[]{:S(2)}) copy-start(f32[1,4096]{1,0:T(1,128)} %gate_ref.1) | copy-start | bytes 49156
  90.2 0.7 collective-permute-start.16
  (7 other events, 38.2 us)

commit v9 on v8

--- a/solution.py
+++ b/solution.py
@@ -22,7 +22,7 @@
 def norm_pack(q, k, v, gain_q, gain_k):
     rows, width = q.shape
     heads = width // 128
-    block = 16
+    block = rows
 
     def body(q_ref, k_ref, v_ref, gq_ref, gk_ref, out_ref):
         def normed(ref, gain):
@@ -60,22 +60,28 @@
     rows, width = w_here.shape
     part = width // 2
 
-    def body(place_ref, here_ref, there_ref, out_ref):
-        here_at = pl.ds(pl.multiple_of(place_ref[1] * rows, rows), rows)
-        there_at = pl.ds(pl.multiple_of((1 - place_ref[1]) * rows, rows), rows)
+    def body(place_ref, here_ref, there_ref, out_ref, sems):
+        core = place_ref[1]
+        at = pl.ds(pl.multiple_of(core * part, part), part)
 
         @pl.when(place_ref[0] == 0)
         def _():
-            at = pl.ds(pl.multiple_of(place_ref[1] * part, part), part)
-            out_ref[here_at] = here_ref[:, at]
-            out_ref[there_at] = there_ref[:, at]
-
+            copies = []
+            for n, (ref, chip_row) in enumerate(((here_ref, core), (there_ref, 1 - core))):
+                to = out_ref.at[pl.ds(pl.multiple_of(chip_row * rows, rows), rows)]
+                copies.append(pltpu.make_async_copy(ref.at[:, at], to, sems.at[n]))
+            for copy in copies:
+                copy.start()
+            for copy in copies:
+                copy.wait()
+
+    whole = pl.BlockSpec(memory_space=pl.ANY)
     return pl.pallas_call(
         body,
         out_shape=jax.ShapeDtypeStruct((2 * rows, part), jnp.bfloat16),
-        in_specs=[smem_spec(), vmem_spec(), vmem_spec()],
-        out_specs=vmem_spec(),
-        compiler_params=pltpu.CompilerParams(vmem_limit_bytes=16 * MIB),
+        in_specs=[smem_spec(), whole, whole],
+        out_specs=whole,
+        scratch_shapes=[pltpu.SemaphoreType.DMA((2,))],
         name="weight_half",
     )(place, w_here, w_there)
 
@@ -236,11 +242,21 @@
     taps = w_mid.reshape(steps, 3, 3, vc, vc)
 
     def block(w_ref, out_ref):
-        up, mid, down = (jnp.transpose(w_ref[0, n, 0]) for n in range(3))
-        ends = 0.5 * (up.astype(jnp.float32) + down.astype(jnp.float32))
-        half = 0.5 * mid.astype(jnp.float32)
+        rows, columns = (lax.broadcasted_iota(jnp.int32, (vc, vc), n) for n in range(2))
+        unit = jnp.where(rows == columns, 1.0, 0.0).astype(jnp.bfloat16)
+        up, mid, down = (
+            lax.dot_general(
+                unit,
+                w_ref[0, n, 0],
+                (((1,), (1,)), ((), ())),
+                preferred_element_type=jnp.float32,
+            )
+            for n in range(3)
+        )
+        ends = 0.5 * (up + down)
+        half = 0.5 * mid
         for n, g in enumerate((up, ends + half, ends - half, down)):
-            out_ref[n] = g.astype(jnp.bfloat16)
+            out_ref[0, n] = g.astype(jnp.bfloat16)
 
     def body(place_ref, w_ref, out_ref):
         @pl.when(place_ref[0] == 1)
@@ -253,12 +269,12 @@
                         (1, 3, 1, vc, vc), lambda i: ((i + start) // 3, 0, (i + start) % 3, 0, 0)
                     )
                 ],
-                out_specs=[pl.BlockSpec((4, vc, vc), lambda i: (0, 0, i))],
+                out_specs=[pl.BlockSpec((1, 4, vc, vc), lambda i: (i, 0, 0, 0))],
             )(w_ref, out_ref)
 
     return pl.pallas_call(
         body,
-        out_shape=jax.ShapeDtypeStruct((4, vc, count * vc), jnp.bfloat16),
+        out_shape=jax.ShapeDtypeStruct((count, 4, vc, vc), jnp.bfloat16),
         in_specs=[smem_spec(), pl.BlockSpec(memory_space=pl.ANY)],
         out_specs=pl.BlockSpec(memory_space=pl.ANY),
         compiler_params=pltpu.CompilerParams(vmem_limit_bytes=56 * MIB),
@@ -272,7 +288,7 @@
     deep = 3 * vc
     lot = 4
     wide = 512
-    cut = filters[0].shape[2]
+    cut = filters[0].shape[0]
 
     def body(
         place_ref, clip_ref, win_ref, fa_ref, fb_ref, rows_ref, out_ref,
@@ -281,8 +297,12 @@
         step = pl.program_id(0)
         here = place_ref[0] == 1
         loads = [
-            pltpu.make_async_copy(fa_ref, w2.at[:, :, pl.ds(0, cut)], sems.at[0]),
-            pltpu.make_async_copy(fb_ref, w2.at[:, :, pl.ds(cut, 3 * deep - cut)], sems.at[1]),
+            pltpu.make_async_copy(
+                fa_ref.at[n] if n < cut else fb_ref.at[n - cut],
+                w2.at[:, :, pl.ds(n * vc, vc)],
+                sems.at[n],
+            )
+            for n in range(9)
         ]
 
         def moved(x):
@@ -332,8 +352,7 @@
             for dx, piece in enumerate(moved(cells)):
                 lat[2:, :, dx * lc : dx * lc + lc] = piece.astype(jnp.bfloat16)
 
-            @pl.loop(0, lot)
-            def _(f):
+            for f in range(lot):
                 first(f)
 
             for load in loads:
@@ -397,7 +416,7 @@
             pltpu.VMEM((3, vc, lw), jnp.float32),
             pltpu.VMEM((4, vc, 3 * deep), jnp.bfloat16),
             pltpu.VMEM((2, vc, lot * lw), jnp.float32),
-            pltpu.SemaphoreType.DMA((2,)),
+            pltpu.SemaphoreType.DMA((9,)),
         ],
         compiler_params=pltpu.CompilerParams(vmem_limit_bytes=48 * MIB),
         cost_estimate=pl.CostEstimate(flops=0, bytes_accessed=0, transcendentals=0),
@@ -479,10 +498,9 @@
 
     here, cells = lax.optimization_barrier((here, cells))
     head = attend(place, here)
-    head, w_back = lax.optimization_barrier((head, w_back))
     head_there = swap(head, 2, 0)
+    head_there, w_next, w_back = lax.optimization_barrier((head_there, w_next, w_back))
     w_far = swap(w_back, 0, 0)
-    head_there, w_next = lax.optimization_barrier((head_there, w_next))
     heads = pair_heads(place, head, head_there)
     from_far = swap(heads[3], 0, 2)
     heads = heads[0], swap(heads[1], 0, 0), swap(heads[2], 0, 1), from_far

time: 93 us -> 122 us (1.31)
  waiting for transfers between devices: 0.05 us -> 30.3 us
    ppermute x3, waiting for transfers between devices: 0.01 us -> 30.3 us  [on_device(): pieces = [lax.ppermute(own, 'grp', [(g, last)]) for g in range(last)]]
    pallas_call x2, Pallas kernels: 13.7 us -> 15.5 us  [filter_weights(): pl.pallas_call(body, out_shape=jax.ShapeDtypeStruct((count, 4, vc, vc), j...]
    unnamed x26 -> x22, local copies, waits for them, and re-layouts: 2.77 us -> 1.02 us
  transfers between devices with their start and end apart: 18 -> 18, of which waited for: 0 -> 3; matrix products, arithmetic and copies ran while one was open for 0% -> 1% of each run, Pallas kernels for 55% -> 43%
where the time goes in v9:
time: 122 us; the launch traced here: 121 us
  Pallas kernels  58.2 us (48%)
  waiting for transfers between devices  30.3 us (25%)
  starting transfers between devices  30 us (25%)
  local copies, waits for them, and re-layouts  1.7 us (1%)
    pallas_call x1, Pallas kernels, decode(): pl.pallas_call(body, grid=(frames // lot,), out_shape=jax.ShapeDtypeStruc...  34.6 us
    ppermute x3, waiting for transfers between devices, on_device(): pieces = [lax.ppermute(own, 'grp', [(g, last)]) for g in range(last)]  30.3 us
    pallas_call x2, Pallas kernels, filter_weights(): pl.pallas_call(body, out_shape=jax.ShapeDtypeStruct((count, 4, vc, vc), j...  15.5 us
    ppermute x12, starting transfers between devices, swap(): return lax.ppermute(x, ('grp',) + SEQ, pairs)  10.3 us
    all_to_all x1, starting transfers between devices, on_device(): here = lax.all_to_all(packed, SEQ, split_axis=0, concat_axis=0, tiled=True)  8.05 us
    ppermute x1, starting transfers between devices, on_device(): below = lax.ppermute(clip, ('grp',) + SEQ, [(b, a) for a, b in links])  5.75 us
    ppermute x3, starting transfers between devices, on_device(): pieces = [lax.ppermute(own, 'grp', [(g, last)]) for g in range(last)]  3.86 us
    pallas_call x1, Pallas kernels, norm_pack(): pl.pallas_call(body, grid=(rows // block,), out_shape=jax.ShapeDtypeStruc...  2.75 us
  transfers between devices with their start and end apart: 18, of which 3 were waited for; matrix products, arithmetic and copies ran while one was open for 1% of the time, Pallas kernels for 43%

profile of v9, /device:TPU:56, one launch (start us, length us, event | category | flops | bytes accessed | tf_op | source)
XLA Modules:
  0.0 121.5 jit_solution(1121594605952589199)
XLA Ops:
  0.6 2.8 %norm_pack.1 = bf16[32,3,48,128]{3,2,1,0:T(8,128)(2,1)} custom-call(bf16[48,4096]{1,0:T(8,128)(2,1)} %bitcast.21, bf16[48,4096]{1,0:T(8,128)(2,1)} %bitcast.22, bf16[48,4096]{1,0:T(8,128)(2,1)} %bitcast.23, f32[1,4096]{1,0:T(1,128)} %bitcast.30, f32[1,4096]{1,0:T(1,128)} %bitcast.31), custom_call_target="tpu_custom_call" | custom-call | tf_op jit(solution)/shard_map/norm_pack/pallas_call | solution.py:44
  3.4 0.7 collective-permute-start
  4.1 8.1 %all-to-all-start = ((bf16[32,3,48,128]{3,2,1,0:T(8,128)(2,1)}), bf16[32,3,48,128]{3,2,1,0:T(8,128)(2,1)S(1)}, u32[]{:S(2)}, u32[]{:S(2)}) async-start(bf16[32,3,48,128]{3,2,1,0:T(8,128)(2,1)} %norm_pack.1), calls=%async_computation | async-start | bytes 2359296 | tf_op jit(solution)/shard_map/all_to_all | solution.py:480
  12.9 1.0 copy-done.6
  13.8 0.7 weight_half.1.w0
  14.5 1.7 %collective-permute-start.7 = (bf16[256,2048]{1,0:T(8,128)(2,1)}, bf16[256,2048]{1,0:T(8,128)(2,1)}, u32[]{:S(2)}, u32[]{:S(2)}) collective-permute-start(bf16[256,2048]{1,0:T(8,128)(2,1)} %weight_half.1.w0), channel_id=1, source_target_pairs={{0,8},{1,3},{2,10},{3,1},{4,12},{5,7},{6,14},{7,5},{8,0},{9,11},{1... | collective-permute-start | bytes 3145736 | tf_op jit(solution)/shard_map/ppermute | solution.py:474
  16.2 1.6 %collective-permute-start.8 = (bf16[256,2048]{1,0:T(8,128)(2,1)}, bf16[256,2048]{1,0:T(8,128)(2,1)}, u32[]{:S(2)}, u32[]{:S(2)}) collective-permute-start(bf16[256,2048]{1,0:T(8,128)(2,1)} %weight_half.1.w0), channel_id=1, source_target_pairs={{0,24},{1,7},{2,26},{3,5},{4,28},{5,3},{6,30},{7,1},{8,16},{9,15},... | collective-permute-start | bytes 3145736 | tf_op jit(solution)/shard_map/ppermute | solution.py:474
  17.9 1.3 %collective-permute-start.1 = (bf16[4,2,16,128]{3,2,1,0:T(8,128)(2,1)S(1)}, bf16[4,2,16,128]{3,2,1,0:T(8,128)(2,1)S(1)}, u32[]{:S(2)}, u32[]{:S(2)}) collective-permute-start(bf16[4,2,16,128]{3,2,1,0:T(8,128)(2,1)S(1)} %bitcast.25), channel_id=1, source_target_pairs={{0,96},{1,97},{2,98},{3,99},{4,100},{5,101},{6,102},{7,103},{8,104... | collective-permute-start | bytes 98312 | tf_op jit(solution)/shard_map/ppermute | solution.py:488
  19.1 1.3 %collective-permute-start.2 = (bf16[4,2,16,128]{3,2,1,0:T(8,128)(2,1)S(1)}, bf16[4,2,16,128]{3,2,1,0:T(8,128)(2,1)S(1)}, u32[]{:S(2)}, u32[]{:S(2)}) collective-permute-start(bf16[4,2,16,128]{3,2,1,0:T(8,128)(2,1)S(1)} %bitcast.26), channel_id=1, source_target_pairs={{32,96},{33,97},{34,98},{35,99},{36,100},{37,101},{38,102},{39,103... | collective-permute-start | bytes 98312 | tf_op jit(solution)/shard_map/ppermute | solution.py:488
  20.4 1.3 %collective-permute-start.3 = (bf16[4,2,16,128]{3,2,1,0:T(8,128)(2,1)S(1)}, bf16[4,2,16,128]{3,2,1,0:T(8,128)(2,1)S(1)}, u32[]{:S(2)}, u32[]{:S(2)}) collective-permute-start(bf16[4,2,16,128]{3,2,1,0:T(8,128)(2,1)S(1)} %bitcast.27), channel_id=1, source_target_pairs={{64,96},{65,97},{66,98},{67,99},{68,100},{69,101},{70,102},{71,103... | collective-permute-start | bytes 98312 | tf_op jit(solution)/shard_map/ppermute | solution.py:488
  21.7 8.5 %filter_weights_0.1.fa_ref = bf16[5,4,384,384]{3,2,1,0:T(8,128)(2,1)} custom-call(s32[6]{0:T(128)} %stack.39.place_ref, bf16[3,3,3,384,384]{4,3,2,1,0:T(8,128)(2,1)} %bitcast.18), custom_call_target="tpu_custom_call" | custom-call | tf_op jit(solution)/shard_map/filter_weights_0/pallas_call | solution.py:275
  30.3 28.4 %collective-permute-done.1 = bf16[4,2,16,128]{3,2,1,0:T(8,128)(2,1)S(1)} collective-permute-done((bf16[4,2,16,128]{3,2,1,0:T(8,128)(2,1)S(1)}, bf16[4,2,16,128]{3,2,1,0:T(8,128)(2,1)S(1)}, u32[]{:S(2)}, u32[]{:S(2)}) %collective-permute-start.1) | collective-permute-done | bytes 32800 | tf_op jit(solution)/shard_map/ppermute | solution.py:488
  58.7 1.7 %collective-permute-done.2 = bf16[4,2,16,128]{3,2,1,0:T(8,128)(2,1)S(1)} collective-permute-done((bf16[4,2,16,128]{3,2,1,0:T(8,128)(2,1)S(1)}, bf16[4,2,16,128]{3,2,1,0:T(8,128)(2,1)S(1)}, u32[]{:S(2)}, u32[]{:S(2)}) %collective-permute-start.2) | collective-permute-done | bytes 32800 | tf_op jit(solution)/shard_map/ppermute | solution.py:488
  60.6 2.1 %collective-permute-start.4 = (bf16[16,2,16,128]{3,2,1,0:T(8,128)(2,1)S(1)}, bf16[16,2,16,128]{3,2,1,0:T(8,128)(2,1)S(1)}, u32[]{:S(2)}, u32[]{:S(2)}) collective-permute-start(bf16[16,2,16,128]{3,2,1,0:T(8,128)(2,1)S(1)} %pad_maximum_fusion.1), channel_id=1, source_target_pairs={{96,97},{97,98},{98,99},{99,100},{100,101},{101,102},{102,103},{10... | collective-permute-start | bytes 393224 | tf_op jit(solution)/shard_map/ppermute | solution.py:493
  62.7 5.8 %collective-permute-start.5 = (bf16[16,2,16,128]{3,2,1,0:T(8,128)(2,1)S(1)}, bf16[16,2,16,128]{3,2,1,0:T(8,128)(2,1)S(1)}, u32[]{:S(2)}, u32[]{:S(2)}) collective-permute-start(bf16[16,2,16,128]{3,2,1,0:T(8,128)(2,1)S(1)} %pad_maximum_fusion.1), channel_id=1, source_target_pairs={{97,96},{98,97},{99,98},{100,99},{101,100},{102,101},{103,102},{10... | collective-permute-start | bytes 393224 | tf_op jit(solution)/shard_map/ppermute | solution.py:494
  68.4 7.0 %filter_weights_5.1.fb_ref = bf16[4,4,384,384]{3,2,1,0:T(8,128)(2,1)} custom-call(s32[6]{0:T(128)} %stack.39.place_ref, bf16[3,3,3,384,384]{4,3,2,1,0:T(8,128)(2,1)} %bitcast.19), custom_call_target="tpu_custom_call" | custom-call | tf_op jit(solution)/shard_map/filter_weights_5/pallas_call | solution.py:275
  76.2 0.8 collective-permute-start.6
  77.1 0.7 collective-permute-start.12
  80.5 1.6 %project.1 = (f32[2,48,2048]{2,1,0:T(8,128)S(1)}, bf16[2,48,2048]{2,1,0:T(8,128)(2,1)S(1)}, bf16[2,48,2048]{2,1,0:T(8,128)(2,1)S(1)}, bf16[2,48,2048]{2,1,0:T(8,128)(2,1)S(1)}) custom-call(s32[6]{0:T(128)S(1)} %copy-done.4, bf16[4,2,48,256]{3,2,1,0:T(8,128)(2,1)S(1)} %get-tuple-element.48.h0, bf16[4,2,48,256]{3,2,1,0:T(8,128)(2,1)S(1)} %collective-permute-done.9.h1, ...), custom_call_target="tpu_custom_call" | custom-call | flops 1610612736 | bytes 8388608 | tf_op jit(solution)/shard_map/project/pallas_call | solution.py:175
  82.1 0.7 collective-permute-start.13
  82.8 0.7 collective-permute-start.14
  83.5 0.7 collective-permute-start.15
  84.3 34.6 %decode.1 = bf16[16,2,128,384]{3,2,1,0:T(8,128)(2,1)} custom-call(s32[6]{0:T(128)S(1)} %copy-done.4, bf16[16,6,16,128]{3,2,1,0:T(8,128)(2,1)S(1)} %pad_maximum_fusion.clip_ref, bf16[432,384]{1,0:T(8,128)(2,1)S(1)} %bitcast.17, bf16[5,4,384,384]{3,2,1,0:T(8,128)(2,1)} %filter_weights_0.1.fa_ref, bf16[4,4,384,384]{3,2,1,0:T(8,128)(2,1)S(1)} %copy-done, ...), custom_call_target="tpu_custom_call" | custom-call | tf_op jit(solution)/shard_map/decode/pallas_call | solution.py:398
  120.1 1.3 %finish.1 = bf16[48,4096]{1,0:T(8,128)(2,1)} custom-call(s32[6]{0:T(128)S(1)} %copy-done.4, bf16[48,4096]{1,0:T(8,128)(2,1)S(1)} %bitcast.16, f32[1,4096]{1,0:T(1,128)S(1)} %copy-done.5, f32[48,2048]{1,0:T(8,128)S(1)} %get-tuple-element.67.kept_ref, bf16[48,2048]{1,0:T(8,128)(2,1)S(1)} %collective-permute-done.16.got_ref), custom_call_target="tpu_custom_call" | custom-call | tf_op jit(solution)/shard_map/finish/pallas_call | solution.py:230
  (51 shorter events, 5.5 us)
Async XLA Ops:
  0.6 17.2 %copy-start.7 = (bf16[4,2,128,16]{2,3,1,0:T(8,128)(2,1)S(1)}, bf16[4,2,128,16]{2,3,1,0:T(8,128)(2,1)}, u32[]{:S(2)}) copy-start(bf16[4,2,128,16]{2,3,1,0:T(8,128)(2,1)} %param.22) | copy-start | bytes 98308
  3.4 9.5 %collective-permute-start = (bf16[128,4096]{1,0:T(8,128)(2,1)}, bf16[128,4096]{1,0:T(8,128)(2,1)S(1)}, u32[]{:S(2)}, u32[]{:S(2)}) collective-permute-start(bf16[128,4096]{1,0:T(8,128)(2,1)} %here_ref), channel_id=1, source_target_pairs={{0,1},{1,0},{2,3},{3,2},{4,5},{5,4},{6,7},{7,6},{8,9},{9,8},{10,11... | collective-permute-start | bytes 3145736 | tf_op jit(solution)/shard_map/ppermute | solution.py:474
  4.1 71.4 %all-to-all-start = ((bf16[32,3,48,128]{3,2,1,0:T(8,128)(2,1)}), bf16[32,3,48,128]{3,2,1,0:T(8,128)(2,1)S(1)}, u32[]{:S(2)}, u32[]{:S(2)}) async-start(bf16[32,3,48,128]{3,2,1,0:T(8,128)(2,1)} %norm_pack.1), calls=%async_computation | async-start | bytes 2359296 | tf_op jit(solution)/shard_map/all_to_all | solution.py:480
  14.5 62.5 %collective-permute-start.7 = (bf16[256,2048]{1,0:T(8,128)(2,1)}, bf16[256,2048]{1,0:T(8,128)(2,1)}, u32[]{:S(2)}, u32[]{:S(2)}) collective-permute-start(bf16[256,2048]{1,0:T(8,128)(2,1)} %weight_half.1.w0), channel_id=1, source_target_pairs={{0,8},{1,3},{2,10},{3,1},{4,12},{5,7},{6,14},{7,5},{8,0},{9,11},{1... | collective-permute-start | bytes 3145736 | tf_op jit(solution)/shard_map/ppermute | solution.py:474
  16.2 60.9 %collective-permute-start.8 = (bf16[256,2048]{1,0:T(8,128)(2,1)}, bf16[256,2048]{1,0:T(8,128)(2,1)}, u32[]{:S(2)}, u32[]{:S(2)}) collective-permute-start(bf16[256,2048]{1,0:T(8,128)(2,1)} %weight_half.1.w0), channel_id=1, source_target_pairs={{0,24},{1,7},{2,26},{3,5},{4,28},{5,3},{6,30},{7,1},{8,16},{9,15},... | collective-permute-start | bytes 3145736 | tf_op jit(solution)/shard_map/ppermute | solution.py:474
  17.9 40.9 %collective-permute-start.1 = (bf16[4,2,16,128]{3,2,1,0:T(8,128)(2,1)S(1)}, bf16[4,2,16,128]{3,2,1,0:T(8,128)(2,1)S(1)}, u32[]{:S(2)}, u32[]{:S(2)}) collective-permute-start(bf16[4,2,16,128]{3,2,1,0:T(8,128)(2,1)S(1)} %bitcast.25), channel_id=1, source_target_pairs={{0,96},{1,97},{2,98},{3,99},{4,100},{5,101},{6,102},{7,103},{8,104... | collective-permute-start | bytes 98312 | tf_op jit(solution)/shard_map/ppermute | solution.py:488
  19.1 41.2 %collective-permute-start.2 = (bf16[4,2,16,128]{3,2,1,0:T(8,128)(2,1)S(1)}, bf16[4,2,16,128]{3,2,1,0:T(8,128)(2,1)S(1)}, u32[]{:S(2)}, u32[]{:S(2)}) collective-permute-start(bf16[4,2,16,128]{3,2,1,0:T(8,128)(2,1)S(1)} %bitcast.26), channel_id=1, source_target_pairs={{32,96},{33,97},{34,98},{35,99},{36,100},{37,101},{38,102},{39,103... | collective-permute-start | bytes 98312 | tf_op jit(solution)/shard_map/ppermute | solution.py:488
  20.4 40.1 %collective-permute-start.3 = (bf16[4,2,16,128]{3,2,1,0:T(8,128)(2,1)S(1)}, bf16[4,2,16,128]{3,2,1,0:T(8,128)(2,1)S(1)}, u32[]{:S(2)}, u32[]{:S(2)}) collective-permute-start(bf16[4,2,16,128]{3,2,1,0:T(8,128)(2,1)S(1)} %bitcast.27), channel_id=1, source_target_pairs={{64,96},{65,97},{66,98},{67,99},{68,100},{69,101},{70,102},{71,103... | collective-permute-start | bytes 98312 | tf_op jit(solution)/shard_map/ppermute | solution.py:488
  60.6 15.0 %copy-start.4 = (s32[6]{0:T(128)S(1)}, s32[6]{0:T(128)}, u32[]{:S(2)}) copy-start(s32[6]{0:T(128)} %stack.39.place_ref) | copy-start | bytes 76
  60.6 19.9 %copy-start.1 = (bf16[256,2048]{1,0:T(8,128)(2,1)S(1)}, bf16[256,2048]{1,0:T(8,128)(2,1)}, u32[]{:S(2)}) copy-start(bf16[256,2048]{1,0:T(8,128)(2,1)} %weight_half.1.w0) | copy-start | bytes 3145732
  60.6 14.8 %collective-permute-start.4 = (bf16[16,2,16,128]{3,2,1,0:T(8,128)(2,1)S(1)}, bf16[16,2,16,128]{3,2,1,0:T(8,128)(2,1)S(1)}, u32[]{:S(2)}, u32[]{:S(2)}) collective-permute-start(bf16[16,2,16,128]{3,2,1,0:T(8,128)(2,1)S(1)} %pad_maximum_fusion.1), channel_id=1, source_target_pairs={{96,97},{97,98},{98,99},{99,100},{100,101},{101,102},{102,103},{10... | collective-permute-start | bytes 393224 | tf_op jit(solution)/shard_map/ppermute | solution.py:493
  62.7 12.8 %collective-permute-start.5 = (bf16[16,2,16,128]{3,2,1,0:T(8,128)(2,1)S(1)}, bf16[16,2,16,128]{3,2,1,0:T(8,128)(2,1)S(1)}, u32[]{:S(2)}, u32[]{:S(2)}) collective-permute-start(bf16[16,2,16,128]{3,2,1,0:T(8,128)(2,1)S(1)} %pad_maximum_fusion.1), channel_id=1, source_target_pairs={{97,96},{98,97},{99,98},{100,99},{101,100},{102,101},{103,102},{10... | collective-permute-start | bytes 393224 | tf_op jit(solution)/shard_map/ppermute | solution.py:494
  75.5 8.8 %copy-start.3 = (bf16[3,144,384]{2,1,0:T(8,128)(2,1)S(1)}, bf16[3,144,384]{2,1,0:T(8,128)(2,1)}, u32[]{:S(2)}) copy-start(bf16[3,144,384]{2,1,0:T(8,128)(2,1)} %param.23) | copy-start | bytes 995332
  76.2 0.8 collective-permute-start.6
  77.1 3.4 %collective-permute-start.12 = (bf16[256,2048]{1,0:T(8,128)(2,1)}, bf16[256,2048]{1,0:T(8,128)(2,1)S(1)}, u32[]{:S(2)}, u32[]{:S(2)}) collective-permute-start(bf16[256,2048]{1,0:T(8,128)(2,1)} %collective-permute-done.8.w2), channel_id=1, source_target_pairs={{0,8},{1,3},{2,10},{3,1},{4,12},{5,7},{6,14},{7,5},{8,0},{9,11},{1... | collective-permute-start | bytes 3145736 | tf_op jit(solution)/shard_map/ppermute | solution.py:474
  78.4 2.0 %collective-permute-start.10 = (bf16[4,2,48,256]{3,2,1,0:T(8,128)(2,1)S(1)}, bf16[4,2,48,256]{3,2,1,0:T(8,128)(2,1)S(1)}, u32[]{:S(2)}, u32[]{:S(2)}) collective-permute-start(bf16[4,2,48,256]{3,2,1,0:T(8,128)(2,1)S(1)} %get-tuple-element.50), channel_id=1, source_target_pairs={{0,24},{1,7},{2,26},{3,5},{4,28},{5,3},{6,30},{7,1},{8,16},{9,15},... | collective-permute-start | bytes 589832 | tf_op jit(solution)/shard_map/ppermute | solution.py:474
  79.1 1.4 %collective-permute-start.11 = (bf16[4,2,48,256]{3,2,1,0:T(8,128)(2,1)S(1)}, bf16[4,2,48,256]{3,2,1,0:T(8,128)(2,1)S(1)}, u32[]{:S(2)}, u32[]{:S(2)}) collective-permute-start(bf16[4,2,48,256]{3,2,1,0:T(8,128)(2,1)S(1)} %get-tuple-element.51), channel_id=1, source_target_pairs={{0,16},{1,5},{2,18},{3,7},{4,20},{5,1},{6,22},{7,3},{8,24},{9,13},... | collective-permute-start | bytes 589832 | tf_op jit(solution)/shard_map/ppermute | solution.py:474
  79.8 0.7 collective-permute-start.9
  82.1 36.8 %collective-permute-start.13 = (bf16[2,48,2048]{2,1,0:T(8,128)(2,1)S(1)}, bf16[2,48,2048]{2,1,0:T(8,128)(2,1)S(1)}, u32[]{:S(2)}, u32[]{:S(2)}) collective-permute-start(bf16[2,48,2048]{2,1,0:T(8,128)(2,1)S(1)} %get-tuple-element.64), channel_id=1, source_target_pairs={{0,4},{1,17},{2,6},{3,19},{4,0},{5,21},{6,2},{7,23},{8,12},{9,25},... | collective-permute-start | bytes 1179656 | tf_op jit(solution)/shard_map/ppermute | solution.py:474
  82.8 36.1 %collective-permute-start.14 = (bf16[2,48,2048]{2,1,0:T(8,128)(2,1)S(1)}, bf16[2,48,2048]{2,1,0:T(8,128)(2,1)S(1)}, u32[]{:S(2)}, u32[]{:S(2)}) collective-permute-start(bf16[2,48,2048]{2,1,0:T(8,128)(2,1)S(1)} %get-tuple-element.65), channel_id=1, source_target_pairs={{0,6},{1,25},{2,4},{3,27},{4,2},{5,29},{6,0},{7,31},{8,14},{9,17},... | collective-permute-start | bytes 1179656 | tf_op jit(solution)/shard_map/ppermute | solution.py:474
  83.5 35.4 %collective-permute-start.15 = (bf16[2,48,2048]{2,1,0:T(8,128)(2,1)S(1)}, bf16[2,48,2048]{2,1,0:T(8,128)(2,1)S(1)}, u32[]{:S(2)}, u32[]{:S(2)}) collective-permute-start(bf16[2,48,2048]{2,1,0:T(8,128)(2,1)S(1)} %get-tuple-element.66), channel_id=1, source_target_pairs={{0,2},{1,9},{2,0},{3,11},{4,6},{5,13},{6,4},{7,15},{8,10},{9,1},{1... | collective-permute-start | bytes 1179656 | tf_op jit(solution)/shard_map/ppermute | solution.py:474
  84.2 35.9 %copy-start.2 = (bf16[1,48,4096]{2,1,0:T(8,128)(2,1)S(1)}, bf16[1,48,4096]{2,1,0:T(8,128)(2,1)}, u32[]{:S(2)}) copy-start(bf16[1,48,4096]{2,1,0:T(8,128)(2,1)} %param.17) | copy-start | bytes 1179652
  84.3 35.9 %copy-start.5 = (f32[1,4096]{1,0:T(1,128)S(1)}, f32[1,4096]{1,0:T(1,128)}, u32[]{:S(2)}) copy-start(f32[1,4096]{1,0:T(1,128)} %gate_ref.1) | copy-start | bytes 49156
  119.4 0.7 collective-permute-start.16
  (5 other events, 35.8 us)

commit v10 on v8

--- a/solution.py
+++ b/solution.py
@@ -22,7 +22,7 @@
 def norm_pack(q, k, v, gain_q, gain_k):
     rows, width = q.shape
     heads = width // 128
-    block = 16
+    block = rows
 
     def body(q_ref, k_ref, v_ref, gq_ref, gk_ref, out_ref):
         def normed(ref, gain):
@@ -61,21 +61,24 @@
     part = width // 2
 
     def body(place_ref, here_ref, there_ref, out_ref):
-        here_at = pl.ds(pl.multiple_of(place_ref[1] * rows, rows), rows)
-        there_at = pl.ds(pl.multiple_of((1 - place_ref[1]) * rows, rows), rows)
+        core = place_ref[1]
 
         @pl.when(place_ref[0] == 0)
         def _():
-            at = pl.ds(pl.multiple_of(place_ref[1] * part, part), part)
-            out_ref[here_at] = here_ref[:, at]
-            out_ref[there_at] = there_ref[:, at]
-
-    return pl.pallas_call(
-        body,
+            out_ref[pl.ds(pl.multiple_of(core * rows, rows), rows)] = here_ref[...]
+            out_ref[pl.ds(pl.multiple_of((1 - core) * rows, rows), rows)] = there_ref[...]
+
+    half = pl.BlockSpec((rows, part), lambda i, where: (0, where[1]))
+    return pl.pallas_call(
+        body,
+        grid_spec=pltpu.PrefetchScalarGridSpec(
+            num_scalar_prefetch=1,
+            grid=(1,),
+            in_specs=[half, half],
+            out_specs=pl.BlockSpec((2 * rows, part), lambda i, where: (0, 0)),
+        ),
         out_shape=jax.ShapeDtypeStruct((2 * rows, part), jnp.bfloat16),
-        in_specs=[smem_spec(), vmem_spec(), vmem_spec()],
-        out_specs=vmem_spec(),
-        compiler_params=pltpu.CompilerParams(vmem_limit_bytes=16 * MIB),
+        compiler_params=pltpu.CompilerParams(vmem_limit_bytes=60 * MIB),
         name="weight_half",
     )(place, w_here, w_there)
 
@@ -240,7 +243,7 @@
         ends = 0.5 * (up.astype(jnp.float32) + down.astype(jnp.float32))
         half = 0.5 * mid.astype(jnp.float32)
         for n, g in enumerate((up, ends + half, ends - half, down)):
-            out_ref[n] = g.astype(jnp.bfloat16)
+            out_ref[0, n] = g.astype(jnp.bfloat16)
 
     def body(place_ref, w_ref, out_ref):
         @pl.when(place_ref[0] == 1)
@@ -253,12 +256,12 @@
                         (1, 3, 1, vc, vc), lambda i: ((i + start) // 3, 0, (i + start) % 3, 0, 0)
                     )
                 ],
-                out_specs=[pl.BlockSpec((4, vc, vc), lambda i: (0, 0, i))],
+                out_specs=[pl.BlockSpec((1, 4, vc, vc), lambda i: (i, 0, 0, 0))],
             )(w_ref, out_ref)
 
     return pl.pallas_call(
         body,
-        out_shape=jax.ShapeDtypeStruct((4, vc, count * vc), jnp.bfloat16),
+        out_shape=jax.ShapeDtypeStruct((count, 4, vc, vc), jnp.bfloat16),
         in_specs=[smem_spec(), pl.BlockSpec(memory_space=pl.ANY)],
         out_specs=pl.BlockSpec(memory_space=pl.ANY),
         compiler_params=pltpu.CompilerParams(vmem_limit_bytes=56 * MIB),
@@ -272,7 +275,7 @@
     deep = 3 * vc
     lot = 4
     wide = 512
-    cut = filters[0].shape[2]
+    cut = filters[0].shape[0]
 
     def body(
         place_ref, clip_ref, win_ref, fa_ref, fb_ref, rows_ref, out_ref,
@@ -281,8 +284,12 @@
         step = pl.program_id(0)
         here = place_ref[0] == 1
         loads = [
-            pltpu.make_async_copy(fa_ref, w2.at[:, :, pl.ds(0, cut)], sems.at[0]),
-            pltpu.make_async_copy(fb_ref, w2.at[:, :, pl.ds(cut, 3 * deep - cut)], sems.at[1]),
+            pltpu.make_async_copy(
+                fa_ref.at[n] if n < cut else fb_ref.at[n - cut],
+                w2.at[:, :, pl.ds(n * vc, vc)],
+                sems.at[n],
+            )
+            for n in range(9)
         ]
 
         def moved(x):
@@ -332,8 +339,7 @@
             for dx, piece in enumerate(moved(cells)):
                 lat[2:, :, dx * lc : dx * lc + lc] = piece.astype(jnp.bfloat16)
 
-            @pl.loop(0, lot)
-            def _(f):
+            for f in range(lot):
                 first(f)
 
             for load in loads:
@@ -397,7 +403,7 @@
             pltpu.VMEM((3, vc, lw), jnp.float32),
             pltpu.VMEM((4, vc, 3 * deep), jnp.bfloat16),
             pltpu.VMEM((2, vc, lot * lw), jnp.float32),
-            pltpu.SemaphoreType.DMA((2,)),
+            pltpu.SemaphoreType.DMA((9,)),
         ],
         compiler_params=pltpu.CompilerParams(vmem_limit_bytes=48 * MIB),
         cost_estimate=pl.CostEstimate(flops=0, bytes_accessed=0, transcendentals=0),

time: 93 us -> 92.1 us (level)
  local copies, waits for them, and re-layouts: 2.86 us -> 1.7 us
    pallas_call x3, Pallas kernels: 14.3 us -> 16.6 us  [the longest x2 13.8 us: filter_weights(): pl.pallas_call(body, out_shape=jax.ShapeDtypeStruct((count, 4, vc, vc), j...]
    unnamed x26 -> x22, local copies, waits for them, and re-layouts: 2.77 us -> 1.02 us
    pallas_call x1, Pallas kernels: 35.6 us -> 34.5 us  [decode(): pl.pallas_call(body, grid=(frames // lot,), out_shape=jax.ShapeDtypeStruc...]
  transfers between devices with their start and end apart: 18 -> 18, of which waited for: 0 -> 0; matrix products, arithmetic and copies ran while one was open for 0% -> 1% of each run, Pallas kernels for 55% -> 57%
where the time goes in v10:
time: 92.1 us; the launch traced here: 91.4 us
  Pallas kernels  58.6 us (64%)
  starting transfers between devices  29.9 us (32%)
  local copies, waits for them, and re-layouts  1.7 us (2%)
  between operations  1.11 us (1%)
    pallas_call x1, Pallas kernels, decode(): pl.pallas_call(body, grid=(frames // lot,), out_shape=jax.ShapeDtypeStruc...  34.5 us
    pallas_call x2, Pallas kernels, filter_weights(): pl.pallas_call(body, out_shape=jax.ShapeDtypeStruct((count, 4, vc, vc), j...  13.8 us
    ppermute x12, starting transfers between devices, swap(): return lax.ppermute(x, ('grp',) + SEQ, pairs)  10.3 us
    all_to_all x1, starting transfers between devices, on_device(): here = lax.all_to_all(packed, SEQ, split_axis=0, concat_axis=0, tiled=True)  8.05 us
    ppermute x1, starting transfers between devices, on_device(): below = lax.ppermute(clip, ('grp',) + SEQ, [(b, a) for a, b in links])  5.61 us
    ppermute x3, starting transfers between devices, on_device(): pieces = [lax.ppermute(own, 'grp', [(g, last)]) for g in range(last)]  3.86 us
    pallas_call x1, Pallas kernels, weight_half(): pl.pallas_call(body, grid_spec=pltpu.PrefetchScalarGridSpec(num_scalar_pr...  2.84 us
    pallas_call x1, Pallas kernels, norm_pack(): pl.pallas_call(body, grid=(rows // block,), out_shape=jax.ShapeDtypeStruc...  2.75 us
  transfers between devices with their start and end apart: 18, of which 0 were waited for; matrix products, arithmetic and copies ran while one was open for 1% of the time, Pallas kernels for 57%

profile of v10, /device:TPU:56, one launch (start us, length us, event | category | flops | bytes accessed | tf_op | source)
XLA Modules:
  0.0 91.4 jit_solution(1987017696838416120)
XLA Ops:
  0.6 2.8 %norm_pack.1 = bf16[32,3,48,128]{3,2,1,0:T(8,128)(2,1)} custom-call(bf16[48,4096]{1,0:T(8,128)(2,1)} %bitcast.21, bf16[48,4096]{1,0:T(8,128)(2,1)} %bitcast.22, bf16[48,4096]{1,0:T(8,128)(2,1)} %bitcast.23, f32[1,4096]{1,0:T(1,128)} %bitcast.30, f32[1,4096]{1,0:T(1,128)} %bitcast.31), custom_call_target="tpu_custom_call" | custom-call | tf_op jit(solution)/shard_map/norm_pack/pallas_call | solution.py:44
  3.4 0.7 collective-permute-start
  4.1 8.1 %all-to-all-start = ((bf16[32,3,48,128]{3,2,1,0:T(8,128)(2,1)}), bf16[32,3,48,128]{3,2,1,0:T(8,128)(2,1)S(1)}, u32[]{:S(2)}, u32[]{:S(2)}) async-start(bf16[32,3,48,128]{3,2,1,0:T(8,128)(2,1)} %norm_pack.1), calls=%async_computation | async-start | bytes 2359296 | tf_op jit(solution)/shard_map/all_to_all | solution.py:467
  12.9 1.0 %copy-done.6 = bf16[128,4096]{1,0:T(8,128)(2,1)} copy-done((bf16[128,4096]{1,0:T(8,128)(2,1)}, bf16[128,4096]{1,0:T(8,128)(2,1)S(1)}, u32[]{:S(2)}) %copy-start.6) | copy-done | bytes 1048600
  13.8 2.8 %weight_half.1.w0 = bf16[256,2048]{1,0:T(8,128)(2,1)} custom-call(s32[6]{0:T(128)} %stack.39.place_ref, bf16[128,4096]{1,0:T(8,128)(2,1)} %here_ref, bf16[128,4096]{1,0:T(8,128)(2,1)} %copy-done.6), custom_call_target="tpu_custom_call" | custom-call | tf_op jit(solution)/shard_map/weight_half/pallas_call | solution.py:72
  16.7 1.7 %collective-permute-start.6 = (bf16[256,2048]{1,0:T(8,128)(2,1)}, bf16[256,2048]{1,0:T(8,128)(2,1)}, u32[]{:S(2)}, u32[]{:S(2)}) collective-permute-start(bf16[256,2048]{1,0:T(8,128)(2,1)} %weight_half.1.w0), channel_id=1, source_target_pairs={{0,24},{1,7},{2,26},{3,5},{4,28},{5,3},{6,30},{7,1},{8,16},{9,15},... | collective-permute-start | bytes 3145736 | tf_op jit(solution)/shard_map/ppermute | solution.py:461
  18.4 1.3 %collective-permute-start.1 = (bf16[4,2,16,128]{3,2,1,0:T(8,128)(2,1)S(1)}, bf16[4,2,16,128]{3,2,1,0:T(8,128)(2,1)S(1)}, u32[]{:S(2)}, u32[]{:S(2)}) collective-permute-start(bf16[4,2,16,128]{3,2,1,0:T(8,128)(2,1)S(1)} %bitcast.25), channel_id=1, source_target_pairs={{0,96},{1,97},{2,98},{3,99},{4,100},{5,101},{6,102},{7,103},{8,104... | collective-permute-start | bytes 98312 | tf_op jit(solution)/shard_map/ppermute | solution.py:475
  19.7 1.3 %collective-permute-start.2 = (bf16[4,2,16,128]{3,2,1,0:T(8,128)(2,1)S(1)}, bf16[4,2,16,128]{3,2,1,0:T(8,128)(2,1)S(1)}, u32[]{:S(2)}, u32[]{:S(2)}) collective-permute-start(bf16[4,2,16,128]{3,2,1,0:T(8,128)(2,1)S(1)} %bitcast.26), channel_id=1, source_target_pairs={{32,96},{33,97},{34,98},{35,99},{36,100},{37,101},{38,102},{39,103... | collective-permute-start | bytes 98312 | tf_op jit(solution)/shard_map/ppermute | solution.py:475
  21.0 1.3 %collective-permute-start.3 = (bf16[4,2,16,128]{3,2,1,0:T(8,128)(2,1)S(1)}, bf16[4,2,16,128]{3,2,1,0:T(8,128)(2,1)S(1)}, u32[]{:S(2)}, u32[]{:S(2)}) collective-permute-start(bf16[4,2,16,128]{3,2,1,0:T(8,128)(2,1)S(1)} %bitcast.27), channel_id=1, source_target_pairs={{64,96},{65,97},{66,98},{67,99},{68,100},{69,101},{70,102},{71,103... | collective-permute-start | bytes 98312 | tf_op jit(solution)/shard_map/ppermute | solution.py:475
  22.3 7.8 %filter_weights_0.1.fa_ref = bf16[5,4,384,384]{3,2,1,0:T(8,128)(2,1)} custom-call(s32[6]{0:T(128)} %stack.39.place_ref, bf16[3,3,3,384,384]{4,3,2,1,0:T(8,128)(2,1)} %bitcast.18), custom_call_target="tpu_custom_call" | custom-call | tf_op jit(solution)/shard_map/filter_weights_0/pallas_call | solution.py:262
  30.2 2.1 %collective-permute-start.4 = (bf16[16,2,16,128]{3,2,1,0:T(8,128)(2,1)S(1)}, bf16[16,2,16,128]{3,2,1,0:T(8,128)(2,1)S(1)}, u32[]{:S(2)}, u32[]{:S(2)}) collective-permute-start(bf16[16,2,16,128]{3,2,1,0:T(8,128)(2,1)S(1)} %pad_maximum_fusion.1), channel_id=1, source_target_pairs={{96,97},{97,98},{98,99},{99,100},{100,101},{101,102},{102,103},{10... | collective-permute-start | bytes 393224 | tf_op jit(solution)/shard_map/ppermute | solution.py:480
  32.2 5.6 %collective-permute-start.5 = (bf16[16,2,16,128]{3,2,1,0:T(8,128)(2,1)S(1)}, bf16[16,2,16,128]{3,2,1,0:T(8,128)(2,1)S(1)}, u32[]{:S(2)}, u32[]{:S(2)}) collective-permute-start(bf16[16,2,16,128]{3,2,1,0:T(8,128)(2,1)S(1)} %pad_maximum_fusion.1), channel_id=1, source_target_pairs={{97,96},{98,97},{99,98},{100,99},{101,100},{102,101},{103,102},{10... | collective-permute-start | bytes 393224 | tf_op jit(solution)/shard_map/ppermute | solution.py:481
  37.8 1.6 %collective-permute-start.8 = (bf16[256,2048]{1,0:T(8,128)(2,1)S(1)}, bf16[256,2048]{1,0:T(8,128)(2,1)}, u32[]{:S(2)}, u32[]{:S(2)}) collective-permute-start(bf16[256,2048]{1,0:T(8,128)(2,1)S(1)} %copy-done.1), channel_id=1, source_target_pairs={{0,8},{1,3},{2,10},{3,1},{4,12},{5,7},{6,14},{7,5},{8,0},{9,11},{1... | collective-permute-start | bytes 3145736 | tf_op jit(solution)/shard_map/ppermute | solution.py:461
  39.5 5.9 %filter_weights_5.1.fb_ref = bf16[4,4,384,384]{3,2,1,0:T(8,128)(2,1)} custom-call(s32[6]{0:T(128)} %stack.39.place_ref, bf16[3,3,3,384,384]{4,3,2,1,0:T(8,128)(2,1)} %bitcast.19), custom_call_target="tpu_custom_call" | custom-call | tf_op jit(solution)/shard_map/filter_weights_5/pallas_call | solution.py:262
  46.2 0.9 collective-permute-start.12
  47.1 0.7 collective-permute-start.7
  48.4 0.7 collective-permute-start.10
  49.1 0.7 collective-permute-start.11
  50.5 1.6 %project.1 = (f32[2,48,2048]{2,1,0:T(8,128)S(1)}, bf16[2,48,2048]{2,1,0:T(8,128)(2,1)S(1)}, bf16[2,48,2048]{2,1,0:T(8,128)(2,1)S(1)}, bf16[2,48,2048]{2,1,0:T(8,128)(2,1)S(1)}) custom-call(s32[6]{0:T(128)S(1)} %copy-done.4, bf16[4,2,48,256]{3,2,1,0:T(8,128)(2,1)S(1)} %get-tuple-element.50.h0, bf16[4,2,48,256]{3,2,1,0:T(8,128)(2,1)S(1)} %collective-permute-done.9.h1, ...), custom_call_target="tpu_custom_call" | custom-call | flops 1610612736 | bytes 8388608 | tf_op jit(solution)/shard_map/project/pallas_call | solution.py:172
  52.0 0.7 collective-permute-start.13
  52.7 0.7 collective-permute-start.14
  53.4 0.7 collective-permute-start.15
  54.2 34.5 %decode.1 = bf16[16,2,128,384]{3,2,1,0:T(8,128)(2,1)} custom-call(s32[6]{0:T(128)S(1)} %copy-done.4, bf16[16,6,16,128]{3,2,1,0:T(8,128)(2,1)S(1)} %pad_maximum_fusion.clip_ref, bf16[432,384]{1,0:T(8,128)(2,1)S(1)} %bitcast.17, bf16[5,4,384,384]{3,2,1,0:T(8,128)(2,1)} %filter_weights_0.1.fa_ref, bf16[4,4,384,384]{3,2,1,0:T(8,128)(2,1)S(1)} %copy-done, ...), custom_call_target="tpu_custom_call" | custom-call | tf_op jit(solution)/shard_map/decode/pallas_call | solution.py:385
  90.1 1.3 %finish.1 = bf16[48,4096]{1,0:T(8,128)(2,1)} custom-call(s32[6]{0:T(128)S(1)} %copy-done.4, bf16[48,4096]{1,0:T(8,128)(2,1)S(1)} %bitcast.16, f32[1,4096]{1,0:T(1,128)S(1)} %copy-done.5, f32[48,2048]{1,0:T(8,128)S(1)} %get-tuple-element.69.kept_ref, bf16[48,2048]{1,0:T(8,128)(2,1)S(1)} %collective-permute-done.16.got_ref), custom_call_target="tpu_custom_call" | custom-call | tf_op jit(solution)/shard_map/finish/pallas_call | solution.py:227
  (51 shorter events, 4.0 us)
Async XLA Ops:
  0.6 17.7 %copy-start.7 = (bf16[4,2,128,16]{2,3,1,0:T(8,128)(2,1)S(1)}, bf16[4,2,128,16]{2,3,1,0:T(8,128)(2,1)}, u32[]{:S(2)}) copy-start(bf16[4,2,128,16]{2,3,1,0:T(8,128)(2,1)} %param.22) | copy-start | bytes 98308
  3.4 9.5 %collective-permute-start = (bf16[128,4096]{1,0:T(8,128)(2,1)}, bf16[128,4096]{1,0:T(8,128)(2,1)S(1)}, u32[]{:S(2)}, u32[]{:S(2)}) collective-permute-start(bf16[128,4096]{1,0:T(8,128)(2,1)} %here_ref), channel_id=1, source_target_pairs={{0,1},{1,0},{2,3},{3,2},{4,5},{5,4},{6,7},{7,6},{8,9},{9,8},{10,11... | collective-permute-start | bytes 3145736 | tf_op jit(solution)/shard_map/ppermute | solution.py:461
  4.1 41.4 %all-to-all-start = ((bf16[32,3,48,128]{3,2,1,0:T(8,128)(2,1)}), bf16[32,3,48,128]{3,2,1,0:T(8,128)(2,1)S(1)}, u32[]{:S(2)}, u32[]{:S(2)}) async-start(bf16[32,3,48,128]{3,2,1,0:T(8,128)(2,1)} %norm_pack.1), calls=%async_computation | async-start | bytes 2359296 | tf_op jit(solution)/shard_map/all_to_all | solution.py:467
  16.7 29.5 %collective-permute-start.6 = (bf16[256,2048]{1,0:T(8,128)(2,1)}, bf16[256,2048]{1,0:T(8,128)(2,1)}, u32[]{:S(2)}, u32[]{:S(2)}) collective-permute-start(bf16[256,2048]{1,0:T(8,128)(2,1)} %weight_half.1.w0), channel_id=1, source_target_pairs={{0,24},{1,7},{2,26},{3,5},{4,28},{5,3},{6,30},{7,1},{8,16},{9,15},... | collective-permute-start | bytes 3145736 | tf_op jit(solution)/shard_map/ppermute | solution.py:461
  18.4 11.7 %collective-permute-start.1 = (bf16[4,2,16,128]{3,2,1,0:T(8,128)(2,1)S(1)}, bf16[4,2,16,128]{3,2,1,0:T(8,128)(2,1)S(1)}, u32[]{:S(2)}, u32[]{:S(2)}) collective-permute-start(bf16[4,2,16,128]{3,2,1,0:T(8,128)(2,1)S(1)} %bitcast.25), channel_id=1, source_target_pairs={{0,96},{1,97},{2,98},{3,99},{4,100},{5,101},{6,102},{7,103},{8,104... | collective-permute-start | bytes 98312 | tf_op jit(solution)/shard_map/ppermute | solution.py:475
  19.7 10.5 %collective-permute-start.2 = (bf16[4,2,16,128]{3,2,1,0:T(8,128)(2,1)S(1)}, bf16[4,2,16,128]{3,2,1,0:T(8,128)(2,1)S(1)}, u32[]{:S(2)}, u32[]{:S(2)}) collective-permute-start(bf16[4,2,16,128]{3,2,1,0:T(8,128)(2,1)S(1)} %bitcast.26), channel_id=1, source_target_pairs={{32,96},{33,97},{34,98},{35,99},{36,100},{37,101},{38,102},{39,103... | collective-permute-start | bytes 98312 | tf_op jit(solution)/shard_map/ppermute | solution.py:475
  21.0 9.2 %collective-permute-start.3 = (bf16[4,2,16,128]{3,2,1,0:T(8,128)(2,1)S(1)}, bf16[4,2,16,128]{3,2,1,0:T(8,128)(2,1)S(1)}, u32[]{:S(2)}, u32[]{:S(2)}) collective-permute-start(bf16[4,2,16,128]{3,2,1,0:T(8,128)(2,1)S(1)} %bitcast.27), channel_id=1, source_target_pairs={{64,96},{65,97},{66,98},{67,99},{68,100},{69,101},{70,102},{71,103... | collective-permute-start | bytes 98312 | tf_op jit(solution)/shard_map/ppermute | solution.py:475
  22.3 15.6 %copy-start.1 = (bf16[256,2048]{1,0:T(8,128)(2,1)S(1)}, bf16[256,2048]{1,0:T(8,128)(2,1)}, u32[]{:S(2)}) copy-start(bf16[256,2048]{1,0:T(8,128)(2,1)} %weight_half.1.w0) | copy-start | bytes 3145732
  30.1 15.4 %copy-start.4 = (s32[6]{0:T(128)S(1)}, s32[6]{0:T(128)}, u32[]{:S(2)}) copy-start(s32[6]{0:T(128)} %stack.39.place_ref) | copy-start | bytes 76
  30.2 15.3 %collective-permute-start.4 = (bf16[16,2,16,128]{3,2,1,0:T(8,128)(2,1)S(1)}, bf16[16,2,16,128]{3,2,1,0:T(8,128)(2,1)S(1)}, u32[]{:S(2)}, u32[]{:S(2)}) collective-permute-start(bf16[16,2,16,128]{3,2,1,0:T(8,128)(2,1)S(1)} %pad_maximum_fusion.1), channel_id=1, source_target_pairs={{96,97},{97,98},{98,99},{99,100},{100,101},{101,102},{102,103},{10... | collective-permute-start | bytes 393224 | tf_op jit(solution)/shard_map/ppermute | solution.py:480
  32.2 13.2 %collective-permute-start.5 = (bf16[16,2,16,128]{3,2,1,0:T(8,128)(2,1)S(1)}, bf16[16,2,16,128]{3,2,1,0:T(8,128)(2,1)S(1)}, u32[]{:S(2)}, u32[]{:S(2)}) collective-permute-start(bf16[16,2,16,128]{3,2,1,0:T(8,128)(2,1)S(1)} %pad_maximum_fusion.1), channel_id=1, source_target_pairs={{97,96},{98,97},{99,98},{100,99},{101,100},{102,101},{103,102},{10... | collective-permute-start | bytes 393224 | tf_op jit(solution)/shard_map/ppermute | solution.py:481
  37.8 9.9 %collective-permute-start.8 = (bf16[256,2048]{1,0:T(8,128)(2,1)S(1)}, bf16[256,2048]{1,0:T(8,128)(2,1)}, u32[]{:S(2)}, u32[]{:S(2)}) collective-permute-start(bf16[256,2048]{1,0:T(8,128)(2,1)S(1)} %copy-done.1), channel_id=1, source_target_pairs={{0,8},{1,3},{2,10},{3,1},{4,12},{5,7},{6,14},{7,5},{8,0},{9,11},{1... | collective-permute-start | bytes 3145736 | tf_op jit(solution)/shard_map/ppermute | solution.py:461
  45.4 8.8 %copy-start.3 = (bf16[3,144,384]{2,1,0:T(8,128)(2,1)S(1)}, bf16[3,144,384]{2,1,0:T(8,128)(2,1)}, u32[]{:S(2)}) copy-start(bf16[3,144,384]{2,1,0:T(8,128)(2,1)} %param.23) | copy-start | bytes 995332
  46.2 4.2 %collective-permute-start.12 = (bf16[256,2048]{1,0:T(8,128)(2,1)}, bf16[256,2048]{1,0:T(8,128)(2,1)S(1)}, u32[]{:S(2)}, u32[]{:S(2)}) collective-permute-start(bf16[256,2048]{1,0:T(8,128)(2,1)} %collective-permute-done.6.w2), channel_id=1, source_target_pairs={{0,8},{1,3},{2,10},{3,1},{4,12},{5,7},{6,14},{7,5},{8,0},{9,11},{1... | collective-permute-start | bytes 3145736 | tf_op jit(solution)/shard_map/ppermute | solution.py:461
  47.1 0.7 collective-permute-start.7
  48.4 2.0 %collective-permute-start.10 = (bf16[4,2,48,256]{3,2,1,0:T(8,128)(2,1)S(1)}, bf16[4,2,48,256]{3,2,1,0:T(8,128)(2,1)S(1)}, u32[]{:S(2)}, u32[]{:S(2)}) collective-permute-start(bf16[4,2,48,256]{3,2,1,0:T(8,128)(2,1)S(1)} %get-tuple-element.52), channel_id=1, source_target_pairs={{0,24},{1,7},{2,26},{3,5},{4,28},{5,3},{6,30},{7,1},{8,16},{9,15},... | collective-permute-start | bytes 589832 | tf_op jit(solution)/shard_map/ppermute | solution.py:461
  49.1 1.4 %collective-permute-start.11 = (bf16[4,2,48,256]{3,2,1,0:T(8,128)(2,1)S(1)}, bf16[4,2,48,256]{3,2,1,0:T(8,128)(2,1)S(1)}, u32[]{:S(2)}, u32[]{:S(2)}) collective-permute-start(bf16[4,2,48,256]{3,2,1,0:T(8,128)(2,1)S(1)} %get-tuple-element.53), channel_id=1, source_target_pairs={{0,16},{1,5},{2,18},{3,7},{4,20},{5,1},{6,22},{7,3},{8,24},{9,13},... | collective-permute-start | bytes 589832 | tf_op jit(solution)/shard_map/ppermute | solution.py:461
  49.7 0.7 collective-permute-start.9
  52.0 36.8 %collective-permute-start.13 = (bf16[2,48,2048]{2,1,0:T(8,128)(2,1)S(1)}, bf16[2,48,2048]{2,1,0:T(8,128)(2,1)S(1)}, u32[]{:S(2)}, u32[]{:S(2)}) collective-permute-start(bf16[2,48,2048]{2,1,0:T(8,128)(2,1)S(1)} %get-tuple-element.66), channel_id=1, source_target_pairs={{0,4},{1,17},{2,6},{3,19},{4,0},{5,21},{6,2},{7,23},{8,12},{9,25},... | collective-permute-start | bytes 1179656 | tf_op jit(solution)/shard_map/ppermute | solution.py:461
  52.7 36.1 %collective-permute-start.14 = (bf16[2,48,2048]{2,1,0:T(8,128)(2,1)S(1)}, bf16[2,48,2048]{2,1,0:T(8,128)(2,1)S(1)}, u32[]{:S(2)}, u32[]{:S(2)}) collective-permute-start(bf16[2,48,2048]{2,1,0:T(8,128)(2,1)S(1)} %get-tuple-element.67), channel_id=1, source_target_pairs={{0,6},{1,25},{2,4},{3,27},{4,2},{5,29},{6,0},{7,31},{8,14},{9,17},... | collective-permute-start | bytes 1179656 | tf_op jit(solution)/shard_map/ppermute | solution.py:461
  53.4 35.4 %collective-permute-start.15 = (bf16[2,48,2048]{2,1,0:T(8,128)(2,1)S(1)}, bf16[2,48,2048]{2,1,0:T(8,128)(2,1)S(1)}, u32[]{:S(2)}, u32[]{:S(2)}) collective-permute-start(bf16[2,48,2048]{2,1,0:T(8,128)(2,1)S(1)} %get-tuple-element.68), channel_id=1, source_target_pairs={{0,2},{1,9},{2,0},{3,11},{4,6},{5,13},{6,4},{7,15},{8,10},{9,1},{1... | collective-permute-start | bytes 1179656 | tf_op jit(solution)/shard_map/ppermute | solution.py:461
  54.2 35.9 %copy-start.2 = (bf16[1,48,4096]{2,1,0:T(8,128)(2,1)S(1)}, bf16[1,48,4096]{2,1,0:T(8,128)(2,1)}, u32[]{:S(2)}) copy-start(bf16[1,48,4096]{2,1,0:T(8,128)(2,1)} %param.17) | copy-start | bytes 1179652
  54.2 35.9 %copy-start.5 = (f32[1,4096]{1,0:T(1,128)S(1)}, f32[1,4096]{1,0:T(1,128)}, u32[]{:S(2)}) copy-start(f32[1,4096]{1,0:T(1,128)} %gate_ref.1) | copy-start | bytes 49156
  89.4 0.7 collective-permute-start.16
  (5 other events, 35.7 us)

commit v11 on v8

--- a/solution.py
+++ b/solution.py
@@ -22,7 +22,7 @@
 def norm_pack(q, k, v, gain_q, gain_k):
     rows, width = q.shape
     heads = width // 128
-    block = 16
+    block = rows
 
     def body(q_ref, k_ref, v_ref, gq_ref, gk_ref, out_ref):
         def normed(ref, gain):
@@ -112,7 +112,7 @@
         out_shape=jax.ShapeDtypeStruct((devices, tok, width), jnp.bfloat16),
         in_specs=[smem_spec(), vmem_spec()],
         out_specs=vmem_spec(),
-        compiler_params=pltpu.CompilerParams(vmem_limit_bytes=40 * MIB),
+        compiler_params=pltpu.CompilerParams(vmem_limit_bytes=20 * MIB),
         cost_estimate=pl.CostEstimate(flops=0, bytes_accessed=0, transcendentals=0),
         name="attend",
     )(place, here)
@@ -172,7 +172,7 @@
         + (jax.ShapeDtypeStruct(shape, jnp.bfloat16),) * 3,
         in_specs=[smem_spec()] + [vmem_spec()] * 8,
         out_specs=(vmem_spec(),) * 4,
-        compiler_params=pltpu.CompilerParams(vmem_limit_bytes=40 * MIB),
+        compiler_params=pltpu.CompilerParams(vmem_limit_bytes=24 * MIB),
         cost_estimate=pl.CostEstimate(
             flops=8 * lot * 1024 * part, bytes_accessed=8 * MIB, transcendentals=0
         ),
@@ -231,60 +231,19 @@
     )(place, resid, gate, kept, got)
 
 
-def filter_weights(place, w_mid, start, count):
-    steps, deep, vc = w_mid.shape
-    taps = w_mid.reshape(steps, 3, 3, vc, vc)
-
-    def block(w_ref, out_ref):
-        up, mid, down = (jnp.transpose(w_ref[0, n, 0]) for n in range(3))
-        ends = 0.5 * (up.astype(jnp.float32) + down.astype(jnp.float32))
-        half = 0.5 * mid.astype(jnp.float32)
-        for n, g in enumerate((up, ends + half, ends - half, down)):
-            out_ref[n] = g.astype(jnp.bfloat16)
-
-    def body(place_ref, w_ref, out_ref):
-        @pl.when(place_ref[0] == 1)
-        def _():
-            pltpu.emit_pipeline(
-                block,
-                grid=(count,),
-                in_specs=[
-                    pl.BlockSpec(
-                        (1, 3, 1, vc, vc), lambda i: ((i + start) // 3, 0, (i + start) % 3, 0, 0)
-                    )
-                ],
-                out_specs=[pl.BlockSpec((4, vc, vc), lambda i: (0, 0, i))],
-            )(w_ref, out_ref)
-
-    return pl.pallas_call(
-        body,
-        out_shape=jax.ShapeDtypeStruct((4, vc, count * vc), jnp.bfloat16),
-        in_specs=[smem_spec(), pl.BlockSpec(memory_space=pl.ANY)],
-        out_specs=pl.BlockSpec(memory_space=pl.ANY),
-        compiler_params=pltpu.CompilerParams(vmem_limit_bytes=56 * MIB),
-        name="filter_weights_%d" % start,
-    )(place, taps)
-
-
-def decode(place, clip, w_in, filters, vectors):
+def decode(place, clip, w_in, w_mid, vectors):
     frames, _, lc, lw = clip.shape
     fan, vc = w_in.shape
     deep = 3 * vc
     lot = 4
     wide = 512
-    cut = filters[0].shape[2]
 
     def body(
-        place_ref, clip_ref, win_ref, fa_ref, fb_ref, rows_ref, out_ref,
-        lat, act, firsts, w1_ref, vec_ref, w2, both, sems,
+        place_ref, clip_ref, win_ref, wm_ref, rows_ref, out_ref,
+        lat, act, firsts, w1_ref, vec_ref, w2, both, raw, sems,
     ):
         step = pl.program_id(0)
         here = place_ref[0] == 1
-        loads = [
-            pltpu.make_async_copy(fa_ref, w2.at[:, :, pl.ds(0, cut)], sems.at[0]),
-            pltpu.make_async_copy(fb_ref, w2.at[:, :, pl.ds(cut, 3 * deep - cut)], sems.at[1]),
-        ]
-
         def moved(x):
             lane = lax.broadcasted_iota(jnp.int32, x.shape, x.ndim - 1)
             left = jnp.where(lane == 0, 0.0, pltpu.roll(x, 1, x.ndim - 1))
@@ -319,6 +278,7 @@
 
         @pl.when(here & (step == 0))
         def _():
+            loads = [pltpu.make_async_copy(wm_ref.at[n], raw.at[n], sems.at[n]) for n in range(3)]
             for load in loads:
                 load.start()
             w1_ref[:, :fan] = jnp.transpose(win_ref[...])
@@ -332,12 +292,19 @@
             for dx, piece in enumerate(moved(cells)):
                 lat[2:, :, dx * lc : dx * lc + lc] = piece.astype(jnp.bfloat16)
 
-            @pl.loop(0, lot)
-            def _(f):
+            for f in range(lot):
                 first(f)
-
-            for load in loads:
+            for time, load in enumerate(loads):
                 load.wait()
+
+                @pl.loop(0, 3)
+                def _(column):
+                    up, mid, down = (jnp.transpose(raw[time, n, column]) for n in range(3))
+                    ends = 0.5 * (up.astype(jnp.float32) + down.astype(jnp.float32))
+                    half = 0.5 * mid.astype(jnp.float32)
+                    at = pl.ds(pl.multiple_of(time * deep + column * vc, vc), vc)
+                    for n, g in enumerate((up, ends + half, ends - half, down)):
+                        w2[n, :, at] = g.astype(jnp.bfloat16)
 
         def second(and_next):
             base = lot * step
@@ -385,7 +352,6 @@
             vmem_spec(),
             vmem_spec(),
             pl.BlockSpec(memory_space=pl.ANY),
-            pl.BlockSpec(memory_space=pl.ANY),
             vmem_spec(),
         ],
         out_specs=pl.BlockSpec((lot, 2, lw, vc), lambda i: (i, 0, 0, 0)),
@@ -397,12 +363,13 @@
             pltpu.VMEM((3, vc, lw), jnp.float32),
             pltpu.VMEM((4, vc, 3 * deep), jnp.bfloat16),
             pltpu.VMEM((2, vc, lot * lw), jnp.float32),
-            pltpu.SemaphoreType.DMA((2,)),
+            pltpu.VMEM(w_mid.shape, jnp.bfloat16),
+            pltpu.SemaphoreType.DMA((3,)),
         ],
-        compiler_params=pltpu.CompilerParams(vmem_limit_bytes=48 * MIB),
+        compiler_params=pltpu.CompilerParams(vmem_limit_bytes=58 * MIB),
         cost_estimate=pl.CostEstimate(flops=0, bytes_accessed=0, transcendentals=0),
         name="decode",
-    )(place, clip, w_in, *filters, vectors)
+    )(place, clip, w_in, w_mid, vectors)
 
 
 def on_device(
@@ -461,20 +428,16 @@
     here = lax.all_to_all(packed, SEQ, split_axis=0, concat_axis=0, tiled=True)
 
     w_own = weight_half(place, w_here, swap(w_here, 2, 0))
-    w_own, latents, w_mid = lax.optimization_barrier((w_own, latents, w_mid))
+    w_own, latents = lax.optimization_barrier((w_own, latents))
     w_back = swap(w_own, 0, 1)
     w_next = swap(w_own, 0, 0)
 
     own = jnp.swapaxes(latents, 2, 3)
     pieces = [lax.ppermute(own, "grp", [(g, last)]) for g in range(last)]
-    early = filter_weights(place, w_mid, 0, 5)
-    pieces, early = lax.optimization_barrier((pieces, early))
     clip = jnp.concatenate(pieces + [own], axis=0)
     links = [(last * count + i, last * count + i + 1) for i in range(count - 1)]
     above = lax.ppermute(clip, ("grp",) + SEQ, links)
     below = lax.ppermute(clip, ("grp",) + SEQ, [(b, a) for a, b in links])
-    late = filter_weights(place, w_mid, 5, 4)
-    above, below, late = lax.optimization_barrier((above, below, late))
     cells = jnp.concatenate([above, clip, below], axis=1)
 
     here, cells = lax.optimization_barrier((here, cells))
@@ -490,7 +453,11 @@
     mine, one, zero, far, cells = lax.optimization_barrier((mine, one, zero, far, cells))
     sums = swap(far, 1, 2), swap(one, 1, 1), swap(zero, 1, 0)
     decoded = decode(
-        place, cells, w_in.reshape(-1, channels), (early, late), jnp.stack([b_in, norm_gain, b_mid])
+        place,
+        cells,
+        w_in.reshape(-1, channels),
+        w_mid.reshape(3, 3, 3, channels, channels),
+        jnp.stack([b_in, norm_gain, b_mid]),
     )
     mine, decoded = lax.optimization_barrier((mine, decoded))
     kept, give = add_up(place, mine, sums)

time: 93 us -> 92.4 us (level)
  the two profiles are of different devices: /device:TPU:56 before, /device:TPU:0 now
where the time goes in v11:
time: 92.4 us; the launch traced here: 90.6 us
  starting transfers between devices  47.6 us (52%)
  waiting for transfers between devices  19.3 us (21%)
  Pallas kernels  18.4 us (20%)
  local copies, waits for them, and re-layouts  2.91 us (3%)
  other arithmetic  1.42 us (2%)
  between operations  0.99 us (1%)
    ppermute x12, starting transfers between devices, swap(): return lax.ppermute(x, ('grp',) + SEQ, pairs)  35.2 us
    ppermute x12, waiting for transfers between devices, swap(): return lax.ppermute(x, ('grp',) + SEQ, pairs)  15.2 us
    all_to_all x1, starting transfers between devices, on_device(): here = lax.all_to_all(packed, SEQ, split_axis=0, concat_axis=0, tiled=True)  8.36 us
    pallas_call x1, Pallas kernels, attend(): pl.pallas_call(body, grid=(steps,), out_shape=jax.ShapeDtypeStruct((devic...  5.54 us
    all_to_all x1, waiting for transfers between devices, on_device(): here = lax.all_to_all(packed, SEQ, split_axis=0, concat_axis=0, tiled=True)  3.88 us
    pallas_call x1, Pallas kernels, decode(): pl.pallas_call(body, grid=(frames // lot,), out_shape=jax.ShapeDtypeStruc...  3.54 us
    pallas_call x1, Pallas kernels, project(): pl.pallas_call(body, out_shape=(jax.ShapeDtypeStruct(shape, jnp.float32),...  3.02 us
    pallas_call x1, Pallas kernels, norm_pack(): pl.pallas_call(body, grid=(rows // block,), out_shape=jax.ShapeDtypeStruc...  2.83 us
  transfers between devices with their start and end apart: 18, of which 9 were waited for; matrix products, arithmetic and copies ran while one was open for 2% of the time, Pallas kernels for 11%

profile of v11, /device:TPU:0, one launch (start us, length us, event | category | flops | bytes accessed | tf_op | source)
XLA Modules:
  0.0 90.6 jit_solution(9583352110126987990)
XLA Ops:
  0.6 2.8 %norm_pack.1 = bf16[32,3,48,128]{3,2,1,0:T(8,128)(2,1)} custom-call(bf16[48,4096]{1,0:T(8,128)(2,1)} %bitcast.19, bf16[48,4096]{1,0:T(8,128)(2,1)} %bitcast.20, bf16[48,4096]{1,0:T(8,128)(2,1)} %bitcast.21, f32[1,4096]{1,0:T(1,128)} %bitcast.29, f32[1,4096]{1,0:T(1,128)} %bitcast.30), custom_call_target="tpu_custom_call" | custom-call | tf_op jit(solution)/shard_map/norm_pack/pallas_call | solution.py:44
  3.5 2.0 %collective-permute-start = (bf16[128,4096]{1,0:T(8,128)(2,1)}, bf16[128,4096]{1,0:T(8,128)(2,1)S(1)}, u32[]{:S(2)}, u32[]{:S(2)}) collective-permute-start(bf16[128,4096]{1,0:T(8,128)(2,1)} %here_ref), channel_id=1, source_target_pairs={{0,1},{1,0},{2,3},{3,2},{4,5},{5,4},{6,7},{7,6},{8,9},{9,8},{10,11... | collective-permute-start | bytes 3145736 | tf_op jit(solution)/shard_map/ppermute | solution.py:422
  5.5 8.4 %all-to-all-start = ((bf16[32,3,48,128]{3,2,1,0:T(8,128)(2,1)}), bf16[32,3,48,128]{3,2,1,0:T(8,128)(2,1)S(1)}, u32[]{:S(2)}, u32[]{:S(2)}) async-start(bf16[32,3,48,128]{3,2,1,0:T(8,128)(2,1)} %norm_pack.1), calls=%async_computation | async-start | bytes 2359296 | tf_op jit(solution)/shard_map/all_to_all | solution.py:428
  16.8 5.0 %collective-permute-start.6 = (bf16[256,2048]{1,0:T(8,128)(2,1)S(1)}, bf16[256,2048]{1,0:T(8,128)(2,1)S(1)}, u32[]{:S(2)}, u32[]{:S(2)}) collective-permute-start(bf16[256,2048]{1,0:T(8,128)(2,1)S(1)} %weight_half.1.w0), channel_id=1, source_target_pairs={{0,24},{1,7},{2,26},{3,5},{4,28},{5,3},{6,30},{7,1},{8,16},{9,15},... | collective-permute-start | bytes 3145736 | tf_op jit(solution)/shard_map/ppermute | solution.py:422
  26.1 2.1 %collective-permute-start.8 = (bf16[256,2048]{1,0:T(8,128)(2,1)S(1)}, bf16[256,2048]{1,0:T(8,128)(2,1)}, u32[]{:S(2)}, u32[]{:S(2)}) collective-permute-start(bf16[256,2048]{1,0:T(8,128)(2,1)S(1)} %weight_half.1.w0), channel_id=1, source_target_pairs={{0,8},{1,3},{2,10},{3,1},{4,12},{5,7},{6,14},{7,5},{8,0},{9,11},{1... | collective-permute-start | bytes 3145736 | tf_op jit(solution)/shard_map/ppermute | solution.py:422
  29.0 3.9 %all-to-all-done.here_ref = bf16[32,3,48,128]{3,2,1,0:T(8,128)(2,1)S(1)} async-done(((bf16[32,3,48,128]{3,2,1,0:T(8,128)(2,1)}), bf16[32,3,48,128]{3,2,1,0:T(8,128)(2,1)S(1)}, u32[]{:S(2)}, u32[]{:S(2)}) %all-to-all-start) | async-done | bytes 1179680 | tf_op jit(solution)/shard_map/all_to_all | solution.py:428
  32.9 5.5 %attend.1.here_ref = bf16[32,48,128]{2,1,0:T(8,128)(2,1)S(1)} custom-call(s32[6]{0:T(128)S(1)} %stack.39.place_ref, bf16[32,3,48,128]{3,2,1,0:T(8,128)(2,1)S(1)} %all-to-all-done.here_ref), custom_call_target="tpu_custom_call" | custom-call | tf_op jit(solution)/shard_map/attend/pallas_call | solution.py:109
  38.5 3.5 %collective-permute-done.6.w2 = bf16[256,2048]{1,0:T(8,128)(2,1)S(1)} collective-permute-done((bf16[256,2048]{1,0:T(8,128)(2,1)S(1)}, bf16[256,2048]{1,0:T(8,128)(2,1)S(1)}, u32[]{:S(2)}, u32[]{:S(2)}) %collective-permute-start.6) | collective-permute-done | bytes 1048608 | tf_op jit(solution)/shard_map/ppermute | solution.py:422
  41.9 2.5 %collective-permute-start.12 = (bf16[256,2048]{1,0:T(8,128)(2,1)S(1)}, bf16[256,2048]{1,0:T(8,128)(2,1)S(1)}, u32[]{:S(2)}, u32[]{:S(2)}) collective-permute-start(bf16[256,2048]{1,0:T(8,128)(2,1)S(1)} %collective-permute-done.6.w2), channel_id=1, source_target_pairs={{0,8},{1,3},{2,10},{3,1},{4,12},{5,7},{6,14},{7,5},{8,0},{9,11},{1... | collective-permute-start | bytes 3145736 | tf_op jit(solution)/shard_map/ppermute | solution.py:422
  44.4 1.9 %collective-permute-start.7 = (bf16[32,48,128]{2,1,0:T(8,128)(2,1)S(1)}, bf16[32,48,128]{2,1,0:T(8,128)(2,1)S(1)}, u32[]{:S(2)}, u32[]{:S(2)}) collective-permute-start(bf16[32,48,128]{2,1,0:T(8,128)(2,1)S(1)} %attend.1.here_ref), channel_id=1, source_target_pairs={{0,1},{1,0},{2,3},{3,2},{4,5},{5,4},{6,7},{7,6},{8,9},{9,8},{10,11... | collective-permute-start | bytes 1179656 | tf_op jit(solution)/shard_map/ppermute | solution.py:422
  46.3 1.7 %collective-permute-done.7.there_ref = bf16[32,48,128]{2,1,0:T(8,128)(2,1)S(1)} collective-permute-done((bf16[32,48,128]{2,1,0:T(8,128)(2,1)S(1)}, bf16[32,48,128]{2,1,0:T(8,128)(2,1)S(1)}, u32[]{:S(2)}, u32[]{:S(2)}) %collective-permute-start.7) | collective-permute-done | bytes 393248 | tf_op jit(solution)/shard_map/ppermute | solution.py:422
  48.8 4.0 %collective-permute-start.10 = (bf16[4,2,48,256]{3,2,1,0:T(8,128)(2,1)S(1)}, bf16[4,2,48,256]{3,2,1,0:T(8,128)(2,1)S(1)}, u32[]{:S(2)}, u32[]{:S(2)}) collective-permute-start(bf16[4,2,48,256]{3,2,1,0:T(8,128)(2,1)S(1)} %get-tuple-element.38), channel_id=1, source_target_pairs={{0,24},{1,7},{2,26},{3,5},{4,28},{5,3},{6,30},{7,1},{8,16},{9,15},... | collective-permute-start | bytes 589832 | tf_op jit(solution)/shard_map/ppermute | solution.py:422
  52.8 3.5 %collective-permute-start.11 = (bf16[4,2,48,256]{3,2,1,0:T(8,128)(2,1)S(1)}, bf16[4,2,48,256]{3,2,1,0:T(8,128)(2,1)S(1)}, u32[]{:S(2)}, u32[]{:S(2)}) collective-permute-start(bf16[4,2,48,256]{3,2,1,0:T(8,128)(2,1)S(1)} %get-tuple-element.39), channel_id=1, source_target_pairs={{0,16},{1,5},{2,18},{3,7},{4,20},{5,1},{6,22},{7,3},{8,24},{9,13},... | collective-permute-start | bytes 589832 | tf_op jit(solution)/shard_map/ppermute | solution.py:422
  56.2 2.5 %collective-permute-start.9 = (bf16[4,2,48,256]{3,2,1,0:T(8,128)(2,1)S(1)}, bf16[4,2,48,256]{3,2,1,0:T(8,128)(2,1)S(1)}, u32[]{:S(2)}, u32[]{:S(2)}) collective-permute-start(bf16[4,2,48,256]{3,2,1,0:T(8,128)(2,1)S(1)} %get-tuple-element.37), channel_id=1, source_target_pairs={{0,8},{1,3},{2,10},{3,1},{4,12},{5,7},{6,14},{7,5},{8,0},{9,11},{1... | collective-permute-start | bytes 589832 | tf_op jit(solution)/shard_map/ppermute | solution.py:422
  58.7 3.1 %collective-permute-done.11.h3 = bf16[4,2,48,256]{3,2,1,0:T(8,128)(2,1)S(1)} collective-permute-done((bf16[4,2,48,256]{3,2,1,0:T(8,128)(2,1)S(1)}, bf16[4,2,48,256]{3,2,1,0:T(8,128)(2,1)S(1)}, u32[]{:S(2)}, u32[]{:S(2)}) %collective-permute-start.11) | collective-permute-done | bytes 196640 | tf_op jit(solution)/shard_map/ppermute | solution.py:422
  61.8 2.0 %collective-permute-done.9.h1 = bf16[4,2,48,256]{3,2,1,0:T(8,128)(2,1)S(1)} collective-permute-done((bf16[4,2,48,256]{3,2,1,0:T(8,128)(2,1)S(1)}, bf16[4,2,48,256]{3,2,1,0:T(8,128)(2,1)S(1)}, u32[]{:S(2)}, u32[]{:S(2)}) %collective-permute-start.9) | collective-permute-done | bytes 196640 | tf_op jit(solution)/shard_map/ppermute | solution.py:422
  63.8 3.0 %project.1 = (f32[2,48,2048]{2,1,0:T(8,128)S(1)}, bf16[2,48,2048]{2,1,0:T(8,128)(2,1)S(1)}, bf16[2,48,2048]{2,1,0:T(8,128)(2,1)S(1)}, bf16[2,48,2048]{2,1,0:T(8,128)(2,1)S(1)}) custom-call(s32[6]{0:T(128)S(1)} %stack.39.place_ref, bf16[4,2,48,256]{3,2,1,0:T(8,128)(2,1)S(1)} %get-tuple-element.36.h0, bf16[4,2,48,256]{3,2,1,0:T(8,128)(2,1)S(1)} %collective-permute-done.9.h1, ...), custom_call_target="tpu_custom_call" | custom-call | flops 1610612736 | bytes 8388608 | tf_op jit(solution)/shard_map/project/pallas_call | solution.py:169
  67.4 4.9 %collective-permute-start.13 = (bf16[2,48,2048]{2,1,0:T(8,128)(2,1)S(1)}, bf16[2,48,2048]{2,1,0:T(8,128)(2,1)S(1)}, u32[]{:S(2)}, u32[]{:S(2)}) collective-permute-start(bf16[2,48,2048]{2,1,0:T(8,128)(2,1)S(1)} %get-tuple-element.50), channel_id=1, source_target_pairs={{0,4},{1,17},{2,6},{3,19},{4,0},{5,21},{6,2},{7,23},{8,12},{9,25},... | collective-permute-start | bytes 1179656 | tf_op jit(solution)/shard_map/ppermute | solution.py:422
  72.3 3.1 %collective-permute-start.14 = (bf16[2,48,2048]{2,1,0:T(8,128)(2,1)S(1)}, bf16[2,48,2048]{2,1,0:T(8,128)(2,1)S(1)}, u32[]{:S(2)}, u32[]{:S(2)}) collective-permute-start(bf16[2,48,2048]{2,1,0:T(8,128)(2,1)S(1)} %get-tuple-element.51), channel_id=1, source_target_pairs={{0,6},{1,25},{2,4},{3,27},{4,2},{5,29},{6,0},{7,31},{8,14},{9,17},... | collective-permute-start | bytes 1179656 | tf_op jit(solution)/shard_map/ppermute | solution.py:422
  75.4 1.9 %collective-permute-start.15 = (bf16[2,48,2048]{2,1,0:T(8,128)(2,1)S(1)}, bf16[2,48,2048]{2,1,0:T(8,128)(2,1)S(1)}, u32[]{:S(2)}, u32[]{:S(2)}) collective-permute-start(bf16[2,48,2048]{2,1,0:T(8,128)(2,1)S(1)} %get-tuple-element.52), channel_id=1, source_target_pairs={{0,2},{1,9},{2,0},{3,11},{4,6},{5,13},{6,4},{7,15},{8,10},{9,1},{1... | collective-permute-start | bytes 1179656 | tf_op jit(solution)/shard_map/ppermute | solution.py:422
  78.0 3.5 %decode.1 = bf16[16,2,128,384]{3,2,1,0:T(8,128)(2,1)} custom-call(s32[6]{0:T(128)} %copy-done.4, bf16[16,6,16,128]{3,2,1,0:T(8,128)(2,1)} %pad_maximum_fusion.clip_ref, bf16[432,384]{1,0:T(8,128)(2,1)} %bitcast.23, bf16[3,3,3,384,384]{4,3,2,1,0:T(8,128)(2,1)} %bitcast.17, f32[3,384]{1,0:T(4,128)} %pad_maximum_fusion.2.rows_ref), custom_call_target="tpu_custom_call" | custom-call | tf_op jit(solution)/shard_map/decode/pallas_call | solution.py:346
  81.6 1.6 %collective-permute-done.14.b_ref = bf16[2,48,2048]{2,1,0:T(8,128)(2,1)S(1)} collective-permute-done((bf16[2,48,2048]{2,1,0:T(8,128)(2,1)S(1)}, bf16[2,48,2048]{2,1,0:T(8,128)(2,1)S(1)}, u32[]{:S(2)}, u32[]{:S(2)}) %collective-permute-start.14) | collective-permute-done | bytes 393248 | tf_op jit(solution)/shard_map/ppermute | solution.py:422
  83.2 1.9 %collective-permute-done.15.c_ref = bf16[2,48,2048]{2,1,0:T(8,128)(2,1)S(1)} collective-permute-done((bf16[2,48,2048]{2,1,0:T(8,128)(2,1)S(1)}, bf16[2,48,2048]{2,1,0:T(8,128)(2,1)S(1)}, u32[]{:S(2)}, u32[]{:S(2)}) %collective-permute-start.15) | collective-permute-done | bytes 393248 | tf_op jit(solution)/shard_map/ppermute | solution.py:422
  85.8 1.9 %collective-permute-start.16 = (bf16[48,2048]{1,0:T(8,128)(2,1)S(1)}, bf16[48,2048]{1,0:T(8,128)(2,1)S(1)}, u32[]{:S(2)}, u32[]{:S(2)}) collective-permute-start(bf16[48,2048]{1,0:T(8,128)(2,1)S(1)} %get-tuple-element.54), channel_id=1, source_target_pairs={{0,1},{1,0},{2,3},{3,2},{4,5},{5,4},{6,7},{7,6},{8,9},{9,8},{10,11... | collective-permute-start | bytes 589832 | tf_op jit(solution)/shard_map/ppermute | solution.py:422
  (49 shorter events, 13.4 us)
Async XLA Ops:
  0.6 14.4 %copy-start = (bf16[128,4096]{1,0:T(8,128)(2,1)S(1)}, bf16[128,4096]{1,0:T(8,128)(2,1)}, u32[]{:S(2)}) copy-start(bf16[128,4096]{1,0:T(8,128)(2,1)} %here_ref) | copy-start | bytes 3145732
  3.5 18.3 %copy-start.7 = (bf16[4,2,128,16]{2,3,1,0:T(8,128)(2,1)S(1)}, bf16[4,2,128,16]{2,3,1,0:T(8,128)(2,1)}, u32[]{:S(2)}) copy-start(bf16[4,2,128,16]{2,3,1,0:T(8,128)(2,1)} %param.22) | copy-start | bytes 98308
  3.5 10.5 %collective-permute-start = (bf16[128,4096]{1,0:T(8,128)(2,1)}, bf16[128,4096]{1,0:T(8,128)(2,1)S(1)}, u32[]{:S(2)}, u32[]{:S(2)}) collective-permute-start(bf16[128,4096]{1,0:T(8,128)(2,1)} %here_ref), channel_id=1, source_target_pairs={{0,1},{1,0},{2,3},{3,2},{4,5},{5,4},{6,7},{7,6},{8,9},{9,8},{10,11... | collective-permute-start | bytes 3145736 | tf_op jit(solution)/shard_map/ppermute | solution.py:422
  5.5 27.4 %all-to-all-start = ((bf16[32,3,48,128]{3,2,1,0:T(8,128)(2,1)}), bf16[32,3,48,128]{3,2,1,0:T(8,128)(2,1)S(1)}, u32[]{:S(2)}, u32[]{:S(2)}) async-start(bf16[32,3,48,128]{3,2,1,0:T(8,128)(2,1)} %norm_pack.1), calls=%async_computation | async-start | bytes 2359296 | tf_op jit(solution)/shard_map/all_to_all | solution.py:428
  16.8 25.1 %collective-permute-start.6 = (bf16[256,2048]{1,0:T(8,128)(2,1)S(1)}, bf16[256,2048]{1,0:T(8,128)(2,1)S(1)}, u32[]{:S(2)}, u32[]{:S(2)}) collective-permute-start(bf16[256,2048]{1,0:T(8,128)(2,1)S(1)} %weight_half.1.w0), channel_id=1, source_target_pairs={{0,24},{1,7},{2,26},{3,5},{4,28},{5,3},{6,30},{7,1},{8,16},{9,15},... | collective-permute-start | bytes 3145736 | tf_op jit(solution)/shard_map/ppermute | solution.py:422
  21.8 2.9 %collective-permute-start.1 = (bf16[4,2,16,128]{3,2,1,0:T(8,128)(2,1)S(1)}, bf16[4,2,16,128]{3,2,1,0:T(8,128)(2,1)S(1)}, u32[]{:S(2)}, u32[]{:S(2)}) collective-permute-start(bf16[4,2,16,128]{3,2,1,0:T(8,128)(2,1)S(1)} %bitcast.24), channel_id=1, source_target_pairs={{0,96},{1,97},{2,98},{3,99},{4,100},{5,101},{6,102},{7,103},{8,104... | collective-permute-start | bytes 98312 | tf_op jit(solution)/shard_map/ppermute | solution.py:436
  23.1 1.6 %collective-permute-start.2 = (bf16[4,2,16,128]{3,2,1,0:T(8,128)(2,1)S(1)}, bf16[4,2,16,128]{3,2,1,0:T(8,128)(2,1)S(1)}, u32[]{:S(2)}, u32[]{:S(2)}) collective-permute-start(bf16[4,2,16,128]{3,2,1,0:T(8,128)(2,1)S(1)} %bitcast.25), channel_id=1, source_target_pairs={{32,96},{33,97},{34,98},{35,99},{36,100},{37,101},{38,102},{39,103... | collective-permute-start | bytes 98312 | tf_op jit(solution)/shard_map/ppermute | solution.py:436
  23.8 0.9 %collective-permute-start.3 = (bf16[4,2,16,128]{3,2,1,0:T(8,128)(2,1)S(1)}, bf16[4,2,16,128]{3,2,1,0:T(8,128)(2,1)S(1)}, u32[]{:S(2)}, u32[]{:S(2)}) collective-permute-start(bf16[4,2,16,128]{3,2,1,0:T(8,128)(2,1)S(1)} %bitcast.26), channel_id=1, source_target_pairs={{64,96},{65,97},{66,98},{67,99},{68,100},{69,101},{70,102},{71,103... | collective-permute-start | bytes 98312 | tf_op jit(solution)/shard_map/ppermute | solution.py:436
  24.7 3.5 %collective-permute-start.4 = (bf16[16,2,16,128]{3,2,1,0:T(8,128)(2,1)S(1)}, bf16[16,2,16,128]{3,2,1,0:T(8,128)(2,1)S(1)}, u32[]{:S(2)}, u32[]{:S(2)}) collective-permute-start(bf16[16,2,16,128]{3,2,1,0:T(8,128)(2,1)S(1)} %pad_maximum_fusion.1), channel_id=1, source_target_pairs={{96,97},{97,98},{98,99},{99,100},{100,101},{101,102},{102,103},{10... | collective-permute-start | bytes 393224 | tf_op jit(solution)/shard_map/ppermute | solution.py:439
  25.4 2.8 %collective-permute-start.5 = (bf16[16,2,16,128]{3,2,1,0:T(8,128)(2,1)S(1)}, bf16[16,2,16,128]{3,2,1,0:T(8,128)(2,1)S(1)}, u32[]{:S(2)}, u32[]{:S(2)}) collective-permute-start(bf16[16,2,16,128]{3,2,1,0:T(8,128)(2,1)S(1)} %pad_maximum_fusion.1), channel_id=1, source_target_pairs={{97,96},{98,97},{99,98},{100,99},{101,100},{102,101},{103,102},{10... | collective-permute-start | bytes 393224 | tf_op jit(solution)/shard_map/ppermute | solution.py:440
  26.1 20.2 %collective-permute-start.8 = (bf16[256,2048]{1,0:T(8,128)(2,1)S(1)}, bf16[256,2048]{1,0:T(8,128)(2,1)}, u32[]{:S(2)}, u32[]{:S(2)}) collective-permute-start(bf16[256,2048]{1,0:T(8,128)(2,1)S(1)} %weight_half.1.w0), channel_id=1, source_target_pairs={{0,8},{1,3},{2,10},{3,1},{4,12},{5,7},{6,14},{7,5},{8,0},{9,11},{1... | collective-permute-start | bytes 3145736 | tf_op jit(solution)/shard_map/ppermute | solution.py:422
  41.9 21.9 %collective-permute-start.12 = (bf16[256,2048]{1,0:T(8,128)(2,1)S(1)}, bf16[256,2048]{1,0:T(8,128)(2,1)S(1)}, u32[]{:S(2)}, u32[]{:S(2)}) collective-permute-start(bf16[256,2048]{1,0:T(8,128)(2,1)S(1)} %collective-permute-done.6.w2), channel_id=1, source_target_pairs={{0,8},{1,3},{2,10},{3,1},{4,12},{5,7},{6,14},{7,5},{8,0},{9,11},{1... | collective-permute-start | bytes 3145736 | tf_op jit(solution)/shard_map/ppermute | solution.py:422
  44.4 3.6 %collective-permute-start.7 = (bf16[32,48,128]{2,1,0:T(8,128)(2,1)S(1)}, bf16[32,48,128]{2,1,0:T(8,128)(2,1)S(1)}, u32[]{:S(2)}, u32[]{:S(2)}) collective-permute-start(bf16[32,48,128]{2,1,0:T(8,128)(2,1)S(1)} %attend.1.here_ref), channel_id=1, source_target_pairs={{0,1},{1,0},{2,3},{3,2},{4,5},{5,4},{6,7},{7,6},{8,9},{9,8},{10,11... | collective-permute-start | bytes 1179656 | tf_op jit(solution)/shard_map/ppermute | solution.py:422
  48.7 28.6 %copy-start.8 = (f32[384]{0:T(512)S(1)}, f32[384]{0:T(512)}, u32[]{:S(2)}) copy-start(f32[384]{0:T(512)} %param.24) | copy-start | bytes 4612
  48.7 28.6 %copy-start.9 = (f32[384]{0:T(512)S(1)}, f32[384]{0:T(512)}, u32[]{:S(2)}) copy-start(f32[384]{0:T(512)} %param.25) | copy-start | bytes 4612
  48.7 28.6 %copy-start.10 = (f32[384]{0:T(512)S(1)}, f32[384]{0:T(512)}, u32[]{:S(2)}) copy-start(f32[384]{0:T(512)} %param.27) | copy-start | bytes 4612
  48.8 10.0 %collective-permute-start.10 = (bf16[4,2,48,256]{3,2,1,0:T(8,128)(2,1)S(1)}, bf16[4,2,48,256]{3,2,1,0:T(8,128)(2,1)S(1)}, u32[]{:S(2)}, u32[]{:S(2)}) collective-permute-start(bf16[4,2,48,256]{3,2,1,0:T(8,128)(2,1)S(1)} %get-tuple-element.38), channel_id=1, source_target_pairs={{0,24},{1,7},{2,26},{3,5},{4,28},{5,3},{6,30},{7,1},{8,16},{9,15},... | collective-permute-start | bytes 589832 | tf_op jit(solution)/shard_map/ppermute | solution.py:422
  52.8 9.1 %collective-permute-start.11 = (bf16[4,2,48,256]{3,2,1,0:T(8,128)(2,1)S(1)}, bf16[4,2,48,256]{3,2,1,0:T(8,128)(2,1)S(1)}, u32[]{:S(2)}, u32[]{:S(2)}) collective-permute-start(bf16[4,2,48,256]{3,2,1,0:T(8,128)(2,1)S(1)} %get-tuple-element.39), channel_id=1, source_target_pairs={{0,16},{1,5},{2,18},{3,7},{4,20},{5,1},{6,22},{7,3},{8,24},{9,13},... | collective-permute-start | bytes 589832 | tf_op jit(solution)/shard_map/ppermute | solution.py:422
  56.2 7.6 %collective-permute-start.9 = (bf16[4,2,48,256]{3,2,1,0:T(8,128)(2,1)S(1)}, bf16[4,2,48,256]{3,2,1,0:T(8,128)(2,1)S(1)}, u32[]{:S(2)}, u32[]{:S(2)}) collective-permute-start(bf16[4,2,48,256]{3,2,1,0:T(8,128)(2,1)S(1)} %get-tuple-element.37), channel_id=1, source_target_pairs={{0,8},{1,3},{2,10},{3,1},{4,12},{5,7},{6,14},{7,5},{8,0},{9,11},{1... | collective-permute-start | bytes 589832 | tf_op jit(solution)/shard_map/ppermute | solution.py:422
  67.4 14.1 %collective-permute-start.13 = (bf16[2,48,2048]{2,1,0:T(8,128)(2,1)S(1)}, bf16[2,48,2048]{2,1,0:T(8,128)(2,1)S(1)}, u32[]{:S(2)}, u32[]{:S(2)}) collective-permute-start(bf16[2,48,2048]{2,1,0:T(8,128)(2,1)S(1)} %get-tuple-element.50), channel_id=1, source_target_pairs={{0,4},{1,17},{2,6},{3,19},{4,0},{5,21},{6,2},{7,23},{8,12},{9,25},... | collective-permute-start | bytes 1179656 | tf_op jit(solution)/shard_map/ppermute | solution.py:422
  72.3 10.9 %collective-permute-start.14 = (bf16[2,48,2048]{2,1,0:T(8,128)(2,1)S(1)}, bf16[2,48,2048]{2,1,0:T(8,128)(2,1)S(1)}, u32[]{:S(2)}, u32[]{:S(2)}) collective-permute-start(bf16[2,48,2048]{2,1,0:T(8,128)(2,1)S(1)} %get-tuple-element.51), channel_id=1, source_target_pairs={{0,6},{1,25},{2,4},{3,27},{4,2},{5,29},{6,0},{7,31},{8,14},{9,17},... | collective-permute-start | bytes 1179656 | tf_op jit(solution)/shard_map/ppermute | solution.py:422
  75.4 9.7 %collective-permute-start.15 = (bf16[2,48,2048]{2,1,0:T(8,128)(2,1)S(1)}, bf16[2,48,2048]{2,1,0:T(8,128)(2,1)S(1)}, u32[]{:S(2)}, u32[]{:S(2)}) collective-permute-start(bf16[2,48,2048]{2,1,0:T(8,128)(2,1)S(1)} %get-tuple-element.52), channel_id=1, source_target_pairs={{0,2},{1,9},{2,0},{3,11},{4,6},{5,13},{6,4},{7,15},{8,10},{9,1},{1... | collective-permute-start | bytes 1179656 | tf_op jit(solution)/shard_map/ppermute | solution.py:422
  78.0 11.1 %copy-start.6 = (f32[1,4096]{1,0:T(1,128)S(1)}, f32[1,4096]{1,0:T(1,128)}, u32[]{:S(2)}) copy-start(f32[1,4096]{1,0:T(1,128)} %gate_ref.1) | copy-start | bytes 49156
  85.8 3.3 %collective-permute-start.16 = (bf16[48,2048]{1,0:T(8,128)(2,1)S(1)}, bf16[48,2048]{1,0:T(8,128)(2,1)S(1)}, u32[]{:S(2)}, u32[]{:S(2)}) collective-permute-start(bf16[48,2048]{1,0:T(8,128)(2,1)S(1)} %get-tuple-element.54), channel_id=1, source_target_pairs={{0,1},{1,0},{2,3},{3,2},{4,5},{5,4},{6,7},{7,6},{8,9},{9,8},{10,11... | collective-permute-start | bytes 589832 | tf_op jit(solution)/shard_map/ppermute | solution.py:422
  (5 other events, 21.0 us)

commit v12 on v11

--- a/solution.py
+++ b/solution.py
@@ -442,10 +442,9 @@
 
     here, cells = lax.optimization_barrier((here, cells))
     head = attend(place, here)
-    head, w_back = lax.optimization_barrier((head, w_back))
     head_there = swap(head, 2, 0)
+    head_there, w_next, w_back = lax.optimization_barrier((head_there, w_next, w_back))
     w_far = swap(w_back, 0, 0)
-    head_there, w_next = lax.optimization_barrier((head_there, w_next))
     heads = pair_heads(place, head, head_there)
     from_far = swap(heads[3], 0, 2)
     heads = heads[0], swap(heads[1], 0, 0), swap(heads[2], 0, 1), from_far

time: 92.4 us -> 93.1 us (level)
  the two profiles are of different devices: /device:TPU:0 before, /device:TPU:31 now
where the time goes in v12:
time: 93.1 us; the launch traced here: 92.3 us
  Pallas kernels  46.1 us (50%)
  starting transfers between devices  29.3 us (31%)
  waiting for transfers between devices  11.6 us (12%)
  local copies, waits for them, and re-layouts  2.91 us (3%)
  other arithmetic  1.41 us (2%)
  between operations  1.05 us (1%)
    pallas_call x1, Pallas kernels, decode(): pl.pallas_call(body, grid=(frames // lot,), out_shape=jax.ShapeDtypeStruc...  38.4 us
    ppermute x12, starting transfers between devices, swap(): return lax.ppermute(x, ('grp',) + SEQ, pairs)  9.51 us
    all_to_all x1, starting transfers between devices, on_device(): here = lax.all_to_all(packed, SEQ, split_axis=0, concat_axis=0, tiled=True)  8.73 us
    ppermute x1, waiting for transfers between devices, on_device(): below = lax.ppermute(clip, ('grp',) + SEQ, [(b, a) for a, b in links])  6.46 us
    ppermute x1, starting transfers between devices, on_device(): above = lax.ppermute(clip, ('grp',) + SEQ, links)  5.23 us
    ppermute x3, waiting for transfers between devices, on_device(): pieces = [lax.ppermute(own, 'grp', [(g, last)]) for g in range(last)]  5.08 us
    ppermute x3, starting transfers between devices, on_device(): pieces = [lax.ppermute(own, 'grp', [(g, last)]) for g in range(last)]  3.86 us
    pallas_call x1, Pallas kernels, norm_pack(): pl.pallas_call(body, grid=(rows // block,), out_shape=jax.ShapeDtypeStruc...  2.83 us
  transfers between devices with their start and end apart: 18, of which 4 were waited for; matrix products, arithmetic and copies ran while one was open for 2% of the time, Pallas kernels for 43%

profile of v12, /device:TPU:31, one launch (start us, length us, event | category | flops | bytes accessed | tf_op | source)
XLA Modules:
  0.0 92.3 jit_solution(17335569919647588615)
XLA Ops:
  0.6 2.8 %norm_pack.1 = bf16[32,3,48,128]{3,2,1,0:T(8,128)(2,1)} custom-call(bf16[48,4096]{1,0:T(8,128)(2,1)} %bitcast.19, bf16[48,4096]{1,0:T(8,128)(2,1)} %bitcast.20, bf16[48,4096]{1,0:T(8,128)(2,1)} %bitcast.21, f32[1,4096]{1,0:T(1,128)} %bitcast.29, f32[1,4096]{1,0:T(1,128)} %bitcast.30), custom_call_target="tpu_custom_call" | custom-call | tf_op jit(solution)/shard_map/norm_pack/pallas_call | solution.py:44
  3.5 0.8 collective-permute-start
  4.3 8.7 %all-to-all-start = ((bf16[32,3,48,128]{3,2,1,0:T(8,128)(2,1)}), bf16[32,3,48,128]{3,2,1,0:T(8,128)(2,1)S(1)}, u32[]{:S(2)}, u32[]{:S(2)}) async-start(bf16[32,3,48,128]{3,2,1,0:T(8,128)(2,1)} %norm_pack.1), calls=%async_computation | async-start | bytes 2359296 | tf_op jit(solution)/shard_map/all_to_all | solution.py:428
  13.2 1.0 %copy-done.1 = bf16[128,4096]{1,0:T(8,128)(2,1)} copy-done((bf16[128,4096]{1,0:T(8,128)(2,1)}, bf16[128,4096]{1,0:T(8,128)(2,1)S(1)}, u32[]{:S(2)}) %copy-start.1) | copy-done | bytes 1048600
  14.2 1.2 %copy-done.2 = bf16[128,4096]{1,0:T(8,128)(2,1)S(1)} copy-done((bf16[128,4096]{1,0:T(8,128)(2,1)S(1)}, bf16[128,4096]{1,0:T(8,128)(2,1)}, u32[]{:S(2)}) %copy-start.2) | copy-done | bytes 1048600
  15.9 0.7 collective-permute-start.7
  16.7 1.6 %collective-permute-start.8 = (bf16[256,2048]{1,0:T(8,128)(2,1)S(1)}, bf16[256,2048]{1,0:T(8,128)(2,1)}, u32[]{:S(2)}, u32[]{:S(2)}) collective-permute-start(bf16[256,2048]{1,0:T(8,128)(2,1)S(1)} %weight_half.1.w0), channel_id=1, source_target_pairs={{0,24},{1,7},{2,26},{3,5},{4,28},{5,3},{6,30},{7,1},{8,16},{9,15},... | collective-permute-start | bytes 3145736 | tf_op jit(solution)/shard_map/ppermute | solution.py:422
  18.3 1.3 %collective-permute-start.1 = (bf16[4,2,16,128]{3,2,1,0:T(8,128)(2,1)S(1)}, bf16[4,2,16,128]{3,2,1,0:T(8,128)(2,1)S(1)}, u32[]{:S(2)}, u32[]{:S(2)}) collective-permute-start(bf16[4,2,16,128]{3,2,1,0:T(8,128)(2,1)S(1)} %bitcast.24), channel_id=1, source_target_pairs={{0,96},{1,97},{2,98},{3,99},{4,100},{5,101},{6,102},{7,103},{8,104... | collective-permute-start | bytes 98312 | tf_op jit(solution)/shard_map/ppermute | solution.py:436
  19.6 1.3 %collective-permute-start.2 = (bf16[4,2,16,128]{3,2,1,0:T(8,128)(2,1)S(1)}, bf16[4,2,16,128]{3,2,1,0:T(8,128)(2,1)S(1)}, u32[]{:S(2)}, u32[]{:S(2)}) collective-permute-start(bf16[4,2,16,128]{3,2,1,0:T(8,128)(2,1)S(1)} %bitcast.25), channel_id=1, source_target_pairs={{32,96},{33,97},{34,98},{35,99},{36,100},{37,101},{38,102},{39,103... | collective-permute-start | bytes 98312 | tf_op jit(solution)/shard_map/ppermute | solution.py:436
  20.9 1.3 %collective-permute-start.3 = (bf16[4,2,16,128]{3,2,1,0:T(8,128)(2,1)S(1)}, bf16[4,2,16,128]{3,2,1,0:T(8,128)(2,1)S(1)}, u32[]{:S(2)}, u32[]{:S(2)}) collective-permute-start(bf16[4,2,16,128]{3,2,1,0:T(8,128)(2,1)S(1)} %bitcast.26), channel_id=1, source_target_pairs={{64,96},{65,97},{66,98},{67,99},{68,100},{69,101},{70,102},{71,103... | collective-permute-start | bytes 98312 | tf_op jit(solution)/shard_map/ppermute | solution.py:436
  22.2 3.2 %collective-permute-done.1 = bf16[4,2,16,128]{3,2,1,0:T(8,128)(2,1)S(1)} collective-permute-done((bf16[4,2,16,128]{3,2,1,0:T(8,128)(2,1)S(1)}, bf16[4,2,16,128]{3,2,1,0:T(8,128)(2,1)S(1)}, u32[]{:S(2)}, u32[]{:S(2)}) %collective-permute-start.1) | collective-permute-done | bytes 32800 | tf_op jit(solution)/shard_map/ppermute | solution.py:436
  25.4 1.7 %collective-permute-done.2 = bf16[4,2,16,128]{3,2,1,0:T(8,128)(2,1)S(1)} collective-permute-done((bf16[4,2,16,128]{3,2,1,0:T(8,128)(2,1)S(1)}, bf16[4,2,16,128]{3,2,1,0:T(8,128)(2,1)S(1)}, u32[]{:S(2)}, u32[]{:S(2)}) %collective-permute-start.2) | collective-permute-done | bytes 32800 | tf_op jit(solution)/shard_map/ppermute | solution.py:436
  27.3 5.2 %collective-permute-start.4 = (bf16[16,2,16,128]{3,2,1,0:T(8,128)(2,1)S(1)}, bf16[16,2,16,128]{3,2,1,0:T(8,128)(2,1)S(1)}, u32[]{:S(2)}, u32[]{:S(2)}) collective-permute-start(bf16[16,2,16,128]{3,2,1,0:T(8,128)(2,1)S(1)} %pad_maximum_fusion.1), channel_id=1, source_target_pairs={{96,97},{97,98},{98,99},{99,100},{100,101},{101,102},{102,103},{10... | collective-permute-start | bytes 393224 | tf_op jit(solution)/shard_map/ppermute | solution.py:439
  32.6 1.9 %collective-permute-start.5 = (bf16[16,2,16,128]{3,2,1,0:T(8,128)(2,1)S(1)}, bf16[16,2,16,128]{3,2,1,0:T(8,128)(2,1)S(1)}, u32[]{:S(2)}, u32[]{:S(2)}) collective-permute-start(bf16[16,2,16,128]{3,2,1,0:T(8,128)(2,1)S(1)} %pad_maximum_fusion.1), channel_id=1, source_target_pairs={{97,96},{98,97},{99,98},{100,99},{101,100},{102,101},{103,102},{10... | collective-permute-start | bytes 393224 | tf_op jit(solution)/shard_map/ppermute | solution.py:440
  34.5 6.5 %collective-permute-done.5 = bf16[16,2,16,128]{3,2,1,0:T(8,128)(2,1)S(1)} collective-permute-done((bf16[16,2,16,128]{3,2,1,0:T(8,128)(2,1)S(1)}, bf16[16,2,16,128]{3,2,1,0:T(8,128)(2,1)S(1)}, u32[]{:S(2)}, u32[]{:S(2)}) %collective-permute-start.5) | collective-permute-done | bytes 131104 | tf_op jit(solution)/shard_map/ppermute | solution.py:440
  41.0 0.8 pad_maximum_fusion.clip_ref
  42.4 0.7 collective-permute-start.6
  43.1 0.7 collective-permute-start.12
  44.5 0.8 collective-permute-start.10
  46.7 1.2 %project.1 = (f32[2,48,2048]{2,1,0:T(8,128)S(1)}, bf16[2,48,2048]{2,1,0:T(8,128)(2,1)S(1)}, bf16[2,48,2048]{2,1,0:T(8,128)(2,1)S(1)}, bf16[2,48,2048]{2,1,0:T(8,128)(2,1)S(1)}) custom-call(s32[6]{0:T(128)S(1)} %stack.39.place_ref, bf16[4,2,48,256]{3,2,1,0:T(8,128)(2,1)S(1)} %get-tuple-element.34.h0, bf16[4,2,48,256]{3,2,1,0:T(8,128)(2,1)S(1)} %collective-permute-done.9.h1, ...), custom_call_target="tpu_custom_call" | custom-call | flops 1610612736 | bytes 8388608 | tf_op jit(solution)/shard_map/project/pallas_call | solution.py:169
  49.2 0.7 collective-permute-start.14
  49.9 0.7 collective-permute-start.15
  51.3 38.4 %decode.1 = bf16[16,2,128,384]{3,2,1,0:T(8,128)(2,1)} custom-call(s32[6]{0:T(128)} %copy-done.4, bf16[16,6,16,128]{3,2,1,0:T(8,128)(2,1)} %pad_maximum_fusion.clip_ref, bf16[432,384]{1,0:T(8,128)(2,1)} %bitcast.23, bf16[3,3,3,384,384]{4,3,2,1,0:T(8,128)(2,1)} %bitcast.17, f32[3,384]{1,0:T(4,128)} %pad_maximum_fusion.2.rows_ref), custom_call_target="tpu_custom_call" | custom-call | tf_op jit(solution)/shard_map/decode/pallas_call | solution.py:346
  90.9 1.3 %finish.1 = bf16[48,4096]{1,0:T(8,128)(2,1)} custom-call(s32[6]{0:T(128)S(1)} %copy-done.5, bf16[48,4096]{1,0:T(8,128)(2,1)S(1)} %bitcast.16, f32[1,4096]{1,0:T(1,128)S(1)} %copy-done.6, f32[48,2048]{1,0:T(8,128)S(1)} %get-tuple-element.51.kept_ref, bf16[48,2048]{1,0:T(8,128)(2,1)S(1)} %collective-permute-done.16.got_ref), custom_call_target="tpu_custom_call" | custom-call | tf_op jit(solution)/shard_map/finish/pallas_call | solution.py:224
  (49 shorter events, 6.5 us)
Async XLA Ops:
  0.6 13.5 %copy-start = (bf16[128,4096]{1,0:T(8,128)(2,1)S(1)}, bf16[128,4096]{1,0:T(8,128)(2,1)}, u32[]{:S(2)}) copy-start(bf16[128,4096]{1,0:T(8,128)(2,1)} %here_ref) | copy-start | bytes 3145732
  3.5 14.9 %copy-start.7 = (bf16[4,2,128,16]{2,3,1,0:T(8,128)(2,1)S(1)}, bf16[4,2,128,16]{2,3,1,0:T(8,128)(2,1)}, u32[]{:S(2)}) copy-start(bf16[4,2,128,16]{2,3,1,0:T(8,128)(2,1)} %param.22) | copy-start | bytes 98308
  3.5 9.7 %collective-permute-start = (bf16[128,4096]{1,0:T(8,128)(2,1)}, bf16[128,4096]{1,0:T(8,128)(2,1)S(1)}, u32[]{:S(2)}, u32[]{:S(2)}) collective-permute-start(bf16[128,4096]{1,0:T(8,128)(2,1)} %here_ref), channel_id=1, source_target_pairs={{0,1},{1,0},{2,3},{3,2},{4,5},{5,4},{6,7},{7,6},{8,9},{9,8},{10,11... | collective-permute-start | bytes 3145736 | tf_op jit(solution)/shard_map/ppermute | solution.py:422
  4.3 37.4 %all-to-all-start = ((bf16[32,3,48,128]{3,2,1,0:T(8,128)(2,1)}), bf16[32,3,48,128]{3,2,1,0:T(8,128)(2,1)S(1)}, u32[]{:S(2)}, u32[]{:S(2)}) async-start(bf16[32,3,48,128]{3,2,1,0:T(8,128)(2,1)} %norm_pack.1), calls=%async_computation | async-start | bytes 2359296 | tf_op jit(solution)/shard_map/all_to_all | solution.py:428
  15.9 27.2 %collective-permute-start.7 = (bf16[256,2048]{1,0:T(8,128)(2,1)S(1)}, bf16[256,2048]{1,0:T(8,128)(2,1)S(1)}, u32[]{:S(2)}, u32[]{:S(2)}) collective-permute-start(bf16[256,2048]{1,0:T(8,128)(2,1)S(1)} %weight_half.1.w0), channel_id=1, source_target_pairs={{0,8},{1,3},{2,10},{3,1},{4,12},{5,7},{6,14},{7,5},{8,0},{9,11},{1... | collective-permute-start | bytes 3145736 | tf_op jit(solution)/shard_map/ppermute | solution.py:422
  16.7 26.4 %collective-permute-start.8 = (bf16[256,2048]{1,0:T(8,128)(2,1)S(1)}, bf16[256,2048]{1,0:T(8,128)(2,1)}, u32[]{:S(2)}, u32[]{:S(2)}) collective-permute-start(bf16[256,2048]{1,0:T(8,128)(2,1)S(1)} %weight_half.1.w0), channel_id=1, source_target_pairs={{0,24},{1,7},{2,26},{3,5},{4,28},{5,3},{6,30},{7,1},{8,16},{9,15},... | collective-permute-start | bytes 3145736 | tf_op jit(solution)/shard_map/ppermute | solution.py:422
  18.3 7.1 %collective-permute-start.1 = (bf16[4,2,16,128]{3,2,1,0:T(8,128)(2,1)S(1)}, bf16[4,2,16,128]{3,2,1,0:T(8,128)(2,1)S(1)}, u32[]{:S(2)}, u32[]{:S(2)}) collective-permute-start(bf16[4,2,16,128]{3,2,1,0:T(8,128)(2,1)S(1)} %bitcast.24), channel_id=1, source_target_pairs={{0,96},{1,97},{2,98},{3,99},{4,100},{5,101},{6,102},{7,103},{8,104... | collective-permute-start | bytes 98312 | tf_op jit(solution)/shard_map/ppermute | solution.py:436
  19.6 7.5 %collective-permute-start.2 = (bf16[4,2,16,128]{3,2,1,0:T(8,128)(2,1)S(1)}, bf16[4,2,16,128]{3,2,1,0:T(8,128)(2,1)S(1)}, u32[]{:S(2)}, u32[]{:S(2)}) collective-permute-start(bf16[4,2,16,128]{3,2,1,0:T(8,128)(2,1)S(1)} %bitcast.25), channel_id=1, source_target_pairs={{32,96},{33,97},{34,98},{35,99},{36,100},{37,101},{38,102},{39,103... | collective-permute-start | bytes 98312 | tf_op jit(solution)/shard_map/ppermute | solution.py:436
  20.9 6.4 %collective-permute-start.3 = (bf16[4,2,16,128]{3,2,1,0:T(8,128)(2,1)S(1)}, bf16[4,2,16,128]{3,2,1,0:T(8,128)(2,1)S(1)}, u32[]{:S(2)}, u32[]{:S(2)}) collective-permute-start(bf16[4,2,16,128]{3,2,1,0:T(8,128)(2,1)S(1)} %bitcast.26), channel_id=1, source_target_pairs={{64,96},{65,97},{66,98},{67,99},{68,100},{69,101},{70,102},{71,103... | collective-permute-start | bytes 98312 | tf_op jit(solution)/shard_map/ppermute | solution.py:436
  27.3 7.2 %collective-permute-start.4 = (bf16[16,2,16,128]{3,2,1,0:T(8,128)(2,1)S(1)}, bf16[16,2,16,128]{3,2,1,0:T(8,128)(2,1)S(1)}, u32[]{:S(2)}, u32[]{:S(2)}) collective-permute-start(bf16[16,2,16,128]{3,2,1,0:T(8,128)(2,1)S(1)} %pad_maximum_fusion.1), channel_id=1, source_target_pairs={{96,97},{97,98},{98,99},{99,100},{100,101},{101,102},{102,103},{10... | collective-permute-start | bytes 393224 | tf_op jit(solution)/shard_map/ppermute | solution.py:439
  32.6 8.4 %collective-permute-start.5 = (bf16[16,2,16,128]{3,2,1,0:T(8,128)(2,1)S(1)}, bf16[16,2,16,128]{3,2,1,0:T(8,128)(2,1)S(1)}, u32[]{:S(2)}, u32[]{:S(2)}) collective-permute-start(bf16[16,2,16,128]{3,2,1,0:T(8,128)(2,1)S(1)} %pad_maximum_fusion.1), channel_id=1, source_target_pairs={{97,96},{98,97},{99,98},{100,99},{101,100},{102,101},{103,102},{10... | collective-permute-start | bytes 393224 | tf_op jit(solution)/shard_map/ppermute | solution.py:440
  42.4 0.7 collective-permute-start.6
  43.1 3.5 %collective-permute-start.12 = (bf16[256,2048]{1,0:T(8,128)(2,1)}, bf16[256,2048]{1,0:T(8,128)(2,1)S(1)}, u32[]{:S(2)}, u32[]{:S(2)}) collective-permute-start(bf16[256,2048]{1,0:T(8,128)(2,1)} %collective-permute-done.8.w2), channel_id=1, source_target_pairs={{0,8},{1,3},{2,10},{3,1},{4,12},{5,7},{6,14},{7,5},{8,0},{9,11},{1... | collective-permute-start | bytes 3145736 | tf_op jit(solution)/shard_map/ppermute | solution.py:422
  44.5 6.2 %copy-start.10 = (f32[384]{0:T(512)S(1)}, f32[384]{0:T(512)}, u32[]{:S(2)}) copy-start(f32[384]{0:T(512)} %param.27) | copy-start | bytes 4612
  44.5 2.2 %collective-permute-start.10 = (bf16[4,2,48,256]{3,2,1,0:T(8,128)(2,1)S(1)}, bf16[4,2,48,256]{3,2,1,0:T(8,128)(2,1)S(1)}, u32[]{:S(2)}, u32[]{:S(2)}) collective-permute-start(bf16[4,2,48,256]{3,2,1,0:T(8,128)(2,1)S(1)} %get-tuple-element.36), channel_id=1, source_target_pairs={{0,24},{1,7},{2,26},{3,5},{4,28},{5,3},{6,30},{7,1},{8,16},{9,15},... | collective-permute-start | bytes 589832 | tf_op jit(solution)/shard_map/ppermute | solution.py:422
  45.3 1.4 %collective-permute-start.11 = (bf16[4,2,48,256]{3,2,1,0:T(8,128)(2,1)S(1)}, bf16[4,2,48,256]{3,2,1,0:T(8,128)(2,1)S(1)}, u32[]{:S(2)}, u32[]{:S(2)}) collective-permute-start(bf16[4,2,48,256]{3,2,1,0:T(8,128)(2,1)S(1)} %get-tuple-element.37), channel_id=1, source_target_pairs={{0,16},{1,5},{2,18},{3,7},{4,20},{5,1},{6,22},{7,3},{8,24},{9,13},... | collective-permute-start | bytes 589832 | tf_op jit(solution)/shard_map/ppermute | solution.py:422
  46.0 0.7 collective-permute-start.9
  48.5 41.1 %collective-permute-start.13 = (bf16[2,48,2048]{2,1,0:T(8,128)(2,1)S(1)}, bf16[2,48,2048]{2,1,0:T(8,128)(2,1)S(1)}, u32[]{:S(2)}, u32[]{:S(2)}) collective-permute-start(bf16[2,48,2048]{2,1,0:T(8,128)(2,1)S(1)} %get-tuple-element.48), channel_id=1, source_target_pairs={{0,4},{1,17},{2,6},{3,19},{4,0},{5,21},{6,2},{7,23},{8,12},{9,25},... | collective-permute-start | bytes 1179656 | tf_op jit(solution)/shard_map/ppermute | solution.py:422
  49.2 40.4 %collective-permute-start.14 = (bf16[2,48,2048]{2,1,0:T(8,128)(2,1)S(1)}, bf16[2,48,2048]{2,1,0:T(8,128)(2,1)S(1)}, u32[]{:S(2)}, u32[]{:S(2)}) collective-permute-start(bf16[2,48,2048]{2,1,0:T(8,128)(2,1)S(1)} %get-tuple-element.49), channel_id=1, source_target_pairs={{0,6},{1,25},{2,4},{3,27},{4,2},{5,29},{6,0},{7,31},{8,14},{9,17},... | collective-permute-start | bytes 1179656 | tf_op jit(solution)/shard_map/ppermute | solution.py:422
  49.9 39.8 %collective-permute-start.15 = (bf16[2,48,2048]{2,1,0:T(8,128)(2,1)S(1)}, bf16[2,48,2048]{2,1,0:T(8,128)(2,1)S(1)}, u32[]{:S(2)}, u32[]{:S(2)}) collective-permute-start(bf16[2,48,2048]{2,1,0:T(8,128)(2,1)S(1)} %get-tuple-element.50), channel_id=1, source_target_pairs={{0,2},{1,9},{2,0},{3,11},{4,6},{5,13},{6,4},{7,15},{8,10},{9,1},{1... | collective-permute-start | bytes 1179656 | tf_op jit(solution)/shard_map/ppermute | solution.py:422
  51.3 38.4 %copy-start.5 = (s32[6]{0:T(128)S(1)}, s32[6]{0:T(128)}, u32[]{:S(2)}) copy-start(s32[6]{0:T(128)} %copy-done.4) | copy-start | bytes 76
  51.3 39.7 %copy-start.3 = (bf16[1,48,4096]{2,1,0:T(8,128)(2,1)S(1)}, bf16[1,48,4096]{2,1,0:T(8,128)(2,1)}, u32[]{:S(2)}) copy-start(bf16[1,48,4096]{2,1,0:T(8,128)(2,1)} %param.17) | copy-start | bytes 1179652
  51.3 39.7 %copy-start.6 = (f32[1,4096]{1,0:T(1,128)S(1)}, f32[1,4096]{1,0:T(1,128)}, u32[]{:S(2)}) copy-start(f32[1,4096]{1,0:T(1,128)} %gate_ref.1) | copy-start | bytes 49156
  90.2 0.7 collective-permute-start.16
  (5 other events, 15.1 us)
